TPU v7x, 32 devices: a whole 2x2x4 slice. The times are simulated.
32 devices in a mesh: dp: 8 (over y, x, core), tensor: 4 (over z).
Axes of the slice: x: 2, y: 2, z: 4, core: 2. Of those that a mesh axis runs over, the one named last changes fastest.
Arguments:
- block_in: float32 [8192, 1536], P(('dp', 'tensor')), may hold values from -6 to 6
- out_grad: float32 [8192, 1536], P(('dp', 'tensor')), may hold values from -6 to 6
- positions: int32 [8192], P('dp'), may hold values from 0 to 4096, as said below
- qkv_weight: float32 [1536, 2560], P('dp', 'tensor'), may hold values from -0.15625 to 0.15625
- qkv_first: float32 [1536, 2560], P('dp', 'tensor'), may hold values from -96 to 96
- qkv_second: float32 [1536, 2560], P('dp', 'tensor'), may hold values from 18.432 to 73.728
- out_weight: float32 [1536, 1536], P('tensor', 'dp'), may hold values from -0.875 to 0.875
- out_first: float32 [1536, 1536], P('tensor', 'dp'), may hold values from -8 to 8
- out_second: float32 [1536, 1536], P('tensor', 'dp'), may hold values from 0.18432 to 0.73728
- gate_up: float32 [2, 1536, 6912], P(None, 'dp', 'tensor'), may hold values from -0.15625 to 0.15625
- gate_up_first: float32 [2, 1536, 6912], P(None, 'dp', 'tensor'), may hold values from -16 to 16
- gate_up_second: float32 [2, 1536, 6912], P(None, 'dp', 'tensor'), may hold values from 0.73728 to 2.94912
- down_weight: float32 [6912, 1536], P('tensor', 'dp'), may hold values from -0.078125 to 0.078125
- down_first: float32 [6912, 1536], P('tensor', 'dp'), may hold values from -32 to 32
- down_second: float32 [6912, 1536], P('tensor', 'dp'), may hold values from 2.94912 to 11.79648
- norm_gains: float32 [3200], P(('dp', 'tensor')), may hold values from 0.5 to 1.5
- norm_gains_first: float32 [3200], P(('dp', 'tensor')), may hold values from -128 to 128
- norm_gains_second: float32 [3200], P(('dp', 'tensor')), may hold values from 32.768 to 131.072
Outputs:
- block_out: float32 [8192, 1536], P(('dp', 'tensor'))
- in_grad: float32 [8192, 1536], P(('dp', 'tensor'))
- qkv_weight_new: float32 [1536, 2560], P('dp', 'tensor')
- qkv_first_new: float32 [1536, 2560], P('dp', 'tensor')
- qkv_second_new: float32 [1536, 2560], P('dp', 'tensor')
- out_weight_new: float32 [1536, 1536], P('tensor', 'dp')
- out_first_new: float32 [1536, 1536], P('tensor', 'dp')
- out_second_new: float32 [1536, 1536], P('tensor', 'dp')
- gate_up_new: float32 [2, 1536, 6912], P(None, 'dp', 'tensor')
- gate_up_first_new: float32 [2, 1536, 6912], P(None, 'dp', 'tensor')
- gate_up_second_new: float32 [2, 1536, 6912], P(None, 'dp', 'tensor')
- down_weight_new: float32 [6912, 1536], P('tensor', 'dp')
- down_first_new: float32 [6912, 1536], P('tensor', 'dp')
- down_second_new: float32 [6912, 1536], P('tensor', 'dp')
- norm_gains_new: float32 [3200], P(('dp', 'tensor'))
- norm_gains_first_new: float32 [3200], P(('dp', 'tensor'))
- norm_gains_second_new: float32 [3200], P(('dp', 'tensor'))
Inputs may be any that keep to these rules, and one draw needn't show every extreme that they name: Within each sequence of 1024 tokens the positions rise by one inside a document and restart at 0 where a new document begins; the first document of a sequence may begin at a larger position.
All inputs are finite; a program needn't handle non-finite values.
Results may differ from a plain program's by a relative error of at most 0.023.
Values may be sent and summed in bfloat16 or wider, within the bound.
No kernel may reach another device: no remote copies, remote signals or barrier semaphores. Data moves between devices by JAX's collectives and lax.ppermute only.
A program may use at most 256 MiB of HBM per device.

v0:
```python
import jax
import jax.numpy as jnp
from jax import lax
from jax.sharding import PartitionSpec as P

HEAD_DIMENSION = 64
STEP = 10
QUERY_GROUP = 3


eps_norm = 1e-05
rope_base = 1000000.0
beta_one = 0.9
beta_two = 0.999
adam_eps = 1e-08
decay_matrix = 0.1
rate_matrix = 0.03
rate_output = 0.15
rate_gains = 0.8


def norm_rows(row_block, gain_vec):
    inverse = lax.rsqrt(jnp.mean(row_block * row_block, axis=-1, keepdims=True) + eps_norm)
    return row_block * inverse * gain_vec


def rope_angles(positions, head_size):
    inverse_freq = rope_base ** (-(jnp.arange(head_size // 2, dtype=jnp.float32) * 2.0) / head_size)
    return positions.astype(jnp.float32)[:, None] * inverse_freq[None, :]


def rotate(vectors, angles):
    half_size = vectors.shape[-1] // 2
    first_half = vectors[..., :half_size]
    second_half = vectors[..., half_size:]
    cos_part = jnp.cos(angles)
    sin_part = jnp.sin(angles)
    return jnp.concatenate(
        [
            first_half * cos_part - second_half * sin_part,
            second_half * cos_part + first_half * sin_part,
        ],
        axis=-1,
    )


def document_ids(positions):
    previous = jnp.concatenate([positions[:1] - 2, positions[:-1]])
    starts = (positions != previous + 1).astype(jnp.int32)
    return jnp.cumsum(starts)


def prepare(projected, gain_q, gain_k, angles):
    length = projected.shape[0]
    grouped_heads = projected.reshape(length, -1, QUERY_GROUP + 2, HEAD_DIMENSION)
    query_rows = grouped_heads[:, :, :QUERY_GROUP, :]
    key_heads = grouped_heads[:, :, QUERY_GROUP, :]
    value_heads = grouped_heads[:, :, QUERY_GROUP + 1, :]
    query_rows = rotate(norm_rows(query_rows, gain_q), angles[:, None, None, :])
    key_heads = rotate(norm_rows(key_heads, gain_k), angles[:, None, :])
    return (query_rows, key_heads, value_heads)


def block_mask(doc_ids, first_row, block_length):
    row_pos = first_row + jnp.arange(block_length, dtype=jnp.int32)
    row_docs = lax.dynamic_slice_in_dim(doc_ids, first_row, block_length)
    key_pos = jnp.arange(doc_ids.shape[0], dtype=jnp.int32)
    return (row_docs[:, None] == doc_ids[None, :]) & (key_pos[None, :] <= row_pos[:, None])


def adam_step(weight, first_old, second_old, gradient, step_rate, decay_rate):
    first_new = beta_one * first_old + (1.0 - beta_one) * gradient
    second_new = beta_two * second_old + (1.0 - beta_two) * gradient * gradient
    fix_one = 1.0 - beta_one**STEP
    fix_two = 1.0 - beta_two**STEP
    update = first_new / fix_one / (jnp.sqrt(second_new / fix_two) + adam_eps)
    return (weight - step_rate * (update + decay_rate * weight), first_new, second_new)


def shards(
    block_in,
    out_grad,
    positions,
    qkv_weight,
    qkv_first,
    qkv_second,
    out_weight,
    out_first,
    out_second,
    gate_up,
    gate_up_first,
    gate_up_second,
    down_weight,
    down_first,
    down_second,
    norm_gains,
    norm_gains_first,
    norm_gains_second,
):
    model_width = block_in.shape[1]
    gains_all = lax.all_gather(norm_gains, ("dp", "tensor"), axis=0, tiled=True)
    gain_attn = gains_all[:model_width]
    gain_q = gains_all[model_width : model_width + HEAD_DIMENSION]
    gain_k = gains_all[model_width + HEAD_DIMENSION : model_width + 2 * HEAD_DIMENSION]
    gain_ffn = gains_all[model_width + 2 * HEAD_DIMENSION :]
    w_qkv, w_out, w_gate_up, w_down = (
        lax.all_gather(qkv_weight.astype(jnp.bfloat16), "dp", axis=0, tiled=True),
        lax.all_gather(out_weight.astype(jnp.bfloat16), "dp", axis=1, tiled=True),
        lax.all_gather(gate_up.astype(jnp.bfloat16), "dp", axis=1, tiled=True),
        lax.all_gather(down_weight.astype(jnp.bfloat16), "dp", axis=1, tiled=True),
    )
    normed, pull_attn_norm = jax.vjp(norm_rows, block_in, gain_attn)
    normed_all = lax.all_gather(normed.astype(jnp.bfloat16), "tensor", axis=0, tiled=True)
    projected = jnp.dot(normed_all, w_qkv, preferred_element_type=jnp.float32)
    angles = rope_angles(positions, HEAD_DIMENSION)

    def prepare_local(projected_in, gain_q_in, gain_k_in):
        return prepare(projected_in, gain_q_in, gain_k_in, angles)

    (query_rows, key_heads, value_heads), pull_prepare = jax.vjp(
        prepare_local, projected, gain_q, gain_k
    )
    queries_b = query_rows.astype(jnp.bfloat16)
    keys_b = key_heads.astype(jnp.bfloat16)
    values_b = value_heads.astype(jnp.bfloat16)
    doc_ids = document_ids(positions)
    length = queries_b.shape[0]
    kv_local = queries_b.shape[1]
    block_length = min(512, length)
    count_of_blocks = length // block_length
    score_scale = HEAD_DIMENSION ** (-0.5)
    query_blocks = queries_b.reshape(
        count_of_blocks, block_length, kv_local, QUERY_GROUP, HEAD_DIMENSION
    )
    first_rows = jnp.arange(count_of_blocks, dtype=jnp.int32) * block_length

    def masked_scores(query_blk, first_row):
        allowed = block_mask(doc_ids, first_row, block_length)
        raw = (
            jnp.einsum("bkgd,skd->kgbs", query_blk, keys_b, preferred_element_type=jnp.float32)
            * score_scale
        )
        return jnp.where(allowed[None, None], raw, -1e30)

    def forward_block(inputs):
        query_blk, first_row = inputs
        scores = masked_scores(query_blk, first_row)
        row_max = jnp.max(scores, axis=-1, keepdims=True)
        weights = jnp.exp(scores - row_max)
        row_sum = jnp.sum(weights, axis=-1, keepdims=True)
        probs_low = (weights / row_sum).astype(jnp.bfloat16)
        output = jnp.einsum(
            "kgbs,skd->bkgd", probs_low, values_b, preferred_element_type=jnp.float32
        )
        return (output, row_max + jnp.log(row_sum))

    attended, log_sums = lax.map(forward_block, (query_blocks, first_rows))
    attended_b = attended.reshape(length, -1).astype(jnp.bfloat16)
    part_rows = attended_b
    middle = block_in + lax.psum_scatter(
        jnp.dot(part_rows, w_out, preferred_element_type=jnp.float32).astype(jnp.bfloat16),
        "tensor",
        scatter_dimension=0,
        tiled=True,
    ).astype(jnp.float32)
    normed_two, pull_ffn_norm = jax.vjp(norm_rows, middle, gain_ffn)
    normed_two_all = lax.all_gather(normed_two.astype(jnp.bfloat16), "tensor", axis=0, tiled=True)
    gate_out = jnp.dot(normed_two_all, w_gate_up[0], preferred_element_type=jnp.float32)
    up_out = jnp.dot(normed_two_all, w_gate_up[1], preferred_element_type=jnp.float32)
    gate_sig = jax.nn.sigmoid(gate_out)
    gate_act = gate_out * gate_sig
    hidden_b = (gate_act * up_out).astype(jnp.bfloat16)
    part_rows = hidden_b
    block_out = middle + lax.psum_scatter(
        jnp.dot(part_rows, w_down, preferred_element_type=jnp.float32).astype(jnp.bfloat16),
        "tensor",
        scatter_dimension=0,
        tiled=True,
    ).astype(jnp.float32)
    w_qkv, w_out, w_gate_up, w_down = (
        lax.all_gather(qkv_weight.astype(jnp.bfloat16), "dp", axis=0, tiled=True),
        lax.all_gather(out_weight.astype(jnp.bfloat16), "dp", axis=1, tiled=True),
        lax.all_gather(gate_up.astype(jnp.bfloat16), "dp", axis=1, tiled=True),
        lax.all_gather(down_weight.astype(jnp.bfloat16), "dp", axis=1, tiled=True),
    )
    grad_all = lax.all_gather(out_grad.astype(jnp.bfloat16), "tensor", axis=0, tiled=True)
    grad_down = jnp.einsum("sf,sd->fd", hidden_b, grad_all, preferred_element_type=jnp.float32)
    grad_hidden = jnp.einsum("sd,fd->sf", grad_all, w_down, preferred_element_type=jnp.float32)
    grad_gate = (grad_hidden * up_out * gate_sig * (1.0 + gate_out * (1.0 - gate_sig))).astype(
        jnp.bfloat16
    )
    grad_up = (grad_hidden * gate_act).astype(jnp.bfloat16)
    grad_gate_up = jnp.stack(
        [
            jnp.einsum("sd,sf->df", normed_two_all, grad_gate, preferred_element_type=jnp.float32),
            jnp.einsum("sd,sf->df", normed_two_all, grad_up, preferred_element_type=jnp.float32),
        ]
    )
    grad_normed_two = lax.psum_scatter(
        (
            jnp.einsum("sf,df->sd", grad_gate, w_gate_up[0], preferred_element_type=jnp.float32)
            + jnp.einsum("sf,df->sd", grad_up, w_gate_up[1], preferred_element_type=jnp.float32)
        ).astype(jnp.bfloat16),
        "tensor",
        scatter_dimension=0,
        tiled=True,
    ).astype(jnp.float32)
    grad_mid_norm, grad_gain_ffn = pull_ffn_norm(grad_normed_two)
    grad_middle = out_grad + grad_mid_norm
    grad_mid_all = lax.all_gather(grad_middle.astype(jnp.bfloat16), "tensor", axis=0, tiled=True)
    grad_out_w = jnp.einsum(
        "sh,sd->hd", attended_b, grad_mid_all, preferred_element_type=jnp.float32
    )
    grad_attended = jnp.einsum(
        "sd,hd->sh", grad_mid_all, w_out, preferred_element_type=jnp.float32
    ).astype(jnp.bfloat16)
    grad_att_blocks = grad_attended.reshape(
        count_of_blocks, block_length, kv_local, QUERY_GROUP, HEAD_DIMENSION
    )

    def backward_block(running, inputs):
        grad_keys, grad_values = running
        query_blk, grad_blk, log_blk, first_row = inputs
        scores = masked_scores(query_blk, first_row)
        probs = jnp.exp(scores - log_blk)
        probs_low = probs.astype(jnp.bfloat16)
        grad_values = grad_values + jnp.einsum(
            "kgbs,bkgd->skd", probs_low, grad_blk, preferred_element_type=jnp.float32
        )
        grad_probs = jnp.einsum(
            "bkgd,skd->kgbs", grad_blk, values_b, preferred_element_type=jnp.float32
        )
        row_dot = jnp.sum(probs * grad_probs, axis=-1, keepdims=True)
        grad_scores = (probs * (grad_probs - row_dot)).astype(jnp.bfloat16)
        grad_query = (
            jnp.einsum("kgbs,skd->bkgd", grad_scores, keys_b, preferred_element_type=jnp.float32)
            * score_scale
        )
        grad_keys = (
            grad_keys
            + jnp.einsum(
                "kgbs,bkgd->skd", grad_scores, query_blk, preferred_element_type=jnp.float32
            )
            * score_scale
        )
        return ((grad_keys, grad_values), grad_query)

    zero_heads = jnp.zeros((length, kv_local, HEAD_DIMENSION), jnp.float32)
    (grad_keys, grad_values), grad_queries = lax.scan(
        backward_block,
        (zero_heads, zero_heads),
        (query_blocks, grad_att_blocks, log_sums, first_rows),
    )
    grad_projected, grad_gain_q, grad_gain_k = pull_prepare(
        (
            grad_queries.reshape(length, kv_local, QUERY_GROUP, HEAD_DIMENSION),
            grad_keys,
            grad_values,
        )
    )
    grad_projected_b = grad_projected.astype(jnp.bfloat16)
    grad_qkv = jnp.einsum(
        "sd,sc->dc", normed_all, grad_projected_b, preferred_element_type=jnp.float32
    )
    part_rows = grad_projected_b
    grad_normed = lax.psum_scatter(
        jnp.einsum("sc,dc->sd", part_rows, w_qkv, preferred_element_type=jnp.float32).astype(
            jnp.bfloat16
        ),
        "tensor",
        scatter_dimension=0,
        tiled=True,
    ).astype(jnp.float32)
    grad_in_norm, grad_gain_attn = pull_attn_norm(grad_normed)
    in_grad = grad_middle + grad_in_norm
    gain_grads = lax.psum_scatter(
        jnp.concatenate([grad_gain_attn, grad_gain_q, grad_gain_k, grad_gain_ffn]),
        ("dp", "tensor"),
        scatter_dimension=0,
        tiled=True,
    )
    sum_qkv, sum_out, sum_gate_up, sum_down = (
        lax.psum_scatter(
            grad_qkv.astype(jnp.bfloat16), "dp", scatter_dimension=0, tiled=True
        ).astype(jnp.float32),
        lax.psum_scatter(
            grad_out_w.astype(jnp.bfloat16), "dp", scatter_dimension=1, tiled=True
        ).astype(jnp.float32),
        lax.psum_scatter(
            grad_gate_up.astype(jnp.bfloat16), "dp", scatter_dimension=1, tiled=True
        ).astype(jnp.float32),
        lax.psum_scatter(
            grad_down.astype(jnp.bfloat16), "dp", scatter_dimension=1, tiled=True
        ).astype(jnp.float32),
    )
    qkv_new = adam_step(qkv_weight, qkv_first, qkv_second, sum_qkv, rate_matrix, decay_matrix)
    out_new = adam_step(out_weight, out_first, out_second, sum_out, rate_output, decay_matrix)
    gate_up_new = adam_step(
        gate_up, gate_up_first, gate_up_second, sum_gate_up, rate_matrix, decay_matrix
    )
    down_new = adam_step(down_weight, down_first, down_second, sum_down, rate_matrix, decay_matrix)
    gains_new = adam_step(
        norm_gains, norm_gains_first, norm_gains_second, gain_grads, rate_gains, 0.0
    )
    return (
        block_out,
        in_grad,
        qkv_new[0],
        qkv_new[1],
        qkv_new[2],
        out_new[0],
        out_new[1],
        out_new[2],
        gate_up_new[0],
        gate_up_new[1],
        gate_up_new[2],
        down_new[0],
        down_new[1],
        down_new[2],
        gains_new[0],
        gains_new[1],
        gains_new[2],
    )


def solution(mesh):
    in_specs = (
        P(("dp", "tensor"), None),
        P(("dp", "tensor"), None),
        P("dp"),
        P("dp", "tensor"),
        P("dp", "tensor"),
        P("dp", "tensor"),
        P("tensor", "dp"),
        P("tensor", "dp"),
        P("tensor", "dp"),
        P(None, "dp", "tensor"),
        P(None, "dp", "tensor"),
        P(None, "dp", "tensor"),
        P("tensor", "dp"),
        P("tensor", "dp"),
        P("tensor", "dp"),
        P(("dp", "tensor")),
        P(("dp", "tensor")),
        P(("dp", "tensor")),
    )
    out_specs = (
        P(("dp", "tensor"), None),
        P(("dp", "tensor"), None),
        P("dp", "tensor"),
        P("dp", "tensor"),
        P("dp", "tensor"),
        P("tensor", "dp"),
        P("tensor", "dp"),
        P("tensor", "dp"),
        P(None, "dp", "tensor"),
        P(None, "dp", "tensor"),
        P(None, "dp", "tensor"),
        P("tensor", "dp"),
        P("tensor", "dp"),
        P("tensor", "dp"),
        P(("dp", "tensor")),
        P(("dp", "tensor")),
        P(("dp", "tensor")),
    )
    return jax.shard_map(shards, mesh=mesh, in_specs=in_specs, out_specs=out_specs, check_vma=False)
```

profile of v0, /device:TPU:0, one launch (start us, length us, event | category | flops | bytes accessed | tf_op | source)
XLA Modules:
  0.0 1071.4 jit_solution(11512685312843924535)
XLA Ops:
  7.3 1.9 convert_element_type.119
  10.1 42.1 %all-reduce.7 = f32[3200]{0:T(1024)S(1)} all-reduce(f32[3200]{0:T(1024)S(1)} %dynamic-update-slice), channel_id=1, replica_groups=mesh['dp'=8,'tensor'=4] {'dp','tensor'}, use_global_device_ids=true, to_apply=%add.7 | all-reduce | flops 3200 | bytes 25600
  58.8 60.2 %all-gather.9.cloned.1.call-done = bf16[1024,1536]{1,0:T(8,128)(2,1)} async-done(((bf16[256,1536]{1,0:T(8,128)(2,1)}), bf16[1024,1536]{1,0:T(8,128)(2,1)}) %all-gather.9.cloned.1.call-update) | async-done | bytes 3145744 | tf_op jit(solution)/shard_map/all_gather | solution.py:113
  119.0 4.7 fusion.97
  125.7 30.2 %while.27 = (s32[]{:T(128)}, bf16[2,512,2,3,64]{1,4,3,2,0:T(8,128)(2,1)}, f32[2,2,3,512,1]{3,2,1,4,0:T(4,128)S(1)}, s32[2]{0:T(128)S(1)}, s32[1024]{0:T(1024)S(1...) while((s32[]{:T(128)}, ...), condition=%wide.region_8.9_spmd, body=%wide.region_5.8_spmd.sunk | while | flops 844625408 | bytes 47974640 | solution.py:157
  129.6 2.3 bitcast_reduce_fusion.2
  131.9 3.6 fusion.147
  135.5 4.4 fusion.148
  144.7 2.3 bitcast_reduce_fusion.2
  146.9 3.6 fusion.147
  150.6 4.4 fusion.148
  155.9 2.0 copy.80
  158.9 5.0 convolution_convert_fusion.5
  164.2 58.8 %reduce-scatter.8.cloned.1.call-done = bf16[256,1536]{1,0:T(8,128)(2,1)} async-done(((bf16[1024,1536]{1,0:T(8,128)(2,1)}), bf16[256,1536]{1,0:T(8,128)(2,1)}) %reduce-scatter.8.cloned.1.call-update) | async-done | bytes 786448 | tf_op jit(solution)/shard_map/reduce_scatter | solution.py:160
  225.7 3.0 convert_element_type.128
  228.8 2.4 convert_element_type.133
  231.3 2.4 convert_element_type.130
  233.7 55.7 %all-gather.15.cloned.1.call-done = bf16[1024,1536]{1,0:T(8,128)(2,1)} async-done(((bf16[256,1536]{1,0:T(8,128)(2,1)}), bf16[1024,1536]{1,0:T(8,128)(2,1)}) %all-gather.15.cloned.1.call-update) | async-done | bytes 3145744 | tf_op jit(solution)/shard_map/all_gather | solution.py:167
  289.4 66.5 %all-gather.17.cloned.1.call-done = bf16[2,1536,1728]{2,1,0:T(8,128)(2,1)} async-done(((bf16[2,192,1728]{2,1,0:T(8,128)(2,1)}), bf16[2,1536,1728]{2,1,0:T(8,128)(2,1)}) %all-gather.17.cloned.1.call-update) | async-done | bytes 10616848 | tf_op jit(solution)/shard_map/all_gather | solution.py:109
  355.9 11.0 %fusion.58 = f32[1024,1728]{0,1:T(8,128)} fusion(bf16[1024,1536]{1,0:T(8,128)(2,1)} %all-gather.15.cloned.1.call-done, bf16[2,1536,1728]{2,1,0:T(8,128)(2,1)} %all-gather.17.cloned.1.call-done), kind=kOutput, calls=%fused_computation.79 | convolution fusion | flops 5435817984 | bytes 15728640 | tf_op jit(solution)/shard_map/dot_general | solution.py:169
  366.9 7.8 fusion.56
  374.6 46.9 %all-gather.21.cloned.1.call-done = bf16[1024,1536]{1,0:T(8,128)(2,1)} async-done(((bf16[256,1536]{1,0:T(8,128)(2,1)}), bf16[1024,1536]{1,0:T(8,128)(2,1)}) %all-gather.21.cloned.1.call-update) | async-done | bytes 3145744 | tf_op jit(solution)/shard_map/all_gather | solution.py:186
  421.5 43.4 %all-gather.19.cloned.1.call-done = bf16[1728,1536]{0,1:T(8,128)(2,1)} async-done(((bf16[1728,192]{0,1:T(8,128)(2,1)}), bf16[1728,1536]{0,1:T(8,128)(2,1)}) %all-gather.19.cloned.1.call-update) | async-done | bytes 5308432 | tf_op jit(solution)/shard_map/all_gather | solution.py:110
  464.9 17.5 %multiply_convert_fusion = (bf16[1024,1728]{0,1:T(8,128)(2,1)}, bf16[1024,1728]{0,1:T(8,128)(2,1)}, bf16[1024,1728]{0,1:T(8,128)(2,1)}) fusion(f32[1024,1728]{0,1:T(8,128)} %fusion.56, f32[1024,1728]{0,1:T(8,128)} %fusion.58, bf16[1024,1536]{1,0:T(8,128)(2,1)} %all-gather.21.cloned.1.call-done, bf16[1728,1536]{0,1:T(8,128)(2,1)} %all-gather.19.cloned.1.call-done), kind=kOutput, calls=%fused_computation.66 | convolution fusion | flops 5462360064 | bytes 33226752 | tf_op jit(solution)/shard_map/sd,fd->sf/dot_general | solution.py:188
  482.4 9.7 fusion.55
  492.1 10.0 add_convert_fusion
  502.1 60.4 %reduce-scatter.12.cloned.1.call-done = bf16[256,1536]{1,0:T(8,128)(2,1)} async-done(((bf16[1024,1536]{1,0:T(8,128)(2,1)}), bf16[256,1536]{1,0:T(8,128)(2,1)}) %reduce-scatter.12.cloned.1.call-update) | async-done | bytes 786448 | tf_op jit(solution)/shard_map/reduce_scatter | solution.py:199
  562.5 2.5 fusion.67
  567.1 8.7 fusion.54
  575.8 5.8 fusion.53
  581.7 4.8 pad_maximum_fusion
  586.4 27.6 %copy.84 = bf16[2,1536,1728]{2,0,1:T(2,128)(2,1)} copy(bf16[2,1536,1728]{1,2,0:T(8,128)(2,1)} %pad_maximum_fusion) | data formatting | bytes 21233664 | tf_op jit(solution)/shard_map/stack | solution.py:193
  614.1 10.2 convolution_convert_fusion.2
  624.4 6.3 all-gather.23.cloned.1.call-done
  630.7 4.0 convolution_convert_fusion.8
  636.6 89.9 %while.28 = (s32[]{:T(128)}, f32[1024,2,64]{0,2,1:T(8,128)S(1)}, f32[1024,2,64]{0,2,1:T(8,128)}, f32[2,512,2,3,64]{1,0,4,3,2:T(2,128)}, bf16[2,512,2,3,64]{1,4,3...) while((s32[]{:T(128)}, f32[1024,2,64]{0,2,1:T(8,128)S(1)}, ...), condition=%wide.region_16.17_spmd.clone, body=%wide.region_14.16_spmd.clone.sunk | while | flops 2062874112 | bytes 104958184 | solution.py:249
  642.5 5.1 fusion.162
  647.6 7.7 fusion.159
  655.3 6.9 fusion.160
  663.5 2.0 fusion.163
  666.4 15.0 %dynamic_update_slice.19 = f32[2,512,2,3,64]{1,0,4,3,2:T(2,128)} dynamic-update-slice(f32[2,512,2,3,64]{1,0,4,3,2:T(2,128)} %get-tuple-element.513, f32[1,512,2,3,64]{1,0,4,3,2:T(1,128)S(1)} %copy.124, s32[]{:T(128)S(6)} %copy.143, s32[]{:T(128)} %constant.52.clone.1..sunk.1, s32[]{:T(128)} %constant.52.clone.1..sunk.1, s32[]{:T(128)} %constant.52.clone.1..sunk.1, s32[]{:T(128)} %constant.52.clone.1..sunk.1) | dynamic-update-slice | bytes 1572868 | tf_op jit(solution)/shard_map/while/body/jit(dynamic_update_index_in_dim)/dynamic_update_slice | solution.py:157
  687.1 5.2 fusion.162
  692.3 7.7 fusion.159
  700.1 6.8 fusion.160
  708.2 2.0 fusion.163
  711.0 15.1 %dynamic_update_slice.19 = f32[2,512,2,3,64]{1,0,4,3,2:T(2,128)} dynamic-update-slice(f32[2,512,2,3,64]{1,0,4,3,2:T(2,128)} %get-tuple-element.513, f32[1,512,2,3,64]{1,0,4,3,2:T(1,128)S(1)} %copy.124, s32[]{:T(128)S(6)} %copy.143, s32[]{:T(128)} %constant.52.clone.1..sunk.1, s32[]{:T(128)} %constant.52.clone.1..sunk.1, s32[]{:T(128)} %constant.52.clone.1..sunk.1, s32[]{:T(128)} %constant.52.clone.1..sunk.1) | dynamic-update-slice | bytes 1572868 | tf_op jit(solution)/shard_map/while/body/jit(dynamic_update_index_in_dim)/dynamic_update_slice | solution.py:157
  726.5 2.7 reshape.377
  731.8 2.9 convolution_convert_fusion.7
  741.0 4.0 convolution_convert_fusion.6
  745.0 5.6 convolution_convert_fusion.3
  750.7 10.6 convolution_convert_fusion.4
  763.2 24.8 %all-reduce.12.cloned.1.call-done = bf16[2,1536,1728]{2,0,1:T(2,128)(2,1)} async-done(((bf16[2,1536,1728]{2,0,1:T(2,128)(2,1)}), bf16[2,1536,1728]{2,0,1:T(2,128)(2,1)}) %all-reduce.12.cloned.1.call-update) | async-done | bytes 10616848
  788.0 2.3 constant_dynamic-slice_fusion
  790.3 8.2 multiply_subtract_fusion
  798.6 51.1 %reduce-scatter.20.cloned.1.call-done = bf16[1728,192]{0,1:T(8,128)(2,1)} async-done(((bf16[1728,1536]{0,1:T(8,128)(2,1)}), bf16[1728,192]{0,1:T(8,128)(2,1)}) %reduce-scatter.20.cloned.1.call-update) | async-done | bytes 663568 | tf_op jit(solution)/shard_map/reduce_scatter | solution.py:292
  849.7 4.6 multiply_subtract_fusion.1
  854.3 36.0 %reduce-scatter.18.cloned.1.call-done = bf16[384,192]{0,1:T(8,128)(2,1)} async-done(((bf16[384,1536]{0,1:T(8,128)(2,1)}), bf16[384,192]{0,1:T(8,128)(2,1)}) %reduce-scatter.18.cloned.1.call-update) | async-done | bytes 147472 | tf_op jit(solution)/shard_map/reduce_scatter | solution.py:286
  890.3 2.0 multiply_subtract_fusion.3
  892.3 41.9 %reduce-scatter.16.cloned.1.call-done = bf16[192,640]{1,0:T(8,128)(2,1)} async-done(((bf16[1536,640]{1,0:T(8,128)(2,1)}), bf16[192,640]{1,0:T(8,128)(2,1)}) %reduce-scatter.16.cloned.1.call-update) | async-done | bytes 245776 | tf_op jit(solution)/shard_map/reduce_scatter | solution.py:283
  934.3 2.8 multiply_subtract_fusion.2
  937.1 59.6 %reduce-scatter.14.cloned.1.call-done = bf16[256,1536]{1,0:T(8,128)(2,1)} async-done(((bf16[1024,1536]{1,0:T(8,128)(2,1)}), bf16[256,1536]{1,0:T(8,128)(2,1)}) %reduce-scatter.14.cloned.1.call-update) | async-done | bytes 786448 | tf_op jit(solution)/shard_map/reduce_scatter | solution.py:266
  998.4 45.1 %all-reduce.9 = f32[3200]{0:T(1024)S(1)} all-reduce(f32[3200]{0:T(1024)S(1)} %concatenate.24), channel_id=10, replica_groups=mesh['dp'=8,'tensor'=4] {'dp','tensor'}, use_global_device_ids=true, to_apply=%region_29.30.clone | all-reduce | flops 3200 | bytes 25600
  1044.2 16.0 %reduce-scatter.10.cloned.1.call-done = bf16[256,1536]{1,0:T(8,128)(2,1)} async-done(((bf16[1024,1536]{1,0:T(8,128)(2,1)}), bf16[256,1536]{1,0:T(8,128)(2,1)}) %reduce-scatter.10.cloned.1.call-update) | async-done | bytes 786448 | tf_op jit(solution)/shard_map/reduce_scatter | solution.py:174
  1060.2 4.4 fusion.70
  (249 shorter events, 46.5 us)
Async XLA Ops:
  7.2 47.2 %copy-start = (f32[256,1536]{1,0:T(8,128)S(1)}, f32[256,1536]{1,0:T(8,128)}, u32[]{:S(2)}) copy-start(f32[256,1536]{1,0:T(8,128)} %param.22) | copy-start | bytes 4718596
  7.2 48.3 %copy-start.19 = (f32[384,192]{0,1:T(8,128)S(1)}, f32[384,192]{0,1:T(8,128)}, u32[]{:S(2)}) copy-start(f32[384,192]{0,1:T(8,128)} %param.28) | copy-start | bytes 884740
  7.2 51.6 %all-gather.11.cloned.1.call-start = ((), (), s32[]{:S(2)}) async-start(), calls=%async_computation.8 | async-start | bytes 2211840 | tf_op jit(solution)/shard_map/all_gather | solution.py:107
  9.2 47.1 %copy-start.38 = (s32[1024]{0:T(1024)S(1)}, s32[1024]{0:T(1024)}, u32[]{:S(2)}) copy-start(s32[1024]{0:T(1024)} %param.24) | copy-start | bytes 12292
  9.2 109.8 %all-gather.9.cloned.1.call-start = ((), (), s32[]{:S(2)}) async-start(), calls=%async_computation.7 | async-start | bytes 3932160 | tf_op jit(solution)/shard_map/all_gather | solution.py:113
  54.3 69.4 %copy-start.42 = (f32[256]{0:T(256)}, f32[256]{0:T(256)S(1)}, u32[]{:S(2)}) copy-start(f32[256]{0:T(256)S(1)} %fusion.82) | copy-start | bytes 3076
  54.3 69.4 %copy-start.34 = (f32[1536]{0:T(1024)}, f32[1536]{0:T(1024)S(1)}, u32[]{:S(2)}) copy-start(f32[1536]{0:T(1024)S(1)} %get-tuple-element.335) | copy-start | bytes 18436
  54.3 510.7 %copy-start.30 = (f32[1536]{0:T(1024)}, f32[1536]{0:T(1024)S(1)}, u32[]{:S(2)}) copy-start(f32[1536]{0:T(1024)S(1)} %get-tuple-element.336) | copy-start | bytes 18436
  55.5 103.5 %all-gather.13.cloned.1.call-start = ((), (), s32[]{:S(2)}) async-start(), calls=%async_computation.9 | async-start | bytes 1327104 | tf_op jit(solution)/shard_map/all_gather | solution.py:108
  56.2 166.8 %reduce-scatter.8.cloned.1.call-start = ((), (), s32[]{:S(2)}) async-start(), calls=%async_computation.10 | async-start | bytes 3932160 | tf_op jit(solution)/shard_map/reduce_scatter | solution.py:160
  56.9 67.3 %copy-start.48 = (f32[64]{0:T(128)}, f32[64]{0:T(128)S(1)}, u32[]{:S(2)}) copy-start(f32[64]{0:T(128)S(1)} %get-tuple-element.333) | copy-start | bytes 772
  56.9 67.4 %copy-start.50 = (f32[64]{0:T(128)}, f32[64]{0:T(128)S(1)}, u32[]{:S(2)}) copy-start(f32[64]{0:T(128)S(1)} %get-tuple-element.334) | copy-start | bytes 772
  58.7 66.6 %copy-start.13 = (f32[1024,32]{0,1:T(8,128)}, f32[1024,32]{0,1:T(8,128)S(1)}, u32[]{:S(2)}) copy-start(f32[1024,32]{0,1:T(8,128)S(1)} %get-tuple-element.337) | copy-start | bytes 393220
  58.8 66.6 %copy-start.15 = (f32[1024,32]{0,1:T(8,128)}, f32[1024,32]{0,1:T(8,128)S(1)}, u32[]{:S(2)}) copy-start(f32[1024,32]{0,1:T(8,128)S(1)} %get-tuple-element.338) | copy-start | bytes 393220
  131.9 3.6 copy-start.22
  146.9 3.6 copy-start.22
  155.9 8.1 copy-start.7
  163.9 125.4 %all-gather.15.cloned.1.call-start = ((), (), s32[]{:S(2)}) async-start(), calls=%async_computation.11 | async-start | bytes 3932160 | tf_op jit(solution)/shard_map/all_gather | solution.py:167
  224.5 340.5 %copy-start.40 = (f32[256]{0:T(256)}, f32[256]{0:T(256)S(1)}, u32[]{:S(2)}) copy-start(f32[256]{0:T(256)S(1)} %fusion.83) | copy-start | bytes 3076
  225.7 130.2 %all-gather.17.cloned.1.call-start = ((), (), s32[]{:S(2)}) async-start(), calls=%async_computation.12 | async-start | bytes 12386304 | tf_op jit(solution)/shard_map/all_gather | solution.py:109
  228.8 192.8 %all-gather.21.cloned.1.call-start = ((), (), s32[]{:S(2)}) async-start(), calls=%async_computation.15 | async-start | bytes 3932160 | tf_op jit(solution)/shard_map/all_gather | solution.py:186
  231.2 233.7 %all-gather.19.cloned.1.call-start = ((), (), s32[]{:S(2)}) async-start(), calls=%async_computation.13 | async-start | bytes 6193152 | tf_op jit(solution)/shard_map/all_gather | solution.py:110
  233.6 328.8 %reduce-scatter.12.cloned.1.call-start = ((), (), s32[]{:S(2)}) async-start(), calls=%async_computation.16 | async-start | bytes 3932160 | tf_op jit(solution)/shard_map/reduce_scatter | solution.py:199
  355.9 11.0 %copy-start.55 = (bf16[2,1536,1728]{2,1,0:T(8,128)(2,1)S(1)}, bf16[2,1536,1728]{2,1,0:T(8,128)(2,1)}, u32[]{:S(2)}) copy-start(bf16[2,1536,1728]{2,1,0:T(8,128)(2,1)} %all-gather.17.cloned.1.call-done) | copy-start | bytes 31850500
  355.9 11.0 %copy-start.58 = (bf16[1024,1536]{1,0:T(8,128)(2,1)S(1)}, bf16[1024,1536]{1,0:T(8,128)(2,1)}, u32[]{:S(2)}) copy-start(bf16[1024,1536]{1,0:T(8,128)(2,1)} %all-gather.15.cloned.1.call-done) | copy-start | bytes 9437188
  482.4 9.7 copy-start.62
  502.1 128.7 %all-gather.23.cloned.1.call-start = ((), (), s32[]{:S(2)}) async-start(), calls=%async_computation.17 | async-start | bytes 3932160 | tf_op jit(solution)/shard_map/all_gather | solution.py:210
  562.5 3.1 copy-start.6
  562.5 3.1 copy-start.9
  567.0 221.0 %all-reduce.12.cloned.1.call-start = ((), (), s32[]{:S(2)}) async-start(), calls=%async_computation.22 | async-start | bytes 22020096
  567.1 8.7 copy-start.59
  567.1 8.7 copy-start.61
  614.1 235.7 %reduce-scatter.20.cloned.1.call-start = ((), (), s32[]{:S(2)}) async-start(), calls=%async_computation.21 | async-start | bytes 6193152 | tf_op jit(solution)/shard_map/reduce_scatter | solution.py:292
  624.4 265.9 %reduce-scatter.18.cloned.1.call-start = ((), (), s32[]{:S(2)}) async-start(), calls=%async_computation.20 | async-start | bytes 1327104 | tf_op jit(solution)/shard_map/reduce_scatter | solution.py:286
  731.8 3.0 copy-start.3
  731.8 3.0 copy-start.33
  731.8 3.0 copy-start.49
  731.8 4.4 copy-start.37
  731.8 4.5 copy-start.25
  731.8 4.5 copy-start.51
  734.7 3.3 copy-start.27
  734.7 199.5 %reduce-scatter.16.cloned.1.call-start = ((), (), s32[]{:S(2)}) async-start(), calls=%async_computation.19 | async-start | bytes 2211840 | tf_op jit(solution)/shard_map/reduce_scatter | solution.py:283
  734.8 3.3 copy-start.17
  734.8 3.3 copy-start.18
  734.8 3.4 copy-start.11
  745.0 251.8 %reduce-scatter.14.cloned.1.call-start = ((), (), s32[]{:S(2)}) async-start(), calls=%async_computation.18 | async-start | bytes 3932160 | tf_op jit(solution)/shard_map/reduce_scatter | solution.py:266
  750.7 309.5 %reduce-scatter.10.cloned.1.call-start = ((), (), s32[]{:S(2)}) async-start(), calls=%async_computation.14 | async-start | bytes 3932160 | tf_op jit(solution)/shard_map/reduce_scatter | solution.py:174
  790.3 59.4 %copy-start.12 = (f32[1728,192]{0,1:T(8,128)S(1)}, f32[1728,192]{0,1:T(8,128)}, u32[]{:S(2)}) copy-start(f32[1728,192]{0,1:T(8,128)} %param.34) | copy-start | bytes 3981316
  798.6 91.7 %copy-start.20 = (f32[384,192]{0,1:T(8,128)S(1)}, f32[384,192]{0,1:T(8,128)}, u32[]{:S(2)}) copy-start(f32[384,192]{0,1:T(8,128)} %param.28) | copy-start | bytes 884740
  798.6 91.7 %copy-start.28 = (f32[384,192]{0,1:T(8,128)S(1)}, f32[384,192]{0,1:T(8,128)}, u32[]{:S(2)}) copy-start(f32[384,192]{0,1:T(8,128)} %param.29) | copy-start | bytes 884740
  798.6 91.7 %copy-start.29 = (f32[384,192]{0,1:T(8,128)S(1)}, f32[384,192]{0,1:T(8,128)}, u32[]{:S(2)}) copy-start(f32[384,192]{0,1:T(8,128)} %param.30) | copy-start | bytes 884740
  854.3 142.4 %copy-start.1 = (f32[256,1536]{1,0:T(8,128)S(1)}, f32[256,1536]{1,0:T(8,128)}, u32[]{:S(2)}) copy-start(f32[256,1536]{1,0:T(8,128)} %param.22) | copy-start | bytes 4718596
  854.3 142.4 %copy-start.35 = (f32[1536]{0:T(1024)S(1)}, f32[1536]{0:T(1024)}, u32[]{:S(2)}) copy-start(f32[1536]{0:T(1024)} %copy-done.34) | copy-start | bytes 18436
  854.3 142.4 %copy-start.43 = (f32[256]{0:T(256)S(1)}, f32[256]{0:T(256)}, u32[]{:S(2)}) copy-start(f32[256]{0:T(256)} %copy-done.42) | copy-start | bytes 3076
  892.3 106.1 %copy-start.39 = (f32[1536]{0:T(1024)S(1)}, f32[1536]{0:T(1024)}, u32[]{:S(2)}) copy-start(f32[1536]{0:T(1024)} %get-tuple-element.257) | copy-start | bytes 18436
  892.3 151.2 %copy-start.47 = (f32[256]{0:T(256)S(1)}, f32[256]{0:T(256)}, u32[]{:S(2)}) copy-start(f32[256]{0:T(256)} %copy-done.46) | copy-start | bytes 3076
  892.3 151.3 %copy-start.52 = (f32[100]{0:T(128)S(1)}, f32[100]{0:T(128)}, u32[]{:S(2)}) copy-start(f32[100]{0:T(128)} %param.37) | copy-start | bytes 1204
  892.3 151.3 %copy-start.53 = (f32[100]{0:T(128)S(1)}, f32[100]{0:T(128)}, u32[]{:S(2)}) copy-start(f32[100]{0:T(128)} %param.38) | copy-start | bytes 1204
  892.3 151.3 %copy-start.54 = (f32[100]{0:T(128)S(1)}, f32[100]{0:T(128)}, u32[]{:S(2)}) copy-start(f32[100]{0:T(128)} %param.39) | copy-start | bytes 1204
  892.3 167.9 %copy-start.5 = (bf16[256,1536]{1,0:T(8,128)(2,1)S(1)}, bf16[256,1536]{1,0:T(8,128)(2,1)}, u32[]{:S(2)}) copy-start(bf16[256,1536]{1,0:T(8,128)(2,1)} %reduce-scatter.8.cloned.1.call-done) | copy-start | bytes 2359300
  892.3 167.9 %copy-start.10 = (bf16[256,1536]{1,0:T(8,128)(2,1)S(1)}, bf16[256,1536]{1,0:T(8,128)(2,1)}, u32[]{:S(2)}) copy-start(bf16[256,1536]{1,0:T(8,128)(2,1)} %reduce-scatter.12.cloned.1.call-done) | copy-start | bytes 2359300
  892.3 167.9 %copy-start.31 = (f32[1536]{0:T(1024)S(1)}, f32[1536]{0:T(1024)}, u32[]{:S(2)}) copy-start(f32[1536]{0:T(1024)} %copy-done.30) | copy-start | bytes 18436
  892.3 167.9 %copy-start.41 = (f32[256]{0:T(256)S(1)}, f32[256]{0:T(256)}, u32[]{:S(2)}) copy-start(f32[256]{0:T(256)} %copy-done.40) | copy-start | bytes 3076
  892.3 167.9 %copy-start.45 = (f32[256]{0:T(256)S(1)}, f32[256]{0:T(256)}, u32[]{:S(2)}) copy-start(f32[256]{0:T(256)} %copy-done.44) | copy-start | bytes 3076
  (17 other events, 26.5 us)
Sparse Core Ops, SparseCore 0:
  10.5 30.2 all-gather.10
  55.6 63.3 all-gather.8
  121.4 22.7 all-gather.12
  164.1 58.8 reduce-scatter.7
  225.8 63.5 all-gather.14
  291.7 64.1 all-gather.16
  358.0 63.4 all-gather.20
  424.0 40.8 all-gather.18
  502.2 60.2 reduce-scatter.11
  567.2 63.5 all-gather.22
  634.3 153.7 all-reduce.11
  791.7 57.9 reduce-scatter.19
  853.5 36.7 reduce-scatter.17
  893.9 40.2 reduce-scatter.15
  936.4 60.2 reduce-scatter.13
  998.9 61.2 reduce-scatter.9
where the time goes:
time: 1080 us; the launch traced here: 1070 us
  waiting for transfers between devices  628 us (58%)
  matrix products  167 us (15%)
  blocking collectives  87.2 us (8%)
  other arithmetic  83.7 us (8%)
  local copies, waits for them, and re-layouts  79.9 us (7%)
  between operations  16.3 us (2%)
    unnamed x2, blocking collectives  87.2 us
    all_gather x1, waiting for transfers between devices, shards(): lax.all_gather(gate_up.astype(jnp.bfloat16), 'dp', axis=1, tiled=True)  66.5 us
    reduce_scatter x1, waiting for transfers between devices, shards(): lax.psum_scatter((jnp.einsum('sf,df->sd', grad_gate, w_gate_up[0], prefer...  60.4 us
    all_gather x1, waiting for transfers between devices, shards(): lax.all_gather(normed.astype(jnp.bfloat16), 'tensor', axis=0, tiled=True)  60.2 us
    reduce_scatter x1, waiting for transfers between devices, shards(): lax.psum_scatter(jnp.einsum('sc,dc->sd', part_rows, w_qkv, preferred_elem...  59.6 us
    reduce_scatter x1, waiting for transfers between devices, shards(): lax.psum_scatter(jnp.dot(part_rows, w_out, preferred_element_type=jnp.flo...  58.8 us
    all_gather x1, waiting for transfers between devices, shards(): lax.all_gather(normed_two.astype(jnp.bfloat16), 'tensor', axis=0, tiled=T...  55.7 us
    reduce_scatter x1, waiting for transfers between devices, shards(): lax.psum_scatter(grad_down.astype(jnp.bfloat16), 'dp', scatter_dimension=...  51.1 us
  transfers between devices with their start and end apart: 16, of which 14 were waited for; matrix products, arithmetic and copies ran while one was open for 25% of the time, Pallas kernels for 0%

commit v1 on v0

v1 whole, which is shorter than its diff:
```python
import functools

import jax
import jax.numpy as jnp
from jax import lax
from jax.experimental import pallas as pl
from jax.experimental.pallas import tpu as pltpu
from jax.sharding import PartitionSpec as P

HEAD_DIMENSION = 64
STEP = 10
QUERY_GROUP = 3
AXES = ("dp", "tensor")

eps_norm = 1e-05
rope_base = 1000000.0
beta_one = 0.9
beta_two = 0.999
adam_eps = 1e-08
decay_matrix = 0.1
rate_matrix = 0.03
rate_output = 0.15
rate_gains = 0.8
bf16 = jnp.bfloat16
f32 = jnp.float32
VMEM_LIMIT = 48 * 1024 * 1024
SMALL = pl.CostEstimate(flops=1000, bytes_accessed=1000, transcendentals=0)


def dot(left, right, left_dim, right_dim):
    return lax.dot_general(
        left, right, (((left_dim,), (right_dim,)), ((), ())), preferred_element_type=f32
    )


def norm_rows(row_block, gain_vec):
    inverse = lax.rsqrt(jnp.mean(row_block * row_block, axis=-1, keepdims=True) + eps_norm)
    return row_block * inverse * gain_vec


def rope_tables(positions, head_size):
    inverse_freq = rope_base ** (-(jnp.arange(head_size // 2, dtype=f32) * 2.0) / head_size)
    angles = positions.astype(f32)[:, None] * inverse_freq[None, :]
    cos_part, sin_part = jnp.cos(angles), jnp.sin(angles)
    return (
        jnp.concatenate([cos_part, cos_part], axis=1),
        jnp.concatenate([-sin_part, sin_part], axis=1),
    )


def adam_step(weight, first_old, second_old, gradient, step_rate, decay_rate):
    first_new = beta_one * first_old + (1.0 - beta_one) * gradient
    second_new = beta_two * second_old + (1.0 - beta_two) * gradient * gradient
    fix_one = 1.0 - beta_one**STEP
    fix_two = 1.0 - beta_two**STEP
    update = first_new / fix_one / (jnp.sqrt(second_new / fix_two) + adam_eps)
    return (weight - step_rate * (update + decay_rate * weight), first_new, second_new)


def swap_halves(value):
    half = value.shape[1] // 2
    return jnp.concatenate([value[:, half:], value[:, :half]], axis=1)


def as_row(column):
    return jnp.broadcast_to(column, (column.shape[0], 128)).T[:1, :]


def place_parts(place_ref, part_refs, whole_ref, scale):
    rows = part_refs[0].shape[0]
    for j, part_ref in enumerate(part_refs):
        at_row = pl.multiple_of((j ^ place_ref[0]) * rows, rows)
        value = part_ref[...]
        if scale is not None:
            value = (value.astype(f32) * scale).astype(bf16)
        whole_ref[pl.ds(at_row, rows), :] = value


def attention_forward_kernel(
    place_ref,
    part_0,
    part_1,
    part_2,
    part_3,
    gain_ref,
    head_gain_ref,
    weight_ref,
    cos_ref,
    sin_ref,
    start_ref,
    normed_ref,
    projected_ref,
    q_ref,
    k_ref,
    v_ref,
    out_ref,
    lse_ref,
):
    size = HEAD_DIMENSION
    heads, length, _ = q_ref.shape
    group = QUERY_GROUP
    kv = heads // group
    block = min(256, length)
    place_parts(place_ref, (part_0, part_1, part_2, part_3), normed_ref, gain_ref[...])
    for i in range(length // block):
        here = pl.ds(i * block, block)
        projected = dot(normed_ref[here, :], weight_ref[:, : projected_ref.shape[1]], 1, 0)
        projected_ref[here, :] = projected
        cos_part, sin_part = cos_ref[here, :], sin_ref[here, :]
        for j in range(kv):
            for g in range(group + 2):
                column = (j * (group + 2) + g) * size
                raw = projected[:, column : column + size]
                if g == group + 1:
                    v_ref[j, here, :] = raw.astype(bf16)
                    continue
                inverse = lax.rsqrt(jnp.mean(raw * raw, axis=1, keepdims=True) + eps_norm)
                gain = head_gain_ref[:1, :] if g < group else head_gain_ref[1:, :]
                normed = raw * inverse * gain
                turned = (normed * cos_part + swap_halves(normed) * sin_part).astype(bf16)
                if g < group:
                    q_ref[j * group + g, here, :] = turned * jnp.asarray(size**-0.5, bf16)
                else:
                    k_ref[j, here, :] = turned
    row_at = lax.broadcasted_iota(jnp.int32, (block, block), 0)
    col_at = lax.broadcasted_iota(jnp.int32, (block, block), 1)
    causal = jnp.concatenate([col_at <= row_at] * group, axis=0)
    col_all = lax.broadcasted_iota(jnp.int32, (group * block, block), 1)
    ones = jnp.ones((block, size), bf16)
    for j in range(kv):
        for i in range(length // block):
            here = pl.ds(i * block, block)
            queries = jnp.concatenate(
                [q_ref[j * group + g, here, :] for g in range(group)], axis=0
            )
            start = jnp.concatenate([start_ref[here, :]] * group, axis=0)
            total = jnp.zeros((group * block, 2 * size), f32)
            for b in range(i + 1):
                there = pl.ds(b * block, block)
                scores = dot(queries, k_ref[j, there, :], 1, 1)
                allowed = col_all >= start - b * block
                if b == i:
                    allowed = allowed & causal
                weights = jnp.where(allowed, jnp.exp(scores), 0.0).astype(bf16)
                values = jnp.concatenate([v_ref[j, there, :], ones], axis=1)
                total = total + dot(weights, values, 1, 0)
            row_sum = total[:, size : size + 1]
            output = (total[:, :size] / row_sum).astype(bf16)
            log_sum = jnp.log(row_sum)
            for g in range(group):
                h = j * group + g
                part = slice(g * block, (g + 1) * block)
                out_ref[here, h * size : (h + 1) * size] = output[part]
                lse_ref[h, :, here] = as_row(log_sum[part])


def attention_forward(place, parts, gain_attn, head_gains, weight, tables, start):
    rows, width = parts[0].shape
    length = 4 * rows
    size = HEAD_DIMENSION
    kv = weight.shape[1] // ((2 * QUERY_GROUP + 2) * size)
    heads = kv * QUERY_GROUP
    vmem = pl.BlockSpec(memory_space=pltpu.VMEM)
    return pl.pallas_call(
        attention_forward_kernel,
        in_specs=[pl.BlockSpec(memory_space=pltpu.SMEM)] + [vmem] * 10,
        out_specs=(vmem,) * 7,
        out_shape=(
            jax.ShapeDtypeStruct((length, width), bf16),
            jax.ShapeDtypeStruct((length, (heads + 2 * kv) * size), f32),
            jax.ShapeDtypeStruct((heads, length, size), bf16),
            jax.ShapeDtypeStruct((kv, length, size), bf16),
            jax.ShapeDtypeStruct((kv, length, size), bf16),
            jax.ShapeDtypeStruct((length, heads * size), bf16),
            jax.ShapeDtypeStruct((heads, 1, length), f32),
        ),
        compiler_params=pltpu.CompilerParams(vmem_limit_bytes=VMEM_LIMIT),
        cost_estimate=SMALL,
    )(place, *parts, gain_attn, head_gains, weight, *tables, start)


def attention_turn_kernel(
    place_ref, part_0, part_1, part_2, part_3, weight_ref, out_ref, grads_ref, dot_ref, dw_ref, whole_ref
):
    size = HEAD_DIMENSION
    place_parts(place_ref, (part_0, part_1, part_2, part_3), whole_ref, None)
    heads, length, _ = grads_ref.shape
    block = min(256, length)
    for i in range(length // block):
        here = pl.ds(i * block, block)
        grads = dot(whole_ref[here, :], weight_ref[...], 1, 0).astype(bf16)
        products = grads.astype(f32) * out_ref[here, :].astype(f32)
        for h in range(heads):
            columns = slice(h * size, (h + 1) * size)
            grads_ref[h, here, :] = grads[:, columns]
            dot_ref[h, :, here] = as_row(jnp.sum(products[:, columns], axis=1, keepdims=True))
    dw_ref[...] = dot(whole_ref[...], out_ref[...], 0, 0).astype(bf16)


def attention_turn(place, parts, weight, attended):
    rows, width = parts[0].shape
    length, columns = attended.shape
    heads = columns // HEAD_DIMENSION
    vmem = pl.BlockSpec(memory_space=pltpu.VMEM)
    return pl.pallas_call(
        attention_turn_kernel,
        in_specs=[pl.BlockSpec(memory_space=pltpu.SMEM)] + [vmem] * 6,
        out_specs=(vmem,) * 3,
        out_shape=(
            jax.ShapeDtypeStruct((heads, length, HEAD_DIMENSION), bf16),
            jax.ShapeDtypeStruct((heads, 1, length), f32),
            jax.ShapeDtypeStruct((width, columns), bf16),
        ),
        scratch_shapes=[pltpu.VMEM((length, width), bf16)],
        compiler_params=pltpu.CompilerParams(vmem_limit_bytes=VMEM_LIMIT),
        cost_estimate=SMALL,
    )(place, *parts, weight, attended)


def attention_backward_kernel(
    q_ref,
    k_ref,
    v_ref,
    g_ref,
    lse_ref,
    dot_ref,
    start_ref,
    projected_ref,
    head_gain_ref,
    cos_ref,
    sin_ref,
    weight_ref,
    normed_ref,
    gain_ref,
    back_ref,
    part_ref,
    head_sum_ref,
    gain_sum_ref,
    dq_ref,
    dk_ref,
    dv_ref,
):
    size = HEAD_DIMENSION
    heads, length, _ = q_ref.shape
    group = QUERY_GROUP
    kv = heads // group
    block = min(256, length)
    lanes = group * block
    key_at = lax.broadcasted_iota(jnp.int32, (block, block), 0)
    row_at = lax.broadcasted_iota(jnp.int32, (block, block), 1)
    causal = jnp.concatenate([key_at <= row_at] * group, axis=1)
    key_all = lax.broadcasted_iota(jnp.int32, (block, lanes), 0)
    dk_ref[...] = jnp.zeros_like(dk_ref)
    dv_ref[...] = jnp.zeros_like(dv_ref)
    head_sum_ref[...] = jnp.zeros_like(head_sum_ref)
    gain_sum_ref[...] = jnp.zeros_like(gain_sum_ref)
    for j in range(kv):
        for i in range(length // block):
            here = pl.ds(i * block, block)
            head = [j * group + g for g in range(group)]
            queries = jnp.concatenate([q_ref[h, here, :] for h in head], axis=0)
            grads = jnp.concatenate([g_ref[h, here, :] for h in head], axis=0)
            lse = jnp.concatenate([lse_ref[h, :, here] for h in head], axis=1)
            row_dot = jnp.concatenate([dot_ref[h, :, here] for h in head], axis=1)
            start = jnp.concatenate([start_ref[:, here]] * group, axis=1)
            dq = jnp.zeros((size, lanes), f32)
            for b in range(i + 1):
                there = pl.ds(b * block, block)
                keys = k_ref[j, there, :]
                scores = dot(keys, queries, 1, 1)
                allowed = key_all >= start - b * block
                if b == i:
                    allowed = allowed & causal
                probs = jnp.where(allowed, jnp.exp(scores - lse), 0.0)
                grad_probs = dot(v_ref[j, there, :], grads, 1, 1)
                grad_scores = (probs * (grad_probs - row_dot)).astype(bf16)
                dv_ref[j, there, :] += dot(probs.astype(bf16), grads, 1, 0)
                dk_ref[j, there, :] += dot(grad_scores, queries, 1, 0)
                dq = dq + dot(keys, grad_scores, 0, 0)
            for g in range(group):
                dq_ref[head[g], here, :] = dq[:, g * block : (g + 1) * block].T * size**-0.5
    for i in range(length // block):
        here = pl.ds(i * block, block)
        cos_part, sin_part = cos_ref[here, :], sin_ref[here, :]
        for j in range(kv):
            for g in range(group + 2):
                column = (j * (group + 2) + g) * size
                if g == group + 1:
                    back = dv_ref[j, here, :]
                else:
                    which = 0 if g < group else 1
                    grad = dq_ref[j * group + g, here, :] if g < group else dk_ref[j, here, :]
                    grad = grad * cos_part + swap_halves(grad * sin_part)
                    raw = projected_ref[here, column : column + size]
                    inverse = lax.rsqrt(jnp.mean(raw * raw, axis=1, keepdims=True) + eps_norm)
                    scaled = raw * inverse
                    head_sum_ref[which : which + 1, :] += jnp.sum(
                        grad * scaled, axis=0, keepdims=True
                    )
                    weighted = grad * head_gain_ref[which : which + 1, :]
                    back = inverse * (
                        weighted - scaled * jnp.mean(weighted * scaled, axis=1, keepdims=True)
                    )
                back_ref[here, column : column + size] = back.astype(bf16)
        term = dot(back_ref[here, :], weight_ref[:, : back_ref.shape[1]], 1, 1)
        gain_sum_ref[...] += jnp.sum(
            term * normed_ref[here, :].astype(f32), axis=0, keepdims=True
        )
        part_ref[here, :] = term.astype(bf16)
    gain_sum_ref[...] = gain_sum_ref[...] / gain_ref[...]


def attention_backward(
    queries, keys, values, grads, lse, row_dot, start, projected, head_gains, tables, weight, normed, gain
):
    heads, length, size = queries.shape
    kv = keys.shape[0]
    width = normed.shape[1]
    vmem = pl.BlockSpec(memory_space=pltpu.VMEM)
    return pl.pallas_call(
        attention_backward_kernel,
        in_specs=[vmem] * 14,
        out_specs=(vmem,) * 4,
        out_shape=(
            jax.ShapeDtypeStruct(projected.shape, bf16),
            jax.ShapeDtypeStruct((length, width), bf16),
            jax.ShapeDtypeStruct((2, size), f32),
            jax.ShapeDtypeStruct((1, width), f32),
        ),
        scratch_shapes=[
            pltpu.VMEM((heads, length, size), f32),
            pltpu.VMEM((kv, length, size), f32),
            pltpu.VMEM((kv, length, size), f32),
        ],
        compiler_params=pltpu.CompilerParams(vmem_limit_bytes=VMEM_LIMIT),
        cost_estimate=SMALL,
    )(
        queries, keys, values, grads, lse, row_dot, start, projected, head_gains, *tables, weight, normed, gain
    )


TILE = 256


def pack_units_kernel(both_ref, down_ref, out_ref):
    columns = both_ref.shape[2]
    rows = both_ref.shape[1]
    for i in range(out_ref.shape[1] // (3 * TILE)):
        first, last = i * TILE, min(columns, (i + 1) * TILE)
        parts = (both_ref[0, :, first:last], both_ref[1, :, first:last], down_ref[:, first:last])
        for k, part in enumerate(parts):
            if last - first < TILE:
                part = jnp.concatenate(
                    [part, jnp.zeros((rows, TILE - (last - first)), f32)], axis=1
                )
            at_column = (3 * i + k) * TILE
            out_ref[:, at_column : at_column + TILE] = part.astype(bf16)


def pack_units(gate_up, down):
    rows, columns = gate_up.shape[1:]
    steps = -(-columns // TILE)
    vmem = pl.BlockSpec(memory_space=pltpu.VMEM)
    return pl.pallas_call(
        pack_units_kernel,
        in_specs=[vmem, vmem],
        out_specs=vmem,
        out_shape=jax.ShapeDtypeStruct((rows, steps * 3 * TILE), bf16),
        compiler_params=pltpu.CompilerParams(vmem_limit_bytes=VMEM_LIMIT),
        cost_estimate=SMALL,
    )(gate_up, down)


def adam_kernel(weight_ref, first_ref, second_ref, sum_ref, *out_refs):
    gradient = sum_ref[...].astype(f32).reshape(weight_ref.shape)
    new = adam_step(
        weight_ref[...], first_ref[...], second_ref[...], gradient, rate_matrix, decay_matrix
    )
    for ref, value in zip(out_refs, new):
        ref[...] = value


def adam_units(weight, first, second, summed):
    parts, rows, columns = weight.shape
    state = pl.BlockSpec((1, rows, TILE), lambda p, i: (p, 0, i))
    return pl.pallas_call(
        adam_kernel,
        grid=(parts, -(-columns // TILE)),
        in_specs=[state] * 3 + [pl.BlockSpec((rows, TILE), lambda p, i: (0, parts * i + p))],
        out_specs=(state,) * 3,
        out_shape=(jax.ShapeDtypeStruct(weight.shape, f32),) * 3,
        compiler_params=pltpu.CompilerParams(vmem_limit_bytes=VMEM_LIMIT),
        cost_estimate=SMALL,
    )(weight, first, second, summed)


def units_forward_kernel(rows_ref, grad_ref, units_ref, *refs):
    rows_out, grads_out, hidden_ref, both_ref = refs[-4:]

    @pl.when(pl.program_id(0) == 0)
    def _():
        rows_out[...] = rows_ref[...]
        grads_out[...] = grad_ref[...]

    rows = rows_ref[...]
    gate_out = dot(rows, units_ref[:, :TILE], 1, 0)
    up_out = dot(rows, units_ref[:, TILE : 2 * TILE], 1, 0)
    grad_hidden = dot(grad_ref[...], units_ref[:, 2 * TILE :], 1, 0)
    gate_sig = jax.nn.sigmoid(gate_out)
    gate_act = gate_out * gate_sig
    hidden_ref[...] = (gate_act * up_out).astype(bf16)
    both_ref[:, :TILE] = (
        grad_hidden * up_out * (gate_sig + gate_act * (1.0 - gate_sig))
    ).astype(bf16)
    both_ref[:, TILE:] = (grad_hidden * gate_act).astype(bf16)


def units_forward(rows, grads, units, buffers, index):
    length, width = rows.shape
    steps = units.shape[1] // (3 * TILE)
    full = pl.BlockSpec((length, width), lambda i: (0, 0))
    kept = pl.BlockSpec((length, width), lambda i: (index, 0))
    held = () if buffers is None else buffers
    return pl.pallas_call(
        units_forward_kernel,
        grid=(steps,),
        in_specs=[full, full, pl.BlockSpec((width, 3 * TILE), lambda i: (0, i))]
        + [pl.BlockSpec(memory_space=pl.ANY)] * len(held),
        out_specs=(
            kept,
            kept,
            pl.BlockSpec((length, TILE), lambda i: (index, i)),
            pl.BlockSpec((length, 2 * TILE), lambda i: (index, i)),
        ),
        out_shape=(
            jax.ShapeDtypeStruct((4 * length, width), bf16),
            jax.ShapeDtypeStruct((4 * length, width), bf16),
            jax.ShapeDtypeStruct((4 * length, steps * TILE), bf16),
            jax.ShapeDtypeStruct((4 * length, steps * 2 * TILE), bf16),
        ),
        input_output_aliases={3 + k: k for k in range(len(held))},
        compiler_params=pltpu.CompilerParams(vmem_limit_bytes=VMEM_LIMIT),
        cost_estimate=SMALL,
    )(rows, grads, units, *held)


def units_back_kernel(both_ref, units_ref, out_ref):
    total = None
    for i in range(both_ref.shape[1] // (2 * TILE)):
        term = dot(
            both_ref[:, i * 2 * TILE : (i + 1) * 2 * TILE],
            units_ref[:, i * 3 * TILE : (i * 3 + 2) * TILE],
            1,
            1,
        )
        total = term if total is None else total + term
    out_ref[...] = total.astype(bf16)


def units_down_kernel(hidden_ref, units_ref, out_ref):
    total = None
    for i in range(hidden_ref.shape[1] // TILE):
        term = dot(
            hidden_ref[:, i * TILE : (i + 1) * TILE],
            units_ref[:, (i * 3 + 2) * TILE : (i * 3 + 3) * TILE],
            1,
            1,
        )
        total = term if total is None else total + term
    out_ref[...] = total.astype(bf16)


def units_to_width(kernel, values, units, first, count):
    width = units.shape[0]
    block, columns = values.shape[0] // 4, values.shape[1]
    length = block * count
    return pl.pallas_call(
        kernel,
        grid=(width // TILE,),
        in_specs=[
            pl.BlockSpec((length, columns), lambda i: (first // count, 0)),
            pl.BlockSpec((TILE, units.shape[1]), lambda i: (i, 0)),
        ],
        out_specs=pl.BlockSpec((length, TILE), lambda i: (0, i)),
        out_shape=jax.ShapeDtypeStruct((length, width), bf16),
        compiler_params=pltpu.CompilerParams(vmem_limit_bytes=VMEM_LIMIT),
        cost_estimate=SMALL,
    )(values, units)


def units_gradient_kernel(core_ref, left_ref, right_ref, kept_ref, given_ref, total_ref):
    total_ref[...] = dot(left_ref[...], right_ref[...], 0, 0)
    core = core_ref[0]
    pairs, rows, _ = kept_ref.shape
    for p in range(pairs):
        for c, ref in ((core, kept_ref), (1 - core, given_ref)):
            at_row = pl.multiple_of((2 * p + c) * rows, 16)
            ref[p] = total_ref[pl.ds(at_row, rows), :].astype(bf16)


def units_gradient_parts(left, right, core):
    length, width = left.shape
    columns = right.shape[1]
    count = lax.axis_size("dp")
    rows = width // count
    tile = 2 * TILE if columns % (2 * TILE) == 0 else TILE
    out = pl.BlockSpec((count // 2, rows, tile), lambda i, c: (0, 0, i))
    shape = jax.ShapeDtypeStruct((count // 2, rows, columns), bf16)
    return pl.pallas_call(
        units_gradient_kernel,
        grid_spec=pltpu.PrefetchScalarGridSpec(
            num_scalar_prefetch=1,
            grid=(columns // tile,),
            in_specs=[
                pl.BlockSpec((length, width), lambda i, c: (0, 0)),
                pl.BlockSpec((length, tile), lambda i, c: (0, i)),
            ],
            out_specs=(out, out),
            scratch_shapes=[pltpu.VMEM((width, tile), f32)],
        ),
        out_shape=(shape, shape),
        compiler_params=pltpu.CompilerParams(vmem_limit_bytes=VMEM_LIMIT),
        cost_estimate=SMALL,
    )(core[None], left, right)


def swap_core(value):
    count = lax.axis_size("dp")
    return lax.ppermute(value, "dp", [(i, i ^ 1) for i in range(count)])


def swap_near(value):
    return lax.ppermute(value, "tensor", [(0, 1), (1, 0), (2, 3), (3, 2)])


def swap_far(value):
    return lax.ppermute(value, "tensor", [(0, 2), (2, 0), (1, 3), (3, 1)])


def swap_middle(value):
    return lax.ppermute(value, "tensor", [(1, 2), (2, 1)])


def to_ends(value):
    return lax.ppermute(value, "tensor", [(1, 0), (2, 3)])


def from_ends(value):
    return lax.ppermute(value, "tensor", [(0, 1), (3, 2)])


def device_of(pair, core, z):
    return (2 * pair + core) * 4 + z


def owner_swap(value):
    perm = []
    for p in range(lax.axis_size("dp") // 2):
        for z in range(4):
            own = z // 2
            perm.append((device_of(p, own, z), device_of(p, own, z ^ 1)))
            perm.append((device_of(p, 1 - own, z), device_of(p, own, z ^ 2)))
    return lax.ppermute(value, AXES, perm)


def guest_swap(value):
    perm = []
    for p in range(lax.axis_size("dp") // 2):
        for z in range(4):
            guest = 1 - z // 2
            perm.append((device_of(p, guest, z), device_of(p, guest, z ^ 1)))
    return lax.ppermute(value, AXES, perm)


def heads_gather(value, first, second, own):
    mine = jnp.where(own, value, first)
    mine_next = jnp.where(own, first, second)
    return mine, mine_next, swap_core(mine), swap_core(mine_next)


def heads_scatter_begin(partial, core):
    rows, width = partial.shape[0] // 8, partial.shape[1]
    halves = partial.reshape(4, 2, rows, width)
    return at(halves, core, 1), swap_core(at(halves, core ^ 1, 1))


def heads_scatter_near(mine, other, z):
    def term(index):
        return at(mine, index, 0).astype(f32) + at(other, index, 0).astype(f32)

    away = swap_near(term(z ^ 3).astype(bf16))
    return term(z), term(z ^ 2), swap_near(term(z ^ 1).astype(bf16)), away


def heads_scatter_end(home, far, own, core):
    kept = jnp.where(own, home, far.astype(f32))
    given = swap_core(jnp.where(own, far, home.astype(bf16))).astype(f32)
    return jnp.concatenate(
        [jnp.where(core == 0, kept, given), jnp.where(core == 0, given, kept)], axis=0
    )


def gather_tensor(value, bit):
    other = lax.ppermute(value, "tensor", [(i, i ^ bit) for i in range(4)])
    upper = (lax.axis_index("tensor") & bit) != 0
    return jnp.concatenate(
        [jnp.where(upper, other, value), jnp.where(upper, value, other)], axis=0
    )


def gather_dp(value):
    bit = 1
    while bit < lax.axis_size("dp"):
        other = swap_dp(value, bit)
        upper = (lax.axis_index("dp") & bit) != 0
        value = jnp.concatenate(
            [jnp.where(upper, other, value), jnp.where(upper, value, other)], axis=0
        )
        bit *= 2
    return value


def sum_dp(value):
    bit = 1
    while bit < lax.axis_size("dp"):
        value = value + swap_dp(value, bit)
        bit *= 2
    return value


def sum_tensor(value):
    value = value + swap_near(value)
    return value + swap_far(value)


def pair_groups():
    count = lax.axis_size("dp")
    return [list(range(c, count, 2)) for c in range(2)]


def swap_dp(value, mask):
    count = lax.axis_size("dp")
    return lax.ppermute(value, "dp", [(i, i ^ mask) for i in range(count)])


def gather_pairs_begin(value):
    if lax.axis_size("dp") != 8:
        return (lax.all_gather(value, "dp", axis=0, tiled=True, axis_index_groups=pair_groups()),)
    return value, swap_dp(value, 2), swap_dp(value, 4)


def gather_pairs_end(parts):
    if len(parts) == 1:
        return parts[0]
    value, by_two, by_four = parts
    pair = lax.axis_index("dp") >> 1
    rows = value.shape[0]
    half = rows // 2
    low, high = swap_dp(by_four[:half], 2), swap_dp(by_two[half:], 4)
    whole = jnp.zeros((4 * rows,) + value.shape[1:], value.dtype)
    for part, index, offset in (
        (value, pair, 0),
        (by_two, pair ^ 1, 0),
        (by_four, pair ^ 2, 0),
        (low, pair ^ 3, 0),
        (high, pair ^ 3, half),
    ):
        whole = lax.dynamic_update_slice_in_dim(whole, part, index * rows + offset, 0)
    return whole


def at(value, index, axis):
    return lax.dynamic_index_in_dim(value, index, axis, keepdims=False)


def add_low(left, right):
    return (left.astype(f32) + right.astype(f32)).astype(bf16)


def scatter_pairs_begin(value):
    if lax.axis_size("dp") != 8:
        return (
            lax.psum_scatter(
                value, "dp", scatter_dimension=0, tiled=True, axis_index_groups=pair_groups()
            ),
        )
    pair = lax.axis_index("dp") >> 1
    one, two = pair & 1, pair >> 1
    rows = value.shape[0] // 8
    parts = value.reshape((2, 2, 2, rows) + value.shape[1:])
    first, second = parts[:, :, 0], parts[:, :, 1]
    by_two = swap_dp(at(first, one ^ 1, 1), 2)
    by_four = swap_dp(at(second, two ^ 1, 0), 4)
    return at(first, one, 1), by_two, at(second, two, 0), by_four


def scatter_pairs_end(parts):
    if len(parts) == 1:
        return parts[0]
    pair = lax.axis_index("dp") >> 1
    one, two = pair & 1, pair >> 1
    first = add_low(parts[0], parts[1])
    second = add_low(parts[2], parts[3])
    by_four = swap_dp(at(first, two ^ 1, 0), 4)
    by_two = swap_dp(at(second, one ^ 1, 0), 2)
    first = add_low(at(first, two, 0), by_four)
    second = add_low(at(second, one, 0), by_two)
    return jnp.concatenate([first, second], axis=0)


def heads_pair(shard, far, own, core):
    kept = jnp.where(own, shard, far)
    other = swap_core(jnp.where(own, far, shard))
    return jnp.concatenate(
        [jnp.where(core == 0, kept, other), jnp.where(core == 0, other, kept)], axis=0
    )


def heads_home(pair, own, core):
    rows = pair.shape[0] // 2
    kept = jnp.where(core == 0, pair[:rows], pair[rows:])
    other = swap_core(jnp.where(core == 0, pair[rows:], pair[:rows]))
    return jnp.where(own, kept, other), jnp.where(own, other, kept)


def units_gradient(summed):
    return lax.psum_scatter(
        summed.reshape(-1, summed.shape[-1]),
        "dp",
        scatter_dimension=0,
        tiled=True,
        axis_index_groups=pair_groups(),
    )


def together(*values):
    return lax.optimization_barrier(values)


def shards(
    block_in,
    out_grad,
    positions,
    qkv_weight,
    qkv_first,
    qkv_second,
    out_weight,
    out_first,
    out_second,
    gate_up,
    gate_up_first,
    gate_up_second,
    down_weight,
    down_first,
    down_second,
    norm_gains,
    norm_gains_first,
    norm_gains_second,
):
    model_width = block_in.shape[1]
    z = lax.axis_index("tensor")
    core = lax.axis_index("dp") & 1
    own = core == z // 2
    place = jnp.where(own, z, z ^ 2)[None]

    units_columns = gate_up.shape[2]
    gains_near = gather_tensor(norm_gains[None], 1)
    heads_own = jnp.concatenate([qkv_weight.astype(bf16), out_weight.astype(bf16).T], axis=1)
    heads_far = swap_far(heads_own)
    inverse_in = lax.rsqrt(jnp.mean(block_in * block_in, axis=-1, keepdims=True) + eps_norm)
    scaled_in = block_in * inverse_in
    head_positions = jnp.where(own, positions, swap_core(positions))
    scaled_b, heads_own, heads_far, head_positions, units_shard, grad_own, gains_near = together(
        scaled_in.astype(bf16),
        heads_own,
        heads_far,
        head_positions,
        pack_units(gate_up, down_weight.T),
        out_grad.astype(bf16),
        gains_near,
    )

    scaled_first = owner_swap(scaled_b)
    heads_parts = gather_pairs_begin(heads_pair(heads_own, heads_far, own, core))
    gains_near = gather_tensor(gains_near, 2)
    tables = rope_tables(head_positions, HEAD_DIMENSION)
    length = head_positions.shape[0]
    start = jnp.maximum(jnp.arange(length, dtype=jnp.int32) - head_positions, 0)
    scaled_first, heads_parts, gains_near, units_shard, tables, start, grad_own = together(
        scaled_first, heads_parts, gains_near, units_shard, tables, start, grad_own
    )

    scaled_second = guest_swap(scaled_first)
    w_heads = gather_pairs_end(heads_parts)
    units = lax.all_gather(units_shard, "dp", axis=0, tiled=True)
    grad_middle_part = swap_middle(grad_own)
    gains_all = gather_dp(gains_near.reshape(1, -1)).reshape(1, -1)
    gain_attn = gains_all[:, :model_width]
    head_gains = gains_all[0, model_width : model_width + 2 * HEAD_DIMENSION].reshape(2, -1)
    gain_ffn = gains_all[:, model_width + 2 * HEAD_DIMENSION :]
    scaled_parts = heads_gather(scaled_b, scaled_first, scaled_second, own)
    w_heads, scaled_parts, gain_attn, head_gains, gain_ffn, grad_own = together(
        w_heads, scaled_parts, gain_attn, head_gains, gain_ffn, grad_own
    )

    qkv_columns = qkv_weight.shape[1]
    grad_far = swap_far(grad_own)
    grad_near = swap_near(grad_own)
    normed_all, projected, queries_b, keys_b, values_b, attended, lse = attention_forward(
        place, scaled_parts, gain_attn, head_gains, w_heads, tables, start[:, None]
    )
    w_qkv, w_out = w_heads[:, :qkv_columns], w_heads[:, qkv_columns:]
    branch = dot(attended, w_out, 1, 1).astype(bf16)
    branch, grad_far, grad_near, grad_middle_part = together(
        branch, grad_far, grad_near, grad_middle_part
    )
    branch_mine, branch_other = together(*heads_scatter_begin(branch, core))
    home, term_far, near, away = heads_scatter_near(branch_mine, branch_other, z)
    away, term_far, grad_far = together(away, term_far, grad_far)
    far = swap_far((term_far + away.astype(f32)).astype(bf16))
    grad_ends = to_ends(grad_far)
    middle = block_in + heads_scatter_end(home + near.astype(f32), far, own, core)

    inverse_mid = lax.rsqrt(jnp.mean(middle * middle, axis=-1, keepdims=True) + eps_norm)
    scaled_mid = middle * inverse_mid
    rows_own = (scaled_mid * gain_ffn).astype(bf16)
    rows_far = swap_far(rows_own)
    rows_near = swap_near(rows_own)
    inner = (z == 1) | (z == 2)
    buffers = units_forward(rows_own, grad_own, units, None, 0)
    rows_far, rows_near, rows_own, buffers = together(rows_far, rows_near, rows_own, buffers)
    rows_ends = to_ends(rows_far)
    rows_middle = swap_middle(rows_own)
    buffers = units_forward(rows_near, grad_near, units, buffers, 1)
    buffers = units_forward(rows_far, grad_far, units, buffers, 2)
    rows_ends, rows_middle, grad_ends, buffers = together(
        rows_ends, rows_middle, grad_ends, buffers
    )
    rows_last = jnp.where(inner, rows_middle, rows_ends)
    grad_last = jnp.where(inner, grad_middle_part, grad_ends)
    rows_all, grad_all, hidden_b, dboth = units_forward(rows_last, grad_last, units, buffers, 3)

    back_last = units_to_width(units_back_kernel, dboth, units, 3, 1)
    back_last, dboth = together(back_last, dboth)
    from_last = from_ends(back_last)
    from_middle = swap_middle(back_last)
    back_rest = units_to_width(units_back_kernel, dboth, units, 0, 3)
    rows = block_in.shape[0]
    back_rest, from_last, rows_all, grad_all, hidden_b, dboth = together(
        back_rest, from_last, rows_all, grad_all, hidden_b, dboth
    )
    back_own, back_near, back_far = (back_rest[k * rows : (k + 1) * rows] for k in range(3))
    from_near = swap_near(back_near)
    from_far = swap_far(add_low(back_far, from_last))
    down_kept, down_given = units_gradient_parts(grad_all, hidden_b, core)
    both_kept, both_given = units_gradient_parts(rows_all, dboth, core)
    from_far, from_near, from_middle, down_kept, down_given, both_kept, both_given = together(
        from_far, from_near, from_middle, down_kept, down_given, both_kept, both_given
    )
    grad_normed_two = (
        back_own.astype(f32)
        + from_near.astype(f32)
        + from_middle.astype(f32)
        + from_far.astype(f32)
    )

    grad_gain_ffn = jnp.sum(grad_normed_two * scaled_mid, axis=0)
    weighted = grad_normed_two * gain_ffn
    grad_middle = out_grad + inverse_mid * (
        weighted - scaled_mid * jnp.mean(weighted * scaled_mid, axis=-1, keepdims=True)
    )
    grad_mid_b, grad_gain_ffn = together(grad_middle.astype(bf16), grad_gain_ffn)
    grad_mid_first = owner_swap(grad_mid_b)
    down_other = swap_core(down_given)
    both_other = swap_core(both_given)
    down_part = units_to_width(units_down_kernel, hidden_b, units, 0, 4)
    grad_mid_first, down_part, down_other, both_other = together(
        grad_mid_first, down_part, down_other, both_other
    )
    grad_mid_second = guest_swap(grad_mid_first)
    down_own, down_near, down_far, down_last = (
        down_part[k * rows : (k + 1) * rows] for k in range(4)
    )
    branch_ends = from_ends(down_last)
    down_sum = add_low(down_kept, down_other)
    both_sum = add_low(both_kept, both_other)
    grad_mid_second, down_sum, both_sum = together(grad_mid_second, down_sum, both_sum)
    sum_down = units_gradient(down_sum)
    sum_both = units_gradient(both_sum)
    grad_mid_parts = heads_gather(grad_mid_b, grad_mid_first, grad_mid_second, own)
    grad_mid_parts, branch_ends = together(grad_mid_parts, branch_ends)

    branch_far = swap_far(add_low(down_far, branch_ends))
    branch_near = swap_near(down_near)
    branch_middle = swap_middle(down_last)
    grad_attended, row_dot, grad_out_w = attention_turn(place, grad_mid_parts, w_out, attended)
    grad_attended, row_dot, grad_out_w = together(grad_attended, row_dot, grad_out_w)
    out_parts = scatter_pairs_begin(grad_out_w)
    grad_projected, grad_normed_b, head_sums, gain_sums = attention_backward(
        queries_b,
        keys_b,
        values_b,
        grad_attended,
        lse,
        row_dot,
        start[None, :],
        projected,
        head_gains,
        tables,
        w_heads,
        normed_all,
        gain_attn,
    )
    grad_projected, grad_normed_b, branch_far, branch_near, branch_middle, out_parts = together(
        grad_projected, grad_normed_b, branch_far, branch_near, branch_middle, out_parts
    )

    part_mine, part_other = heads_scatter_begin(grad_normed_b, core)
    grad_qkv = dot(normed_all, grad_projected, 0, 0).astype(bf16)
    part_mine, part_other, grad_qkv = together(part_mine, part_other, grad_qkv)
    home, term_far, near, away = heads_scatter_near(part_mine, part_other, z)
    qkv_parts = scatter_pairs_begin(grad_qkv)
    out_pair = scatter_pairs_end(out_parts)
    gain_total = jnp.concatenate([gain_sums[0], head_sums.reshape(-1), grad_gain_ffn])
    down_new = adam_units(
        down_weight.T[None], down_first.T[None], down_second.T[None], sum_down
    )
    away, term_far, qkv_parts, out_pair, gain_total, down_new = together(
        away, term_far, qkv_parts, out_pair, gain_total, down_new
    )
    far = swap_far((term_far + away.astype(f32)).astype(bf16))
    heads_home_own, heads_home_away = heads_home(
        jnp.concatenate([scatter_pairs_end(qkv_parts), out_pair], axis=1), own, core
    )
    gain_total = sum_dp(gain_total)
    gate_up_new = adam_units(gate_up, gate_up_first, gate_up_second, sum_both)
    far, home, near, heads_home_own, heads_home_away, gain_total, gate_up_new = together(
        far, home, near, heads_home_own, heads_home_away, gain_total, gate_up_new
    )
    heads_away = swap_far(heads_home_away)
    grad_normed = heads_scatter_end(home + near.astype(f32), far, own, core)
    gain_total = sum_tensor(gain_total)
    block_out = (
        middle
        + down_own.astype(f32)
        + branch_near.astype(f32)
        + branch_middle.astype(f32)
        + branch_far.astype(f32)
    )
    weighted = grad_normed * gain_attn
    in_grad = grad_middle + inverse_in * (
        weighted - scaled_in * jnp.mean(weighted * scaled_in, axis=-1, keepdims=True)
    )
    heads_away, block_out, in_grad = together(heads_away, block_out, in_grad)
    sum_heads = heads_home_own.astype(f32) + heads_away.astype(f32)
    down_new = tuple(value[0].T for value in down_new)
    sum_qkv = sum_heads[:, :qkv_columns]
    sum_out = sum_heads[:, qkv_columns:].T
    gain_count = norm_gains.shape[0]
    gain_at = (lax.axis_index("dp") * 4 + z) * gain_count
    gain_grads = lax.dynamic_slice_in_dim(gain_total, gain_at, gain_count)

    qkv_new = adam_step(qkv_weight, qkv_first, qkv_second, sum_qkv, rate_matrix, decay_matrix)
    out_new = adam_step(out_weight, out_first, out_second, sum_out, rate_output, decay_matrix)
    gains_new = adam_step(
        norm_gains, norm_gains_first, norm_gains_second, gain_grads, rate_gains, 0.0
    )
    return (block_out, in_grad, *qkv_new, *out_new, *gate_up_new, *down_new, *gains_new)


def solution(mesh):
    tokens = P(("dp", "tensor"), None)
    by_rows = (P("dp", "tensor"),) * 3
    by_columns = (P("tensor", "dp"),) * 3
    stacked = (P(None, "dp", "tensor"),) * 3
    gains = (P(("dp", "tensor")),) * 3
    states = by_rows + by_columns + stacked + by_columns + gains
    return jax.shard_map(
        shards,
        mesh=mesh,
        in_specs=(tokens, tokens, P("dp")) + states,
        out_specs=(tokens, tokens) + states,
        check_vma=False,
    )
```

time: 1080 us -> 561 us (0.52)
  waiting for transfers between devices: 628 us -> 172 us
  Pallas kernels: 0 us -> 184 us
  matrix products: 167 us -> 8.39 us
  blocking collectives: 87.2 us -> 0 us
  starting transfers between devices: 0.88 us -> 69.1 us
  local copies, waits for them, and re-layouts: 79.9 us -> 42.7 us
  other arithmetic: 83.7 us -> 62.6 us
    reduce_scatter x7 -> x2, waiting for transfers between devices: 324 us -> 0.02 us  [units_gradient(): lax.psum_scatter(summed.reshape(-1, summed.shape[-1]), 'dp', scatter_dime...]
    all_gather x8 -> x1, waiting for transfers between devices: 279 us -> 0.02 us  [shards(): units = lax.all_gather(units_shard, 'dp', axis=0, tiled=True)]
    pallas_call x0 -> x15, Pallas kernels: none -> 184 us  [the longest x4 46.7 us: units_forward(): pl.pallas_call(units_forward_kernel, grid=(steps,), in_specs=[full, full,...]
    ppermute x0 -> x63, waiting for transfers between devices: none -> 171 us  [the longest x9 71.4 us: swap_far(): return lax.ppermute(value, 'tensor', [(0, 2), (2, 0), (1, 3), (3, 1)])]
    dot_general x29 -> x2, matrix products: 167 us -> 8.39 us  [dot(): lax.dot_general(left, right, (((left_dim,), (right_dim,)), ((), ())), pre...]
    unnamed x2 -> x0, blocking collectives: 87.2 us -> none
    ppermute x0 -> x63, starting transfers between devices: none -> 69 us  [the longest x18 18.2 us: swap_dp(): return lax.ppermute(value, 'dp', [(i, i ^ mask) for i in range(count)])]
    another operation x2 -> x1, local copies, waits for them, and re-layouts: 27.7 us -> 0.08 us  [shards(): gains_all[0, model_width:model_width + 2 * HEAD_DIMENSION].reshape(2, -1)]
  transfers between devices with their start and end apart: 16 -> 66, of which waited for: 14 -> 32; matrix products, arithmetic and copies ran while one was open for 25% -> 16% of each run, Pallas kernels for 0% -> 30%
where the time goes in v1:
time: 561 us; the launch traced here: 554 us
  Pallas kernels  184 us (33%)
  waiting for transfers between devices  172 us (31%)
  starting transfers between devices  69.1 us (12%)
  other arithmetic  62.6 us (11%)
  local copies, waits for them, and re-layouts  42.7 us (8%)
  between operations  15.2 us (3%)
  matrix products  8.39 us (1%)
    ppermute x9, waiting for transfers between devices, swap_far(): return lax.ppermute(value, 'tensor', [(0, 2), (2, 0), (1, 3), (3, 1)])  71.4 us
    pallas_call x4, Pallas kernels, units_forward(): pl.pallas_call(units_forward_kernel, grid=(steps,), in_specs=[full, full,...  46.7 us
    ppermute x18, waiting for transfers between devices, swap_dp(): return lax.ppermute(value, 'dp', [(i, i ^ mask) for i in range(count)])  35 us
    pallas_call x3, Pallas kernels, units_to_width(): pl.pallas_call(kernel, grid=(width // TILE,), in_specs=[pl.BlockSpec((len...  34.2 us
    pallas_call x1, Pallas kernels, attention_backward(): pl.pallas_call(attention_backward_kernel, in_specs=[vmem] * 14, out_specs...  26.9 us
    pallas_call x2, Pallas kernels, units_gradient_parts(): pl.pallas_call(units_gradient_kernel, grid_spec=pltpu.PrefetchScalarGridS...  26.8 us
    ppermute x9, waiting for transfers between devices, swap_near(): return lax.ppermute(value, 'tensor', [(0, 1), (1, 0), (2, 3), (3, 2)])  23.7 us
    pallas_call x1, Pallas kernels, attention_forward(): pl.pallas_call(attention_forward_kernel, in_specs=[pl.BlockSpec(memory_sp...  22 us
  transfers between devices with their start and end apart: 66, of which 32 were waited for; matrix products, arithmetic and copies ran while one was open for 16% of the time, Pallas kernels for 30%

profile of v1, /device:TPU:0, one launch (start us, length us, event | category | flops | bytes accessed | tf_op | source)
XLA Modules:
  0.0 554.2 jit_solution(17706022487231136805)
XLA Ops:
  7.8 2.7 collective-permute-start.2
  12.5 2.7 collective-permute-start
  20.4 12.7 %collective-permute-done = bf16[192,1024]{1,0:T(8,128)(2,1)} collective-permute-done((bf16[192,1024]{1,0:T(8,128)(2,1)S(1)}, bf16[192,1024]{1,0:T(8,128)(2,1)}, u32[]{:S(2)}, u32[]{:S(2)}) %collective-permute-start) | collective-permute-done | bytes 393248 | tf_op jit(solution)/shard_map/ppermute | solution.py:537
  39.2 2.3 collective-permute-start.7
  41.5 1.9 fusion.12
  43.8 11.6 %collective-permute-done.7 = f32[2,100]{1,0:T(2,128)S(1)} collective-permute-done((f32[2,100]{1,0:T(2,128)S(1)}, f32[2,100]{1,0:T(2,128)S(1)}, u32[]{:S(2)}, u32[]{:S(2)}) %collective-permute-start.7) | collective-permute-done | bytes 832 | tf_op jit(solution)/shard_map/ppermute | solution.py:604
  66.6 2.0 broadcast_in_dim.35
  71.6 5.8 %collective-permute-done.14 = f32[2,400]{1,0:T(2,128)S(1)} collective-permute-done((f32[2,400]{1,0:T(2,128)S(1)}, f32[2,400]{1,0:T(2,128)S(1)}, u32[]{:S(2)}, u32[]{:S(2)}) %collective-permute-start.14) | collective-permute-done | bytes 3232 | tf_op jit(solution)/shard_map/ppermute | solution.py:643
  80.0 2.6 collective-permute-done.15
  90.9 22.0 %shard_map.306 = (bf16[1024,1536]{1,0:T(8,128)(2,1)}, f32[1024,640]{1,0:T(8,128)}, bf16[6,1024,64]{2,1,0:T(8,128)(2,1)}, bf16[2,1024,64]{2,1,0:T(8,128)(2,1)S(1)...) custom-call(s32[1]{0:T(128)} %bitcast.place_ref, ...), custom_call_target="tpu_custom_call" | custom-call | flops 1000 | bytes 1000 | tf_op jit(solution)/shard_map/pallas_call | solution.py:164
  112.9 3.8 convolution_convert_fusion
  116.8 9.2 %collective-permute-done.16.grad_ref = bf16[256,1536]{1,0:T(8,128)(2,1)} collective-permute-done((bf16[256,1536]{1,0:T(8,128)(2,1)S(1)}, bf16[256,1536]{1,0:T(8,128)(2,1)}, u32[]{:S(2)}, u32[]{:S(2)}) %collective-permute-start.16) | collective-permute-done | bytes 786464 | tf_op jit(solution)/shard_map/ppermute | solution.py:537
  127.3 3.6 collective-permute-done.19
  132.0 1.9 collective-permute-start.20
  133.9 9.9 %collective-permute-done.21 = bf16[128,1536]{1,0:T(8,128)(2,1)S(1)} collective-permute-done((bf16[128,1536]{1,0:T(8,128)(2,1)S(1)}, bf16[128,1536]{1,0:T(8,128)(2,1)S(1)}, u32[]{:S(2)}, u32[]{:S(2)}) %collective-permute-start.21) | collective-permute-done | bytes 393248 | tf_op jit(solution)/shard_map/ppermute | solution.py:533
  145.8 10.8 %collective-permute-done.20 = bf16[128,1536]{1,0:T(8,128)(2,1)} collective-permute-done((bf16[128,1536]{1,0:T(8,128)(2,1)}, bf16[128,1536]{1,0:T(8,128)(2,1)}, u32[]{:S(2)}, u32[]{:S(2)}) %collective-permute-start.20) | collective-permute-done | bytes 393248 | tf_op jit(solution)/shard_map/ppermute | solution.py:533
  156.6 7.4 %collective-permute-done.22 = bf16[128,1536]{1,0:T(8,128)(2,1)} collective-permute-done((bf16[128,1536]{1,0:T(8,128)(2,1)}, bf16[128,1536]{1,0:T(8,128)(2,1)}, u32[]{:S(2)}, u32[]{:S(2)}) %collective-permute-start.22) | collective-permute-done | bytes 393248 | tf_op jit(solution)/shard_map/ppermute | solution.py:537
  164.0 2.1 convert_select_fusion.6
  166.1 2.0 collective-permute-done.23
  176.4 11.6 %shard_map.307 = (bf16[1024,1536]{1,0:T(8,128)(2,1)S(1)}, bf16[1024,1536]{1,0:T(8,128)(2,1)}, bf16[1024,1792]{1,0:T(8,128)(2,1)}, bf16[1024,3584]{1,0:T(8,128)(2,1)}) custom-call(bf16[256,1536]{1,0:T(8,128)(2,1)} %multiply_convert_fusion.rows_ref, bf16[256,1536]{1,0:T(8,128)(2,1)S(1)} %copy-done.9, bf16[1536,5376]{1,0:T(8,128)(2,1)} %all-gather.2.cloned.1.call-done.units_ref), custom_call_target="tpu_custom_call" | custom-call | flops 1000 | bytes 1000 | tf_op jit(solution)/shard_map/pallas_call | solution.py:424
  188.0 20.5 %collective-permute-done.24.rows_ref = bf16[256,1536]{1,0:T(8,128)(2,1)} collective-permute-done((bf16[256,1536]{1,0:T(8,128)(2,1)}, bf16[256,1536]{1,0:T(8,128)(2,1)}, u32[]{:S(2)}, u32[]{:S(2)}) %collective-permute-start.24) | collective-permute-done | bytes 786464 | tf_op jit(solution)/shard_map/ppermute | solution.py:537
  212.7 11.8 %shard_map.308 = (bf16[1024,1536]{1,0:T(8,128)(2,1)S(1)}, bf16[1024,1536]{1,0:T(8,128)(2,1)}, bf16[1024,1792]{1,0:T(8,128)(2,1)}, bf16[1024,3584]{1,0:T(8,128)(2,1)}) custom-call(bf16[256,1536]{1,0:T(8,128)(2,1)} %collective-permute-done.25.rows_ref, ...), custom_call_target="tpu_custom_call", output_to_operand_aliasing={{0}: (3, {}), {1}: (4, {}), {2}: (5, {}), {3}: (6, {})} | custom-call | flops 1000 | bytes 1000 | tf_op jit(solution)/shard_map/pallas_call | solution.py:424
  224.5 11.9 %shard_map.309 = (bf16[1024,1536]{1,0:T(8,128)(2,1)S(1)}, bf16[1024,1536]{1,0:T(8,128)(2,1)}, bf16[1024,1792]{1,0:T(8,128)(2,1)}, bf16[1024,3584]{1,0:T(8,128)(2,1)}) custom-call(bf16[256,1536]{1,0:T(8,128)(2,1)} %collective-permute-done.24.rows_ref, ...), custom_call_target="tpu_custom_call", output_to_operand_aliasing={{0}: (3, {}), {1}: (4, {}), {2}: (5, {}), {3}: (6, {})} | custom-call | flops 1000 | bytes 1000 | tf_op jit(solution)/shard_map/pallas_call | solution.py:424
  236.4 6.2 %collective-permute-done.26 = bf16[256,1536]{1,0:T(8,128)(2,1)} collective-permute-done((bf16[256,1536]{1,0:T(8,128)(2,1)}, bf16[256,1536]{1,0:T(8,128)(2,1)}, u32[]{:S(2)}, u32[]{:S(2)}) %collective-permute-start.26) | collective-permute-done | bytes 786464 | tf_op jit(solution)/shard_map/ppermute | solution.py:545
  245.1 11.4 %shard_map.310 = (bf16[1024,1536]{1,0:T(8,128)(2,1)S(1)}, bf16[1024,1536]{1,0:T(8,128)(2,1)}, bf16[1024,1792]{1,0:T(8,128)(2,1)}, bf16[1024,3584]{1,0:T(8,128)(2,1)}) custom-call(bf16[256,1536]{1,0:T(8,128)(2,1)S(1)} %broadcast_select_fusion.1.rows_ref, ...), custom_call_target="tpu_custom_call", output_to_operand_aliasing={{0}: (3, {}), {1}: (4, {}), {2}: (5, {}), {3}: (6, {})} | custom-call | flops 1000 | bytes 1000 | tf_op jit(solution)/shard_map/pallas_call | solution.py:424
  256.5 9.2 %shard_map.311 = bf16[256,1536]{1,0:T(8,128)(2,1)S(1)} custom-call(bf16[1024,3584]{1,0:T(8,128)(2,1)} %get-tuple-element.248.both_ref.right_ref, bf16[1536,5376]{1,0:T(8,128)(2,1)} %all-gather.2.cloned.1.call-done.units_ref), custom_call_target="tpu_custom_call" | custom-call | flops 1000 | bytes 1000 | tf_op jit(solution)/shard_map/pallas_call | solution.py:477
  267.9 13.6 %shard_map.312 = bf16[768,1536]{1,0:T(8,128)(2,1)S(1)} custom-call(bf16[1024,3584]{1,0:T(8,128)(2,1)} %get-tuple-element.248.both_ref.right_ref, bf16[1536,5376]{1,0:T(8,128)(2,1)} %all-gather.2.cloned.1.call-done.units_ref), custom_call_target="tpu_custom_call" | custom-call | flops 1000 | bytes 1000 | tf_op jit(solution)/shard_map/pallas_call | solution.py:477
  281.5 2.0 collective-permute-done.29
  285.5 3.5 collective-permute-start.30
  289.0 16.4 %shard_map.314 = (bf16[4,192,3584]{2,1,0:T(8,128)(2,1)}, bf16[4,192,3584]{2,1,0:T(8,128)(2,1)}) custom-call(s32[1]{0:T(128)} %bitcast.12.core_ref, bf16[1024,1536]{1,0:T(8,128)(2,1)S(1)} %get-tuple-element.247.left_ref, bf16[1024,3584]{1,0:T(8,128)(2,1)} %get-tuple-element.248.both_ref.right_ref), custom_call_target="tpu_custom_call" | custom-call | flops 1000 | bytes 1000 | tf_op jit(solution)/shard_map/pallas_call | solution.py:509
  305.4 10.4 %shard_map.313 = (bf16[4,192,1792]{2,1,0:T(8,128)(2,1)S(1)}, bf16[4,192,1792]{2,1,0:T(8,128)(2,1)S(1)}) custom-call(s32[1]{0:T(128)} %bitcast.12.core_ref, bf16[1024,1536]{1,0:T(8,128)(2,1)} %get-tuple-element.243.left_ref, bf16[1024,1792]{1,0:T(8,128)(2,1)} %get-tuple-element.244.right_ref.hidden_ref), custom_call_target="tpu_custom_call" | custom-call | flops 1000 | bytes 1000 | tf_op jit(solution)/shard_map/pallas_call | solution.py:509
  315.8 6.6 %collective-permute-done.30 = bf16[256,1536]{1,0:T(8,128)(2,1)S(1)} collective-permute-done((bf16[256,1536]{1,0:T(8,128)(2,1)}, bf16[256,1536]{1,0:T(8,128)(2,1)S(1)}, u32[]{:S(2)}, u32[]{:S(2)}) %collective-permute-start.30) | collective-permute-done | bytes 786464 | tf_op jit(solution)/shard_map/ppermute | solution.py:537
  324.1 2.4 multiply_reduce_fusion.1
  326.6 3.2 fusion.18
  331.2 11.4 %shard_map.315 = bf16[1024,1536]{1,0:T(8,128)(2,1)S(1)} custom-call(bf16[1024,1792]{1,0:T(8,128)(2,1)} %get-tuple-element.244.right_ref.hidden_ref, bf16[1536,5376]{1,0:T(8,128)(2,1)} %all-gather.2.cloned.1.call-done.units_ref), custom_call_target="tpu_custom_call" | custom-call | flops 1000 | bytes 1000 | tf_op jit(solution)/shard_map/pallas_call | solution.py:477
  342.6 6.8 %collective-permute-done.33 = bf16[256,1536]{1,0:T(8,128)(2,1)S(1)} collective-permute-done((bf16[256,1536]{1,0:T(8,128)(2,1)S(1)}, bf16[256,1536]{1,0:T(8,128)(2,1)S(1)}, u32[]{:S(2)}, u32[]{:S(2)}) %collective-permute-start.33) | collective-permute-done | bytes 786464 | tf_op jit(solution)/shard_map/ppermute | solution.py:563
  350.1 8.0 %add_convert_fusion = bf16[4,192,3584]{2,1,0:T(8,128)(2,1)} fusion(bf16[4,192,3584]{2,1,0:T(8,128)(2,1)} %collective-permute-done.35, bf16[4,192,3584]{2,1,0:T(8,128)(2,1)} %get-tuple-element.260), kind=kLoop, calls=%fused_computation | loop fusion | flops 11010048 | bytes 16515072 | tf_op jit(solution)/shard_map/convert_element_type | solution.py:677
  358.1 4.0 add_convert_fusion.1
  365.0 4.4 collective-permute-start.39
  370.6 2.2 collective-permute-start.37
  372.8 2.5 slice.70.weight_ref
  378.1 7.1 %collective-permute-done.39 = bf16[256,1536]{1,0:T(8,128)(2,1)} collective-permute-done((bf16[256,1536]{1,0:T(8,128)(2,1)}, bf16[256,1536]{1,0:T(8,128)(2,1)}, u32[]{:S(2)}, u32[]{:S(2)}) %collective-permute-start.39) | collective-permute-done | bytes 786464 | tf_op jit(solution)/shard_map/ppermute | solution.py:549
  385.2 10.9 %shard_map.316 = (bf16[6,1024,64]{2,1,0:T(8,128)(2,1)}, f32[6,1,1024]{2,1,0:T(1,128)S(1)}, bf16[1536,384]{1,0:T(8,128)(2,1)S(1)}) custom-call(s32[1]{0:T(128)} %bitcast.place_ref, bf16[256,1536]{1,0:T(8,128)(2,1)} %get-tuple-element.264.part_0, bf16[256,1536]{1,0:T(8,128)(2,1)} %get-tuple-element.265.part_1, ...), custom_call_target="tpu_custom_call" | custom-call | flops 1000 | bytes 1000 | tf_op jit(solution)/shard_map/pallas_call | solution.py:205
  397.5 5.8 %collective-permute-start.40 = (bf16[256,1536]{1,0:T(8,128)(2,1)S(1)}, bf16[256,1536]{1,0:T(8,128)(2,1)S(1)}, u32[]{:S(2)}, u32[]{:S(2)}) collective-permute-start(bf16[256,1536]{1,0:T(8,128)(2,1)S(1)} %add_convert_fusion.2), channel_id=1, source_target_pairs={{0,2},{2,0},{1,3},{3,1},{4,6},{6,4},{5,7},{7,5},{8,10},{10,8},{9,1... | collective-permute-start | bytes 2359304 | tf_op jit(solution)/shard_map/ppermute | solution.py:537
  405.8 2.5 collective-permute-start.44
  408.3 26.9 %shard_map.317 = (bf16[1024,640]{1,0:T(8,128)(2,1)S(1)}, bf16[1024,1536]{1,0:T(8,128)(2,1)}, f32[2,64]{1,0:T(2,128)S(1)}, f32[1,1536]{1,0:T(1,128)S(1)}) custom-call(bf16[6,1024,64]{2,1,0:T(8,128)(2,1)S(1)} %copy-done.11, bf16[2,1024,64]{2,1,0:T(8,128)(2,1)S(1)} %copy-done.19, bf16[2,1024,64]{2,1,0:T(8,128)(2,1)S(1)} %copy-done.21, ...), custom_call_target="tpu_custom_call" | custom-call | flops 1000 | bytes 1000 | tf_op jit(solution)/shard_map/pallas_call | solution.py:320
  435.2 2.4 collective-permute-done.40
  437.7 4.0 dynamic-slice_bitcast_fusion
  443.2 2.5 collective-permute-start.49
  447.0 4.6 convolution_convert_fusion.1
  452.8 2.0 collective-permute-start.47
  455.9 3.0 fusion.8
  464.6 4.0 shard_map.318
  469.8 3.2 collective-permute-done.47
  472.9 4.7 collective-permute-done.48
  480.4 8.4 %collective-permute-done.53 = bf16[192,640]{1,0:T(8,128)(2,1)S(1)} collective-permute-done((bf16[192,640]{1,0:T(8,128)(2,1)S(1)}, bf16[192,640]{1,0:T(8,128)(2,1)S(1)}, u32[]{:S(2)}, u32[]{:S(2)}) %collective-permute-start.53) | collective-permute-done | bytes 245792 | tf_op jit(solution)/shard_map/ppermute | solution.py:643
  490.8 1.8 add_convert_fusion.7
  494.3 3.4 collective-permute-done.57
  498.0 3.4 collective-permute-done.58
  501.5 2.2 broadcast_select_fusion.6
  506.8 11.4 %shard_map.319 = (f32[2,192,1728]{2,1,0:T(8,128)}, f32[2,192,1728]{2,1,0:T(8,128)}, f32[2,192,1728]{2,1,0:T(8,128)}) custom-call(f32[2,192,1728]{2,1,0:T(8,128)S(1)} %copy-done.1, f32[2,192,1728]{2,1,0:T(8,128)} %first_ref.1, f32[2,192,1728]{2,1,0:T(8,128)} %second_ref.1, bf16[192,3584]{1,0:T(8,128)(2,1)S(1)} %copy-done.12), custom_call_target="tpu_custom_call" | custom-call | flops 1000 | bytes 1000 | tf_op jit(solution)/shard_map/pallas_call | solution.py:386
  518.2 2.4 collective-permute-start.61
  522.4 2.5 collective-permute-start.62
  532.3 12.6 %collective-permute-done.59 = bf16[192,1024]{1,0:T(8,128)(2,1)S(1)} collective-permute-done((bf16[192,1024]{1,0:T(8,128)(2,1)S(1)}, bf16[192,1024]{1,0:T(8,128)(2,1)S(1)}, u32[]{:S(2)}, u32[]{:S(2)}) %collective-permute-start.59) | collective-permute-done | bytes 393248 | tf_op jit(solution)/shard_map/ppermute | solution.py:537
  (339 shorter events, 110.1 us)
Async XLA Ops:
  7.2 168.1 %all-gather.2.cloned.1.call-start = ((), (), s32[]{:S(2)}) async-start(), calls=%async_computation.2 | async-start | bytes 18579456 | tf_op jit(solution)/shard_map/all_gather | solution.py:795
  7.2 13.1 %collective-permute-start.1 = (s32[1024]{0:T(1024)}, s32[1024]{0:T(1024)S(1)}, u32[]{:S(2)}, u32[]{:S(2)}) collective-permute-start(s32[1024]{0:T(1024)} %param.20), channel_id=1, source_target_pairs={{0,4},{4,0},{8,12},{12,8},{16,20},{20,16},{24,28},{28,24},{1,5},{5... | collective-permute-start | bytes 12296 | tf_op jit(solution)/shard_map/ppermute | solution.py:529
  7.8 12.5 %collective-permute-start.2 = (f32[1,100]{1,0:T(1,128)}, f32[1,100]{1,0:T(1,128)S(1)}, u32[]{:S(2)}, u32[]{:S(2)}) collective-permute-start(f32[1,100]{1,0:T(1,128)} %bitcast.144), channel_id=1, source_target_pairs={{0,1},{1,0},{2,3},{3,2},{4,5},{5,4},{6,7},{7,6},{8,9},{9,8},{10,11... | collective-permute-start | bytes 1208 | tf_op jit(solution)/shard_map/ppermute | solution.py:604
  12.5 20.5 %collective-permute-start = (bf16[192,1024]{1,0:T(8,128)(2,1)S(1)}, bf16[192,1024]{1,0:T(8,128)(2,1)}, u32[]{:S(2)}, u32[]{:S(2)}) collective-permute-start(bf16[192,1024]{1,0:T(8,128)(2,1)S(1)} %pad_maximum_fusion.4), channel_id=1, source_target_pairs={{0,2},{2,0},{1,3},{3,1},{4,6},{6,4},{5,7},{7,5},{8,10},{10,8},{9,1... | collective-permute-start | bytes 1179656 | tf_op jit(solution)/shard_map/ppermute | solution.py:537
  34.2 21.2 %collective-permute-start.3 = (bf16[256,1536]{1,0:T(8,128)(2,1)}, bf16[256,1536]{1,0:T(8,128)(2,1)S(1)}, u32[]{:S(2)}, u32[]{:S(2)}) collective-permute-start(bf16[256,1536]{1,0:T(8,128)(2,1)} %multiply_convert_fusion.1), channel_id=1, source_target_pairs={{0,1},{4,2},{1,0},{5,3},{6,7},{2,4},{7,6},{3,5},{8,9},{12,10},{9,8... | collective-permute-start | bytes 2359304 | tf_op jit(solution)/shard_map/ppermute | solution.py:563
  36.0 20.3 %collective-permute-start.5 = (bf16[384,1024]{1,0:T(8,128)(2,1)S(1)}, bf16[384,1024]{1,0:T(8,128)(2,1)S(1)}, u32[]{:S(2)}, u32[]{:S(2)}) collective-permute-start(bf16[384,1024]{1,0:T(8,128)(2,1)S(1)} %pad_maximum_fusion), channel_id=1, source_target_pairs={{0,8},{4,12},{8,0},{12,4},{16,24},{20,28},{24,16},{28,20},{1,9},{5... | collective-permute-start | bytes 2359304 | tf_op jit(solution)/shard_map/ppermute | solution.py:643
  37.6 20.3 %collective-permute-start.6 = (bf16[384,1024]{1,0:T(8,128)(2,1)S(1)}, bf16[384,1024]{1,0:T(8,128)(2,1)S(1)}, u32[]{:S(2)}, u32[]{:S(2)}) collective-permute-start(bf16[384,1024]{1,0:T(8,128)(2,1)S(1)} %pad_maximum_fusion), channel_id=1, source_target_pairs={{0,16},{4,20},{8,24},{12,28},{16,0},{20,4},{24,8},{28,12},{1,17},{... | collective-permute-start | bytes 2359304 | tf_op jit(solution)/shard_map/ppermute | solution.py:643
  39.2 16.2 %collective-permute-start.7 = (f32[2,100]{1,0:T(2,128)S(1)}, f32[2,100]{1,0:T(2,128)S(1)}, u32[]{:S(2)}, u32[]{:S(2)}) collective-permute-start(f32[2,100]{1,0:T(2,128)S(1)} %pad_maximum_fusion.11), channel_id=1, source_target_pairs={{0,2},{1,3},{2,0},{3,1},{4,6},{5,7},{6,4},{7,5},{8,10},{9,11},{10,... | collective-permute-start | bytes 2408 | tf_op jit(solution)/shard_map/ppermute | solution.py:604
  58.0 401.1 %reduce-scatter.3.cloned.1.call-start = ((), (), s32[]{:S(2)}) async-start(), calls=%async_computation.3 | async-start | bytes 3440640 | tf_op jit(solution)/shard_map/reduce_scatter | solution.py:727
  58.1 11.4 %collective-permute-start.13 = (f32[1,400]{1,0:T(1,128)S(1)}, f32[1,400]{1,0:T(1,128)S(1)}, u32[]{:S(2)}, u32[]{:S(2)}) collective-permute-start(f32[1,400]{1,0:T(1,128)S(1)} %reshape.145), channel_id=1, source_target_pairs={{0,4},{4,0},{8,12},{12,8},{16,20},{20,16},{24,28},{28,24},{1,5},{5... | collective-permute-start | bytes 4808 | tf_op jit(solution)/shard_map/ppermute | solution.py:643
  58.1 24.6 %collective-permute-start.10 = (bf16[256,1536]{1,0:T(8,128)(2,1)}, bf16[256,1536]{1,0:T(8,128)(2,1)}, u32[]{:S(2)}, u32[]{:S(2)}) collective-permute-start(bf16[256,1536]{1,0:T(8,128)(2,1)} %copy-done.56), channel_id=1, source_target_pairs={{4,5},{5,4},{2,3},{3,2},{12,13},{13,12},{10,11},{11,10},{20,21},{2... | collective-permute-start | bytes 2359304 | tf_op jit(solution)/shard_map/ppermute | solution.py:572
  60.5 24.5 %collective-permute-start.8 = (bf16[192,1024]{1,0:T(8,128)(2,1)}, bf16[192,1024]{1,0:T(8,128)(2,1)}, u32[]{:S(2)}, u32[]{:S(2)}) collective-permute-start(bf16[192,1024]{1,0:T(8,128)(2,1)} %slice.65), channel_id=1, source_target_pairs={{0,8},{4,12},{8,0},{12,4},{16,24},{20,28},{24,16},{28,20},{1,9},{5... | collective-permute-start | bytes 1179656 | tf_op jit(solution)/shard_map/ppermute | solution.py:643
  63.4 23.4 %collective-permute-start.9 = (bf16[192,1024]{1,0:T(8,128)(2,1)}, bf16[192,1024]{1,0:T(8,128)(2,1)}, u32[]{:S(2)}, u32[]{:S(2)}) collective-permute-start(bf16[192,1024]{1,0:T(8,128)(2,1)} %slice.66), channel_id=1, source_target_pairs={{0,16},{4,20},{8,24},{12,28},{16,0},{20,4},{24,8},{28,12},{1,17},{... | collective-permute-start | bytes 1179656 | tf_op jit(solution)/shard_map/ppermute | solution.py:643
  64.8 51.9 %collective-permute-start.18 = (bf16[256,1536]{1,0:T(8,128)(2,1)S(1)}, bf16[256,1536]{1,0:T(8,128)(2,1)}, u32[]{:S(2)}, u32[]{:S(2)}) collective-permute-start(bf16[256,1536]{1,0:T(8,128)(2,1)S(1)} %convert_element_type.304.grad_ref), channel_id=1, source_target_pairs={{1,2},{2,1},{5,6},{6,5},{9,10},{10,9},{13,14},{14,13},{17,18},{18,... | collective-permute-start | bytes 2359304 | tf_op jit(solution)/shard_map/ppermute | solution.py:541
  69.6 7.8 %collective-permute-start.14 = (f32[2,400]{1,0:T(2,128)S(1)}, f32[2,400]{1,0:T(2,128)S(1)}, u32[]{:S(2)}, u32[]{:S(2)}) collective-permute-start(f32[2,400]{1,0:T(2,128)S(1)} %pad_maximum_fusion.9), channel_id=1, source_target_pairs={{0,8},{4,12},{8,0},{12,4},{16,24},{20,28},{24,16},{28,20},{1,9},{5... | collective-permute-start | bytes 9608 | tf_op jit(solution)/shard_map/ppermute | solution.py:643
  77.4 5.2 collective-permute-start.15
  84.3 4.3 collective-permute-start.11
  84.3 4.2 collective-permute-start.12
  88.5 37.4 %collective-permute-start.16 = (bf16[256,1536]{1,0:T(8,128)(2,1)S(1)}, bf16[256,1536]{1,0:T(8,128)(2,1)}, u32[]{:S(2)}, u32[]{:S(2)}) collective-permute-start(bf16[256,1536]{1,0:T(8,128)(2,1)S(1)} %convert_element_type.304.grad_ref), channel_id=1, source_target_pairs={{0,2},{2,0},{1,3},{3,1},{4,6},{6,4},{5,7},{7,5},{8,10},{10,8},{9,1... | collective-permute-start | bytes 2359304 | tf_op jit(solution)/shard_map/ppermute | solution.py:537
  88.6 37.4 %collective-permute-start.17 = (bf16[256,1536]{1,0:T(8,128)(2,1)S(1)}, bf16[256,1536]{1,0:T(8,128)(2,1)}, u32[]{:S(2)}, u32[]{:S(2)}) collective-permute-start(bf16[256,1536]{1,0:T(8,128)(2,1)S(1)} %convert_element_type.304.grad_ref), channel_id=1, source_target_pairs={{0,1},{1,0},{2,3},{3,2},{4,5},{5,4},{6,7},{7,6},{8,9},{9,8},{10,11... | collective-permute-start | bytes 2359304 | tf_op jit(solution)/shard_map/ppermute | solution.py:533
  127.3 3.6 collective-permute-start.19
  131.9 12.0 %collective-permute-start.21 = (bf16[128,1536]{1,0:T(8,128)(2,1)S(1)}, bf16[128,1536]{1,0:T(8,128)(2,1)S(1)}, u32[]{:S(2)}, u32[]{:S(2)}) collective-permute-start(bf16[128,1536]{1,0:T(8,128)(2,1)S(1)} %get-tuple-element.350), channel_id=1, source_target_pairs={{0,1},{1,0},{2,3},{3,2},{4,5},{5,4},{6,7},{7,6},{8,9},{9,8},{10,11... | collective-permute-start | bytes 1179656 | tf_op jit(solution)/shard_map/ppermute | solution.py:533
  132.0 24.6 %collective-permute-start.20 = (bf16[128,1536]{1,0:T(8,128)(2,1)}, bf16[128,1536]{1,0:T(8,128)(2,1)}, u32[]{:S(2)}, u32[]{:S(2)}) collective-permute-start(bf16[128,1536]{1,0:T(8,128)(2,1)} %get-tuple-element.348), channel_id=1, source_target_pairs={{0,1},{1,0},{2,3},{3,2},{4,5},{5,4},{6,7},{7,6},{8,9},{9,8},{10,11... | collective-permute-start | bytes 1179656 | tf_op jit(solution)/shard_map/ppermute | solution.py:533
  144.7 19.3 %collective-permute-start.22 = (bf16[128,1536]{1,0:T(8,128)(2,1)}, bf16[128,1536]{1,0:T(8,128)(2,1)}, u32[]{:S(2)}, u32[]{:S(2)}) collective-permute-start(bf16[128,1536]{1,0:T(8,128)(2,1)} %add_convert_fusion.9), channel_id=1, source_target_pairs={{0,2},{2,0},{1,3},{3,1},{4,6},{6,4},{5,7},{7,5},{8,10},{10,8},{9,1... | collective-permute-start | bytes 1179656 | tf_op jit(solution)/shard_map/ppermute | solution.py:537
  166.1 2.1 collective-permute-start.23
  172.1 36.4 %collective-permute-start.24 = (bf16[256,1536]{1,0:T(8,128)(2,1)}, bf16[256,1536]{1,0:T(8,128)(2,1)}, u32[]{:S(2)}, u32[]{:S(2)}) collective-permute-start(bf16[256,1536]{1,0:T(8,128)(2,1)} %multiply_convert_fusion.rows_ref), channel_id=1, source_target_pairs={{0,2},{2,0},{1,3},{3,1},{4,6},{6,4},{5,7},{7,5},{8,10},{10,8},{9,1... | collective-permute-start | bytes 2359304 | tf_op jit(solution)/shard_map/ppermute | solution.py:537
  172.2 37.6 %collective-permute-start.25 = (bf16[256,1536]{1,0:T(8,128)(2,1)}, bf16[256,1536]{1,0:T(8,128)(2,1)}, u32[]{:S(2)}, u32[]{:S(2)}) collective-permute-start(bf16[256,1536]{1,0:T(8,128)(2,1)} %multiply_convert_fusion.rows_ref), channel_id=1, source_target_pairs={{0,1},{1,0},{2,3},{3,2},{4,5},{5,4},{6,7},{7,6},{8,9},{9,8},{10,11... | collective-permute-start | bytes 2359304 | tf_op jit(solution)/shard_map/ppermute | solution.py:533
  174.0 62.4 %collective-permute-start.28 = (bf16[256,1536]{1,0:T(8,128)(2,1)}, bf16[256,1536]{1,0:T(8,128)(2,1)}, u32[]{:S(2)}, u32[]{:S(2)}) collective-permute-start(bf16[256,1536]{1,0:T(8,128)(2,1)} %collective-permute-done.16.grad_ref), channel_id=1, source_target_pairs={{1,0},{2,3},{5,4},{6,7},{9,8},{10,11},{13,12},{14,15},{17,16},{18,... | collective-permute-start | bytes 2359304 | tf_op jit(solution)/shard_map/ppermute | solution.py:545
  209.7 32.9 %collective-permute-start.26 = (bf16[256,1536]{1,0:T(8,128)(2,1)}, bf16[256,1536]{1,0:T(8,128)(2,1)}, u32[]{:S(2)}, u32[]{:S(2)}) collective-permute-start(bf16[256,1536]{1,0:T(8,128)(2,1)} %collective-permute-done.24.rows_ref), channel_id=1, source_target_pairs={{1,0},{2,3},{5,4},{6,7},{9,8},{10,11},{13,12},{14,15},{17,16},{18,... | collective-permute-start | bytes 2359304 | tf_op jit(solution)/shard_map/ppermute | solution.py:545
  211.0 31.6 %collective-permute-start.27 = (bf16[256,1536]{1,0:T(8,128)(2,1)}, bf16[256,1536]{1,0:T(8,128)(2,1)}, u32[]{:S(2)}, u32[]{:S(2)}) collective-permute-start(bf16[256,1536]{1,0:T(8,128)(2,1)} %multiply_convert_fusion.rows_ref), channel_id=1, source_target_pairs={{1,2},{2,1},{5,6},{6,5},{9,10},{10,9},{13,14},{14,13},{17,18},{18,... | collective-permute-start | bytes 2359304 | tf_op jit(solution)/shard_map/ppermute | solution.py:541
  265.7 17.8 %collective-permute-start.29 = (bf16[256,1536]{1,0:T(8,128)(2,1)S(1)}, bf16[256,1536]{1,0:T(8,128)(2,1)S(1)}, u32[]{:S(2)}, u32[]{:S(2)}) collective-permute-start(bf16[256,1536]{1,0:T(8,128)(2,1)S(1)} %shard_map.311), channel_id=1, source_target_pairs={{0,1},{3,2},{4,5},{7,6},{8,9},{11,10},{12,13},{15,14},{16,17},{19,... | collective-permute-start | bytes 2359304 | tf_op jit(solution)/shard_map/ppermute | solution.py:549
  267.2 48.6 %collective-permute-start.32 = (bf16[256,1536]{1,0:T(8,128)(2,1)S(1)}, bf16[256,1536]{1,0:T(8,128)(2,1)S(1)}, u32[]{:S(2)}, u32[]{:S(2)}) collective-permute-start(bf16[256,1536]{1,0:T(8,128)(2,1)S(1)} %shard_map.311), channel_id=1, source_target_pairs={{1,2},{2,1},{5,6},{6,5},{9,10},{10,9},{13,14},{14,13},{17,18},{18,... | collective-permute-start | bytes 2359304 | tf_op jit(solution)/shard_map/ppermute | solution.py:541
  285.5 36.9 %collective-permute-start.30 = (bf16[256,1536]{1,0:T(8,128)(2,1)}, bf16[256,1536]{1,0:T(8,128)(2,1)S(1)}, u32[]{:S(2)}, u32[]{:S(2)}) collective-permute-start(bf16[256,1536]{1,0:T(8,128)(2,1)} %add_convert_fusion.3), channel_id=1, source_target_pairs={{0,2},{2,0},{1,3},{3,1},{4,6},{6,4},{5,7},{7,5},{8,10},{10,8},{9,1... | collective-permute-start | bytes 2359304 | tf_op jit(solution)/shard_map/ppermute | solution.py:537
  289.0 33.7 %collective-permute-start.31 = (bf16[256,1536]{1,0:T(8,128)(2,1)}, bf16[256,1536]{1,0:T(8,128)(2,1)S(1)}, u32[]{:S(2)}, u32[]{:S(2)}) collective-permute-start(bf16[256,1536]{1,0:T(8,128)(2,1)} %slice.73), channel_id=1, source_target_pairs={{0,1},{1,0},{2,3},{3,2},{4,5},{5,4},{6,7},{7,6},{8,9},{9,8},{10,11... | collective-permute-start | bytes 2359304 | tf_op jit(solution)/shard_map/ppermute | solution.py:533
  323.6 25.8 %collective-permute-start.35 = (bf16[4,192,3584]{2,1,0:T(8,128)(2,1)}, bf16[4,192,3584]{2,1,0:T(8,128)(2,1)}, u32[]{:S(2)}, u32[]{:S(2)}) collective-permute-start(bf16[4,192,3584]{2,1,0:T(8,128)(2,1)} %get-tuple-element.256), channel_id=1, source_target_pairs={{0,4},{4,0},{8,12},{12,8},{16,20},{20,16},{24,28},{28,24},{1,5},{5... | collective-permute-start | bytes 16515080 | tf_op jit(solution)/shard_map/ppermute | solution.py:529
  323.6 25.8 %collective-permute-start.34 = (bf16[4,192,1792]{2,1,0:T(8,128)(2,1)S(1)}, bf16[4,192,1792]{2,1,0:T(8,128)(2,1)}, u32[]{:S(2)}, u32[]{:S(2)}) collective-permute-start(bf16[4,192,1792]{2,1,0:T(8,128)(2,1)S(1)} %get-tuple-element.255), channel_id=1, source_target_pairs={{0,4},{4,0},{8,12},{12,8},{16,20},{20,16},{24,28},{28,24},{1,5},{5... | collective-permute-start | bytes 8257544 | tf_op jit(solution)/shard_map/ppermute | solution.py:529
  329.8 19.6 %collective-permute-start.33 = (bf16[256,1536]{1,0:T(8,128)(2,1)S(1)}, bf16[256,1536]{1,0:T(8,128)(2,1)S(1)}, u32[]{:S(2)}, u32[]{:S(2)}) collective-permute-start(bf16[256,1536]{1,0:T(8,128)(2,1)S(1)} %get-tuple-element.254), channel_id=1, source_target_pairs={{0,1},{4,2},{1,0},{5,3},{6,7},{2,4},{7,6},{3,5},{8,9},{12,10},{9,8... | collective-permute-start | bytes 2359304 | tf_op jit(solution)/shard_map/ppermute | solution.py:563
  349.4 12.7 %collective-permute-start.36 = (bf16[256,1536]{1,0:T(8,128)(2,1)S(1)}, bf16[256,1536]{1,0:T(8,128)(2,1)S(1)}, u32[]{:S(2)}, u32[]{:S(2)}) collective-permute-start(bf16[256,1536]{1,0:T(8,128)(2,1)S(1)} %collective-permute-done.33), channel_id=1, source_target_pairs={{4,5},{5,4},{2,3},{3,2},{12,13},{13,12},{10,11},{11,10},{20,21},{2... | collective-permute-start | bytes 2359304 | tf_op jit(solution)/shard_map/ppermute | solution.py:572
  363.0 140.7 %reduce-scatter.5.cloned.1.call-start = ((), (), s32[]{:S(2)}) async-start(), calls=%async_computation.4 | async-start | bytes 6881280 | tf_op jit(solution)/shard_map/reduce_scatter | solution.py:727
  365.0 20.2 %collective-permute-start.39 = (bf16[256,1536]{1,0:T(8,128)(2,1)}, bf16[256,1536]{1,0:T(8,128)(2,1)}, u32[]{:S(2)}, u32[]{:S(2)}) collective-permute-start(bf16[256,1536]{1,0:T(8,128)(2,1)} %get-tuple-element.347), channel_id=1, source_target_pairs={{0,1},{3,2},{4,5},{7,6},{8,9},{11,10},{12,13},{15,14},{16,17},{19,... | collective-permute-start | bytes 2359304 | tf_op jit(solution)/shard_map/ppermute | solution.py:549
  370.6 14.6 %collective-permute-start.37 = (bf16[256,1536]{1,0:T(8,128)(2,1)}, bf16[256,1536]{1,0:T(8,128)(2,1)}, u32[]{:S(2)}, u32[]{:S(2)}) collective-permute-start(bf16[256,1536]{1,0:T(8,128)(2,1)} %get-tuple-element.264.part_0), channel_id=1, source_target_pairs={{0,4},{4,0},{8,12},{12,8},{16,20},{20,16},{24,28},{28,24},{1,5},{5... | collective-permute-start | bytes 2359304 | tf_op jit(solution)/shard_map/ppermute | solution.py:529
  372.8 12.4 %collective-permute-start.38 = (bf16[256,1536]{1,0:T(8,128)(2,1)}, bf16[256,1536]{1,0:T(8,128)(2,1)}, u32[]{:S(2)}, u32[]{:S(2)}) collective-permute-start(bf16[256,1536]{1,0:T(8,128)(2,1)} %get-tuple-element.265.part_1), channel_id=1, source_target_pairs={{0,4},{4,0},{8,12},{12,8},{16,20},{20,16},{24,28},{28,24},{1,5},{5... | collective-permute-start | bytes 2359304 | tf_op jit(solution)/shard_map/ppermute | solution.py:529
  375.3 59.8 %collective-permute-start.42 = (bf16[256,1536]{1,0:T(8,128)(2,1)}, bf16[256,1536]{1,0:T(8,128)(2,1)S(1)}, u32[]{:S(2)}, u32[]{:S(2)}) collective-permute-start(bf16[256,1536]{1,0:T(8,128)(2,1)} %get-tuple-element.347), channel_id=1, source_target_pairs={{1,2},{2,1},{5,6},{6,5},{9,10},{10,9},{13,14},{14,13},{17,18},{18,... | collective-permute-start | bytes 2359304 | tf_op jit(solution)/shard_map/ppermute | solution.py:541
  376.5 58.7 %collective-permute-start.41 = (bf16[256,1536]{1,0:T(8,128)(2,1)S(1)}, bf16[256,1536]{1,0:T(8,128)(2,1)S(1)}, u32[]{:S(2)}, u32[]{:S(2)}) collective-permute-start(bf16[256,1536]{1,0:T(8,128)(2,1)S(1)} %copy-done.57), channel_id=1, source_target_pairs={{0,1},{1,0},{2,3},{3,2},{4,5},{5,4},{6,7},{7,6},{8,9},{9,8},{10,11... | collective-permute-start | bytes 2359304 | tf_op jit(solution)/shard_map/ppermute | solution.py:533
  397.5 40.2 %collective-permute-start.40 = (bf16[256,1536]{1,0:T(8,128)(2,1)S(1)}, bf16[256,1536]{1,0:T(8,128)(2,1)S(1)}, u32[]{:S(2)}, u32[]{:S(2)}) collective-permute-start(bf16[256,1536]{1,0:T(8,128)(2,1)S(1)} %add_convert_fusion.2), channel_id=1, source_target_pairs={{0,2},{2,0},{1,3},{3,1},{4,6},{6,4},{5,7},{7,5},{8,10},{10,8},{9,1... | collective-permute-start | bytes 2359304 | tf_op jit(solution)/shard_map/ppermute | solution.py:537
  403.6 31.6 %collective-permute-start.43 = (bf16[2,192,384]{2,1,0:T(8,128)(2,1)S(1)}, bf16[2,192,384]{2,1,0:T(8,128)(2,1)S(1)}, u32[]{:S(2)}, u32[]{:S(2)}) collective-permute-start(bf16[2,192,384]{2,1,0:T(8,128)(2,1)S(1)} %get-tuple-element.373), channel_id=1, source_target_pairs={{0,8},{4,12},{8,0},{12,4},{16,24},{20,28},{24,16},{28,20},{1,9},{5... | collective-permute-start | bytes 884744 | tf_op jit(solution)/shard_map/ppermute | solution.py:643
  405.8 29.5 %collective-permute-start.44 = (bf16[2,192,384]{2,1,0:T(8,128)(2,1)S(1)}, bf16[2,192,384]{2,1,0:T(8,128)(2,1)S(1)}, u32[]{:S(2)}, u32[]{:S(2)}) collective-permute-start(bf16[2,192,384]{2,1,0:T(8,128)(2,1)S(1)} %get-tuple-element.371), channel_id=1, source_target_pairs={{0,16},{4,20},{8,24},{12,28},{16,0},{20,4},{24,8},{28,12},{1,17},{... | collective-permute-start | bytes 884744 | tf_op jit(solution)/shard_map/ppermute | solution.py:643
  441.7 9.9 %collective-permute-start.45 = (bf16[4,128,1536]{2,1,0:T(8,128)(2,1)}, bf16[4,128,1536]{2,1,0:T(8,128)(2,1)}, u32[]{:S(2)}, u32[]{:S(2)}) collective-permute-start(bf16[4,128,1536]{2,1,0:T(8,128)(2,1)} %get-tuple-element.344), channel_id=1, source_target_pairs={{0,4},{4,0},{8,12},{12,8},{16,20},{20,16},{24,28},{28,24},{1,5},{5... | collective-permute-start | bytes 4718600 | tf_op jit(solution)/shard_map/ppermute | solution.py:529
  443.2 15.7 %collective-permute-start.49 = (bf16[192,384]{1,0:T(8,128)(2,1)S(1)}, bf16[192,384]{1,0:T(8,128)(2,1)S(1)}, u32[]{:S(2)}, u32[]{:S(2)}) collective-permute-start(bf16[192,384]{1,0:T(8,128)(2,1)S(1)} %dynamic-slice_bitcast_fusion.15), channel_id=1, source_target_pairs={{0,16},{4,20},{8,24},{12,28},{16,0},{20,4},{24,8},{28,12},{1,17},{... | collective-permute-start | bytes 442376 | tf_op jit(solution)/shard_map/ppermute | solution.py:643
  446.9 12.1 %collective-permute-start.50 = (bf16[192,384]{1,0:T(8,128)(2,1)S(1)}, bf16[192,384]{1,0:T(8,128)(2,1)S(1)}, u32[]{:S(2)}, u32[]{:S(2)}) collective-permute-start(bf16[192,384]{1,0:T(8,128)(2,1)S(1)} %dynamic-slice_bitcast_fusion.14), channel_id=1, source_target_pairs={{0,8},{4,12},{8,0},{12,4},{16,24},{20,28},{24,16},{28,20},{1,9},{5... | collective-permute-start | bytes 442376 | tf_op jit(solution)/shard_map/ppermute | solution.py:643
  452.8 20.1 %collective-permute-start.47 = (bf16[2,192,640]{2,1,0:T(8,128)(2,1)}, bf16[2,192,640]{2,1,0:T(8,128)(2,1)}, u32[]{:S(2)}, u32[]{:S(2)}) collective-permute-start(bf16[2,192,640]{2,1,0:T(8,128)(2,1)} %get-tuple-element.365), channel_id=1, source_target_pairs={{0,8},{4,12},{8,0},{12,4},{16,24},{20,28},{24,16},{28,20},{1,9},{5... | collective-permute-start | bytes 1474568 | tf_op jit(solution)/shard_map/ppermute | solution.py:643
  455.9 21.8 %collective-permute-start.48 = (bf16[2,192,640]{2,1,0:T(8,128)(2,1)}, bf16[2,192,640]{2,1,0:T(8,128)(2,1)}, u32[]{:S(2)}, u32[]{:S(2)}) collective-permute-start(bf16[2,192,640]{2,1,0:T(8,128)(2,1)} %get-tuple-element.363), channel_id=1, source_target_pairs={{0,16},{4,20},{8,24},{12,28},{16,0},{20,4},{24,8},{28,12},{1,17},{... | collective-permute-start | bytes 1474568 | tf_op jit(solution)/shard_map/ppermute | solution.py:643
  458.9 10.9 %collective-permute-start.46 = (bf16[128,1536]{1,0:T(8,128)(2,1)}, bf16[128,1536]{1,0:T(8,128)(2,1)}, u32[]{:S(2)}, u32[]{:S(2)}) collective-permute-start(bf16[128,1536]{1,0:T(8,128)(2,1)} %get-tuple-element.343), channel_id=1, source_target_pairs={{0,1},{1,0},{2,3},{3,2},{4,5},{5,4},{6,7},{7,6},{8,9},{9,8},{10,11... | collective-permute-start | bytes 1179656 | tf_op jit(solution)/shard_map/ppermute | solution.py:533
  478.9 9.9 %collective-permute-start.53 = (bf16[192,640]{1,0:T(8,128)(2,1)S(1)}, bf16[192,640]{1,0:T(8,128)(2,1)S(1)}, u32[]{:S(2)}, u32[]{:S(2)}) collective-permute-start(bf16[192,640]{1,0:T(8,128)(2,1)S(1)} %dynamic-slice_bitcast_fusion.13), channel_id=1, source_target_pairs={{0,16},{4,20},{8,24},{12,28},{16,0},{20,4},{24,8},{28,12},{1,17},{... | collective-permute-start | bytes 737288 | tf_op jit(solution)/shard_map/ppermute | solution.py:643
  480.2 8.7 %collective-permute-start.54 = (bf16[192,640]{1,0:T(8,128)(2,1)S(1)}, bf16[192,640]{1,0:T(8,128)(2,1)S(1)}, u32[]{:S(2)}, u32[]{:S(2)}) collective-permute-start(bf16[192,640]{1,0:T(8,128)(2,1)S(1)} %dynamic-slice_bitcast_fusion.12), channel_id=1, source_target_pairs={{0,8},{4,12},{8,0},{12,4},{16,24},{20,28},{24,16},{28,20},{1,9},{5... | collective-permute-start | bytes 737288 | tf_op jit(solution)/shard_map/ppermute | solution.py:643
  480.3 37.9 %collective-permute-start.52 = (bf16[128,1536]{1,0:T(8,128)(2,1)}, bf16[128,1536]{1,0:T(8,128)(2,1)}, u32[]{:S(2)}, u32[]{:S(2)}) collective-permute-start(bf16[128,1536]{1,0:T(8,128)(2,1)} %get-tuple-element.340), channel_id=1, source_target_pairs={{0,1},{1,0},{2,3},{3,2},{4,5},{5,4},{6,7},{7,6},{8,9},{9,8},{10,11... | collective-permute-start | bytes 1179656 | tf_op jit(solution)/shard_map/ppermute | solution.py:533
  490.8 10.7 %collective-permute-start.55 = (bf16[192,1024]{1,0:T(8,128)(2,1)}, bf16[192,1024]{1,0:T(8,128)(2,1)}, u32[]{:S(2)}, u32[]{:S(2)}) collective-permute-start(bf16[192,1024]{1,0:T(8,128)(2,1)} %broadcast_select_fusion.10), channel_id=1, source_target_pairs={{0,4},{4,0},{8,12},{12,8},{16,20},{20,16},{24,28},{28,24},{1,5},{5... | collective-permute-start | bytes 1179656 | tf_op jit(solution)/shard_map/ppermute | solution.py:529
  492.6 25.6 %collective-permute-start.51 = (bf16[128,1536]{1,0:T(8,128)(2,1)}, bf16[128,1536]{1,0:T(8,128)(2,1)}, u32[]{:S(2)}, u32[]{:S(2)}) collective-permute-start(bf16[128,1536]{1,0:T(8,128)(2,1)} %add_convert_fusion.7), channel_id=1, source_target_pairs={{0,2},{2,0},{1,3},{3,1},{4,6},{6,4},{5,7},{7,5},{8,10},{10,8},{9,1... | collective-permute-start | bytes 1179656 | tf_op jit(solution)/shard_map/ppermute | solution.py:537
  494.0 3.7 collective-permute-start.57
  497.7 3.7 collective-permute-start.58
  518.2 4.2 collective-permute-start.61
  521.9 5.8 %collective-permute-start.60 = (bf16[128,1536]{1,0:T(8,128)(2,1)S(1)}, bf16[128,1536]{1,0:T(8,128)(2,1)S(1)}, u32[]{:S(2)}, u32[]{:S(2)}) collective-permute-start(bf16[128,1536]{1,0:T(8,128)(2,1)S(1)} %fusion.4), channel_id=1, source_target_pairs={{0,4},{4,0},{8,12},{12,8},{16,20},{20,16},{24,28},{28,24},{1,5},{5... | collective-permute-start | bytes 1179656 | tf_op jit(solution)/shard_map/ppermute | solution.py:529
  522.4 4.7 collective-permute-start.62
  526.5 18.4 %collective-permute-start.59 = (bf16[192,1024]{1,0:T(8,128)(2,1)S(1)}, bf16[192,1024]{1,0:T(8,128)(2,1)S(1)}, u32[]{:S(2)}, u32[]{:S(2)}) collective-permute-start(bf16[192,1024]{1,0:T(8,128)(2,1)S(1)} %copy-done.64), channel_id=1, source_target_pairs={{0,2},{2,0},{1,3},{3,1},{4,6},{6,4},{5,7},{7,5},{8,10},{10,8},{9,1... | collective-permute-start | bytes 1179656 | tf_op jit(solution)/shard_map/ppermute | solution.py:537
  (75 other events, 553.6 us)
Sparse Core Ops, SparseCore 0:
  58.1 91.6 all-gather.1
  363.1 44.8 reduce-scatter.2
  411.0 78.1 reduce-scatter.4

commit v2 on v1

v2 whole, which is shorter than its diff:
```python
import functools

import jax
import jax.numpy as jnp
from jax import lax
from jax.experimental import pallas as pl
from jax.experimental.pallas import tpu as pltpu
from jax.sharding import PartitionSpec as P

HEAD_DIMENSION = 64
STEP = 10
QUERY_GROUP = 3
AXES = ("dp", "tensor")

eps_norm = 1e-05
rope_base = 1000000.0
beta_one = 0.9
beta_two = 0.999
adam_eps = 1e-08
decay_matrix = 0.1
rate_matrix = 0.03
rate_output = 0.15
rate_gains = 0.8
bf16 = jnp.bfloat16
f32 = jnp.float32
VMEM_LIMIT = 58 * 1024 * 1024
SMALL = pl.CostEstimate(flops=1000, bytes_accessed=1000, transcendentals=0)


def whole(value):
    zeros = (0,) * len(value.shape)
    return pl.BlockSpec(value.shape, lambda i: zeros, pipeline_mode=pl.Buffered(1))


def scalars(count):
    return [pl.BlockSpec(memory_space=pltpu.SMEM)] * count


def dot(left, right, left_dim, right_dim):
    return lax.dot_general(
        left, right, (((left_dim,), (right_dim,)), ((), ())), preferred_element_type=f32
    )


def norm_rows(row_block, gain_vec):
    inverse = lax.rsqrt(jnp.mean(row_block * row_block, axis=-1, keepdims=True) + eps_norm)
    return row_block * inverse * gain_vec


def rope_tables(positions, head_size):
    inverse_freq = rope_base ** (-(jnp.arange(head_size // 2, dtype=f32) * 2.0) / head_size)
    angles = positions.astype(f32)[:, None] * inverse_freq[None, :]
    cos_part, sin_part = jnp.cos(angles), jnp.sin(angles)
    return (
        jnp.concatenate([cos_part] * 4, axis=1),
        jnp.concatenate([-sin_part, sin_part] * 2, axis=1),
    )


def adam_step(weight, first_old, second_old, gradient, step_rate, decay_rate):
    first_new = beta_one * first_old + (1.0 - beta_one) * gradient
    second_new = beta_two * second_old + (1.0 - beta_two) * gradient * gradient
    fix_one = 1.0 - beta_one**STEP
    fix_two = 1.0 - beta_two**STEP
    update = first_new / fix_one / (jnp.sqrt(second_new / fix_two) + adam_eps)
    return (weight - step_rate * (update + decay_rate * weight), first_new, second_new)


PAIR = 2 * HEAD_DIMENSION


def lanes_of(value):
    return lax.broadcasted_iota(jnp.int32, value.shape, 1)


def swap_halves(value):
    half = HEAD_DIMENSION // 2
    low = lanes_of(value) % HEAD_DIMENSION < half
    return jnp.where(low, pltpu.roll(value, PAIR - half, 1), pltpu.roll(value, half, 1))


def two_parts(value):
    high = value.astype(bf16)
    return high, (value - high.astype(f32)).astype(bf16)


def head_means(value):
    shape = (PAIR, PAIR)
    one, two = (lax.broadcasted_iota(jnp.int32, shape, d) // HEAD_DIMENSION for d in (0, 1))
    weights = jnp.where(one == two, 1.0 / HEAD_DIMENSION, 0.0).astype(bf16)
    high, low = two_parts(value)
    return dot(high, weights, 1, 0) + dot(low, weights, 1, 0)


def is_value(index, value):
    at_head = [(2 * index + k) % (QUERY_GROUP + 2) == QUERY_GROUP + 1 for k in range(2)]
    if not any(at_head):
        return None
    return (lanes_of(value) < HEAD_DIMENSION) == at_head[0]


def unless(mask, value, other):
    return value if mask is None else jnp.where(mask, other, value)


def as_row(column):
    return jnp.broadcast_to(column, (column.shape[0], 128)).T[:1, :]


def place_parts(place_ref, part_refs, whole_ref, scale):
    rows = part_refs[0].shape[0]
    for j, part_ref in enumerate(part_refs):
        at_row = pl.multiple_of((j ^ place_ref[0]) * rows, rows)
        value = part_ref[...]
        if scale is not None:
            value = (value.astype(f32) * scale).astype(bf16)
        whole_ref[pl.ds(at_row, rows), :] = value


def split_halves(core_ref, value, stage_ref, mine_ref, other_ref, index):
    half = value.shape[0] // 2
    stage_ref[...] = value
    core = core_ref[0]
    mine_ref[index] = stage_ref[pl.ds(pl.multiple_of(core * half, half), half), :]
    other_ref[index] = stage_ref[pl.ds(pl.multiple_of((1 - core) * half, half), half), :]


def place_blocks(begins_ref, block_refs, whole_ref):
    for k, block_ref in enumerate(block_refs):
        begin = pl.multiple_of(begins_ref[k], 16)
        whole_ref[pl.ds(begin, block_ref.shape[0]), :] = block_ref[...]


def attention_forward_kernel(count, place_ref, begins_ref, *refs):
    part_refs, refs = refs[:4], refs[4:]
    block_refs, refs = refs[:count], refs[count:]
    (
        gain_ref,
        head_gain_ref,
        cos_ref,
        sin_ref,
        start_ref,
        weight_ref,
        normed_ref,
        projected_ref,
        q_ref,
        k_ref,
        v_ref,
        out_ref,
        lse_ref,
    ) = refs
    place_blocks(begins_ref, block_refs, weight_ref)
    size = HEAD_DIMENSION
    heads, length, _ = q_ref.shape
    group = QUERY_GROUP
    kv = heads // group
    block = min(256, length)
    place_parts(place_ref, part_refs, normed_ref, gain_ref[...])
    for i in range(length // block):
        here = pl.ds(i * block, block)
        projected = dot(normed_ref[here, :], weight_ref[...], 1, 0)
        projected_ref[here, :] = projected
        cos_part, sin_part = cos_ref[here, :], sin_ref[here, :]
        for t in range(projected.shape[1] // PAIR):
            raw = projected[:, t * PAIR : (t + 1) * PAIR]
            keep = is_value(t, raw)
            inverse = unless(keep, lax.rsqrt(head_means(raw * raw) + eps_norm), 1.0)
            normed = raw * inverse * head_gain_ref[:, t * PAIR : (t + 1) * PAIR]
            turned = normed * unless(keep, cos_part, 1.0) + swap_halves(normed) * unless(
                keep, sin_part, 0.0
            )
            turned = turned.astype(bf16)
            for k in range(2):
                j, g = divmod(2 * t + k, group + 2)
                piece = turned[:, k * size : (k + 1) * size]
                if g < group:
                    q_ref[j * group + g, here, :] = piece * jnp.asarray(size**-0.5, bf16)
                elif g == group:
                    k_ref[j, here, :] = piece
                else:
                    v_ref[j, here, :] = piece
    row_at = lax.broadcasted_iota(jnp.int32, (block, block), 0)
    col_at = lax.broadcasted_iota(jnp.int32, (block, block), 1)
    causal = jnp.concatenate([col_at <= row_at] * group, axis=0)
    col_all = lax.broadcasted_iota(jnp.int32, (group * block, block), 1)
    ones = jnp.ones((block, size), bf16)
    for j in range(kv):
        for i in range(length // block):
            here = pl.ds(i * block, block)
            queries = jnp.concatenate(
                [q_ref[j * group + g, here, :] for g in range(group)], axis=0
            )
            start = jnp.concatenate([start_ref[here, :]] * group, axis=0)
            total = jnp.zeros((group * block, 2 * size), f32)
            for b in range(i + 1):
                there = pl.ds(b * block, block)
                scores = dot(queries, k_ref[j, there, :], 1, 1)
                allowed = col_all >= start - b * block
                if b == i:
                    allowed = allowed & causal
                weights = jnp.where(allowed, jnp.exp(scores), 0.0).astype(bf16)
                values = jnp.concatenate([v_ref[j, there, :], ones], axis=1)
                total = total + dot(weights, values, 1, 0)
            row_sum = total[:, size : size + 1]
            output = (total[:, :size] / row_sum).astype(bf16)
            log_sum = jnp.log(row_sum)
            for g in range(group):
                h = j * group + g
                part = slice(g * block, (g + 1) * block)
                out_ref[here, h * size : (h + 1) * size] = output[part]
                lse_ref[h, :, here] = as_row(log_sum[part])


def attention_branch_kernel(count, core_ref, begins_ref, *refs):
    block_refs = refs[:count]
    attended_ref, weight_ref, mine_ref, other_ref, stage_ref = refs[count:]
    place_blocks(begins_ref, block_refs, weight_ref)
    shard = attended_ref.shape[0] // 4
    for i in range(4):
        value = dot(attended_ref[i * shard : (i + 1) * shard, :], weight_ref[...], 1, 1)
        split_halves(core_ref, value.astype(bf16), stage_ref, mine_ref, other_ref, i)


def attention_forward(place, parts, blocks, begins, gain_attn, head_gains, tables, start):
    rows, width = parts[0].shape
    length = 4 * rows
    size = HEAD_DIMENSION
    columns = blocks[0].shape[1]
    kv = columns // ((QUERY_GROUP + 2) * size)
    heads = kv * QUERY_GROUP
    operands = (*parts, *blocks, gain_attn, head_gains, *tables, start)
    results = (
        jax.ShapeDtypeStruct((width, columns), bf16),
        jax.ShapeDtypeStruct((length, width), bf16),
        jax.ShapeDtypeStruct((length, columns), f32),
        jax.ShapeDtypeStruct((heads, length, size), bf16),
        jax.ShapeDtypeStruct((kv, length, size), bf16),
        jax.ShapeDtypeStruct((kv, length, size), bf16),
        jax.ShapeDtypeStruct((length, heads * size), bf16),
        jax.ShapeDtypeStruct((heads, 1, length), f32),
    )
    return pl.pallas_call(
        functools.partial(attention_forward_kernel, len(blocks)),
        grid=(1,),
        in_specs=scalars(2) + [whole(value) for value in operands],
        out_specs=tuple(whole(value) for value in results),
        out_shape=results,
        compiler_params=pltpu.CompilerParams(vmem_limit_bytes=VMEM_LIMIT),
        cost_estimate=SMALL,
    )(place, begins, *operands)


def attention_branch(core, blocks, begins, attended):
    length, columns = attended.shape
    width = 4 * (blocks[0].shape[0]) if len(blocks) > 1 else blocks[0].shape[0]
    half = jax.ShapeDtypeStruct((4, length // 8, width), bf16)
    operands = (*blocks, attended)
    results = (jax.ShapeDtypeStruct((width, columns), bf16), half, half)
    return pl.pallas_call(
        functools.partial(attention_branch_kernel, len(blocks)),
        grid=(1,),
        in_specs=scalars(2) + [whole(value) for value in operands],
        out_specs=tuple(whole(value) for value in results),
        out_shape=results,
        scratch_shapes=[pltpu.VMEM((length // 4, width), bf16)],
        compiler_params=pltpu.CompilerParams(vmem_limit_bytes=VMEM_LIMIT),
        cost_estimate=SMALL,
    )(core, begins, *operands)


def attention_turn_kernel(
    place_ref, part_0, part_1, part_2, part_3, weight_ref, out_ref, grads_ref, dot_ref, dw_ref, whole_ref
):
    size = HEAD_DIMENSION
    place_parts(place_ref, (part_0, part_1, part_2, part_3), whole_ref, None)
    heads, length, _ = grads_ref.shape
    block = min(256, length)
    shape = (dot_ref.shape[0], heads * size)
    of_head = (
        lax.broadcasted_iota(jnp.int32, shape, 0)
        == lax.broadcasted_iota(jnp.int32, shape, 1) // size
    ).astype(bf16)
    for i in range(length // block):
        here = pl.ds(i * block, block)
        grads = dot(whole_ref[here, :], weight_ref[...], 1, 0).astype(bf16)
        high, low = two_parts(grads.astype(f32) * out_ref[here, :].astype(f32))
        dot_ref[:, here] = dot(of_head, high, 1, 1) + dot(of_head, low, 1, 1)
        for h in range(heads):
            grads_ref[h, here, :] = grads[:, h * size : (h + 1) * size]
    dw_ref[...] = dot(whole_ref[...], out_ref[...], 0, 0).astype(bf16)


def attention_turn(place, parts, weight, attended):
    rows, width = parts[0].shape
    length, columns = attended.shape
    heads = columns // HEAD_DIMENSION
    operands = (*parts, weight, attended)
    results = (
        jax.ShapeDtypeStruct((heads, length, HEAD_DIMENSION), bf16),
        jax.ShapeDtypeStruct((-(-heads // 8) * 8, length), f32),
        jax.ShapeDtypeStruct((width, columns), bf16),
    )
    return pl.pallas_call(
        attention_turn_kernel,
        grid=(1,),
        in_specs=scalars(1) + [whole(value) for value in operands],
        out_specs=tuple(whole(value) for value in results),
        out_shape=results,
        scratch_shapes=[pltpu.VMEM((length, width), bf16)],
        compiler_params=pltpu.CompilerParams(vmem_limit_bytes=VMEM_LIMIT),
        cost_estimate=SMALL,
    )(place, *operands)


def attention_backward_kernel(
    core_ref,
    q_ref,
    k_ref,
    v_ref,
    g_ref,
    lse_ref,
    dot_ref,
    start_ref,
    projected_ref,
    head_gain_ref,
    cos_ref,
    sin_ref,
    weight_ref,
    normed_ref,
    gain_ref,
    back_ref,
    mine_ref,
    other_ref,
    head_sum_ref,
    gain_sum_ref,
    grad_ref,
    dk_ref,
    dv_ref,
    stage_ref,
):
    size = HEAD_DIMENSION
    heads, length, _ = q_ref.shape
    group = QUERY_GROUP
    kv = heads // group
    block = min(256, length)
    lanes = group * block
    key_at = lax.broadcasted_iota(jnp.int32, (block, block), 0)
    row_at = lax.broadcasted_iota(jnp.int32, (block, block), 1)
    causal = jnp.concatenate([key_at <= row_at] * group, axis=1)
    key_all = lax.broadcasted_iota(jnp.int32, (block, lanes), 0)
    dk_ref[...] = jnp.zeros_like(dk_ref)
    dv_ref[...] = jnp.zeros_like(dv_ref)
    head_sum_ref[...] = jnp.zeros_like(head_sum_ref)
    gain_sum_ref[...] = jnp.zeros_like(gain_sum_ref)
    for j in range(kv):
        for i in range(length // block):
            here = pl.ds(i * block, block)
            head = [j * group + g for g in range(group)]
            queries = jnp.concatenate([q_ref[h, here, :] for h in head], axis=0)
            grads = jnp.concatenate([g_ref[h, here, :] for h in head], axis=0)
            lse = jnp.concatenate([lse_ref[h, :, here] for h in head], axis=1)
            row_dot = jnp.concatenate([dot_ref[h : h + 1, here] for h in head], axis=1)
            start = jnp.concatenate([start_ref[:, here]] * group, axis=1)
            dq = jnp.zeros((size, lanes), f32)
            for b in range(i + 1):
                there = pl.ds(b * block, block)
                keys = k_ref[j, there, :]
                scores = dot(keys, queries, 1, 1)
                allowed = key_all >= start - b * block
                if b == i:
                    allowed = allowed & causal
                probs = jnp.where(allowed, jnp.exp(scores - lse), 0.0)
                grad_probs = dot(v_ref[j, there, :], grads, 1, 1)
                grad_scores = (probs * (grad_probs - row_dot)).astype(bf16)
                dv_ref[j, there, :] += dot(probs.astype(bf16), grads, 1, 0)
                dk_ref[j, there, :] += dot(grad_scores, queries, 1, 0)
                dq = dq + dot(keys, grad_scores, 0, 0)
            for g in range(group):
                column = (j * (group + 2) + g) * size
                grad_ref[here, column : column + size] = (
                    dq[:, g * block : (g + 1) * block].T * size**-0.5
                )
        key_column = (j * (group + 2) + group) * size
        grad_ref[:, key_column : key_column + size] = dk_ref[j]
        grad_ref[:, key_column + size : key_column + 2 * size] = dv_ref[j]
    shard = length // 4
    for i in range(4):
        here = pl.ds(i * shard, shard)
        cos_part, sin_part = cos_ref[here, :], sin_ref[here, :]
        for t in range(back_ref.shape[1] // PAIR):
            columns = slice(t * PAIR, (t + 1) * PAIR)
            given = grad_ref[here, columns]
            keep = is_value(t, given)
            grad = given * unless(keep, cos_part, 1.0) + swap_halves(
                given * unless(keep, sin_part, 0.0)
            )
            raw = projected_ref[here, columns]
            inverse = lax.rsqrt(head_means(raw * raw) + eps_norm)
            scaled = raw * inverse
            head_sum_ref[:, columns] += jnp.sum(grad * scaled, axis=0, keepdims=True)
            weighted = grad * head_gain_ref[:, columns]
            back = inverse * (weighted - scaled * head_means(weighted * scaled))
            back_ref[here, columns] = unless(keep, back, given).astype(bf16)
        term = dot(back_ref[here, :], weight_ref[...], 1, 1)
        gain_sum_ref[...] += jnp.sum(
            term * normed_ref[here, :].astype(f32), axis=0, keepdims=True
        )
        split_halves(core_ref, term.astype(bf16), stage_ref, mine_ref, other_ref, i)
    gain_sum_ref[...] = gain_sum_ref[...] / gain_ref[...]


def attention_backward(core, queries, keys, values, grads, lse, row_dot, start, projected, *rest):
    heads, length, size = queries.shape
    kv = keys.shape[0]
    normed = rest[-2]
    width = normed.shape[1]
    half = jax.ShapeDtypeStruct((4, length // 8, width), bf16)
    operands = (queries, keys, values, grads, lse, row_dot, start, projected) + rest
    results = (
        jax.ShapeDtypeStruct(projected.shape, bf16),
        half,
        half,
        jax.ShapeDtypeStruct((1, projected.shape[1]), f32),
        jax.ShapeDtypeStruct((1, width), f32),
    )
    return pl.pallas_call(
        attention_backward_kernel,
        grid=(1,),
        in_specs=scalars(1) + [whole(value) for value in operands],
        out_specs=tuple(whole(value) for value in results),
        out_shape=results,
        scratch_shapes=[
            pltpu.VMEM(projected.shape, f32),
            pltpu.VMEM((kv, length, size), f32),
            pltpu.VMEM((kv, length, size), f32),
            pltpu.VMEM((length // 4, width), bf16),
        ],
        compiler_params=pltpu.CompilerParams(vmem_limit_bytes=VMEM_LIMIT),
        cost_estimate=SMALL,
    )(core, *operands)


TILE = 256


def pack_units_kernel(both_ref, down_ref, out_ref):
    columns = both_ref.shape[2]
    rows = both_ref.shape[1]
    for i in range(out_ref.shape[1] // (3 * TILE)):
        first, last = i * TILE, min(columns, (i + 1) * TILE)
        parts = (both_ref[0, :, first:last], both_ref[1, :, first:last], down_ref[:, first:last])
        for k, part in enumerate(parts):
            if last - first < TILE:
                part = jnp.concatenate(
                    [part, jnp.zeros((rows, TILE - (last - first)), f32)], axis=1
                )
            at_column = (3 * i + k) * TILE
            out_ref[:, at_column : at_column + TILE] = part.astype(bf16)


def pack_units(gate_up, down):
    rows, columns = gate_up.shape[1:]
    steps = -(-columns // TILE)
    vmem = pl.BlockSpec(memory_space=pltpu.VMEM)
    return pl.pallas_call(
        pack_units_kernel,
        in_specs=[vmem, vmem],
        out_specs=vmem,
        out_shape=jax.ShapeDtypeStruct((rows, steps * 3 * TILE), bf16),
        compiler_params=pltpu.CompilerParams(vmem_limit_bytes=VMEM_LIMIT),
        cost_estimate=SMALL,
    )(gate_up, down)


def adam_kernel(weight_ref, first_ref, second_ref, sum_ref, *out_refs):
    parts = weight_ref.shape[0]
    groups = sum_ref.shape[1] // (parts * TILE)
    for p in range(parts):
        for k in range(groups):
            columns = slice(k * TILE, (k + 1) * TILE)
            at_sum = (k * parts + p) * TILE
            new = adam_step(
                weight_ref[p, :, columns],
                first_ref[p, :, columns],
                second_ref[p, :, columns],
                sum_ref[:, at_sum : at_sum + TILE].astype(f32),
                rate_matrix,
                decay_matrix,
            )
            for ref, value in zip(out_refs, new):
                ref[p, :, columns] = value


def adam_units(weight, first, second, summed, begin):
    parts, rows, columns = weight.shape
    groups = 2
    state = pl.BlockSpec((parts, rows, groups * TILE), lambda i: (0, 0, i))
    wide = parts * groups * TILE
    return pl.pallas_call(
        adam_kernel,
        grid=(-(-columns // (groups * TILE)),),
        in_specs=[state] * 3 + [pl.BlockSpec((rows, wide), lambda i: (0, begin // wide + i))],
        out_specs=(state,) * 3,
        out_shape=(jax.ShapeDtypeStruct(weight.shape, f32),) * 3,
        compiler_params=pltpu.CompilerParams(vmem_limit_bytes=VMEM_LIMIT),
        cost_estimate=SMALL,
    )(weight, first, second, summed)


def units_forward_kernel(count, *refs):
    row_refs, grad_refs, units_ref = refs[:count], refs[count : 2 * count], refs[2 * count]
    rows_out, grads_out, hidden_ref, both_ref = refs[-4:]

    @pl.when(pl.program_id(0) == 0)
    def _():
        for k in range(count):
            part = pl.ds(k * row_refs[k].shape[0], row_refs[k].shape[0])
            rows_out[part, :] = row_refs[k][...]
            grads_out[part, :] = grad_refs[k][...]

    rows = rows_out[...]
    gate_out = dot(rows, units_ref[:, :TILE], 1, 0)
    up_out = dot(rows, units_ref[:, TILE : 2 * TILE], 1, 0)
    grad_hidden = dot(grads_out[...], units_ref[:, 2 * TILE :], 1, 0)
    gate_sig = jax.nn.sigmoid(gate_out)
    gate_act = gate_out * gate_sig
    hidden_ref[...] = (gate_act * up_out).astype(bf16)
    both_ref[:, :TILE] = (
        grad_hidden * up_out * (gate_sig + gate_act * (1.0 - gate_sig))
    ).astype(bf16)
    both_ref[:, TILE:] = (grad_hidden * gate_act).astype(bf16)


def units_forward(rows, grads, units, buffers, index):
    count, (length, width) = len(rows), rows[0].shape
    steps = units.shape[1] // (3 * TILE)
    full = pl.BlockSpec((length, width), lambda i: (0, 0))
    kept = pl.BlockSpec((count * length, width), lambda i: (index, 0))
    held = () if buffers is None else buffers
    return pl.pallas_call(
        functools.partial(units_forward_kernel, count),
        grid=(steps,),
        in_specs=[full] * (2 * count)
        + [pl.BlockSpec((width, 3 * TILE), lambda i: (0, i))]
        + [pl.BlockSpec(memory_space=pl.ANY)] * len(held),
        out_specs=(
            kept,
            kept,
            pl.BlockSpec((count * length, TILE), lambda i: (index, i)),
            pl.BlockSpec((count * length, 2 * TILE), lambda i: (index, i)),
        ),
        out_shape=(
            jax.ShapeDtypeStruct((4 * length, width), bf16),
            jax.ShapeDtypeStruct((4 * length, width), bf16),
            jax.ShapeDtypeStruct((4 * length, steps * TILE), bf16),
            jax.ShapeDtypeStruct((4 * length, steps * 2 * TILE), bf16),
        ),
        input_output_aliases={2 * count + 1 + k: k for k in range(len(held))},
        compiler_params=pltpu.CompilerParams(vmem_limit_bytes=VMEM_LIMIT),
        cost_estimate=SMALL,
    )(*rows, *grads, units, *held)


def units_back_kernel(both_ref, units_ref, out_ref):
    total = None
    for i in range(both_ref.shape[1] // (2 * TILE)):
        term = dot(
            both_ref[:, i * 2 * TILE : (i + 1) * 2 * TILE],
            units_ref[:, i * 3 * TILE : (i * 3 + 2) * TILE],
            1,
            1,
        )
        total = term if total is None else total + term
    out_ref[...] = total.astype(bf16)


def units_down_kernel(hidden_ref, units_ref, out_ref):
    total = None
    for i in range(hidden_ref.shape[1] // TILE):
        term = dot(
            hidden_ref[:, i * TILE : (i + 1) * TILE],
            units_ref[:, (i * 3 + 2) * TILE : (i * 3 + 3) * TILE],
            1,
            1,
        )
        total = term if total is None else total + term
    out_ref[...] = total.astype(bf16)


def units_to_width(kernel, values, units, first, count):
    width = units.shape[0]
    block, columns = values.shape[0] // 4, values.shape[1]
    length = block * count
    return pl.pallas_call(
        kernel,
        grid=(width // TILE,),
        in_specs=[
            pl.BlockSpec((length, columns), lambda i: (first // count, 0)),
            pl.BlockSpec((TILE, units.shape[1]), lambda i: (i, 0)),
        ],
        out_specs=pl.BlockSpec((length, TILE), lambda i: (0, i)),
        out_shape=jax.ShapeDtypeStruct((length, width), bf16),
        compiler_params=pltpu.CompilerParams(vmem_limit_bytes=VMEM_LIMIT),
        cost_estimate=SMALL,
    )(values, units)


def units_add_kernel(*refs):
    out_ref = refs[-1]
    begin = 0
    for kept_ref, other_ref in zip(refs[0:-1:2], refs[1:-1:2]):
        columns = kept_ref.shape[2]
        out_ref[0, :, begin : begin + columns] = (
            kept_ref[0].astype(f32) + other_ref[0].astype(f32)
        ).astype(bf16)
        begin += columns


def units_add(*values):
    pairs, rows, _ = values[0].shape
    columns = sum(value.shape[2] for value in values[::2])
    return pl.pallas_call(
        units_add_kernel,
        grid=(pairs,),
        in_specs=[
            pl.BlockSpec((1, rows, value.shape[2]), lambda i: (i, 0, 0)) for value in values
        ],
        out_specs=pl.BlockSpec((1, rows, columns), lambda i: (i, 0, 0)),
        out_shape=jax.ShapeDtypeStruct((pairs, rows, columns), bf16),
        compiler_params=pltpu.CompilerParams(vmem_limit_bytes=VMEM_LIMIT),
        cost_estimate=SMALL,
    )(*values)


def units_gradient_kernel(core_ref, left_ref, right_ref, kept_ref, given_ref, total_ref):
    total_ref[...] = dot(left_ref[...], right_ref[...], 0, 0)
    core = core_ref[0]
    pairs, rows, _ = kept_ref.shape
    for p in range(pairs):
        for c, ref in ((core, kept_ref), (1 - core, given_ref)):
            at_row = pl.multiple_of((2 * p + c) * rows, 16)
            ref[p] = total_ref[pl.ds(at_row, rows), :].astype(bf16)


def units_gradient_parts(left, right, core):
    length, width = left.shape
    columns = right.shape[1]
    count = lax.axis_size("dp")
    rows = width // count
    tile = 2 * TILE if columns % (2 * TILE) == 0 else TILE
    out = pl.BlockSpec((count // 2, rows, tile), lambda i, c: (0, 0, i))
    shape = jax.ShapeDtypeStruct((count // 2, rows, columns), bf16)
    return pl.pallas_call(
        units_gradient_kernel,
        grid_spec=pltpu.PrefetchScalarGridSpec(
            num_scalar_prefetch=1,
            grid=(columns // tile,),
            in_specs=[
                pl.BlockSpec((length, width), lambda i, c: (0, 0)),
                pl.BlockSpec((length, tile), lambda i, c: (0, i)),
            ],
            out_specs=(out, out),
            scratch_shapes=[pltpu.VMEM((width, tile), f32)],
        ),
        out_shape=(shape, shape),
        compiler_params=pltpu.CompilerParams(vmem_limit_bytes=VMEM_LIMIT),
        cost_estimate=SMALL,
    )(core[None], left, right)


def swap_core(value):
    count = lax.axis_size("dp")
    return lax.ppermute(value, "dp", [(i, i ^ 1) for i in range(count)])


def swap_near(value):
    return lax.ppermute(value, "tensor", [(0, 1), (1, 0), (2, 3), (3, 2)])


def swap_far(value):
    return lax.ppermute(value, "tensor", [(0, 2), (2, 0), (1, 3), (3, 1)])


def swap_middle(value):
    return lax.ppermute(value, "tensor", [(1, 2), (2, 1)])


def swap_opposite(value):
    return lax.ppermute(value, "tensor", [(i, 3 - i) for i in range(4)])


def to_ends(value):
    return lax.ppermute(value, "tensor", [(1, 0), (2, 3)])


def from_ends(value):
    return lax.ppermute(value, "tensor", [(0, 1), (3, 2)])


def device_of(pair, core, z):
    return (2 * pair + core) * 4 + z


def owner_swap(value):
    perm = []
    for p in range(lax.axis_size("dp") // 2):
        for z in range(4):
            own = z // 2
            perm.append((device_of(p, own, z), device_of(p, own, z ^ 1)))
            perm.append((device_of(p, 1 - own, z), device_of(p, own, z ^ 2)))
    return lax.ppermute(value, AXES, perm)


def guest_swap(value):
    perm = []
    for p in range(lax.axis_size("dp") // 2):
        for z in range(4):
            guest = 1 - z // 2
            perm.append((device_of(p, guest, z), device_of(p, guest, z ^ 1)))
    return lax.ppermute(value, AXES, perm)


def heads_scatter_near(mine, other, z):
    def term(index):
        return at(mine, index, 0).astype(f32) + at(other, index, 0).astype(f32)

    away = swap_near(term(z ^ 3).astype(bf16))
    return term(z), term(z ^ 2), swap_near(term(z ^ 1).astype(bf16)), away


def heads_scatter_end(home, far, own, core):
    kept = jnp.where(own, home, far.astype(f32))
    given = swap_core(jnp.where(own, far, home.astype(bf16))).astype(f32)
    return jnp.concatenate(
        [jnp.where(core == 0, kept, given), jnp.where(core == 0, given, kept)], axis=0
    )


def gather_dp(value):
    bit = 1
    while bit < lax.axis_size("dp"):
        other = swap_dp(value, bit)
        upper = (lax.axis_index("dp") & bit) != 0
        value = jnp.concatenate(
            [jnp.where(upper, other, value), jnp.where(upper, value, other)], axis=0
        )
        bit *= 2
    return value


def gather_tensor(value, bit):
    other = lax.ppermute(value, "tensor", [(i, i ^ bit) for i in range(4)])
    upper = (lax.axis_index("tensor") & bit) != 0
    return jnp.concatenate(
        [jnp.where(upper, other, value), jnp.where(upper, value, other)], axis=1
    )


def sum_dp(value, first, last):
    bit = first
    while bit < last:
        value = value + swap_dp(value, bit)
        bit *= 2
    return value


def pair_groups():
    count = lax.axis_size("dp")
    return [list(range(c, count, 2)) for c in range(2)]


def swap_dp(value, mask):
    count = lax.axis_size("dp")
    return lax.ppermute(value, "dp", [(i, i ^ mask) for i in range(count)])


def gather_pairs_begin(value):
    if lax.axis_size("dp") != 8:
        return (lax.all_gather(value, "dp", axis=0, tiled=True, axis_index_groups=pair_groups()),)
    return value, swap_dp(value, 2), swap_dp(value, 4)


def gather_pairs_end(parts):
    if len(parts) == 1:
        return parts, jnp.zeros((1,), jnp.int32)
    value, by_two, by_four = parts
    pair = lax.axis_index("dp") >> 1
    rows = value.shape[0]
    half = rows // 2
    low, high = swap_dp(by_four[:half], 2), swap_dp(by_two[half:], 4)
    begins = jnp.stack([pair, pair ^ 1, pair ^ 2, pair ^ 3, pair ^ 3]) * rows
    begins = begins + jnp.array([0, 0, 0, 0, half], jnp.int32)
    return (value, by_two, by_four, low, high), begins


def at(value, index, axis):
    return lax.dynamic_index_in_dim(value, index, axis, keepdims=False)


def add_low(left, right):
    return (left.astype(f32) + right.astype(f32)).astype(bf16)


def scatter_pairs_begin(value):
    if lax.axis_size("dp") != 8:
        return (
            lax.psum_scatter(
                value, "dp", scatter_dimension=0, tiled=True, axis_index_groups=pair_groups()
            ),
        )
    pair = lax.axis_index("dp") >> 1
    one, two = pair & 1, pair >> 1
    rows = value.shape[0] // 8
    parts = value.reshape((2, 2, 2, rows) + value.shape[1:])
    first, second = parts[:, :, 0], parts[:, :, 1]
    by_two = swap_dp(at(first, one ^ 1, 1), 2)
    by_four = swap_dp(at(second, two ^ 1, 0), 4)
    return at(first, one, 1), by_two, at(second, two, 0), by_four


def scatter_pairs_middle(parts):
    if len(parts) == 1:
        return parts
    return add_low(parts[0], parts[1]), add_low(parts[2], parts[3])


def scatter_pairs_end(parts):
    if len(parts) == 1:
        return parts[0]
    pair = lax.axis_index("dp") >> 1
    one, two = pair & 1, pair >> 1
    first, second = parts
    by_four = swap_dp(at(first, two ^ 1, 0), 4)
    by_two = swap_dp(at(second, one ^ 1, 0), 2)
    first = add_low(at(first, two, 0), by_four)
    second = add_low(at(second, one, 0), by_two)
    return jnp.concatenate([first, second], axis=0)


def heads_pair(shard, far, own, core):
    kept = jnp.where(own, shard, far)
    other = swap_core(jnp.where(own, far, shard))
    return jnp.concatenate(
        [jnp.where(core == 0, kept, other), jnp.where(core == 0, other, kept)], axis=0
    )


def heads_home(pair, own, core):
    rows = pair.shape[0] // 2
    kept = jnp.where(core == 0, pair[:rows], pair[rows:])
    other = swap_core(jnp.where(core == 0, pair[rows:], pair[:rows]))
    return jnp.where(own, kept, other), jnp.where(own, other, kept)


def units_gradient(summed):
    return lax.psum_scatter(
        summed.reshape(-1, summed.shape[-1]),
        "dp",
        scatter_dimension=0,
        tiled=True,
        axis_index_groups=pair_groups(),
    )


def together(*values):
    return lax.optimization_barrier(values)


def shards(
    block_in,
    out_grad,
    positions,
    qkv_weight,
    qkv_first,
    qkv_second,
    out_weight,
    out_first,
    out_second,
    gate_up,
    gate_up_first,
    gate_up_second,
    down_weight,
    down_first,
    down_second,
    norm_gains,
    norm_gains_first,
    norm_gains_second,
):
    model_width = block_in.shape[1]
    z = lax.axis_index("tensor")
    core = lax.axis_index("dp") & 1
    own = core == z // 2
    place = jnp.where(own, z, z ^ 2)[None]

    units_columns = gate_up.shape[2]
    qkv_own = qkv_weight.astype(bf16)
    qkv_own, gains_own, positions = together(qkv_own, norm_gains[None], positions)
    qkv_far = swap_far(qkv_own)
    out_own = out_weight.astype(bf16).T
    out_far = swap_far(out_own)
    gains_near = gather_tensor(gather_dp(gains_own)[:, None], 1)
    inverse_in = lax.rsqrt(jnp.mean(block_in * block_in, axis=-1, keepdims=True) + eps_norm)
    scaled_in = block_in * inverse_in
    head_positions = jnp.where(own, positions, swap_core(positions))
    (
        scaled_b,
        qkv_own,
        qkv_far,
        head_positions,
        units_shard,
        grad_own,
        out_own,
        out_far,
        gains_near,
    ) = together(
        scaled_in.astype(bf16),
        qkv_own,
        qkv_far,
        head_positions,
        pack_units(gate_up, down_weight.T),
        out_grad.astype(bf16),
        out_own,
        out_far,
        gains_near,
    )

    scaled_first = owner_swap(scaled_b)
    qkv_parts = gather_pairs_begin(heads_pair(qkv_own, qkv_far, own, core))
    out_parts = gather_pairs_begin(heads_pair(out_own, out_far, own, core))
    gains_all = gather_tensor(gains_near, 2).reshape(1, -1)
    tables = rope_tables(head_positions, HEAD_DIMENSION)
    length = head_positions.shape[0]
    start = jnp.maximum(jnp.arange(length, dtype=jnp.int32) - head_positions, 0)
    start_column = start[:, None]
    scaled_first, qkv_parts, gains_all, units_shard, tables, start_column, grad_own, out_parts = (
        together(
            scaled_first,
            qkv_parts,
            gains_all,
            units_shard,
            tables,
            start_column,
            grad_own,
            out_parts,
        )
    )
    gain_attn = gains_all[:, :model_width]
    gain_q = gains_all[0, model_width : model_width + HEAD_DIMENSION]
    gain_k = gains_all[0, model_width + HEAD_DIMENSION : model_width + 2 * HEAD_DIMENSION]
    kv_local = qkv_weight.shape[1] // ((QUERY_GROUP + 2) * HEAD_DIMENSION)
    head_gains = jnp.concatenate(
        ([gain_q] * QUERY_GROUP + [gain_k, jnp.ones_like(gain_k)]) * kv_local
    )[None]
    gain_ffn = gains_all[:, model_width + 2 * HEAD_DIMENSION :]

    scaled_second = guest_swap(scaled_first)
    scaled_mine = jnp.where(own, scaled_b, scaled_first)
    scaled_other = swap_core(scaled_mine)
    qkv_blocks, qkv_begins = gather_pairs_end(qkv_parts)
    out_blocks, out_begins = gather_pairs_end(out_parts)
    half = grad_own.shape[0] // 2
    grad_far = swap_far(grad_own[:half])
    (
        qkv_blocks,
        scaled_second,
        scaled_mine,
        scaled_other,
        units_shard,
        grad_own,
        grad_far,
        out_blocks,
    ) = together(
        qkv_blocks,
        scaled_second,
        scaled_mine,
        scaled_other,
        units_shard,
        grad_own,
        grad_far,
        out_blocks,
    )

    units = lax.all_gather(units_shard, "dp", axis=0, tiled=True)
    grad_far_rest = swap_far(grad_own[half:])
    grad_near = swap_near(grad_own)
    scaled_next = jnp.where(own, scaled_first, scaled_second)
    scaled_parts = (scaled_mine, scaled_next, scaled_other, swap_core(scaled_next))
    w_qkv, normed_all, projected, queries_b, keys_b, values_b, attended, lse = attention_forward(
        place, scaled_parts, qkv_blocks, qkv_begins, gain_attn, head_gains, tables, start_column
    )
    attended, grad_far, grad_far_rest, grad_near, grad_own = together(
        attended, grad_far, grad_far_rest, grad_near, grad_own
    )
    grad_middle_part = swap_middle(grad_own)
    grad_far = jnp.concatenate([grad_far, grad_far_rest], axis=0)
    w_out, branch_mine, branch_other = attention_branch(
        core[None], out_blocks, out_begins, attended
    )
    branch_mine, branch_other, grad_far = together(
        branch_mine, swap_core(branch_other), grad_far
    )
    home, term_far, near, away = heads_scatter_near(branch_mine, branch_other, z)
    away, term_far, grad_middle_part = together(away, term_far, grad_middle_part)
    far = swap_far((term_far + away.astype(f32)).astype(bf16))
    far, home, near = together(far, home, near)
    middle = block_in + heads_scatter_end(home + near.astype(f32), far, own, core)

    inverse_mid = lax.rsqrt(jnp.mean(middle * middle, axis=-1, keepdims=True) + eps_norm)
    scaled_mid = middle * inverse_mid
    rows_own = (scaled_mid * gain_ffn).astype(bf16)
    rows_far = swap_far(rows_own)
    rows_near = swap_near(rows_own)
    inner = (z == 1) | (z == 2)
    buffers = units_forward((rows_own,), (grad_own,), units, None, 2)
    rows_far, rows_near, rows_own, buffers = together(rows_far, rows_near, rows_own, buffers)
    grad_ends = to_ends(grad_far)
    rows_ends = to_ends(rows_far)
    rows_middle = swap_middle(rows_own)
    buffers = units_forward((rows_near, rows_far), (grad_near, grad_far), units, buffers, 0)
    rows_all, grad_all, hidden_b, dboth = buffers
    back_first = units_to_width(units_back_kernel, dboth, units, 0, 2)
    rows_ends, rows_middle, grad_ends, back_first, buffers = together(
        rows_ends, rows_middle, grad_ends, back_first, buffers
    )
    rows = block_in.shape[0]
    from_near = swap_near(back_first[:rows])
    from_far = swap_far(back_first[rows:])
    rows_last = jnp.where(inner, rows_middle, rows_ends)
    grad_last = jnp.where(inner, grad_middle_part, grad_ends)
    rows_all, grad_all, hidden_b, dboth = units_forward(
        (rows_last,), (grad_last,), units, buffers, 3
    )
    back_second = units_to_width(units_back_kernel, dboth, units, 2, 2)
    from_near, from_far, back_second, rows_all, grad_all, hidden_b, dboth = together(
        from_near, from_far, back_second, rows_all, grad_all, hidden_b, dboth
    )
    from_last = swap_opposite(back_second[rows:])
    back_own = back_second[:rows]
    down_kept, down_given = units_gradient_parts(grad_all, hidden_b, core)
    both_kept, both_given = units_gradient_parts(rows_all, dboth, core)
    from_last, down_kept, down_given, both_kept, both_given = together(
        from_last, down_kept, down_given, both_kept, both_given
    )
    grad_normed_two = (
        back_own.astype(f32)
        + from_near.astype(f32)
        + from_far.astype(f32)
        + from_last.astype(f32)
    )

    grad_gain_ffn = jnp.sum(grad_normed_two * scaled_mid, axis=0)
    weighted = grad_normed_two * gain_ffn
    grad_middle = out_grad + inverse_mid * (
        weighted - scaled_mid * jnp.mean(weighted * scaled_mid, axis=-1, keepdims=True)
    )
    grad_mid_b, grad_gain_ffn, hidden_b, down_kept, down_given, both_kept, both_given = together(
        grad_middle.astype(bf16),
        grad_gain_ffn,
        hidden_b,
        down_kept,
        down_given,
        both_kept,
        both_given,
    )
    grad_mid_first = owner_swap(grad_mid_b)
    units_sum = units_add(both_kept, swap_core(both_given), down_kept, swap_core(down_given))
    down_last = units_to_width(units_down_kernel, hidden_b, units, 3, 1)
    grad_mid_first, down_last, units_sum = together(grad_mid_first, down_last, units_sum)
    units_sum = units_gradient(units_sum)
    grad_mid_second = guest_swap(grad_mid_first)
    branch_ends = from_ends(down_last)
    branch_middle = swap_middle(down_last)
    grad_mid_mine = jnp.where(own, grad_mid_b, grad_mid_first)
    grad_mid_other = swap_core(grad_mid_mine)
    down_rest = units_to_width(units_down_kernel, hidden_b, units, 0, 3)
    down_near, down_far, down_own = (down_rest[k * rows : (k + 1) * rows] for k in range(3))
    (
        grad_mid_second,
        grad_mid_mine,
        grad_mid_other,
        branch_ends,
        branch_middle,
        down_near,
        down_far,
        down_own,
    ) = together(
        grad_mid_second,
        grad_mid_mine,
        grad_mid_other,
        branch_ends,
        branch_middle,
        down_near,
        down_far,
        down_own,
    )
    down_far = add_low(down_far, branch_ends)
    grad_mid_next = jnp.where(own, grad_mid_first, grad_mid_second)
    grad_mid_parts = (grad_mid_mine, grad_mid_next, grad_mid_other, swap_core(grad_mid_next))
    grad_mid_parts, down_far, down_near = together(grad_mid_parts, down_far, down_near)

    branch_far = swap_far(down_far)
    branch_near = swap_near(down_near)
    grad_attended, row_dot, grad_out_w = attention_turn(place, grad_mid_parts, w_out, attended)
    grad_attended, row_dot, grad_out_w = together(grad_attended, row_dot, grad_out_w)
    grad_projected, part_mine, part_other, head_sums, gain_sums = attention_backward(
        core[None],
        queries_b,
        keys_b,
        values_b,
        grad_attended,
        lse,
        row_dot,
        start[None, :],
        projected,
        head_gains,
        *tables,
        w_qkv,
        normed_all,
        gain_attn,
    )
    head_sums = head_sums.reshape(-1, QUERY_GROUP + 2, HEAD_DIMENSION)
    gain_total = jnp.concatenate(
        [
            gain_sums[0],
            jnp.sum(head_sums[:, :QUERY_GROUP], axis=(0, 1)),
            jnp.sum(head_sums[:, QUERY_GROUP], axis=0),
            grad_gain_ffn,
        ]
    )
    (
        grad_projected,
        part_mine,
        part_other,
        gain_total,
        branch_far,
        branch_near,
        grad_out_w,
    ) = together(
        grad_projected,
        part_mine,
        part_other,
        gain_total,
        branch_far,
        branch_near,
        grad_out_w,
    )

    part_other = swap_core(part_other)
    grad_qkv = dot(normed_all, grad_projected, 0, 0).astype(bf16)
    gain_total = sum_dp(gain_total, 1, 2)
    part_mine, part_other, grad_qkv, gain_total, grad_out_w, branch_far = together(
        part_mine, part_other, grad_qkv, gain_total, grad_out_w, branch_far
    )
    home, term_far, near, away = heads_scatter_near(part_mine, part_other, z)
    qkv_parts = scatter_pairs_begin(grad_qkv)
    out_parts = scatter_pairs_begin(grad_out_w)
    gain_total = gain_total + swap_far(gain_total)
    block_out = (
        middle
        + down_own.astype(f32)
        + branch_near.astype(f32)
        + branch_middle.astype(f32)
        + branch_far.astype(f32)
    )
    qkv_parts, out_parts = scatter_pairs_middle(qkv_parts), scatter_pairs_middle(out_parts)
    far_term = (term_far + away.astype(f32)).astype(bf16)
    far_term, qkv_parts, out_parts, gain_total, block_out = together(
        far_term, qkv_parts, out_parts, gain_total, block_out
    )
    far = swap_far(far_term)
    qkv_pair = scatter_pairs_end(qkv_parts)
    out_pair = scatter_pairs_end(out_parts)
    far, home, near, qkv_pair, out_pair, gain_total = together(
        far, home, near, qkv_pair, out_pair, gain_total
    )
    heads_home_own, heads_home_away = heads_home(
        jnp.concatenate([qkv_pair, out_pair], axis=1), own, core
    )
    grad_normed = heads_scatter_end(home + near.astype(f32), far, own, core)
    heads_home_own, heads_home_away, gain_total, grad_normed, units_sum = together(
        heads_home_own, heads_home_away, gain_total, grad_normed, units_sum
    )
    heads_away = swap_far(heads_home_away)
    gain_total = gain_total + swap_near(gain_total)
    gate_up_new = adam_units(gate_up, gate_up_first, gate_up_second, units_sum, 0)
    down_new = adam_units(
        down_weight.T[None],
        down_first.T[None],
        down_second.T[None],
        units_sum,
        2 * units_sum.shape[1] // 3,
    )
    gain_total = sum_dp(gain_total, 2, lax.axis_size("dp"))
    weighted = grad_normed * gain_attn
    in_grad = grad_middle + inverse_in * (
        weighted - scaled_in * jnp.mean(weighted * scaled_in, axis=-1, keepdims=True)
    )
    heads_away, in_grad, gate_up_new, down_new = together(
        heads_away, in_grad, gate_up_new, down_new
    )
    sum_heads = heads_home_own.astype(f32) + heads_away.astype(f32)
    down_new = tuple(value[0].T for value in down_new)
    qkv_columns = qkv_weight.shape[1]
    sum_qkv = sum_heads[:, :qkv_columns]
    sum_out = sum_heads[:, qkv_columns:].T
    gain_count = norm_gains.shape[0]
    gain_at = (lax.axis_index("dp") * 4 + z) * gain_count
    gain_grads = lax.dynamic_slice_in_dim(gain_total, gain_at, gain_count)

    qkv_new = adam_step(qkv_weight, qkv_first, qkv_second, sum_qkv, rate_matrix, decay_matrix)
    out_new = adam_step(out_weight, out_first, out_second, sum_out, rate_output, decay_matrix)
    gains_new = adam_step(
        norm_gains, norm_gains_first, norm_gains_second, gain_grads, rate_gains, 0.0
    )
    return (block_out, in_grad, *qkv_new, *out_new, *gate_up_new, *down_new, *gains_new)


def solution(mesh):
    tokens = P(("dp", "tensor"), None)
    by_rows = (P("dp", "tensor"),) * 3
    by_columns = (P("tensor", "dp"),) * 3
    stacked = (P(None, "dp", "tensor"),) * 3
    gains = (P(("dp", "tensor")),) * 3
    states = by_rows + by_columns + stacked + by_columns + gains
    return jax.shard_map(
        shards,
        mesh=mesh,
        in_specs=(tokens, tokens, P("dp")) + states,
        out_specs=(tokens, tokens) + states,
        check_vma=False,
    )
```

time: 561 us -> 518 us (0.923)
  waiting for transfers between devices: 172 us -> 137 us
  local copies, waits for them, and re-layouts: 42.7 us -> 22.8 us
  starting transfers between devices: 69.1 us -> 88 us
  other arithmetic: 62.6 us -> 52.7 us
  Pallas kernels: 184 us -> 190 us
    convert_element_type x12 -> x9, other arithmetic: 19.2 us -> 3.02 us  [add_low(): return (left.astype(f32) + right.astype(f32)).astype(bf16)]
    ppermute x9, waiting for transfers between devices: 23.7 us -> 36.2 us  [swap_near(): return lax.ppermute(value, 'tensor', [(0, 1), (1, 0), (2, 3), (3, 2)])]
    unnamed x146 -> x113, local copies, waits for them, and re-layouts: 16.9 us -> 4.62 us
    ppermute x9 -> x11, waiting for transfers between devices: 71.4 us -> 59.6 us  [swap_far(): return lax.ppermute(value, 'tensor', [(0, 2), (2, 0), (1, 3), (3, 1)])]
    pallas_call x3 -> x4, Pallas kernels: 34.2 us -> 45.2 us  [units_to_width(): pl.pallas_call(kernel, grid=(width // TILE,), in_specs=[pl.BlockSpec((len...]
    pallas_call x9 -> x10, Pallas kernels: 122 us -> 112 us  [the longest x3 39 us: units_forward(): pl.pallas_call(functools.partial(units_forward_kernel, count), grid=(step...]
    ppermute x2, waiting for transfers between devices: 11.6 us -> 2.02 us  [gather_tensor(): other = lax.ppermute(value, 'tensor', [(i, i ^ bit) for i in range(4)])]
    squeeze x10 -> x8, local copies, waits for them, and re-layouts: 8.39 us -> 0.25 us  [at(): return lax.dynamic_index_in_dim(value, index, axis, keepdims=False)]
  transfers between devices with their start and end apart: 66 -> 71, of which waited for: 32 -> 31; matrix products, arithmetic and copies ran while one was open for 16% -> 12% of each run, Pallas kernels for 30% -> 37%
where the time goes in v2:
time: 518 us; the launch traced here: 511 us
  Pallas kernels  190 us (37%)
  waiting for transfers between devices  137 us (26%)
  starting transfers between devices  88 us (17%)
  other arithmetic  52.7 us (10%)
  local copies, waits for them, and re-layouts  22.8 us (4%)
  between operations  15.5 us (3%)
    ppermute x11, waiting for transfers between devices, swap_far(): return lax.ppermute(value, 'tensor', [(0, 2), (2, 0), (1, 3), (3, 1)])  59.6 us
    pallas_call x4, Pallas kernels, units_to_width(): pl.pallas_call(kernel, grid=(width // TILE,), in_specs=[pl.BlockSpec((len...  45.2 us
    pallas_call x3, Pallas kernels, units_forward(): pl.pallas_call(functools.partial(units_forward_kernel, count), grid=(step...  39 us
    ppermute x9, waiting for transfers between devices, swap_near(): return lax.ppermute(value, 'tensor', [(0, 1), (1, 0), (2, 3), (3, 2)])  36.2 us
    ppermute x22, waiting for transfers between devices, swap_dp(): return lax.ppermute(value, 'dp', [(i, i ^ mask) for i in range(count)])  28.9 us
    pallas_call x2, Pallas kernels, units_gradient_parts(): pl.pallas_call(units_gradient_kernel, grid_spec=pltpu.PrefetchScalarGridS...  28.8 us
    ppermute x22, starting transfers between devices, swap_dp(): return lax.ppermute(value, 'dp', [(i, i ^ mask) for i in range(count)])  23.2 us
    pallas_call x1, Pallas kernels, attention_backward(): pl.pallas_call(attention_backward_kernel, grid=(1,), in_specs=scalars(1)...  23.1 us
  transfers between devices with their start and end apart: 71, of which 31 were waited for; matrix products, arithmetic and copies ran while one was open for 12% of the time, Pallas kernels for 37%

profile of v2, /device:TPU:0, one launch (start us, length us, event | category | flops | bytes accessed | tf_op | source)
XLA Modules:
  0.0 511.1 jit_solution(17332330581570715646)
XLA Ops:
  9.0 4.0 collective-permute-start
  20.5 1.9 collective-permute-start.5
  22.4 3.7 shard_map.323
  29.3 2.0 collective-permute-done.6
  32.1 2.6 collective-permute-start.11
  36.6 1.9 fusion.19
  38.5 1.9 pad_maximum_fusion.2
  45.6 15.1 %collective-permute-done.13.refs_1_ = bf16[384,384]{1,0:T(8,128)(2,1)} collective-permute-done((bf16[384,384]{1,0:T(8,128)(2,1)S(1)}, bf16[384,384]{1,0:T(8,128)(2,1)}, u32[]{:S(2)}, u32[]{:S(2)}) %collective-permute-start.13) | collective-permute-done | bytes 294944 | tf_op jit(solution)/shard_map/ppermute | solution.py:774
  74.6 5.8 %collective-permute-done.15.refs_7_ = bf16[192,640]{1,0:T(8,128)(2,1)S(1)} collective-permute-done((bf16[192,640]{1,0:T(8,128)(2,1)S(1)}, bf16[192,640]{1,0:T(8,128)(2,1)S(1)}, u32[]{:S(2)}, u32[]{:S(2)}) %collective-permute-start.15) | collective-permute-done | bytes 245792 | tf_op jit(solution)/shard_map/ppermute | solution.py:774
  80.4 2.2 collective-permute-done.16.refs_8_
  82.6 7.0 %collective-permute-done.19 = bf16[128,1536]{1,0:T(8,128)(2,1)S(1)} collective-permute-done((bf16[128,1536]{1,0:T(8,128)(2,1)S(1)}, bf16[128,1536]{1,0:T(8,128)(2,1)S(1)}, u32[]{:S(2)}, u32[]{:S(2)}) %collective-permute-start.19) | collective-permute-done | bytes 393248 | tf_op jit(solution)/shard_map/ppermute | solution.py:681
  102.4 13.5 %shard_map.324 = (bf16[1536,640]{1,0:T(8,128)(2,1)}, bf16[1024,1536]{1,0:T(8,128)(2,1)}, f32[1024,640]{1,0:T(8,128)}, bf16[6,1024,64]{2,1,0:T(8,128)(2,1)}, bf16...) custom-call(s32[1]{0:T(128)} %bitcast.1.place_ref, ...), custom_call_target="tpu_custom_call" | custom-call | flops 1000 | bytes 1000 | tf_op jit(solution)/shard_map/pallas_call | solution.py:242
  115.9 3.9 collective-permute-done.23
  119.7 2.3 collective-permute-done.24.refs_2_
  122.0 5.3 %shard_map.325 = (bf16[1536,384]{1,0:T(8,128)(2,1)}, bf16[4,128,1536]{2,1,0:T(8,128)(2,1)}, bf16[4,128,1536]{2,1,0:T(8,128)(2,1)}) custom-call(s32[1]{0:T(128)} %bitcast.core_ref, s32[5]{0:T(128)} %multiply_add_fusion.5.begins_ref, bf16[384,384]{1,0:T(8,128)(2,1)} %copy-done.20, bf16[384,384]{1,0:T(8,128)(2,1)} %collective-permute-done.13.refs_1_, ...), custom_call_target="tpu_custom_call" | custom-call | flops 1000 | bytes 1000 | tf_op jit(solution)/shard_map/pallas_call | solution.py:259
  128.2 2.0 pad_maximum_fusion.1.refs_3_
  131.1 1.9 fusion.13
  133.0 2.0 collective-permute-start.26
  135.2 9.9 %collective-permute-done.26 = bf16[128,1536]{1,0:T(8,128)(2,1)S(1)} collective-permute-done((bf16[128,1536]{1,0:T(8,128)(2,1)S(1)}, bf16[128,1536]{1,0:T(8,128)(2,1)S(1)}, u32[]{:S(2)}, u32[]{:S(2)}) %collective-permute-start.26) | collective-permute-done | bytes 393248 | tf_op jit(solution)/shard_map/ppermute | solution.py:677
  145.1 5.5 %collective-permute-start.28 = (bf16[128,1536]{1,0:T(8,128)(2,1)S(1)}, bf16[128,1536]{1,0:T(8,128)(2,1)S(1)}, u32[]{:S(2)}, u32[]{:S(2)}) collective-permute-start(bf16[128,1536]{1,0:T(8,128)(2,1)S(1)} %add_convert_fusion.4), channel_id=1, source_target_pairs={{0,2},{2,0},{1,3},{3,1},{4,6},{6,4},{5,7},{7,5},{8,10},{10,8},{9,1... | collective-permute-start | bytes 1179656 | tf_op jit(solution)/shard_map/ppermute | solution.py:681
  150.6 5.8 %collective-permute-done.29 = bf16[128,1536]{1,0:T(8,128)(2,1)S(1)} collective-permute-done((bf16[128,1536]{1,0:T(8,128)(2,1)S(1)}, bf16[128,1536]{1,0:T(8,128)(2,1)S(1)}, u32[]{:S(2)}, u32[]{:S(2)}) %collective-permute-start.29) | collective-permute-done | bytes 393248 | tf_op jit(solution)/shard_map/ppermute | solution.py:677
  156.4 11.8 %collective-permute-done.28 = bf16[128,1536]{1,0:T(8,128)(2,1)S(1)} collective-permute-done((bf16[128,1536]{1,0:T(8,128)(2,1)S(1)}, bf16[128,1536]{1,0:T(8,128)(2,1)S(1)}, u32[]{:S(2)}, u32[]{:S(2)}) %collective-permute-start.28) | collective-permute-done | bytes 393248 | tf_op jit(solution)/shard_map/ppermute | solution.py:681
  171.8 2.1 collective-permute-start.32
  175.2 2.8 all-gather.2.cloned.1.call-done.refs_2_.refs_4_.units_ref
  178.0 11.8 %shard_map.326 = (bf16[1024,1536]{1,0:T(8,128)(2,1)}, bf16[1024,1536]{1,0:T(8,128)(2,1)}, bf16[1024,1792]{1,0:T(8,128)(2,1)}, bf16[1024,3584]{1,0:T(8,128)(2,1)}) custom-call(bf16[256,1536]{1,0:T(8,128)(2,1)} %multiply_convert_fusion.refs_0_, bf16[256,1536]{1,0:T(8,128)(2,1)} %copy-done.2, ...), custom_call_target="tpu_custom_call" | custom-call | flops 1000 | bytes 1000 | tf_op jit(solution)/shard_map/pallas_call | solution.py:540
  189.8 18.6 %collective-permute-done.31.refs_1_ = bf16[256,1536]{1,0:T(8,128)(2,1)} collective-permute-done((bf16[256,1536]{1,0:T(8,128)(2,1)}, bf16[256,1536]{1,0:T(8,128)(2,1)}, u32[]{:S(2)}, u32[]{:S(2)}) %collective-permute-start.31) | collective-permute-done | bytes 786464 | tf_op jit(solution)/shard_map/ppermute | solution.py:681
  212.3 15.4 %shard_map.327 = (bf16[1024,1536]{1,0:T(8,128)(2,1)}, bf16[1024,1536]{1,0:T(8,128)(2,1)}, bf16[1024,1792]{1,0:T(8,128)(2,1)}, bf16[1024,3584]{1,0:T(8,128)(2,1)}) custom-call(bf16[256,1536]{1,0:T(8,128)(2,1)} %collective-permute-done.32.refs_0_, ...), custom_call_target="tpu_custom_call", output_to_operand_aliasing={{0}: (5, {}), {1}: (6, {}), {2}: (7, {}), {3}: (8, {})} | custom-call | flops 1000 | bytes 1000 | tf_op jit(solution)/shard_map/pallas_call | solution.py:540
  227.6 12.3 %shard_map.328 = bf16[512,1536]{1,0:T(8,128)(2,1)} custom-call(bf16[1024,3584]{1,0:T(8,128)(2,1)} %get-tuple-element.286.both_ref.refs_6_, bf16[1536,5376]{1,0:T(8,128)(2,1)} %all-gather.2.cloned.1.call-done.refs_2_.refs_4_.units_ref), custom_call_target="tpu_custom_call" | custom-call | flops 1000 | bytes 1000 | tf_op jit(solution)/shard_map/pallas_call | solution.py:594
  239.9 2.4 collective-permute-done.33
  242.4 2.7 fusion.27
  245.0 2.8 collective-permute-start.36
  248.0 2.1 broadcast_select_fusion.refs_1_
  250.1 2.1 broadcast_select_fusion.1.refs_0_
  252.2 11.9 %shard_map.329 = (bf16[1024,1536]{1,0:T(8,128)(2,1)}, bf16[1024,1536]{1,0:T(8,128)(2,1)}, bf16[1024,1792]{1,0:T(8,128)(2,1)}, bf16[1024,3584]{1,0:T(8,128)(2,1)}) custom-call(bf16[256,1536]{1,0:T(8,128)(2,1)} %broadcast_select_fusion.1.refs_0_, ...), custom_call_target="tpu_custom_call", output_to_operand_aliasing={{0}: (3, {}), {1}: (4, {}), {2}: (5, {}), {3}: (6, {})} | custom-call | flops 1000 | bytes 1000 | tf_op jit(solution)/shard_map/pallas_call | solution.py:540
  264.0 12.3 %shard_map.330 = bf16[512,1536]{1,0:T(8,128)(2,1)} custom-call(bf16[1024,3584]{1,0:T(8,128)(2,1)} %get-tuple-element.299.both_ref.right_ref, bf16[1536,5376]{1,0:T(8,128)(2,1)} %all-gather.2.cloned.1.call-done.refs_2_.refs_4_.units_ref), custom_call_target="tpu_custom_call" | custom-call | flops 1000 | bytes 1000 | tf_op jit(solution)/shard_map/pallas_call | solution.py:594
  276.3 3.7 collective-permute-done.36
  280.0 3.4 collective-permute-done.37
  283.5 2.3 slice.96
  287.4 17.4 %shard_map.332 = (bf16[4,192,3584]{2,1,0:T(8,128)(2,1)}, bf16[4,192,3584]{2,1,0:T(8,128)(2,1)}) custom-call(s32[1]{0:T(128)} %bitcast.core_ref, bf16[1024,1536]{1,0:T(8,128)(2,1)} %get-tuple-element.298.left_ref, bf16[1024,3584]{1,0:T(8,128)(2,1)} %get-tuple-element.299.both_ref.right_ref), custom_call_target="tpu_custom_call" | custom-call | flops 1000 | bytes 1000 | tf_op jit(solution)/shard_map/pallas_call | solution.py:653
  304.8 11.4 %shard_map.331 = (bf16[4,192,1792]{2,1,0:T(8,128)(2,1)}, bf16[4,192,1792]{2,1,0:T(8,128)(2,1)}) custom-call(s32[1]{0:T(128)} %bitcast.core_ref, bf16[1024,1536]{1,0:T(8,128)(2,1)} %get-tuple-element.294.left_ref, bf16[1024,1792]{1,0:T(8,128)(2,1)} %get-tuple-element.308.right_ref.hidden_ref), custom_call_target="tpu_custom_call" | custom-call | flops 1000 | bytes 1000 | tf_op jit(solution)/shard_map/pallas_call | solution.py:653
  316.2 2.3 multiply_reduce_fusion.1
  318.6 3.2 fusion.24
  322.3 3.2 collective-permute-start.39
  325.4 8.9 %shard_map.333 = bf16[256,1536]{1,0:T(8,128)(2,1)} custom-call(bf16[1024,1792]{1,0:T(8,128)(2,1)} %get-tuple-element.308.right_ref.hidden_ref, bf16[1536,5376]{1,0:T(8,128)(2,1)} %all-gather.2.cloned.1.call-done.refs_2_.refs_4_.units_ref), custom_call_target="tpu_custom_call" | custom-call | flops 1000 | bytes 1000 | tf_op jit(solution)/shard_map/pallas_call | solution.py:594
  335.1 9.3 %shard_map.334 = bf16[4,192,5376]{2,1,0:T(8,128)(2,1)} custom-call(bf16[4,192,3584]{2,1,0:T(8,128)(2,1)} %get-tuple-element.309.refs_0_, bf16[4,192,3584]{2,1,0:T(8,128)(2,1)} %collective-permute-done.40.refs_1_, bf16[4,192,1792]{2,1,0:T(8,128)(2,1)} %get-tuple-element.311.refs_2_, bf16[4,192,1792]{2,1,0:T(8,128)(2,1)} %collective-permute-done.41.refs_3_), custom_call_target="tpu_custom_call" | custom-call | flops 1000 | bytes 1000 | tf_op jit(solution)/shard_map/pallas_call | solution.py:622
  347.4 3.5 collective-permute-start.43
  350.9 3.1 collective-permute-start.44
  354.7 11.8 %shard_map.335 = bf16[768,1536]{1,0:T(8,128)(2,1)} custom-call(bf16[1024,1792]{1,0:T(8,128)(2,1)} %get-tuple-element.308.right_ref.hidden_ref, bf16[1536,5376]{1,0:T(8,128)(2,1)} %all-gather.2.cloned.1.call-done.refs_2_.refs_4_.units_ref), custom_call_target="tpu_custom_call" | custom-call | flops 1000 | bytes 1000 | tf_op jit(solution)/shard_map/pallas_call | solution.py:594
  366.5 2.9 fusion.25
  372.7 4.4 collective-permute-start.46
  377.1 2.3 add_convert_fusion
  379.4 4.4 collective-permute-start.47
  383.9 8.1 %shard_map.336 = (bf16[6,1024,64]{2,1,0:T(8,128)(2,1)}, f32[8,1024]{1,0:T(8,128)}, bf16[1536,384]{1,0:T(8,128)(2,1)}) custom-call(s32[1]{0:T(128)} %bitcast.1.place_ref, bf16[256,1536]{1,0:T(8,128)(2,1)} %copy-done.7, bf16[256,1536]{1,0:T(8,128)(2,1)} %copy-done.8, bf16[256,1536]{1,0:T(8,128)(2,1)} %collective-permute-done.43.part_2, ...), custom_call_target="tpu_custom_call" | custom-call | flops 1000 | bytes 1000 | tf_op jit(solution)/shard_map/pallas_call | solution.py:303
  392.0 23.1 %shard_map.337 = (bf16[1024,640]{1,0:T(8,128)(2,1)}, bf16[4,128,1536]{2,1,0:T(8,128)(2,1)}, bf16[4,128,1536]{2,1,0:T(8,128)(2,1)}, f32[1,640]{1,0:T(1,128)}, f32[1,1536]{1,0:T(1,128)}) custom-call(s32[1]{0:T(128)} %bitcast.core_ref, bf16[6,1024,64]{2,1,0:T(8,128)(2,1)} %get-tuple-element.236.q_ref, bf16[2,1024,64]{2,1,0:T(8,128)(2,1)} %get-tuple-element.237.k_ref, ...), custom_call_target="tpu_custom_call" | custom-call | flops 1000 | bytes 1000 | tf_op jit(solution)/shard_map/pallas_call | solution.py:426
  416.7 2.5 collective-permute-done.47
  420.9 5.0 convolution_convert_fusion
  431.1 3.0 convert_add_fusion
  438.5 9.2 %collective-permute-done.51 = bf16[128,1536]{1,0:T(8,128)(2,1)S(1)} collective-permute-done((bf16[128,1536]{1,0:T(8,128)(2,1)S(1)}, bf16[128,1536]{1,0:T(8,128)(2,1)S(1)}, u32[]{:S(2)}, u32[]{:S(2)}) %collective-permute-start.51) | collective-permute-done | bytes 393248 | tf_op jit(solution)/shard_map/ppermute | solution.py:677
  454.6 2.7 collective-permute-start.57
  458.6 12.2 %collective-permute-done.57 = bf16[128,1536]{1,0:T(8,128)(2,1)S(1)} collective-permute-done((bf16[128,1536]{1,0:T(8,128)(2,1)S(1)}, bf16[128,1536]{1,0:T(8,128)(2,1)S(1)}, u32[]{:S(2)}, u32[]{:S(2)}) %collective-permute-start.57) | collective-permute-done | bytes 393248 | tf_op jit(solution)/shard_map/ppermute | solution.py:681
  477.1 3.2 collective-permute-done.66
  481.2 1.9 collective-permute-start.65
  486.4 8.3 %shard_map.338 = (f32[2,192,1728]{2,1,0:T(8,128)}, f32[2,192,1728]{2,1,0:T(8,128)}, f32[2,192,1728]{2,1,0:T(8,128)}) custom-call(f32[2,192,1728]{2,1,0:T(8,128)} %weight_ref.1, f32[2,192,1728]{2,1,0:T(8,128)} %first_ref.1, f32[2,192,1728]{2,1,0:T(8,128)} %second_ref.1, bf16[192,5376]{1,0:T(8,128)(2,1)} %reduce-scatter.2.cloned.1.call-done.sum_ref), custom_call_target="tpu_custom_call" | custom-call | flops 1000 | bytes 1000 | tf_op jit(solution)/shard_map/pallas_call | solution.py:499
  494.7 5.3 %shard_map.339 = (f32[1,192,1728]{2,1,0:T(8,128)}, f32[1,192,1728]{2,1,0:T(8,128)}, f32[1,192,1728]{2,1,0:T(8,128)}) custom-call(f32[1,192,1728]{2,1,0:T(8,128)} %bitcast.130, f32[1,192,1728]{2,1,0:T(8,128)} %bitcast.132, f32[1,192,1728]{2,1,0:T(8,128)} %bitcast.133, bf16[192,5376]{1,0:T(8,128)(2,1)} %reduce-scatter.2.cloned.1.call-done.sum_ref), custom_call_target="tpu_custom_call" | custom-call | flops 1000 | bytes 1000 | tf_op jit(solution)/shard_map/pallas_call | solution.py:499
  (321 shorter events, 102.1 us)
Async XLA Ops:
  7.2 170.8 %all-gather.2.cloned.1.call-start = ((), (), s32[]{:S(2)}) async-start(), calls=%async_computation.1 | async-start | bytes 18579456 | tf_op jit(solution)/shard_map/all_gather | solution.py:983
  8.4 8.3 %collective-permute-start.3 = (f32[1,100]{1,0:T(1,128)}, f32[1,100]{1,0:T(1,128)S(1)}, u32[]{:S(2)}, u32[]{:S(2)}) collective-permute-start(f32[1,100]{1,0:T(1,128)} %bitcast.137), channel_id=1, source_target_pairs={{0,4},{4,0},{8,12},{12,8},{16,20},{20,16},{24,28},{28,24},{1,5},{5... | collective-permute-start | bytes 1208 | tf_op jit(solution)/shard_map/ppermute | solution.py:774
  8.9 20.3 %collective-permute-start.1 = (s32[1024]{0:T(1024)}, s32[1024]{0:T(1024)S(1)}, u32[]{:S(2)}, u32[]{:S(2)}) collective-permute-start(s32[1024]{0:T(1024)} %param.22), channel_id=1, source_target_pairs={{0,4},{4,0},{8,12},{12,8},{16,20},{20,16},{24,28},{28,24},{1,5},{5... | collective-permute-start | bytes 12296 | tf_op jit(solution)/shard_map/ppermute | solution.py:673
  9.0 22.3 %collective-permute-start = (bf16[192,640]{1,0:T(8,128)(2,1)S(1)}, bf16[192,640]{1,0:T(8,128)(2,1)S(1)}, u32[]{:S(2)}, u32[]{:S(2)}) collective-permute-start(bf16[192,640]{1,0:T(8,128)(2,1)S(1)} %convert_element_type.284), channel_id=1, source_target_pairs={{0,2},{2,0},{1,3},{3,1},{4,6},{6,4},{5,7},{7,5},{8,10},{10,8},{9,1... | collective-permute-start | bytes 737288 | tf_op jit(solution)/shard_map/ppermute | solution.py:681
  14.0 17.3 %collective-permute-start.2 = (bf16[192,384]{1,0:T(8,128)(2,1)S(1)}, bf16[192,384]{1,0:T(8,128)(2,1)S(1)}, u32[]{:S(2)}, u32[]{:S(2)}) collective-permute-start(bf16[192,384]{1,0:T(8,128)(2,1)S(1)} %convert_bitcast_fusion), channel_id=1, source_target_pairs={{0,2},{2,0},{1,3},{3,1},{4,6},{6,4},{5,7},{7,5},{8,10},{10,8},{9,1... | collective-permute-start | bytes 442376 | tf_op jit(solution)/shard_map/ppermute | solution.py:681
  20.5 7.1 %collective-permute-start.5 = (f32[4,100]{1,0:T(4,128)S(1)}, f32[4,100]{1,0:T(4,128)S(1)}, u32[]{:S(2)}, u32[]{:S(2)}) collective-permute-start(f32[4,100]{1,0:T(4,128)S(1)} %pad_maximum_fusion.10), channel_id=1, source_target_pairs={{0,16},{4,20},{8,24},{12,28},{16,0},{20,4},{24,8},{28,12},{1,17},{... | collective-permute-start | bytes 4808 | tf_op jit(solution)/shard_map/ppermute | solution.py:774
  31.4 12.4 %collective-permute-start.12 = (bf16[192,384]{1,0:T(8,128)(2,1)S(1)}, bf16[192,384]{1,0:T(8,128)(2,1)S(1)}, u32[]{:S(2)}, u32[]{:S(2)}) collective-permute-start(bf16[192,384]{1,0:T(8,128)(2,1)S(1)} %broadcast_select_fusion.14), channel_id=1, source_target_pairs={{0,4},{4,0},{8,12},{12,8},{16,20},{20,16},{24,28},{28,24},{1,5},{5... | collective-permute-start | bytes 442376 | tf_op jit(solution)/shard_map/ppermute | solution.py:673
  32.1 12.4 %collective-permute-start.11 = (f32[8,2,100]{2,0,1:T(8,128)S(1)}, f32[8,2,100]{2,0,1:T(8,128)S(1)}, u32[]{:S(2)}, u32[]{:S(2)}) collective-permute-start(f32[8,2,100]{2,0,1:T(8,128)S(1)} %pad_maximum_fusion.9), channel_id=1, source_target_pairs={{0,2},{1,3},{2,0},{3,1},{4,6},{5,7},{6,4},{7,5},{8,10},{9,11},{10,... | collective-permute-start | bytes 19208 | tf_op jit(solution)/shard_map/ppermute | solution.py:752
  34.7 5.6 %collective-permute-start.8 = (bf16[192,640]{1,0:T(8,128)(2,1)S(1)}, bf16[192,640]{1,0:T(8,128)(2,1)S(1)}, u32[]{:S(2)}, u32[]{:S(2)}) collective-permute-start(bf16[192,640]{1,0:T(8,128)(2,1)S(1)} %broadcast_select_fusion.10), channel_id=1, source_target_pairs={{0,4},{4,0},{8,12},{12,8},{16,20},{20,16},{24,28},{28,24},{1,5},{5... | collective-permute-start | bytes 737288 | tf_op jit(solution)/shard_map/ppermute | solution.py:673
  35.0 25.8 %collective-permute-start.7 = (bf16[256,1536]{1,0:T(8,128)(2,1)}, bf16[256,1536]{1,0:T(8,128)(2,1)S(1)}, u32[]{:S(2)}, u32[]{:S(2)}) collective-permute-start(bf16[256,1536]{1,0:T(8,128)(2,1)} %multiply_convert_fusion.1), channel_id=1, source_target_pairs={{0,1},{4,2},{1,0},{5,3},{6,7},{2,4},{7,6},{3,5},{8,9},{12,10},{9,8... | collective-permute-start | bytes 2359304 | tf_op jit(solution)/shard_map/ppermute | solution.py:711
  41.3 19.5 %collective-permute-start.10 = (bf16[384,640]{1,0:T(8,128)(2,1)}, bf16[384,640]{1,0:T(8,128)(2,1)}, u32[]{:S(2)}, u32[]{:S(2)}) collective-permute-start(bf16[384,640]{1,0:T(8,128)(2,1)} %pad_maximum_fusion.4.refs_4_), channel_id=1, source_target_pairs={{0,16},{4,20},{8,24},{12,28},{16,0},{20,4},{24,8},{28,12},{1,17},{... | collective-permute-start | bytes 1474568 | tf_op jit(solution)/shard_map/ppermute | solution.py:774
  42.3 18.5 %collective-permute-start.9 = (bf16[384,640]{1,0:T(8,128)(2,1)}, bf16[384,640]{1,0:T(8,128)(2,1)}, u32[]{:S(2)}, u32[]{:S(2)}) collective-permute-start(bf16[384,640]{1,0:T(8,128)(2,1)} %pad_maximum_fusion.4.refs_4_), channel_id=1, source_target_pairs={{0,8},{4,12},{8,0},{12,4},{16,24},{20,28},{24,16},{28,20},{1,9},{5... | collective-permute-start | bytes 1474568 | tf_op jit(solution)/shard_map/ppermute | solution.py:774
  43.9 16.9 %collective-permute-start.13 = (bf16[384,384]{1,0:T(8,128)(2,1)S(1)}, bf16[384,384]{1,0:T(8,128)(2,1)}, u32[]{:S(2)}, u32[]{:S(2)}) collective-permute-start(bf16[384,384]{1,0:T(8,128)(2,1)S(1)} %pad_maximum_fusion.6.refs_0_), channel_id=1, source_target_pairs={{0,8},{4,12},{8,0},{12,4},{16,24},{20,28},{24,16},{28,20},{1,9},{5... | collective-permute-start | bytes 884744 | tf_op jit(solution)/shard_map/ppermute | solution.py:774
  44.5 16.3 %collective-permute-start.14 = (bf16[384,384]{1,0:T(8,128)(2,1)S(1)}, bf16[384,384]{1,0:T(8,128)(2,1)}, u32[]{:S(2)}, u32[]{:S(2)}) collective-permute-start(bf16[384,384]{1,0:T(8,128)(2,1)S(1)} %pad_maximum_fusion.6.refs_0_), channel_id=1, source_target_pairs={{0,16},{4,20},{8,24},{12,28},{16,0},{20,4},{24,8},{28,12},{1,17},{... | collective-permute-start | bytes 884744 | tf_op jit(solution)/shard_map/ppermute | solution.py:774
  62.9 26.8 %collective-permute-start.18 = (bf16[256,1536]{1,0:T(8,128)(2,1)S(1)}, bf16[256,1536]{1,0:T(8,128)(2,1)S(1)}, u32[]{:S(2)}, u32[]{:S(2)}) collective-permute-start(bf16[256,1536]{1,0:T(8,128)(2,1)S(1)} %broadcast_select_fusion.5.refs_0_), channel_id=1, source_target_pairs={{0,4},{4,0},{8,12},{12,8},{16,20},{20,16},{24,28},{28,24},{1,5},{5... | collective-permute-start | bytes 2359304 | tf_op jit(solution)/shard_map/ppermute | solution.py:673
  62.9 28.4 %collective-permute-start.17 = (bf16[256,1536]{1,0:T(8,128)(2,1)S(1)}, bf16[256,1536]{1,0:T(8,128)(2,1)}, u32[]{:S(2)}, u32[]{:S(2)}) collective-permute-start(bf16[256,1536]{1,0:T(8,128)(2,1)S(1)} %collective-permute-done.7), channel_id=1, source_target_pairs={{4,5},{5,4},{2,3},{3,2},{12,13},{13,12},{10,11},{11,10},{20,21},{2... | collective-permute-start | bytes 2359304 | tf_op jit(solution)/shard_map/ppermute | solution.py:720
  65.3 6.7 %collective-permute-start.20 = (bf16[192,384]{1,0:T(8,128)(2,1)S(1)}, bf16[192,384]{1,0:T(8,128)(2,1)S(1)}, u32[]{:S(2)}, u32[]{:S(2)}) collective-permute-start(bf16[192,384]{1,0:T(8,128)(2,1)S(1)} %slice.86), channel_id=1, source_target_pairs={{0,8},{4,12},{8,0},{12,4},{16,24},{20,28},{24,16},{28,20},{1,9},{5... | collective-permute-start | bytes 442376 | tf_op jit(solution)/shard_map/ppermute | solution.py:774
  67.8 6.0 %collective-permute-start.21 = (bf16[192,384]{1,0:T(8,128)(2,1)S(1)}, bf16[192,384]{1,0:T(8,128)(2,1)S(1)}, u32[]{:S(2)}, u32[]{:S(2)}) collective-permute-start(bf16[192,384]{1,0:T(8,128)(2,1)S(1)} %slice.87), channel_id=1, source_target_pairs={{0,16},{4,20},{8,24},{12,28},{16,0},{20,4},{24,8},{28,12},{1,17},{... | collective-permute-start | bytes 442376 | tf_op jit(solution)/shard_map/ppermute | solution.py:774
  68.8 20.8 %collective-permute-start.19 = (bf16[128,1536]{1,0:T(8,128)(2,1)S(1)}, bf16[128,1536]{1,0:T(8,128)(2,1)S(1)}, u32[]{:S(2)}, u32[]{:S(2)}) collective-permute-start(bf16[128,1536]{1,0:T(8,128)(2,1)S(1)} %slice.85), channel_id=1, source_target_pairs={{0,2},{2,0},{1,3},{3,1},{4,6},{6,4},{5,7},{7,5},{8,10},{10,8},{9,1... | collective-permute-start | bytes 1179656 | tf_op jit(solution)/shard_map/ppermute | solution.py:681
  72.0 8.4 %collective-permute-start.15 = (bf16[192,640]{1,0:T(8,128)(2,1)S(1)}, bf16[192,640]{1,0:T(8,128)(2,1)S(1)}, u32[]{:S(2)}, u32[]{:S(2)}) collective-permute-start(bf16[192,640]{1,0:T(8,128)(2,1)S(1)} %slice.83), channel_id=1, source_target_pairs={{0,8},{4,12},{8,0},{12,4},{16,24},{20,28},{24,16},{28,20},{1,9},{5... | collective-permute-start | bytes 737288 | tf_op jit(solution)/shard_map/ppermute | solution.py:774
  73.9 8.7 %collective-permute-start.16 = (bf16[192,640]{1,0:T(8,128)(2,1)S(1)}, bf16[192,640]{1,0:T(8,128)(2,1)S(1)}, u32[]{:S(2)}, u32[]{:S(2)}) collective-permute-start(bf16[192,640]{1,0:T(8,128)(2,1)S(1)} %slice.84), channel_id=1, source_target_pairs={{0,16},{4,20},{8,24},{12,28},{16,0},{20,4},{24,8},{28,12},{1,17},{... | collective-permute-start | bytes 737288 | tf_op jit(solution)/shard_map/ppermute | solution.py:774
  91.3 384.9 %reduce-scatter.2.cloned.1.call-start = ((), (), s32[]{:S(2)}) async-start(), calls=%async_computation.2 | async-start | bytes 10321920 | tf_op jit(solution)/shard_map/reduce_scatter | solution.py:856
  92.5 9.0 %collective-permute-start.22 = (bf16[256,1536]{1,0:T(8,128)(2,1)}, bf16[256,1536]{1,0:T(8,128)(2,1)S(1)}, u32[]{:S(2)}, u32[]{:S(2)}) collective-permute-start(bf16[256,1536]{1,0:T(8,128)(2,1)} %broadcast_select_fusion.4.refs_1_), channel_id=1, source_target_pairs={{0,4},{4,0},{8,12},{12,8},{16,20},{20,16},{24,28},{28,24},{1,5},{5... | collective-permute-start | bytes 2359304 | tf_op jit(solution)/shard_map/ppermute | solution.py:673
  94.1 28.0 %collective-permute-start.24 = (bf16[256,1536]{1,0:T(8,128)(2,1)S(1)}, bf16[256,1536]{1,0:T(8,128)(2,1)}, u32[]{:S(2)}, u32[]{:S(2)}) collective-permute-start(bf16[256,1536]{1,0:T(8,128)(2,1)S(1)} %convert_element_type.285.refs_1_), channel_id=1, source_target_pairs={{0,1},{1,0},{2,3},{3,2},{4,5},{5,4},{6,7},{7,6},{8,9},{9,8},{10,11... | collective-permute-start | bytes 2359304 | tf_op jit(solution)/shard_map/ppermute | solution.py:677
  94.7 25.0 %collective-permute-start.23 = (bf16[128,1536]{1,0:T(8,128)(2,1)S(1)}, bf16[128,1536]{1,0:T(8,128)(2,1)}, u32[]{:S(2)}, u32[]{:S(2)}) collective-permute-start(bf16[128,1536]{1,0:T(8,128)(2,1)S(1)} %slice.91), channel_id=1, source_target_pairs={{0,2},{2,0},{1,3},{3,1},{4,6},{6,4},{5,7},{7,5},{8,10},{10,8},{9,1... | collective-permute-start | bytes 1179656 | tf_op jit(solution)/shard_map/ppermute | solution.py:681
  127.3 7.8 %collective-permute-start.27 = (bf16[256,1536]{1,0:T(8,128)(2,1)S(1)}, bf16[256,1536]{1,0:T(8,128)(2,1)S(1)}, u32[]{:S(2)}, u32[]{:S(2)}) collective-permute-start(bf16[256,1536]{1,0:T(8,128)(2,1)S(1)} %convert_element_type.285.refs_1_), channel_id=1, source_target_pairs={{1,2},{2,1},{5,6},{6,5},{9,10},{10,9},{13,14},{14,13},{17,18},{18,... | collective-permute-start | bytes 2359304 | tf_op jit(solution)/shard_map/ppermute | solution.py:685
  133.0 12.0 %collective-permute-start.26 = (bf16[128,1536]{1,0:T(8,128)(2,1)S(1)}, bf16[128,1536]{1,0:T(8,128)(2,1)S(1)}, u32[]{:S(2)}, u32[]{:S(2)}) collective-permute-start(bf16[128,1536]{1,0:T(8,128)(2,1)S(1)} %get-tuple-element.412), channel_id=1, source_target_pairs={{0,1},{1,0},{2,3},{3,2},{4,5},{5,4},{6,7},{7,6},{8,9},{9,8},{10,11... | collective-permute-start | bytes 1179656 | tf_op jit(solution)/shard_map/ppermute | solution.py:677
  135.1 21.3 %collective-permute-start.29 = (bf16[128,1536]{1,0:T(8,128)(2,1)S(1)}, bf16[128,1536]{1,0:T(8,128)(2,1)S(1)}, u32[]{:S(2)}, u32[]{:S(2)}) collective-permute-start(bf16[128,1536]{1,0:T(8,128)(2,1)S(1)} %get-tuple-element.409), channel_id=1, source_target_pairs={{0,1},{1,0},{2,3},{3,2},{4,5},{5,4},{6,7},{7,6},{8,9},{9,8},{10,11... | collective-permute-start | bytes 1179656 | tf_op jit(solution)/shard_map/ppermute | solution.py:677
  145.1 23.1 %collective-permute-start.28 = (bf16[128,1536]{1,0:T(8,128)(2,1)S(1)}, bf16[128,1536]{1,0:T(8,128)(2,1)S(1)}, u32[]{:S(2)}, u32[]{:S(2)}) collective-permute-start(bf16[128,1536]{1,0:T(8,128)(2,1)S(1)} %add_convert_fusion.4), channel_id=1, source_target_pairs={{0,2},{2,0},{1,3},{3,1},{4,6},{6,4},{5,7},{7,5},{8,10},{10,8},{9,1... | collective-permute-start | bytes 1179656 | tf_op jit(solution)/shard_map/ppermute | solution.py:681
  171.8 36.7 %collective-permute-start.31 = (bf16[256,1536]{1,0:T(8,128)(2,1)}, bf16[256,1536]{1,0:T(8,128)(2,1)}, u32[]{:S(2)}, u32[]{:S(2)}) collective-permute-start(bf16[256,1536]{1,0:T(8,128)(2,1)} %multiply_convert_fusion.refs_0_), channel_id=1, source_target_pairs={{0,2},{2,0},{1,3},{3,1},{4,6},{6,4},{5,7},{7,5},{8,10},{10,8},{9,1... | collective-permute-start | bytes 2359304 | tf_op jit(solution)/shard_map/ppermute | solution.py:681
  171.8 37.7 %collective-permute-start.32 = (bf16[256,1536]{1,0:T(8,128)(2,1)}, bf16[256,1536]{1,0:T(8,128)(2,1)}, u32[]{:S(2)}, u32[]{:S(2)}) collective-permute-start(bf16[256,1536]{1,0:T(8,128)(2,1)} %multiply_convert_fusion.refs_0_), channel_id=1, source_target_pairs={{0,1},{1,0},{2,3},{3,2},{4,5},{5,4},{6,7},{7,6},{8,9},{9,8},{10,11... | collective-permute-start | bytes 2359304 | tf_op jit(solution)/shard_map/ppermute | solution.py:677
  173.9 66.0 %collective-permute-start.35 = (bf16[256,1536]{1,0:T(8,128)(2,1)}, bf16[256,1536]{1,0:T(8,128)(2,1)}, u32[]{:S(2)}, u32[]{:S(2)}) collective-permute-start(bf16[256,1536]{1,0:T(8,128)(2,1)} %pad_maximum_fusion.1.refs_3_), channel_id=1, source_target_pairs={{1,0},{2,3},{5,4},{6,7},{9,8},{10,11},{13,12},{14,15},{17,16},{18,... | collective-permute-start | bytes 2359304 | tf_op jit(solution)/shard_map/ppermute | solution.py:693
  209.4 32.9 %collective-permute-start.33 = (bf16[256,1536]{1,0:T(8,128)(2,1)}, bf16[256,1536]{1,0:T(8,128)(2,1)}, u32[]{:S(2)}, u32[]{:S(2)}) collective-permute-start(bf16[256,1536]{1,0:T(8,128)(2,1)} %collective-permute-done.31.refs_1_), channel_id=1, source_target_pairs={{1,0},{2,3},{5,4},{6,7},{9,8},{10,11},{13,12},{14,15},{17,16},{18,... | collective-permute-start | bytes 2359304 | tf_op jit(solution)/shard_map/ppermute | solution.py:693
  210.7 31.6 %collective-permute-start.34 = (bf16[256,1536]{1,0:T(8,128)(2,1)}, bf16[256,1536]{1,0:T(8,128)(2,1)}, u32[]{:S(2)}, u32[]{:S(2)}) collective-permute-start(bf16[256,1536]{1,0:T(8,128)(2,1)} %multiply_convert_fusion.refs_0_), channel_id=1, source_target_pairs={{1,2},{2,1},{5,6},{6,5},{9,10},{10,9},{13,14},{14,13},{17,18},{18,... | collective-permute-start | bytes 2359304 | tf_op jit(solution)/shard_map/ppermute | solution.py:685
  245.0 35.0 %collective-permute-start.36 = (bf16[256,1536]{1,0:T(8,128)(2,1)}, bf16[256,1536]{1,0:T(8,128)(2,1)S(1)}, u32[]{:S(2)}, u32[]{:S(2)}) collective-permute-start(bf16[256,1536]{1,0:T(8,128)(2,1)} %get-tuple-element.423), channel_id=1, source_target_pairs={{0,1},{1,0},{2,3},{3,2},{4,5},{5,4},{6,7},{7,6},{8,9},{9,8},{10,11... | collective-permute-start | bytes 2359304 | tf_op jit(solution)/shard_map/ppermute | solution.py:677
  247.8 35.7 %collective-permute-start.37 = (bf16[256,1536]{1,0:T(8,128)(2,1)}, bf16[256,1536]{1,0:T(8,128)(2,1)S(1)}, u32[]{:S(2)}, u32[]{:S(2)}) collective-permute-start(bf16[256,1536]{1,0:T(8,128)(2,1)} %get-tuple-element.422), channel_id=1, source_target_pairs={{0,2},{2,0},{1,3},{3,1},{4,6},{6,4},{5,7},{7,5},{8,10},{10,8},{9,1... | collective-permute-start | bytes 2359304 | tf_op jit(solution)/shard_map/ppermute | solution.py:681
  285.8 30.4 %collective-permute-start.38 = (bf16[256,1536]{1,0:T(8,128)(2,1)}, bf16[256,1536]{1,0:T(8,128)(2,1)}, u32[]{:S(2)}, u32[]{:S(2)}) collective-permute-start(bf16[256,1536]{1,0:T(8,128)(2,1)} %slice.96), channel_id=1, source_target_pairs={{0,3},{1,2},{2,1},{3,0},{4,7},{5,6},{6,5},{7,4},{8,11},{9,10},{10,... | collective-permute-start | bytes 2359304 | tf_op jit(solution)/shard_map/ppermute | solution.py:689
  321.8 13.3 %collective-permute-start.40 = (bf16[4,192,3584]{2,1,0:T(8,128)(2,1)}, bf16[4,192,3584]{2,1,0:T(8,128)(2,1)}, u32[]{:S(2)}, u32[]{:S(2)}) collective-permute-start(bf16[4,192,3584]{2,1,0:T(8,128)(2,1)} %get-tuple-element.310), channel_id=1, source_target_pairs={{0,4},{4,0},{8,12},{12,8},{16,20},{20,16},{24,28},{28,24},{1,5},{5... | collective-permute-start | bytes 16515080 | tf_op jit(solution)/shard_map/ppermute | solution.py:673
  321.8 13.3 %collective-permute-start.41 = (bf16[4,192,1792]{2,1,0:T(8,128)(2,1)}, bf16[4,192,1792]{2,1,0:T(8,128)(2,1)}, u32[]{:S(2)}, u32[]{:S(2)}) collective-permute-start(bf16[4,192,1792]{2,1,0:T(8,128)(2,1)} %get-tuple-element.312), channel_id=1, source_target_pairs={{0,4},{4,0},{8,12},{12,8},{16,20},{20,16},{24,28},{28,24},{1,5},{5... | collective-permute-start | bytes 8257544 | tf_op jit(solution)/shard_map/ppermute | solution.py:673
  322.3 22.2 %collective-permute-start.39 = (bf16[256,1536]{1,0:T(8,128)(2,1)S(1)}, bf16[256,1536]{1,0:T(8,128)(2,1)}, u32[]{:S(2)}, u32[]{:S(2)}) collective-permute-start(bf16[256,1536]{1,0:T(8,128)(2,1)S(1)} %get-tuple-element.307), channel_id=1, source_target_pairs={{0,1},{4,2},{1,0},{5,3},{6,7},{2,4},{7,6},{3,5},{8,9},{12,10},{9,8... | collective-permute-start | bytes 2359304 | tf_op jit(solution)/shard_map/ppermute | solution.py:711
  344.5 25.0 %collective-permute-start.42 = (bf16[256,1536]{1,0:T(8,128)(2,1)}, bf16[256,1536]{1,0:T(8,128)(2,1)}, u32[]{:S(2)}, u32[]{:S(2)}) collective-permute-start(bf16[256,1536]{1,0:T(8,128)(2,1)} %collective-permute-done.39), channel_id=1, source_target_pairs={{4,5},{5,4},{2,3},{3,2},{12,13},{13,12},{10,11},{11,10},{20,21},{2... | collective-permute-start | bytes 2359304 | tf_op jit(solution)/shard_map/ppermute | solution.py:720
  347.4 22.0 %collective-permute-start.43 = (bf16[256,1536]{1,0:T(8,128)(2,1)S(1)}, bf16[256,1536]{1,0:T(8,128)(2,1)}, u32[]{:S(2)}, u32[]{:S(2)}) collective-permute-start(bf16[256,1536]{1,0:T(8,128)(2,1)S(1)} %broadcast_select_fusion.3.part_0), channel_id=1, source_target_pairs={{0,4},{4,0},{8,12},{12,8},{16,20},{20,16},{24,28},{28,24},{1,5},{5... | collective-permute-start | bytes 2359304 | tf_op jit(solution)/shard_map/ppermute | solution.py:673
  350.9 20.2 %collective-permute-start.44 = (bf16[256,1536]{1,0:T(8,128)(2,1)S(1)}, bf16[256,1536]{1,0:T(8,128)(2,1)}, u32[]{:S(2)}, u32[]{:S(2)}) collective-permute-start(bf16[256,1536]{1,0:T(8,128)(2,1)S(1)} %copy-done.25), channel_id=1, source_target_pairs={{0,1},{3,2},{4,5},{7,6},{8,9},{11,10},{12,13},{15,14},{16,17},{19,... | collective-permute-start | bytes 2359304 | tf_op jit(solution)/shard_map/ppermute | solution.py:697
  354.0 17.1 %collective-permute-start.45 = (bf16[256,1536]{1,0:T(8,128)(2,1)S(1)}, bf16[256,1536]{1,0:T(8,128)(2,1)S(1)}, u32[]{:S(2)}, u32[]{:S(2)}) collective-permute-start(bf16[256,1536]{1,0:T(8,128)(2,1)S(1)} %copy-done.25), channel_id=1, source_target_pairs={{1,2},{2,1},{5,6},{6,5},{9,10},{10,9},{13,14},{14,13},{17,18},{18,... | collective-permute-start | bytes 2359304 | tf_op jit(solution)/shard_map/ppermute | solution.py:685
  372.7 6.8 %collective-permute-start.46 = (bf16[256,1536]{1,0:T(8,128)(2,1)S(1)}, bf16[256,1536]{1,0:T(8,128)(2,1)S(1)}, u32[]{:S(2)}, u32[]{:S(2)}) collective-permute-start(bf16[256,1536]{1,0:T(8,128)(2,1)S(1)} %broadcast_select_fusion.2.part_1), channel_id=1, source_target_pairs={{0,4},{4,0},{8,12},{12,8},{16,20},{20,16},{24,28},{28,24},{1,5},{5... | collective-permute-start | bytes 2359304 | tf_op jit(solution)/shard_map/ppermute | solution.py:673
  379.4 39.8 %collective-permute-start.47 = (bf16[256,1536]{1,0:T(8,128)(2,1)}, bf16[256,1536]{1,0:T(8,128)(2,1)}, u32[]{:S(2)}, u32[]{:S(2)}) collective-permute-start(bf16[256,1536]{1,0:T(8,128)(2,1)} %add_convert_fusion), channel_id=1, source_target_pairs={{0,2},{2,0},{1,3},{3,1},{4,6},{6,4},{5,7},{7,5},{8,10},{10,8},{9,1... | collective-permute-start | bytes 2359304 | tf_op jit(solution)/shard_map/ppermute | solution.py:681
  383.9 36.5 %collective-permute-start.48 = (bf16[256,1536]{1,0:T(8,128)(2,1)}, bf16[256,1536]{1,0:T(8,128)(2,1)}, u32[]{:S(2)}, u32[]{:S(2)}) collective-permute-start(bf16[256,1536]{1,0:T(8,128)(2,1)} %get-tuple-element.339), channel_id=1, source_target_pairs={{0,1},{1,0},{2,3},{3,2},{4,5},{5,4},{6,7},{7,6},{8,9},{9,8},{10,11... | collective-permute-start | bytes 2359304 | tf_op jit(solution)/shard_map/ppermute | solution.py:677
  420.4 5.6 %collective-permute-start.49 = (bf16[4,128,1536]{2,1,0:T(8,128)(2,1)}, bf16[4,128,1536]{2,1,0:T(8,128)(2,1)}, u32[]{:S(2)}, u32[]{:S(2)}) collective-permute-start(bf16[4,128,1536]{2,1,0:T(8,128)(2,1)} %get-tuple-element.342), channel_id=1, source_target_pairs={{0,4},{4,0},{8,12},{12,8},{16,20},{20,16},{24,28},{28,24},{1,5},{5... | collective-permute-start | bytes 4718600 | tf_op jit(solution)/shard_map/ppermute | solution.py:673
  420.4 5.5 %collective-permute-start.50 = (f32[3200]{0:T(1024)S(1)}, f32[3200]{0:T(1024)S(1)}, u32[]{:S(2)}, u32[]{:S(2)}) collective-permute-start(f32[3200]{0:T(1024)S(1)} %concatenate.63), channel_id=1, source_target_pairs={{0,4},{4,0},{8,12},{12,8},{16,20},{20,16},{24,28},{28,24},{1,5},{5... | collective-permute-start | bytes 38408 | tf_op jit(solution)/shard_map/ppermute | solution.py:774
  425.9 9.7 %collective-permute-start.56 = (f32[3200]{0:T(1024)S(1)}, f32[3200]{0:T(1024)S(1)}, u32[]{:S(2)}, u32[]{:S(2)}) collective-permute-start(f32[3200]{0:T(1024)S(1)} %add.280), channel_id=1, source_target_pairs={{0,2},{2,0},{1,3},{3,1},{4,6},{6,4},{5,7},{7,5},{8,10},{10,8},{9,1... | collective-permute-start | bytes 38408 | tf_op jit(solution)/shard_map/ppermute | solution.py:681
  426.4 10.7 %collective-permute-start.55 = (bf16[2,192,384]{2,1,0:T(8,128)(2,1)S(1)}, bf16[2,192,384]{2,1,0:T(8,128)(2,1)S(1)}, u32[]{:S(2)}, u32[]{:S(2)}) collective-permute-start(bf16[2,192,384]{2,1,0:T(8,128)(2,1)S(1)} %dynamic-slice_bitcast_fusion.2), channel_id=1, source_target_pairs={{0,16},{4,20},{8,24},{12,28},{16,0},{20,4},{24,8},{28,12},{1,17},{... | collective-permute-start | bytes 884744 | tf_op jit(solution)/shard_map/ppermute | solution.py:774
  427.7 10.7 %collective-permute-start.54 = (bf16[2,192,384]{2,1,0:T(8,128)(2,1)S(1)}, bf16[2,192,384]{2,1,0:T(8,128)(2,1)S(1)}, u32[]{:S(2)}, u32[]{:S(2)}) collective-permute-start(bf16[2,192,384]{2,1,0:T(8,128)(2,1)S(1)} %dynamic-slice_bitcast_fusion.3), channel_id=1, source_target_pairs={{0,8},{4,12},{8,0},{12,4},{16,24},{20,28},{24,16},{28,20},{1,9},{5... | collective-permute-start | bytes 884744 | tf_op jit(solution)/shard_map/ppermute | solution.py:774
  428.7 20.3 %collective-permute-start.53 = (bf16[2,192,640]{2,1,0:T(8,128)(2,1)S(1)}, bf16[2,192,640]{2,1,0:T(8,128)(2,1)S(1)}, u32[]{:S(2)}, u32[]{:S(2)}) collective-permute-start(bf16[2,192,640]{2,1,0:T(8,128)(2,1)S(1)} %dynamic-slice_bitcast_fusion), channel_id=1, source_target_pairs={{0,16},{4,20},{8,24},{12,28},{16,0},{20,4},{24,8},{28,12},{1,17},{... | collective-permute-start | bytes 1474568 | tf_op jit(solution)/shard_map/ppermute | solution.py:774
  429.7 19.4 %collective-permute-start.52 = (bf16[2,192,640]{2,1,0:T(8,128)(2,1)S(1)}, bf16[2,192,640]{2,1,0:T(8,128)(2,1)S(1)}, u32[]{:S(2)}, u32[]{:S(2)}) collective-permute-start(bf16[2,192,640]{2,1,0:T(8,128)(2,1)S(1)} %dynamic-slice_bitcast_fusion.1), channel_id=1, source_target_pairs={{0,8},{4,12},{8,0},{12,4},{16,24},{20,28},{24,16},{28,20},{1,9},{5... | collective-permute-start | bytes 1474568 | tf_op jit(solution)/shard_map/ppermute | solution.py:774
  435.6 12.1 %collective-permute-start.51 = (bf16[128,1536]{1,0:T(8,128)(2,1)S(1)}, bf16[128,1536]{1,0:T(8,128)(2,1)S(1)}, u32[]{:S(2)}, u32[]{:S(2)}) collective-permute-start(bf16[128,1536]{1,0:T(8,128)(2,1)S(1)} %get-tuple-element.408), channel_id=1, source_target_pairs={{0,1},{1,0},{2,3},{3,2},{4,5},{5,4},{6,7},{7,6},{8,9},{9,8},{10,11... | collective-permute-start | bytes 1179656 | tf_op jit(solution)/shard_map/ppermute | solution.py:677
  437.1 21.5 %collective-permute-start.58 = (bf16[128,1536]{1,0:T(8,128)(2,1)S(1)}, bf16[128,1536]{1,0:T(8,128)(2,1)S(1)}, u32[]{:S(2)}, u32[]{:S(2)}) collective-permute-start(bf16[128,1536]{1,0:T(8,128)(2,1)S(1)} %get-tuple-element.406), channel_id=1, source_target_pairs={{0,1},{1,0},{2,3},{3,2},{4,5},{5,4},{6,7},{7,6},{8,9},{9,8},{10,11... | collective-permute-start | bytes 1179656 | tf_op jit(solution)/shard_map/ppermute | solution.py:677
  449.3 5.4 %collective-permute-start.61 = (bf16[192,384]{1,0:T(8,128)(2,1)S(1)}, bf16[192,384]{1,0:T(8,128)(2,1)S(1)}, u32[]{:S(2)}, u32[]{:S(2)}) collective-permute-start(bf16[192,384]{1,0:T(8,128)(2,1)S(1)} %dynamic-slice_bitcast_fusion.7), channel_id=1, source_target_pairs={{0,16},{4,20},{8,24},{12,28},{16,0},{20,4},{24,8},{28,12},{1,17},{... | collective-permute-start | bytes 442376 | tf_op jit(solution)/shard_map/ppermute | solution.py:774
  450.5 6.9 %collective-permute-start.62 = (bf16[192,384]{1,0:T(8,128)(2,1)S(1)}, bf16[192,384]{1,0:T(8,128)(2,1)S(1)}, u32[]{:S(2)}, u32[]{:S(2)}) collective-permute-start(bf16[192,384]{1,0:T(8,128)(2,1)S(1)} %dynamic-slice_bitcast_fusion.6), channel_id=1, source_target_pairs={{0,8},{4,12},{8,0},{12,4},{16,24},{20,28},{24,16},{28,20},{1,9},{5... | collective-permute-start | bytes 442376 | tf_op jit(solution)/shard_map/ppermute | solution.py:774
  451.2 6.3 %collective-permute-start.59 = (bf16[192,640]{1,0:T(8,128)(2,1)S(1)}, bf16[192,640]{1,0:T(8,128)(2,1)S(1)}, u32[]{:S(2)}, u32[]{:S(2)}) collective-permute-start(bf16[192,640]{1,0:T(8,128)(2,1)S(1)} %dynamic-slice_bitcast_fusion.5), channel_id=1, source_target_pairs={{0,16},{4,20},{8,24},{12,28},{16,0},{20,4},{24,8},{28,12},{1,17},{... | collective-permute-start | bytes 737288 | tf_op jit(solution)/shard_map/ppermute | solution.py:774
  452.2 6.3 %collective-permute-start.60 = (bf16[192,640]{1,0:T(8,128)(2,1)S(1)}, bf16[192,640]{1,0:T(8,128)(2,1)S(1)}, u32[]{:S(2)}, u32[]{:S(2)}) collective-permute-start(bf16[192,640]{1,0:T(8,128)(2,1)S(1)} %dynamic-slice_bitcast_fusion.4), channel_id=1, source_target_pairs={{0,8},{4,12},{8,0},{12,4},{16,24},{20,28},{24,16},{28,20},{1,9},{5... | collective-permute-start | bytes 737288 | tf_op jit(solution)/shard_map/ppermute | solution.py:774
  454.6 16.2 %collective-permute-start.57 = (bf16[128,1536]{1,0:T(8,128)(2,1)S(1)}, bf16[128,1536]{1,0:T(8,128)(2,1)S(1)}, u32[]{:S(2)}, u32[]{:S(2)}) collective-permute-start(bf16[128,1536]{1,0:T(8,128)(2,1)S(1)} %fusion.2), channel_id=1, source_target_pairs={{0,2},{2,0},{1,3},{3,1},{4,6},{6,4},{5,7},{7,5},{8,10},{10,8},{9,1... | collective-permute-start | bytes 1179656 | tf_op jit(solution)/shard_map/ppermute | solution.py:681
  476.2 4.0 collective-permute-start.66
  481.2 19.5 %collective-permute-start.65 = (bf16[192,1024]{1,0:T(8,128)(2,1)S(1)}, bf16[192,1024]{1,0:T(8,128)(2,1)S(1)}, u32[]{:S(2)}, u32[]{:S(2)}) collective-permute-start(bf16[192,1024]{1,0:T(8,128)(2,1)S(1)} %copy-done.37), channel_id=1, source_target_pairs={{0,2},{2,0},{1,3},{3,1},{4,6},{6,4},{5,7},{7,5},{8,10},{10,8},{9,1... | collective-permute-start | bytes 1179656 | tf_op jit(solution)/shard_map/ppermute | solution.py:681
  484.0 16.0 %collective-permute-start.68 = (f32[3200]{0:T(1024)S(1)}, f32[3200]{0:T(1024)S(1)}, u32[]{:S(2)}, u32[]{:S(2)}) collective-permute-start(f32[3200]{0:T(1024)S(1)} %add.319), channel_id=1, source_target_pairs={{0,16},{4,20},{8,24},{12,28},{16,0},{20,4},{24,8},{28,12},{1,17},{... | collective-permute-start | bytes 38408 | tf_op jit(solution)/shard_map/ppermute | solution.py:774
  (63 other events, 536.1 us)
Sparse Core Ops, SparseCore 0:
  91.4 86.5 all-gather.1
  344.6 85.7 reduce-scatter.1

commit v3 on v2

--- a/solution.py
+++ b/solution.py
@@ -105,6 +105,10 @@
 
 def as_row(column):
     return jnp.broadcast_to(column, (column.shape[0], 128)).T[:1, :]
+
+
+def as_column(row):
+    return jnp.broadcast_to(row, (128, row.shape[1])).T[:, :1]
 
 
 def place_parts(place_ref, part_refs, whole_ref, scale):
@@ -158,7 +162,7 @@
     place_parts(place_ref, part_refs, normed_ref, gain_ref[...])
     for i in range(length // block):
         here = pl.ds(i * block, block)
-        projected = dot(normed_ref[here, :], weight_ref[...], 1, 0)
+        projected = dot(normed_ref[here, :], weight_ref[:, : projected_ref.shape[1]], 1, 0)
         projected_ref[here, :] = projected
         cos_part, sin_part = cos_ref[here, :], sin_ref[here, :]
         for t in range(projected.shape[1] // PAIR):
@@ -182,7 +186,7 @@
     row_at = lax.broadcasted_iota(jnp.int32, (block, block), 0)
     col_at = lax.broadcasted_iota(jnp.int32, (block, block), 1)
     causal = jnp.concatenate([col_at <= row_at] * group, axis=0)
-    col_all = lax.broadcasted_iota(jnp.int32, (group * block, block), 1)
+    col_all = lax.broadcasted_iota(jnp.int32, (group * block, block), 1).astype(f32)
     ones = jnp.ones((block, size), bf16)
     for j in range(kv):
         for i in range(length // block):
@@ -190,7 +194,7 @@
             queries = jnp.concatenate(
                 [q_ref[j * group + g, here, :] for g in range(group)], axis=0
             )
-            start = jnp.concatenate([start_ref[here, :]] * group, axis=0)
+            start = jnp.concatenate([as_column(start_ref[:, here])] * group, axis=0)
             total = jnp.zeros((group * block, 2 * size), f32)
             for b in range(i + 1):
                 there = pl.ds(b * block, block)
@@ -211,13 +215,12 @@
                 lse_ref[h, :, here] = as_row(log_sum[part])
 
 
-def attention_branch_kernel(count, core_ref, begins_ref, *refs):
-    block_refs = refs[:count]
-    attended_ref, weight_ref, mine_ref, other_ref, stage_ref = refs[count:]
-    place_blocks(begins_ref, block_refs, weight_ref)
-    shard = attended_ref.shape[0] // 4
+def attention_branch_kernel(core_ref, attended_ref, weight_ref, mine_ref, other_ref, stage_ref):
+    shard, columns = attended_ref.shape[0] // 4, attended_ref.shape[1]
     for i in range(4):
-        value = dot(attended_ref[i * shard : (i + 1) * shard, :], weight_ref[...], 1, 1)
+        value = dot(
+            attended_ref[i * shard : (i + 1) * shard, :], weight_ref[:, -columns:], 1, 1
+        )
         split_halves(core_ref, value.astype(bf16), stage_ref, mine_ref, other_ref, i)
 
 
@@ -226,13 +229,13 @@
     length = 4 * rows
     size = HEAD_DIMENSION
     columns = blocks[0].shape[1]
-    kv = columns // ((QUERY_GROUP + 2) * size)
+    kv = columns // ((2 * QUERY_GROUP + 2) * size)
     heads = kv * QUERY_GROUP
     operands = (*parts, *blocks, gain_attn, head_gains, *tables, start)
     results = (
         jax.ShapeDtypeStruct((width, columns), bf16),
         jax.ShapeDtypeStruct((length, width), bf16),
-        jax.ShapeDtypeStruct((length, columns), f32),
+        jax.ShapeDtypeStruct((length, (heads + 2 * kv) * size), f32),
         jax.ShapeDtypeStruct((heads, length, size), bf16),
         jax.ShapeDtypeStruct((kv, length, size), bf16),
         jax.ShapeDtypeStruct((kv, length, size), bf16),
@@ -250,29 +253,110 @@
     )(place, begins, *operands)
 
 
-def attention_branch(core, blocks, begins, attended):
-    length, columns = attended.shape
-    width = 4 * (blocks[0].shape[0]) if len(blocks) > 1 else blocks[0].shape[0]
+def attention_branch(core, attended, weight):
+    length = attended.shape[0]
+    width = weight.shape[0]
     half = jax.ShapeDtypeStruct((4, length // 8, width), bf16)
-    operands = (*blocks, attended)
-    results = (jax.ShapeDtypeStruct((width, columns), bf16), half, half)
     return pl.pallas_call(
-        functools.partial(attention_branch_kernel, len(blocks)),
+        attention_branch_kernel,
         grid=(1,),
-        in_specs=scalars(2) + [whole(value) for value in operands],
-        out_specs=tuple(whole(value) for value in results),
-        out_shape=results,
+        in_specs=scalars(1) + [whole(attended), whole(weight)],
+        out_specs=(whole(half), whole(half)),
+        out_shape=(half, half),
         scratch_shapes=[pltpu.VMEM((length // 4, width), bf16)],
         compiler_params=pltpu.CompilerParams(vmem_limit_bytes=VMEM_LIMIT),
         cost_estimate=SMALL,
-    )(core, begins, *operands)
-
-
-def attention_turn_kernel(
-    place_ref, part_0, part_1, part_2, part_3, weight_ref, out_ref, grads_ref, dot_ref, dw_ref, whole_ref
+    )(core, attended, weight)
+
+
+def split_pieces(total_ref, pair_ref, piece_refs):
+    if len(piece_refs) == 1:
+        piece_refs[0][...] = total_ref[...].astype(bf16)
+        return
+    keep_x, send_x, keep_y, send_y = piece_refs
+    rows = keep_x.shape[1]
+    x, y = pair_ref[0], pair_ref[1]
+    for k in range(2):
+        for ref, pair, core in (
+            (keep_x, 2 * k + x, 0),
+            (send_x, 2 * k + 1 - x, 0),
+            (keep_y, 2 * y + k, 1),
+            (send_y, 2 * (1 - y) + k, 1),
+        ):
+            begin = pl.multiple_of((2 * pair + core) * rows, 16)
+            ref[k] = total_ref[pl.ds(begin, rows), :].astype(bf16)
+
+
+def pieces_shapes(width, columns):
+    if lax.axis_size("dp") != 8:
+        return (jax.ShapeDtypeStruct((width, columns), bf16),)
+    return (jax.ShapeDtypeStruct((2, width // 8, columns), bf16),) * 4
+
+
+def heads_gradient_kernel(pair_ref, left_ref, right_ref, *refs):
+    refs[-1][...] = dot(left_ref[...], right_ref[...], 0, 0)
+    split_pieces(refs[-1], pair_ref, refs[:-1])
+
+
+def heads_gradient(pair, left, right):
+    width, columns = left.shape[1], right.shape[1]
+    results = pieces_shapes(width, columns)
+    return pl.pallas_call(
+        heads_gradient_kernel,
+        grid=(1,),
+        in_specs=scalars(1) + [whole(left), whole(right)],
+        out_specs=tuple(whole(value) for value in results),
+        out_shape=results,
+        scratch_shapes=[pltpu.VMEM((width, columns), f32)],
+        compiler_params=pltpu.CompilerParams(vmem_limit_bytes=VMEM_LIMIT),
+        cost_estimate=SMALL,
+    )(pair, left, right)
+
+
+def add_refs(left, right):
+    return (left.astype(f32) + right.astype(f32)).astype(bf16)
+
+
+def pieces_middle_kernel(
+    pair_ref, keep_x, got_x, keep_y, got_y, keep_one, send_one, keep_two, send_two
 ):
+    x, y = pair_ref[0], pair_ref[1]
+    keep_one[...] = add_refs(keep_x[y], got_x[y])
+    send_one[...] = add_refs(keep_x[1 - y], got_x[1 - y])
+    keep_two[...] = add_refs(keep_y[x], got_y[x])
+    send_two[...] = add_refs(keep_y[1 - x], got_y[1 - x])
+
+
+def pieces_end_kernel(core_ref, keep_one, got_one, keep_two, got_two, kept, given):
+    @pl.when(core_ref[0] == 0)
+    def _():
+        kept[...] = add_refs(keep_one[...], got_one[...])
+        given[...] = add_refs(keep_two[...], got_two[...])
+
+    @pl.when(core_ref[0] != 0)
+    def _():
+        given[...] = add_refs(keep_one[...], got_one[...])
+        kept[...] = add_refs(keep_two[...], got_two[...])
+
+
+def pieces_call(kernel, scalar, values, count):
+    result = jax.ShapeDtypeStruct(values[0].shape[-2:], bf16)
+    vmem = pl.BlockSpec(memory_space=pltpu.VMEM)
+    return pl.pallas_call(
+        kernel,
+        in_specs=scalars(1) + [vmem] * len(values),
+        out_specs=(vmem,) * count,
+        out_shape=(result,) * count,
+        compiler_params=pltpu.CompilerParams(vmem_limit_bytes=VMEM_LIMIT),
+        cost_estimate=SMALL,
+    )(scalar, *values)
+
+
+def attention_turn_kernel(place_ref, pair_ref, *refs):
+    part_refs, (weight_ref, out_ref, grads_ref, dot_ref) = refs[:4], refs[4:8]
+    piece_refs, (whole_ref, total_ref) = refs[8:-2], refs[-2:]
     size = HEAD_DIMENSION
-    place_parts(place_ref, (part_0, part_1, part_2, part_3), whole_ref, None)
+    place_parts(place_ref, part_refs, whole_ref, None)
     heads, length, _ = grads_ref.shape
     block = min(256, length)
     shape = (dot_ref.shape[0], heads * size)
@@ -282,15 +366,16 @@
     ).astype(bf16)
     for i in range(length // block):
         here = pl.ds(i * block, block)
-        grads = dot(whole_ref[here, :], weight_ref[...], 1, 0).astype(bf16)
+        grads = dot(whole_ref[here, :], weight_ref[:, -heads * size :], 1, 0).astype(bf16)
         high, low = two_parts(grads.astype(f32) * out_ref[here, :].astype(f32))
         dot_ref[:, here] = dot(of_head, high, 1, 1) + dot(of_head, low, 1, 1)
         for h in range(heads):
             grads_ref[h, here, :] = grads[:, h * size : (h + 1) * size]
-    dw_ref[...] = dot(whole_ref[...], out_ref[...], 0, 0).astype(bf16)
-
-
-def attention_turn(place, parts, weight, attended):
+    total_ref[...] = dot(whole_ref[...], out_ref[...], 0, 0)
+    split_pieces(total_ref, pair_ref, piece_refs)
+
+
+def attention_turn(place, pair, parts, weight, attended):
     rows, width = parts[0].shape
     length, columns = attended.shape
     heads = columns // HEAD_DIMENSION
@@ -298,18 +383,18 @@
     results = (
         jax.ShapeDtypeStruct((heads, length, HEAD_DIMENSION), bf16),
         jax.ShapeDtypeStruct((-(-heads // 8) * 8, length), f32),
-        jax.ShapeDtypeStruct((width, columns), bf16),
+        *pieces_shapes(width, columns),
     )
     return pl.pallas_call(
         attention_turn_kernel,
         grid=(1,),
-        in_specs=scalars(1) + [whole(value) for value in operands],
+        in_specs=scalars(2) + [whole(value) for value in operands],
         out_specs=tuple(whole(value) for value in results),
         out_shape=results,
-        scratch_shapes=[pltpu.VMEM((length, width), bf16)],
+        scratch_shapes=[pltpu.VMEM((length, width), bf16), pltpu.VMEM((width, columns), f32)],
         compiler_params=pltpu.CompilerParams(vmem_limit_bytes=VMEM_LIMIT),
         cost_estimate=SMALL,
-    )(place, *operands)
+    )(place, pair, *operands)
 
 
 def attention_backward_kernel(
@@ -347,7 +432,7 @@
     key_at = lax.broadcasted_iota(jnp.int32, (block, block), 0)
     row_at = lax.broadcasted_iota(jnp.int32, (block, block), 1)
     causal = jnp.concatenate([key_at <= row_at] * group, axis=1)
-    key_all = lax.broadcasted_iota(jnp.int32, (block, lanes), 0)
+    key_all = lax.broadcasted_iota(jnp.int32, (block, lanes), 0).astype(f32)
     dk_ref[...] = jnp.zeros_like(dk_ref)
     dv_ref[...] = jnp.zeros_like(dv_ref)
     head_sum_ref[...] = jnp.zeros_like(head_sum_ref)
@@ -401,7 +486,7 @@
             weighted = grad * head_gain_ref[:, columns]
             back = inverse * (weighted - scaled * head_means(weighted * scaled))
             back_ref[here, columns] = unless(keep, back, given).astype(bf16)
-        term = dot(back_ref[here, :], weight_ref[...], 1, 1)
+        term = dot(back_ref[here, :], weight_ref[:, : back_ref.shape[1]], 1, 1)
         gain_sum_ref[...] += jnp.sum(
             term * normed_ref[here, :].astype(f32), axis=0, keepdims=True
         )
@@ -438,6 +523,32 @@
         compiler_params=pltpu.CompilerParams(vmem_limit_bytes=VMEM_LIMIT),
         cost_estimate=SMALL,
     )(core, *operands)
+
+
+def input_gradient_kernel(core_ref, kept_ref, given_ref, rows_ref, gain_ref, middle_ref, out_ref):
+    half = kept_ref.shape[0]
+    core = core_ref[0]
+    for index, ref in ((core, kept_ref), (1 - core, given_ref)):
+        part = pl.ds(pl.multiple_of(index * half, half), half)
+        rows = rows_ref[part, :]
+        inverse = lax.rsqrt(jnp.mean(rows * rows, axis=1, keepdims=True) + eps_norm)
+        scaled = rows * inverse
+        weighted = ref[...].astype(f32) * gain_ref[...]
+        out_ref[part, :] = middle_ref[part, :] + inverse * (
+            weighted - scaled * jnp.mean(weighted * scaled, axis=1, keepdims=True)
+        )
+
+
+def input_gradient(core, kept, given, rows, gain, middle):
+    vmem = pl.BlockSpec(memory_space=pltpu.VMEM)
+    return pl.pallas_call(
+        input_gradient_kernel,
+        in_specs=scalars(1) + [vmem] * 5,
+        out_specs=vmem,
+        out_shape=jax.ShapeDtypeStruct(rows.shape, f32),
+        compiler_params=pltpu.CompilerParams(vmem_limit_bytes=VMEM_LIMIT),
+        cost_estimate=SMALL,
+    )(core, kept, given, rows, gain, middle)
 
 
 TILE = 256
@@ -507,16 +618,24 @@
     )(weight, first, second, summed)
 
 
-def units_forward_kernel(count, *refs):
+def units_forward_kernel(count, pick, pick_ref, *refs):
     row_refs, grad_refs, units_ref = refs[:count], refs[count : 2 * count], refs[2 * count]
     rows_out, grads_out, hidden_ref, both_ref = refs[-4:]
 
     @pl.when(pl.program_id(0) == 0)
     def _():
         for k in range(count):
-            part = pl.ds(k * row_refs[k].shape[0], row_refs[k].shape[0])
-            rows_out[part, :] = row_refs[k][...]
-            grads_out[part, :] = grad_refs[k][...]
+            if pick:
+
+                @pl.when(pick_ref[0] == k)
+                def _():
+                    rows_out[...] = row_refs[k][...]
+                    grads_out[...] = grad_refs[k][...]
+
+            else:
+                part = pl.ds(k * row_refs[k].shape[0], row_refs[k].shape[0])
+                rows_out[part, :] = row_refs[k][...]
+                grads_out[part, :] = grad_refs[k][...]
 
     rows = rows_out[...]
     gate_out = dot(rows, units_ref[:, :TILE], 1, 0)
@@ -531,23 +650,25 @@
     both_ref[:, TILE:] = (grad_hidden * gate_act).astype(bf16)
 
 
-def units_forward(rows, grads, units, buffers, index):
+def units_forward(rows, grads, units, buffers, index, pick=None):
     count, (length, width) = len(rows), rows[0].shape
+    blocks = count if pick is None else 1
     steps = units.shape[1] // (3 * TILE)
     full = pl.BlockSpec((length, width), lambda i: (0, 0))
-    kept = pl.BlockSpec((count * length, width), lambda i: (index, 0))
+    kept = pl.BlockSpec((blocks * length, width), lambda i: (index, 0))
     held = () if buffers is None else buffers
     return pl.pallas_call(
-        functools.partial(units_forward_kernel, count),
+        functools.partial(units_forward_kernel, count, pick is not None),
         grid=(steps,),
-        in_specs=[full] * (2 * count)
+        in_specs=scalars(1)
+        + [full] * (2 * count)
         + [pl.BlockSpec((width, 3 * TILE), lambda i: (0, i))]
         + [pl.BlockSpec(memory_space=pl.ANY)] * len(held),
         out_specs=(
             kept,
             kept,
-            pl.BlockSpec((count * length, TILE), lambda i: (index, i)),
-            pl.BlockSpec((count * length, 2 * TILE), lambda i: (index, i)),
+            pl.BlockSpec((blocks * length, TILE), lambda i: (index, i)),
+            pl.BlockSpec((blocks * length, 2 * TILE), lambda i: (index, i)),
         ),
         out_shape=(
             jax.ShapeDtypeStruct((4 * length, width), bf16),
@@ -555,13 +676,19 @@
             jax.ShapeDtypeStruct((4 * length, steps * TILE), bf16),
             jax.ShapeDtypeStruct((4 * length, steps * 2 * TILE), bf16),
         ),
-        input_output_aliases={2 * count + 1 + k: k for k in range(len(held))},
+        input_output_aliases={2 * count + 2 + k: k for k in range(len(held))},
         compiler_params=pltpu.CompilerParams(vmem_limit_bytes=VMEM_LIMIT),
         cost_estimate=SMALL,
-    )(*rows, *grads, units, *held)
-
-
-def units_back_kernel(both_ref, units_ref, out_ref):
+    )(jnp.zeros((1,), jnp.int32) if pick is None else pick, *rows, *grads, units, *held)
+
+
+def write_blocks(total, out_refs):
+    rows = out_refs[0].shape[0]
+    for k, ref in enumerate(out_refs):
+        ref[...] = total[k * rows : (k + 1) * rows].astype(bf16)
+
+
+def units_back_kernel(both_ref, units_ref, *out_refs):
     total = None
     for i in range(both_ref.shape[1] // (2 * TILE)):
         term = dot(
@@ -571,10 +698,10 @@
             1,
         )
         total = term if total is None else total + term
-    out_ref[...] = total.astype(bf16)
-
-
-def units_down_kernel(hidden_ref, units_ref, out_ref):
+    write_blocks(total, out_refs)
+
+
+def units_down_kernel(hidden_ref, units_ref, *out_refs):
     total = None
     for i in range(hidden_ref.shape[1] // TILE):
         term = dot(
@@ -584,7 +711,7 @@
             1,
         )
         total = term if total is None else total + term
-    out_ref[...] = total.astype(bf16)
+    write_blocks(total, out_refs)
 
 
 def units_to_width(kernel, values, units, first, count):
@@ -598,8 +725,8 @@
             pl.BlockSpec((length, columns), lambda i: (first // count, 0)),
             pl.BlockSpec((TILE, units.shape[1]), lambda i: (i, 0)),
         ],
-        out_specs=pl.BlockSpec((length, TILE), lambda i: (0, i)),
-        out_shape=jax.ShapeDtypeStruct((length, width), bf16),
+        out_specs=(pl.BlockSpec((block, TILE), lambda i: (0, i)),) * count,
+        out_shape=(jax.ShapeDtypeStruct((block, width), bf16),) * count,
         compiler_params=pltpu.CompilerParams(vmem_limit_bytes=VMEM_LIMIT),
         cost_estimate=SMALL,
     )(values, units)
@@ -730,7 +857,11 @@
 
 def heads_scatter_end(home, far, own, core):
     kept = jnp.where(own, home, far.astype(f32))
-    given = swap_core(jnp.where(own, far, home.astype(bf16))).astype(f32)
+    return kept, swap_core(jnp.where(own, far, home.astype(bf16)))
+
+
+def both_halves(kept, given, core):
+    given = given.astype(f32)
     return jnp.concatenate(
         [jnp.where(core == 0, kept, given), jnp.where(core == 0, given, kept)], axis=0
     )
@@ -801,40 +932,37 @@
     return (left.astype(f32) + right.astype(f32)).astype(bf16)
 
 
-def scatter_pairs_begin(value):
-    if lax.axis_size("dp") != 8:
+def scatter_pairs_begin(pieces):
+    if len(pieces) == 1:
         return (
             lax.psum_scatter(
-                value, "dp", scatter_dimension=0, tiled=True, axis_index_groups=pair_groups()
+                pieces[0], "dp", scatter_dimension=0, tiled=True, axis_index_groups=pair_groups()
             ),
         )
-    pair = lax.axis_index("dp") >> 1
-    one, two = pair & 1, pair >> 1
-    rows = value.shape[0] // 8
-    parts = value.reshape((2, 2, 2, rows) + value.shape[1:])
-    first, second = parts[:, :, 0], parts[:, :, 1]
-    by_two = swap_dp(at(first, one ^ 1, 1), 2)
-    by_four = swap_dp(at(second, two ^ 1, 0), 4)
-    return at(first, one, 1), by_two, at(second, two, 0), by_four
-
-
-def scatter_pairs_middle(parts):
+    keep_x, send_x, keep_y, send_y = pieces
+    return keep_x, swap_dp(send_x, 2), keep_y, swap_dp(send_y, 4)
+
+
+def scatter_pairs_middle(pair, parts):
     if len(parts) == 1:
         return parts
-    return add_low(parts[0], parts[1]), add_low(parts[2], parts[3])
-
-
-def scatter_pairs_end(parts):
+    return pieces_call(pieces_middle_kernel, pair, parts, 4)
+
+
+def scatter_pairs_send(parts):
     if len(parts) == 1:
-        return parts[0]
-    pair = lax.axis_index("dp") >> 1
-    one, two = pair & 1, pair >> 1
-    first, second = parts
-    by_four = swap_dp(at(first, two ^ 1, 0), 4)
-    by_two = swap_dp(at(second, one ^ 1, 0), 2)
-    first = add_low(at(first, two, 0), by_four)
-    second = add_low(at(second, one, 0), by_two)
-    return jnp.concatenate([first, second], axis=0)
+        return parts
+    keep_one, send_one, keep_two, send_two = parts
+    return keep_one, swap_dp(send_one, 4), keep_two, swap_dp(send_two, 2)
+
+
+def scatter_pairs_end(core, parts):
+    if len(parts) == 1:
+        rows = parts[0].shape[0] // 2
+        return at(parts[0].reshape(2, rows, -1), core, 0), at(
+            parts[0].reshape(2, rows, -1), core ^ 1, 0
+        )
+    return pieces_call(pieces_end_kernel, core[None], parts, 2)
 
 
 def heads_pair(shard, far, own, core):
@@ -843,13 +971,6 @@
     return jnp.concatenate(
         [jnp.where(core == 0, kept, other), jnp.where(core == 0, other, kept)], axis=0
     )
-
-
-def heads_home(pair, own, core):
-    rows = pair.shape[0] // 2
-    kept = jnp.where(core == 0, pair[:rows], pair[rows:])
-    other = swap_core(jnp.where(core == 0, pair[rows:], pair[:rows]))
-    return jnp.where(own, kept, other), jnp.where(own, other, kept)
 
 
 def units_gradient(summed):
@@ -864,6 +985,10 @@
 
 def together(*values):
     return lax.optimization_barrier(values)
+
+
+def after(value, earlier):
+    return lax.optimization_barrier((value, earlier))[0]
 
 
 def shards(
@@ -891,59 +1016,34 @@
     core = lax.axis_index("dp") & 1
     own = core == z // 2
     place = jnp.where(own, z, z ^ 2)[None]
+    pair = (lax.axis_index("dp") >> 1)[None]
+    pair = jnp.concatenate([pair & 1, pair >> 1])
 
     units_columns = gate_up.shape[2]
-    qkv_own = qkv_weight.astype(bf16)
-    qkv_own, gains_own, positions = together(qkv_own, norm_gains[None], positions)
-    qkv_far = swap_far(qkv_own)
-    out_own = out_weight.astype(bf16).T
-    out_far = swap_far(out_own)
-    gains_near = gather_tensor(gather_dp(gains_own)[:, None], 1)
+    heads_own = jnp.concatenate([qkv_weight.astype(bf16), out_weight.astype(bf16).T], axis=1)
+    heads_own, gains_own, positions = together(heads_own, norm_gains[None], positions)
+    heads_far = swap_far(heads_own)
+    gains_dp = gather_dp(gains_own)[:, None]
+    gains_all = gather_tensor(gather_tensor(gains_dp, 1), 2).reshape(1, -1)
     inverse_in = lax.rsqrt(jnp.mean(block_in * block_in, axis=-1, keepdims=True) + eps_norm)
     scaled_in = block_in * inverse_in
     head_positions = jnp.where(own, positions, swap_core(positions))
-    (
-        scaled_b,
-        qkv_own,
-        qkv_far,
+    scaled_b, heads_own, heads_far, head_positions, units_shard, grad_own, gains_all = together(
+        scaled_in.astype(bf16),
+        heads_own,
+        heads_far,
         head_positions,
-        units_shard,
-        grad_own,
-        out_own,
-        out_far,
-        gains_near,
-    ) = together(
-        scaled_in.astype(bf16),
-        qkv_own,
-        qkv_far,
-        head_positions,
-        pack_units(gate_up, down_weight.T),
-        out_grad.astype(bf16),
-        out_own,
-        out_far,
-        gains_near,
+        pack_units(after(gate_up, gains_dp), down_weight.T),
+        after(out_grad, gains_dp).astype(bf16),
+        gains_all,
     )
 
     scaled_first = owner_swap(scaled_b)
-    qkv_parts = gather_pairs_begin(heads_pair(qkv_own, qkv_far, own, core))
-    out_parts = gather_pairs_begin(heads_pair(out_own, out_far, own, core))
-    gains_all = gather_tensor(gains_near, 2).reshape(1, -1)
+    heads_parts = gather_pairs_begin(heads_pair(heads_own, heads_far, own, core))
     tables = rope_tables(head_positions, HEAD_DIMENSION)
     length = head_positions.shape[0]
     start = jnp.maximum(jnp.arange(length, dtype=jnp.int32) - head_positions, 0)
-    start_column = start[:, None]
-    scaled_first, qkv_parts, gains_all, units_shard, tables, start_column, grad_own, out_parts = (
-        together(
-            scaled_first,
-            qkv_parts,
-            gains_all,
-            units_shard,
-            tables,
-            start_column,
-            grad_own,
-            out_parts,
-        )
-    )
+    start = start.astype(f32)[None]
     gain_attn = gains_all[:, :model_width]
     gain_q = gains_all[0, model_width : model_width + HEAD_DIMENSION]
     gain_k = gains_all[0, model_width + HEAD_DIMENSION : model_width + 2 * HEAD_DIMENSION]
@@ -952,58 +1052,75 @@
         ([gain_q] * QUERY_GROUP + [gain_k, jnp.ones_like(gain_k)]) * kv_local
     )[None]
     gain_ffn = gains_all[:, model_width + 2 * HEAD_DIMENSION :]
+    (
+        scaled_first,
+        heads_parts,
+        gain_attn,
+        head_gains,
+        gain_ffn,
+        units_shard,
+        tables,
+        start,
+        grad_own,
+    ) = together(
+        scaled_first,
+        heads_parts,
+        gain_attn,
+        head_gains,
+        gain_ffn,
+        units_shard,
+        tables,
+        start,
+        grad_own,
+    )
 
     scaled_second = guest_swap(scaled_first)
     scaled_mine = jnp.where(own, scaled_b, scaled_first)
     scaled_other = swap_core(scaled_mine)
-    qkv_blocks, qkv_begins = gather_pairs_end(qkv_parts)
-    out_blocks, out_begins = gather_pairs_end(out_parts)
-    half = grad_own.shape[0] // 2
-    grad_far = swap_far(grad_own[:half])
+    heads_blocks, heads_begins = gather_pairs_end(heads_parts)
+    half, quarter = grad_own.shape[0] // 2, grad_own.shape[0] // 4
+    grad_far = swap_far(grad_own[:quarter])
     (
-        qkv_blocks,
+        heads_blocks,
         scaled_second,
         scaled_mine,
         scaled_other,
         units_shard,
         grad_own,
         grad_far,
-        out_blocks,
     ) = together(
-        qkv_blocks,
+        heads_blocks,
         scaled_second,
         scaled_mine,
         scaled_other,
         units_shard,
         grad_own,
         grad_far,
-        out_blocks,
     )
 
     units = lax.all_gather(units_shard, "dp", axis=0, tiled=True)
-    grad_far_rest = swap_far(grad_own[half:])
+    grad_far_rest = swap_far(grad_own[quarter:])
     grad_near = swap_near(grad_own)
     scaled_next = jnp.where(own, scaled_first, scaled_second)
     scaled_parts = (scaled_mine, scaled_next, scaled_other, swap_core(scaled_next))
-    w_qkv, normed_all, projected, queries_b, keys_b, values_b, attended, lse = attention_forward(
-        place, scaled_parts, qkv_blocks, qkv_begins, gain_attn, head_gains, tables, start_column
-    )
-    attended, grad_far, grad_far_rest, grad_near, grad_own = together(
-        attended, grad_far, grad_far_rest, grad_near, grad_own
-    )
+    w_heads, normed_all, projected, queries_b, keys_b, values_b, attended, lse = attention_forward(
+        place, scaled_parts, heads_blocks, heads_begins, gain_attn, head_gains, tables, start
+    )
+    branch_mine, branch_other = attention_branch(core[None], attended, w_heads)
+    branch_mine, branch_other, grad_far, grad_far_rest, grad_near, grad_own = together(
+        branch_mine, branch_other, grad_far, grad_far_rest, grad_near, grad_own
+    )
+    grad_far = jnp.concatenate([grad_far, grad_far_rest], axis=0)
+    branch_other = swap_core(branch_other)
     grad_middle_part = swap_middle(grad_own)
-    grad_far = jnp.concatenate([grad_far, grad_far_rest], axis=0)
-    w_out, branch_mine, branch_other = attention_branch(
-        core[None], out_blocks, out_begins, attended
-    )
-    branch_mine, branch_other, grad_far = together(
-        branch_mine, swap_core(branch_other), grad_far
-    )
+    branch_mine, branch_other, grad_far = together(branch_mine, branch_other, grad_far)
     home, term_far, near, away = heads_scatter_near(branch_mine, branch_other, z)
     away, term_far, grad_middle_part = together(away, term_far, grad_middle_part)
     far = swap_far((term_far + away.astype(f32)).astype(bf16))
     far, home, near = together(far, home, near)
-    middle = block_in + heads_scatter_end(home + near.astype(f32), far, own, core)
+    middle = block_in + both_halves(
+        *heads_scatter_end(home + near.astype(f32), far, own, core), core
+    )
 
     inverse_mid = lax.rsqrt(jnp.mean(middle * middle, axis=-1, keepdims=True) + eps_norm)
     scaled_mid = middle * inverse_mid
@@ -1018,28 +1135,31 @@
     rows_middle = swap_middle(rows_own)
     buffers = units_forward((rows_near, rows_far), (grad_near, grad_far), units, buffers, 0)
     rows_all, grad_all, hidden_b, dboth = buffers
-    back_first = units_to_width(units_back_kernel, dboth, units, 0, 2)
-    rows_ends, rows_middle, grad_ends, back_first, buffers = together(
-        rows_ends, rows_middle, grad_ends, back_first, buffers
-    )
-    rows = block_in.shape[0]
-    from_near = swap_near(back_first[:rows])
-    from_far = swap_far(back_first[rows:])
-    rows_last = jnp.where(inner, rows_middle, rows_ends)
-    grad_last = jnp.where(inner, grad_middle_part, grad_ends)
+    back_near, back_far = units_to_width(units_back_kernel, dboth, units, 0, 2)
+    rows_ends, rows_middle, grad_ends, back_near, back_far, buffers = together(
+        rows_ends, rows_middle, grad_ends, back_near, back_far, buffers
+    )
+    from_far = swap_far(back_far)
+    from_near = swap_near(back_near)
     rows_all, grad_all, hidden_b, dboth = units_forward(
-        (rows_last,), (grad_last,), units, buffers, 3
-    )
-    back_second = units_to_width(units_back_kernel, dboth, units, 2, 2)
-    from_near, from_far, back_second, rows_all, grad_all, hidden_b, dboth = together(
-        from_near, from_far, back_second, rows_all, grad_all, hidden_b, dboth
-    )
-    from_last = swap_opposite(back_second[rows:])
-    back_own = back_second[:rows]
+        (rows_ends, rows_middle),
+        (grad_ends, grad_middle_part),
+        units,
+        buffers,
+        3,
+        inner.astype(jnp.int32)[None],
+    )
+    back_own, back_last = units_to_width(units_back_kernel, dboth, units, 2, 2)
+    from_near, from_far, back_last, back_own, rows_all, grad_all, hidden_b, dboth = together(
+        from_near, from_far, back_last, back_own, rows_all, grad_all, hidden_b, dboth
+    )
+    from_last = swap_opposite(back_last)
     down_kept, down_given = units_gradient_parts(grad_all, hidden_b, core)
+    (down_last,) = units_to_width(units_down_kernel, hidden_b, units, 3, 1)
+    branch_ends = [from_ends(down_last[:half]), from_ends(down_last[half:])]
     both_kept, both_given = units_gradient_parts(rows_all, dboth, core)
-    from_last, down_kept, down_given, both_kept, both_given = together(
-        from_last, down_kept, down_given, both_kept, both_given
+    from_last, branch_ends, down_kept, down_given, both_kept, both_given, down_last = together(
+        from_last, branch_ends, down_kept, down_given, both_kept, both_given, down_last
     )
     grad_normed_two = (
         back_own.astype(f32)
@@ -1064,44 +1184,29 @@
     )
     grad_mid_first = owner_swap(grad_mid_b)
     units_sum = units_add(both_kept, swap_core(both_given), down_kept, swap_core(down_given))
-    down_last = units_to_width(units_down_kernel, hidden_b, units, 3, 1)
-    grad_mid_first, down_last, units_sum = together(grad_mid_first, down_last, units_sum)
+    down_near, down_far, down_own = units_to_width(units_down_kernel, hidden_b, units, 0, 3)
+    down_far = add_low(down_far, jnp.concatenate(branch_ends, axis=0))
+    grad_mid_first, units_sum, down_near, down_far, down_own = together(
+        grad_mid_first, units_sum, down_near, down_far, down_own
+    )
     units_sum = units_gradient(units_sum)
     grad_mid_second = guest_swap(grad_mid_first)
-    branch_ends = from_ends(down_last)
-    branch_middle = swap_middle(down_last)
+    branch_far = swap_far(down_far[:half])
     grad_mid_mine = jnp.where(own, grad_mid_b, grad_mid_first)
     grad_mid_other = swap_core(grad_mid_mine)
-    down_rest = units_to_width(units_down_kernel, hidden_b, units, 0, 3)
-    down_near, down_far, down_own = (down_rest[k * rows : (k + 1) * rows] for k in range(3))
-    (
-        grad_mid_second,
-        grad_mid_mine,
-        grad_mid_other,
-        branch_ends,
-        branch_middle,
-        down_near,
-        down_far,
-        down_own,
-    ) = together(
-        grad_mid_second,
-        grad_mid_mine,
-        grad_mid_other,
-        branch_ends,
-        branch_middle,
-        down_near,
-        down_far,
-        down_own,
-    )
-    down_far = add_low(down_far, branch_ends)
+    grad_mid_second, grad_mid_mine, grad_mid_other, branch_far, down_far = together(
+        grad_mid_second, grad_mid_mine, grad_mid_other, branch_far, down_far
+    )
     grad_mid_next = jnp.where(own, grad_mid_first, grad_mid_second)
     grad_mid_parts = (grad_mid_mine, grad_mid_next, grad_mid_other, swap_core(grad_mid_next))
-    grad_mid_parts, down_far, down_near = together(grad_mid_parts, down_far, down_near)
-
-    branch_far = swap_far(down_far)
+
+    branch_far_rest = swap_far(down_far[half:])
     branch_near = swap_near(down_near)
-    grad_attended, row_dot, grad_out_w = attention_turn(place, grad_mid_parts, w_out, attended)
-    grad_attended, row_dot, grad_out_w = together(grad_attended, row_dot, grad_out_w)
+    branch_middle = swap_middle(down_last)
+    grad_attended, row_dot, *out_pieces = attention_turn(
+        place, pair, grad_mid_parts, w_heads, attended
+    )
+    out_parts = scatter_pairs_begin(tuple(out_pieces))
     grad_projected, part_mine, part_other, head_sums, gain_sums = attention_backward(
         core[None],
         queries_b,
@@ -1110,14 +1215,43 @@
         grad_attended,
         lse,
         row_dot,
-        start[None, :],
+        start,
         projected,
         head_gains,
         *tables,
-        w_qkv,
+        w_heads,
         normed_all,
         gain_attn,
     )
+    (
+        grad_projected,
+        part_mine,
+        part_other,
+        branch_far,
+        branch_far_rest,
+        branch_near,
+        branch_middle,
+        out_parts,
+    ) = together(
+        grad_projected,
+        part_mine,
+        part_other,
+        branch_far,
+        branch_far_rest,
+        branch_near,
+        branch_middle,
+        out_parts,
+    )
+
+    part_other = swap_core(part_other)
+    qkv_pieces = heads_gradient(pair, normed_all, grad_projected)
+    part_mine, part_other, qkv_pieces, out_parts, branch_far = together(
+        part_mine, part_other, qkv_pieces, out_parts, branch_far
+    )
+    home, term_far, near, away = heads_scatter_near(part_mine, part_other, z)
+    qkv_parts = scatter_pairs_begin(qkv_pieces)
+    out_parts = scatter_pairs_middle(pair, out_parts)
+    gain_sums, head_sums = after((gain_sums, head_sums), qkv_pieces)
     head_sums = head_sums.reshape(-1, QUERY_GROUP + 2, HEAD_DIMENSION)
     gain_total = jnp.concatenate(
         [
@@ -1127,82 +1261,54 @@
             grad_gain_ffn,
         ]
     )
-    (
-        grad_projected,
-        part_mine,
-        part_other,
-        gain_total,
-        branch_far,
-        branch_near,
-        grad_out_w,
-    ) = together(
-        grad_projected,
-        part_mine,
-        part_other,
-        gain_total,
-        branch_far,
-        branch_near,
-        grad_out_w,
-    )
-
-    part_other = swap_core(part_other)
-    grad_qkv = dot(normed_all, grad_projected, 0, 0).astype(bf16)
-    gain_total = sum_dp(gain_total, 1, 2)
-    part_mine, part_other, grad_qkv, gain_total, grad_out_w, branch_far = together(
-        part_mine, part_other, grad_qkv, gain_total, grad_out_w, branch_far
-    )
-    home, term_far, near, away = heads_scatter_near(part_mine, part_other, z)
-    qkv_parts = scatter_pairs_begin(grad_qkv)
-    out_parts = scatter_pairs_begin(grad_out_w)
-    gain_total = gain_total + swap_far(gain_total)
+    gain_total = sum_dp(gain_total, 1, lax.axis_size("dp") // 2)
     block_out = (
         middle
         + down_own.astype(f32)
         + branch_near.astype(f32)
         + branch_middle.astype(f32)
-        + branch_far.astype(f32)
-    )
-    qkv_parts, out_parts = scatter_pairs_middle(qkv_parts), scatter_pairs_middle(out_parts)
+        + jnp.concatenate([branch_far, branch_far_rest], axis=0).astype(f32)
+    )
     far_term = (term_far + away.astype(f32)).astype(bf16)
-    far_term, qkv_parts, out_parts, gain_total, block_out = together(
-        far_term, qkv_parts, out_parts, gain_total, block_out
-    )
     far = swap_far(far_term)
-    qkv_pair = scatter_pairs_end(qkv_parts)
-    out_pair = scatter_pairs_end(out_parts)
-    far, home, near, qkv_pair, out_pair, gain_total = together(
-        far, home, near, qkv_pair, out_pair, gain_total
-    )
-    heads_home_own, heads_home_away = heads_home(
-        jnp.concatenate([qkv_pair, out_pair], axis=1), own, core
-    )
-    grad_normed = heads_scatter_end(home + near.astype(f32), far, own, core)
-    heads_home_own, heads_home_away, gain_total, grad_normed, units_sum = together(
-        heads_home_own, heads_home_away, gain_total, grad_normed, units_sum
-    )
-    heads_away = swap_far(heads_home_away)
-    gain_total = gain_total + swap_near(gain_total)
-    gate_up_new = adam_units(gate_up, gate_up_first, gate_up_second, units_sum, 0)
+    qkv_parts = scatter_pairs_middle(pair, after(qkv_parts, (far_term, gain_total, block_out)))
+    out_parts = scatter_pairs_send(after(out_parts, qkv_parts))
+    qkv_parts = scatter_pairs_send(qkv_parts)
     down_new = adam_units(
         down_weight.T[None],
         down_first.T[None],
         down_second.T[None],
-        units_sum,
+        after(units_sum, (near, out_parts[0])),
         2 * units_sum.shape[1] // 3,
     )
-    gain_total = sum_dp(gain_total, 2, lax.axis_size("dp"))
-    weighted = grad_normed * gain_attn
-    in_grad = grad_middle + inverse_in * (
-        weighted - scaled_in * jnp.mean(weighted * scaled_in, axis=-1, keepdims=True)
-    )
-    heads_away, in_grad, gate_up_new, down_new = together(
-        heads_away, in_grad, gate_up_new, down_new
-    )
-    sum_heads = heads_home_own.astype(f32) + heads_away.astype(f32)
+    gain_total = after(gain_total, down_new)
+    gain_last = swap_dp(gain_total, lax.axis_size("dp") // 2)
+    qkv_kept, qkv_given = scatter_pairs_end(core, after(qkv_parts, (down_new, far)))
+    gain_total = gain_total + after(gain_last, qkv_kept)
+    gain_last = swap_near(gain_total)
+    out_kept, out_given = scatter_pairs_end(core, after(out_parts, (down_new, far)))
+    qkv_other, out_other = swap_core(qkv_given), swap_core(out_given)
+    gain_total = gain_total + after(gain_last, out_kept)
+    heads_away = jnp.concatenate(
+        [jnp.where(own, qkv_other, qkv_kept), jnp.where(own, out_other, out_kept)], axis=1
+    )
+    kept, given = heads_scatter_end(home + near.astype(f32), far, own, core)
+    units_sum = after(units_sum, heads_away)
+    gain_last = swap_far(gain_total)
+    heads_away = swap_far(heads_away)
+    gain_total = gain_total + gain_last
+    in_grad = input_gradient(core[None], kept, given, block_in, gain_attn, grad_middle)
+    gate_up_new = adam_units(gate_up, gate_up_first, gate_up_second, units_sum, 0)
+    heads_away, in_grad, gate_up_new = together(heads_away, in_grad, gate_up_new)
     down_new = tuple(value[0].T for value in down_new)
     qkv_columns = qkv_weight.shape[1]
-    sum_qkv = sum_heads[:, :qkv_columns]
-    sum_out = sum_heads[:, qkv_columns:].T
+    sum_qkv = jnp.where(own, qkv_kept, qkv_other).astype(f32) + heads_away[
+        :, :qkv_columns
+    ].astype(f32)
+    sum_out = jnp.where(own, out_kept, out_other).astype(f32) + heads_away[
+        :, qkv_columns:
+    ].astype(f32)
+    sum_out = sum_out.T
     gain_count = norm_gains.shape[0]
     gain_at = (lax.axis_index("dp") * 4 + z) * gain_count
     gain_grads = lax.dynamic_slice_in_dim(gain_total, gain_at, gain_count)

time: 518 us -> 506 us (0.977)
  Pallas kernels: 190 us -> 211 us
  other arithmetic: 52.7 us -> 41.8 us
  local copies, waits for them, and re-layouts: 22.8 us -> 15.7 us
  waiting for transfers between devices: 137 us -> 130 us
    pallas_call x5 -> x11, Pallas kernels: 52.4 us -> 73.3 us  [the longest x3 39.6 us: units_forward(): pl.pallas_call(functools.partial(units_forward_kernel, count, pick is not...]
    ppermute x22 -> x18, waiting for transfers between devices: 28.9 us -> 12.8 us  [swap_dp(): return lax.ppermute(value, 'dp', [(i, i ^ mask) for i in range(count)])]
    ppermute x9, starting transfers between devices: 9.17 us -> 18.4 us  [swap_near(): return lax.ppermute(value, 'tensor', [(0, 1), (1, 0), (2, 3), (3, 2)])]
    ppermute x2, waiting for transfers between devices: 0.01 us -> 9.18 us  [owner_swap(): return lax.ppermute(value, AXES, perm)]
    unnamed x113 -> x124, local copies, waits for them, and re-layouts: 4.62 us -> 11.1 us
    slice x8 -> x6, local copies, waits for them, and re-layouts: 9.88 us -> 3.46 us  [the longest x1 1.91 us: shards(): branch_ends = [from_ends(down_last[:half]), from_ends(down_last[half:])]]
    ppermute x22 -> x18, starting transfers between devices: 23.2 us -> 20.2 us  [swap_dp(): return lax.ppermute(value, 'dp', [(i, i ^ mask) for i in range(count)])]
  transfers between devices with their start and end apart: 71 -> 68, of which waited for: 31 -> 27; matrix products, arithmetic and copies ran while one was open for 12% -> 8% of each run, Pallas kernels for 37% -> 42%
where the time goes in v3:
time: 506 us; the launch traced here: 499 us
  Pallas kernels  211 us (42%)
  waiting for transfers between devices  130 us (26%)
  starting transfers between devices  85.6 us (17%)
  other arithmetic  41.8 us (8%)
  local copies, waits for them, and re-layouts  15.7 us (3%)
  between operations  15.2 us (3%)
    ppermute x11, waiting for transfers between devices, swap_far(): return lax.ppermute(value, 'tensor', [(0, 2), (2, 0), (1, 3), (3, 1)])  62.6 us
    pallas_call x4, Pallas kernels, units_to_width(): pl.pallas_call(kernel, grid=(width // TILE,), in_specs=[pl.BlockSpec((len...  44.2 us
    pallas_call x3, Pallas kernels, units_forward(): pl.pallas_call(functools.partial(units_forward_kernel, count, pick is not...  39.6 us
    ppermute x9, waiting for transfers between devices, swap_near(): return lax.ppermute(value, 'tensor', [(0, 1), (1, 0), (2, 3), (3, 2)])  32.2 us
    pallas_call x2, Pallas kernels, units_gradient_parts(): pl.pallas_call(units_gradient_kernel, grid_spec=pltpu.PrefetchScalarGridS...  28.8 us
    ppermute x11, starting transfers between devices, swap_far(): return lax.ppermute(value, 'tensor', [(0, 2), (2, 0), (1, 3), (3, 1)])  23.9 us
    pallas_call x1, Pallas kernels, attention_backward(): pl.pallas_call(attention_backward_kernel, grid=(1,), in_specs=scalars(1)...  23.1 us
    ppermute x18, starting transfers between devices, swap_dp(): return lax.ppermute(value, 'dp', [(i, i ^ mask) for i in range(count)])  20.2 us
  transfers between devices with their start and end apart: 68, of which 27 were waited for; matrix products, arithmetic and copies ran while one was open for 8% of the time, Pallas kernels for 42%

profile of v3, /device:TPU:0, one launch (start us, length us, event | category | flops | bytes accessed | tf_op | source)
XLA Modules:
  0.0 499.1 jit_solution(12794135287703213865)
XLA Ops:
  10.1 4.0 collective-permute-start
  15.9 2.1 collective-permute-done.3
  23.8 3.7 shard_map.314
  30.1 3.6 collective-permute-done.6
  41.5 1.9 fusion.12
  43.4 1.9 pad_maximum_fusion.2
  45.9 9.2 %collective-permute-done.7 = bf16[256,1536]{1,0:T(8,128)(2,1)S(1)} collective-permute-done((bf16[256,1536]{1,0:T(8,128)(2,1)}, bf16[256,1536]{1,0:T(8,128)(2,1)S(1)}, u32[]{:S(2)}, u32[]{:S(2)}) %collective-permute-start.7) | collective-permute-done | bytes 786464 | tf_op jit(solution)/shard_map/ppermute | solution.py:838
  55.0 3.1 collective-permute-done.10.refs_6_
  64.4 2.9 collective-permute-start.15
  67.2 6.9 %collective-permute-done.15 = bf16[64,1536]{1,0:T(8,128)(2,1)S(1)} collective-permute-done((bf16[64,1536]{1,0:T(8,128)(2,1)S(1)}, bf16[64,1536]{1,0:T(8,128)(2,1)S(1)}, u32[]{:S(2)}, u32[]{:S(2)}) %collective-permute-start.15) | collective-permute-done | bytes 196640 | tf_op jit(solution)/shard_map/ppermute | solution.py:808
  77.2 4.8 collective-permute-start.16
  86.8 14.7 %shard_map.315 = (bf16[1536,1024]{1,0:T(8,128)(2,1)}, bf16[1024,1536]{1,0:T(8,128)(2,1)}, f32[1024,640]{1,0:T(8,128)}, bf16[6,1024,64]{2,1,0:T(8,128)(2,1)}, bf1...) custom-call(s32[1]{0:T(128)} %bitcast.1.place_ref, ...), custom_call_target="tpu_custom_call" | custom-call | flops 1000 | bytes 1000 | tf_op jit(solution)/shard_map/pallas_call | solution.py:245
  101.5 5.8 %shard_map.316 = (bf16[4,128,1536]{2,1,0:T(8,128)(2,1)}, bf16[4,128,1536]{2,1,0:T(8,128)(2,1)}) custom-call(s32[1]{0:T(128)} %bitcast.core_ref, bf16[1024,384]{1,0:T(8,128)(2,1)} %get-tuple-element.263.attended_ref.refs_5_, bf16[1536,1024]{1,0:T(8,128)(2,1)} %get-tuple-element.264.weight_ref.refs_4_), custom_call_target="tpu_custom_call" | custom-call | flops 1000 | bytes 1000 | tf_op jit(solution)/shard_map/pallas_call | solution.py:260
  107.3 6.7 %collective-permute-done.17 = bf16[192,1536]{1,0:T(8,128)(2,1)} collective-permute-done((bf16[192,1536]{1,0:T(8,128)(2,1)}, bf16[192,1536]{1,0:T(8,128)(2,1)}, u32[]{:S(2)}, u32[]{:S(2)}) %collective-permute-start.17) | collective-permute-done | bytes 589856 | tf_op jit(solution)/shard_map/ppermute | solution.py:808
  116.0 2.0 pad_maximum_fusion.1.refs_3_
  118.5 2.2 fusion.7
  120.7 4.2 collective-permute-start.20
  124.9 9.8 %collective-permute-done.20 = bf16[128,1536]{1,0:T(8,128)(2,1)S(1)} collective-permute-done((bf16[128,1536]{1,0:T(8,128)(2,1)S(1)}, bf16[128,1536]{1,0:T(8,128)(2,1)S(1)}, u32[]{:S(2)}, u32[]{:S(2)}) %collective-permute-start.20) | collective-permute-done | bytes 393248 | tf_op jit(solution)/shard_map/ppermute | solution.py:804
  134.8 5.1 %collective-permute-start.22 = (bf16[128,1536]{1,0:T(8,128)(2,1)S(1)}, bf16[128,1536]{1,0:T(8,128)(2,1)S(1)}, u32[]{:S(2)}, u32[]{:S(2)}) collective-permute-start(bf16[128,1536]{1,0:T(8,128)(2,1)S(1)} %add_convert_fusion.4), channel_id=1, source_target_pairs={{0,2},{2,0},{1,3},{3,1},{4,6},{6,4},{5,7},{7,5},{8,10},{10,8},{9,1... | collective-permute-start | bytes 1179656 | tf_op jit(solution)/shard_map/ppermute | solution.py:808
  139.9 5.9 %collective-permute-done.23 = bf16[128,1536]{1,0:T(8,128)(2,1)S(1)} collective-permute-done((bf16[128,1536]{1,0:T(8,128)(2,1)S(1)}, bf16[128,1536]{1,0:T(8,128)(2,1)S(1)}, u32[]{:S(2)}, u32[]{:S(2)}) %collective-permute-start.23) | collective-permute-done | bytes 393248 | tf_op jit(solution)/shard_map/ppermute | solution.py:804
  145.8 11.7 %collective-permute-done.22 = bf16[128,1536]{1,0:T(8,128)(2,1)S(1)} collective-permute-done((bf16[128,1536]{1,0:T(8,128)(2,1)S(1)}, bf16[128,1536]{1,0:T(8,128)(2,1)S(1)}, u32[]{:S(2)}, u32[]{:S(2)}) %collective-permute-start.22) | collective-permute-done | bytes 393248 | tf_op jit(solution)/shard_map/ppermute | solution.py:808
  157.7 1.8 collective-permute-done.24
  161.4 1.9 collective-permute-start.26
  164.6 3.5 all-gather.2.cloned.1.call-done.refs_2_.refs_4_.units_ref
  168.1 12.0 %shard_map.317 = (bf16[1024,1536]{1,0:T(8,128)(2,1)}, bf16[1024,1536]{1,0:T(8,128)(2,1)}, bf16[1024,1792]{1,0:T(8,128)(2,1)}, bf16[1024,3584]{1,0:T(8,128)(2,1)}) custom-call(s32[1]{0:T(128)} %constant.122.clone.1.pick_ref, bf16[256,1536]{1,0:T(8,128)(2,1)} %copy-done.11, bf16[256,1536]{1,0:T(8,128)(2,1)} %copy-done.1, ...), custom_call_target="tpu_custom_call" | custom-call | flops 1000 | bytes 1000 | tf_op jit(solution)/shard_map/pallas_call | solution.py:660
  180.1 17.8 %collective-permute-done.25.refs_1_ = bf16[256,1536]{1,0:T(8,128)(2,1)} collective-permute-done((bf16[256,1536]{1,0:T(8,128)(2,1)S(1)}, bf16[256,1536]{1,0:T(8,128)(2,1)}, u32[]{:S(2)}, u32[]{:S(2)}) %collective-permute-start.25) | collective-permute-done | bytes 786464 | tf_op jit(solution)/shard_map/ppermute | solution.py:808
  200.8 15.4 %shard_map.318 = (bf16[1024,1536]{1,0:T(8,128)(2,1)}, bf16[1024,1536]{1,0:T(8,128)(2,1)}, bf16[1024,1792]{1,0:T(8,128)(2,1)}, bf16[1024,3584]{1,0:T(8,128)(2,1)}) custom-call(s32[1]{0:T(128)} %constant.122.clone.1.pick_ref, ...), custom_call_target="tpu_custom_call", output_to_operand_aliasing={{0}: (6, {}), {1}: (7, {}), {2}: (8, {}), {3}: (9, {})} | custom-call | flops 1000 | bytes 1000 | tf_op jit(solution)/shard_map/pallas_call | solution.py:660
  216.1 12.1 %shard_map.319 = (bf16[256,1536]{1,0:T(8,128)(2,1)}, bf16[256,1536]{1,0:T(8,128)(2,1)}) custom-call(bf16[1024,3584]{1,0:T(8,128)(2,1)} %get-tuple-element.311.both_ref.refs_8_, bf16[1536,5376]{1,0:T(8,128)(2,1)} %all-gather.2.cloned.1.call-done.refs_2_.refs_4_.units_ref), custom_call_target="tpu_custom_call" | custom-call | flops 1000 | bytes 1000 | tf_op jit(solution)/shard_map/pallas_call | solution.py:721
  228.3 3.4 collective-permute-done.27.refs_0_
  232.6 1.8 collective-permute-start.30
  235.3 12.3 %shard_map.320 = (bf16[1024,1536]{1,0:T(8,128)(2,1)}, bf16[1024,1536]{1,0:T(8,128)(2,1)}, bf16[1024,1792]{1,0:T(8,128)(2,1)}, bf16[1024,3584]{1,0:T(8,128)(2,1)}) custom-call(s32[1]{0:T(128)} %bitcast.17.pick_ref, bf16[256,1536]{1,0:T(8,128)(2,1)} %copy-done.31, ...), custom_call_target="tpu_custom_call", output_to_operand_aliasing={{0}: (6, {}), {1}: (7, {}), {2}: (8, {}), {3}: (9, {})} | custom-call | flops 1000 | bytes 1000 | tf_op jit(solution)/shard_map/pallas_call | solution.py:660
  247.6 12.1 %shard_map.321 = (bf16[256,1536]{1,0:T(8,128)(2,1)}, bf16[256,1536]{1,0:T(8,128)(2,1)}) custom-call(bf16[1024,3584]{1,0:T(8,128)(2,1)} %get-tuple-element.327.both_ref.right_ref, bf16[1536,5376]{1,0:T(8,128)(2,1)} %all-gather.2.cloned.1.call-done.refs_2_.refs_4_.units_ref), custom_call_target="tpu_custom_call" | custom-call | flops 1000 | bytes 1000 | tf_op jit(solution)/shard_map/pallas_call | solution.py:721
  259.7 7.9 %collective-permute-done.30 = bf16[256,1536]{1,0:T(8,128)(2,1)S(1)} collective-permute-done((bf16[256,1536]{1,0:T(8,128)(2,1)}, bf16[256,1536]{1,0:T(8,128)(2,1)S(1)}, u32[]{:S(2)}, u32[]{:S(2)}) %collective-permute-start.30) | collective-permute-done | bytes 786464 | tf_op jit(solution)/shard_map/ppermute | solution.py:804
  267.5 3.0 collective-permute-done.31
  271.9 8.9 %shard_map.322 = bf16[256,1536]{1,0:T(8,128)(2,1)} custom-call(bf16[1024,1792]{1,0:T(8,128)(2,1)} %get-tuple-element.340.hidden_ref.right_ref, bf16[1536,5376]{1,0:T(8,128)(2,1)} %all-gather.2.cloned.1.call-done.refs_2_.refs_4_.units_ref), custom_call_target="tpu_custom_call" | custom-call | flops 1000 | bytes 1000 | tf_op jit(solution)/shard_map/pallas_call | solution.py:721
  280.8 1.9 fusion.19
  285.3 11.3 %shard_map.323 = (bf16[4,192,1792]{2,1,0:T(8,128)(2,1)}, bf16[4,192,1792]{2,1,0:T(8,128)(2,1)}) custom-call(s32[1]{0:T(128)} %bitcast.core_ref, bf16[1024,1536]{1,0:T(8,128)(2,1)} %get-tuple-element.323.left_ref, bf16[1024,1792]{1,0:T(8,128)(2,1)} %get-tuple-element.340.hidden_ref.right_ref), custom_call_target="tpu_custom_call" | custom-call | flops 1000 | bytes 1000 | tf_op jit(solution)/shard_map/pallas_call | solution.py:780
  296.6 17.5 %shard_map.324 = (bf16[4,192,3584]{2,1,0:T(8,128)(2,1)}, bf16[4,192,3584]{2,1,0:T(8,128)(2,1)}) custom-call(s32[1]{0:T(128)} %bitcast.core_ref, bf16[1024,1536]{1,0:T(8,128)(2,1)} %get-tuple-element.326.left_ref, bf16[1024,3584]{1,0:T(8,128)(2,1)} %get-tuple-element.327.both_ref.right_ref), custom_call_target="tpu_custom_call" | custom-call | flops 1000 | bytes 1000 | tf_op jit(solution)/shard_map/pallas_call | solution.py:780
  315.7 2.0 fusion.18
  318.2 11.1 %shard_map.326 = (bf16[256,1536]{1,0:T(8,128)(2,1)}, bf16[256,1536]{1,0:T(8,128)(2,1)}, bf16[256,1536]{1,0:T(8,128)(2,1)}) custom-call(bf16[1024,1792]{1,0:T(8,128)(2,1)} %get-tuple-element.340.hidden_ref.right_ref, bf16[1536,5376]{1,0:T(8,128)(2,1)} %all-gather.2.cloned.1.call-done.refs_2_.refs_4_.units_ref), custom_call_target="tpu_custom_call" | custom-call | flops 1000 | bytes 1000 | tf_op jit(solution)/shard_map/pallas_call | solution.py:721
  331.0 9.3 %shard_map.325 = bf16[4,192,5376]{2,1,0:T(8,128)(2,1)} custom-call(bf16[4,192,3584]{2,1,0:T(8,128)(2,1)} %get-tuple-element.336.refs_0_, bf16[4,192,3584]{2,1,0:T(8,128)(2,1)} %collective-permute-done.36.refs_1_, bf16[4,192,1792]{2,1,0:T(8,128)(2,1)} %get-tuple-element.338.refs_2_, bf16[4,192,1792]{2,1,0:T(8,128)(2,1)} %collective-permute-done.37.refs_3_), custom_call_target="tpu_custom_call" | custom-call | flops 1000 | bytes 1000 | tf_op jit(solution)/shard_map/pallas_call | solution.py:749
  342.6 4.3 collective-permute-start.40
  346.9 13.7 %collective-permute-done.40 = bf16[128,1536]{1,0:T(8,128)(2,1)S(1)} collective-permute-done((bf16[128,1536]{1,0:T(8,128)(2,1)S(1)}, bf16[128,1536]{1,0:T(8,128)(2,1)S(1)}, u32[]{:S(2)}, u32[]{:S(2)}) %collective-permute-start.40) | collective-permute-done | bytes 393248 | tf_op jit(solution)/shard_map/ppermute | solution.py:808
  362.4 2.3 collective-permute-start.41
  365.6 5.0 collective-permute-start.43
  372.5 8.7 %shard_map.327 = (bf16[6,1024,64]{2,1,0:T(8,128)(2,1)}, f32[8,1024]{1,0:T(8,128)}, bf16[2,192,384]{2,1,0:T(8,128)(2,1)}, bf16[2,192,384]{2,1,0:T(8,128)(2,1)}, b...) custom-call(s32[1]{0:T(128)} %bitcast.1.place_ref, s32[2]{0:T(128)} %pad_add_fusion.pair_ref, ...), custom_call_target="tpu_custom_call" | custom-call | flops 1000 | bytes 1000 | tf_op jit(solution)/shard_map/pallas_call | solution.py:388
  383.2 23.1 %shard_map.328 = (bf16[1024,640]{1,0:T(8,128)(2,1)}, bf16[4,128,1536]{2,1,0:T(8,128)(2,1)}, bf16[4,128,1536]{2,1,0:T(8,128)(2,1)}, f32[1,640]{1,0:T(1,128)}, f32[1,1536]{1,0:T(1,128)}) custom-call(s32[1]{0:T(128)} %bitcast.core_ref, bf16[6,1024,64]{2,1,0:T(8,128)(2,1)} %get-tuple-element.347.q_ref, bf16[2,1024,64]{2,1,0:T(8,128)(2,1)} %get-tuple-element.348.k_ref, ...), custom_call_target="tpu_custom_call" | custom-call | flops 1000 | bytes 1000 | tf_op jit(solution)/shard_map/pallas_call | solution.py:511
  407.6 6.4 %shard_map.329 = (bf16[2,192,640]{2,1,0:T(8,128)(2,1)}, bf16[2,192,640]{2,1,0:T(8,128)(2,1)}, bf16[2,192,640]{2,1,0:T(8,128)(2,1)}, bf16[2,192,640]{2,1,0:T(8,128)(2,1)}) custom-call(s32[2]{0:T(128)} %pad_add_fusion.pair_ref, bf16[1024,1536]{1,0:T(8,128)(2,1)} %get-tuple-element.359.normed_ref.left_ref, bf16[1024,640]{1,0:T(8,128)(2,1)} %get-tuple-element.375.right_ref), custom_call_target="tpu_custom_call" | custom-call | flops 1000 | bytes 1000 | tf_op jit(solution)/shard_map/pallas_call | solution.py:304
  416.2 2.1 collective-permute-start.50
  422.5 6.1 %collective-permute-done.50 = bf16[128,1536]{1,0:T(8,128)(2,1)} collective-permute-done((bf16[128,1536]{1,0:T(8,128)(2,1)}, bf16[128,1536]{1,0:T(8,128)(2,1)}, u32[]{:S(2)}, u32[]{:S(2)}) %collective-permute-start.50) | collective-permute-done | bytes 393248 | tf_op jit(solution)/shard_map/ppermute | solution.py:804
  428.5 2.0 fusion
  432.2 3.3 convert_add_fusion
  435.5 5.2 %collective-permute-done.52 = f32[3200]{0:T(1024)S(1)} collective-permute-done((f32[3200]{0:T(1024)S(1)}, f32[3200]{0:T(1024)S(1)}, u32[]{:S(2)}, u32[]{:S(2)}) %collective-permute-start.52) | collective-permute-done | bytes 12832 | tf_op jit(solution)/shard_map/ppermute | solution.py:905
  442.3 2.5 shard_map.330
  446.8 2.1 shard_map.331
  449.2 1.7 collective-permute-start.59
  450.9 5.3 %shard_map.332 = (f32[1,192,1728]{2,1,0:T(8,128)}, f32[1,192,1728]{2,1,0:T(8,128)}, f32[1,192,1728]{2,1,0:T(8,128)}) custom-call(f32[1,192,1728]{2,1,0:T(8,128)} %bitcast.73, f32[1,192,1728]{2,1,0:T(8,128)} %bitcast.74, f32[1,192,1728]{2,1,0:T(8,128)} %bitcast.75, bf16[192,5376]{1,0:T(8,128)(2,1)} %reduce-scatter.2.cloned.1.call-done.sum_ref), custom_call_target="tpu_custom_call" | custom-call | flops 1000 | bytes 1000 | tf_op jit(solution)/shard_map/pallas_call | solution.py:610
  457.8 2.2 shard_map.333
  460.1 1.9 shard_map.334
  467.0 2.4 collective-permute-start.65
  470.8 2.1 convert_select_fusion.2.kept_ref
  473.6 4.1 shard_map.335
  478.4 8.3 %shard_map.336 = (f32[2,192,1728]{2,1,0:T(8,128)}, f32[2,192,1728]{2,1,0:T(8,128)}, f32[2,192,1728]{2,1,0:T(8,128)}) custom-call(f32[2,192,1728]{2,1,0:T(8,128)} %weight_ref.1, f32[2,192,1728]{2,1,0:T(8,128)} %first_ref.1, f32[2,192,1728]{2,1,0:T(8,128)} %second_ref.1, bf16[192,5376]{1,0:T(8,128)(2,1)} %reduce-scatter.2.cloned.1.call-done.sum_ref), custom_call_target="tpu_custom_call" | custom-call | flops 1000 | bytes 1000 | tf_op jit(solution)/shard_map/pallas_call | solution.py:610
  486.7 2.8 collective-permute-done.61
  (301 shorter events, 87.5 us)
Async XLA Ops:
  7.2 160.9 %all-gather.2.cloned.1.call-start = ((), (), s32[]{:S(2)}) async-start(), calls=%async_computation.1 | async-start | bytes 18579456 | tf_op jit(solution)/shard_map/all_gather | solution.py:1101
  9.5 4.8 collective-permute-start.2
  10.0 19.5 %collective-permute-start.1 = (s32[1024]{0:T(1024)S(1)}, s32[1024]{0:T(1024)S(1)}, u32[]{:S(2)}, u32[]{:S(2)}) collective-permute-start(s32[1024]{0:T(1024)S(1)} %copy-done.54), channel_id=1, source_target_pairs={{0,4},{4,0},{8,12},{12,8},{16,20},{20,16},{24,28},{28,24},{1,5},{5... | collective-permute-start | bytes 12296 | tf_op jit(solution)/shard_map/ppermute | solution.py:800
  10.1 23.7 %collective-permute-start = (bf16[192,1024]{1,0:T(8,128)(2,1)S(1)}, bf16[192,1024]{1,0:T(8,128)(2,1)S(1)}, u32[]{:S(2)}, u32[]{:S(2)}) collective-permute-start(bf16[192,1024]{1,0:T(8,128)(2,1)S(1)} %pad_maximum_fusion.4), channel_id=1, source_target_pairs={{0,2},{2,0},{1,3},{3,1},{4,6},{6,4},{5,7},{7,5},{8,10},{10,8},{9,1... | collective-permute-start | bytes 1179656 | tf_op jit(solution)/shard_map/ppermute | solution.py:808
  18.0 3.7 collective-permute-start.4
  21.7 7.3 %collective-permute-start.5 = (f32[8,1,100]{2,0,1:T(8,128)S(1)}, f32[8,1,100]{2,0,1:T(8,128)S(1)}, u32[]{:S(2)}, u32[]{:S(2)}) collective-permute-start(f32[8,1,100]{2,0,1:T(8,128)S(1)} %maximum_bitcast_fusion), channel_id=1, source_target_pairs={{0,1},{1,0},{2,3},{3,2},{4,5},{5,4},{6,7},{7,6},{8,9},{9,8},{10,11... | collective-permute-start | bytes 9608 | tf_op jit(solution)/shard_map/ppermute | solution.py:883
  29.1 4.6 collective-permute-start.6
  35.5 19.6 %collective-permute-start.7 = (bf16[256,1536]{1,0:T(8,128)(2,1)}, bf16[256,1536]{1,0:T(8,128)(2,1)S(1)}, u32[]{:S(2)}, u32[]{:S(2)}) collective-permute-start(bf16[256,1536]{1,0:T(8,128)(2,1)} %multiply_convert_fusion.1), channel_id=1, source_target_pairs={{0,1},{4,2},{1,0},{5,3},{6,7},{2,4},{7,6},{3,5},{8,9},{12,10},{9,8... | collective-permute-start | bytes 2359304 | tf_op jit(solution)/shard_map/ppermute | solution.py:838
  38.4 19.8 %collective-permute-start.10 = (bf16[384,1024]{1,0:T(8,128)(2,1)S(1)}, bf16[384,1024]{1,0:T(8,128)(2,1)S(1)}, u32[]{:S(2)}, u32[]{:S(2)}) collective-permute-start(bf16[384,1024]{1,0:T(8,128)(2,1)S(1)} %pad_maximum_fusion.refs_4_), channel_id=1, source_target_pairs={{0,16},{4,20},{8,24},{12,28},{16,0},{20,4},{24,8},{28,12},{1,17},{... | collective-permute-start | bytes 2359304 | tf_op jit(solution)/shard_map/ppermute | solution.py:905
  40.0 19.4 %collective-permute-start.9 = (bf16[384,1024]{1,0:T(8,128)(2,1)S(1)}, bf16[384,1024]{1,0:T(8,128)(2,1)S(1)}, u32[]{:S(2)}, u32[]{:S(2)}) collective-permute-start(bf16[384,1024]{1,0:T(8,128)(2,1)S(1)} %pad_maximum_fusion.refs_4_), channel_id=1, source_target_pairs={{0,8},{4,12},{8,0},{12,4},{16,24},{20,28},{24,16},{28,20},{1,9},{5... | collective-permute-start | bytes 2359304 | tf_op jit(solution)/shard_map/ppermute | solution.py:905
  60.5 13.7 %collective-permute-start.14 = (bf16[256,1536]{1,0:T(8,128)(2,1)S(1)}, bf16[256,1536]{1,0:T(8,128)(2,1)S(1)}, u32[]{:S(2)}, u32[]{:S(2)}) collective-permute-start(bf16[256,1536]{1,0:T(8,128)(2,1)S(1)} %broadcast_select_fusion.3.refs_0_), channel_id=1, source_target_pairs={{0,4},{4,0},{8,12},{12,8},{16,20},{20,16},{24,28},{28,24},{1,5},{5... | collective-permute-start | bytes 2359304 | tf_op jit(solution)/shard_map/ppermute | solution.py:800
  60.5 15.4 %collective-permute-start.13 = (bf16[256,1536]{1,0:T(8,128)(2,1)S(1)}, bf16[256,1536]{1,0:T(8,128)(2,1)}, u32[]{:S(2)}, u32[]{:S(2)}) collective-permute-start(bf16[256,1536]{1,0:T(8,128)(2,1)S(1)} %collective-permute-done.7), channel_id=1, source_target_pairs={{4,5},{5,4},{2,3},{3,2},{12,13},{13,12},{10,11},{11,10},{20,21},{2... | collective-permute-start | bytes 2359304 | tf_op jit(solution)/shard_map/ppermute | solution.py:847
  62.2 12.0 %collective-permute-start.11 = (bf16[192,1024]{1,0:T(8,128)(2,1)S(1)}, bf16[192,1024]{1,0:T(8,128)(2,1)S(1)}, u32[]{:S(2)}, u32[]{:S(2)}) collective-permute-start(bf16[192,1024]{1,0:T(8,128)(2,1)S(1)} %slice.52), channel_id=1, source_target_pairs={{0,8},{4,12},{8,0},{12,4},{16,24},{20,28},{24,16},{28,20},{1,9},{5... | collective-permute-start | bytes 1179656 | tf_op jit(solution)/shard_map/ppermute | solution.py:905
  63.7 10.5 %collective-permute-start.12 = (bf16[192,1024]{1,0:T(8,128)(2,1)S(1)}, bf16[192,1024]{1,0:T(8,128)(2,1)S(1)}, u32[]{:S(2)}, u32[]{:S(2)}) collective-permute-start(bf16[192,1024]{1,0:T(8,128)(2,1)S(1)} %slice.53), channel_id=1, source_target_pairs={{0,16},{4,20},{8,24},{12,28},{16,0},{20,4},{24,8},{28,12},{1,17},{... | collective-permute-start | bytes 1179656 | tf_op jit(solution)/shard_map/ppermute | solution.py:905
  64.4 9.8 %collective-permute-start.15 = (bf16[64,1536]{1,0:T(8,128)(2,1)S(1)}, bf16[64,1536]{1,0:T(8,128)(2,1)S(1)}, u32[]{:S(2)}, u32[]{:S(2)}) collective-permute-start(bf16[64,1536]{1,0:T(8,128)(2,1)S(1)} %slice.54), channel_id=1, source_target_pairs={{0,2},{2,0},{1,3},{3,1},{4,6},{6,4},{5,7},{7,5},{8,10},{10,8},{9,1... | collective-permute-start | bytes 589832 | tf_op jit(solution)/shard_map/ppermute | solution.py:808
  76.0 374.9 %reduce-scatter.2.cloned.1.call-start = ((), (), s32[]{:S(2)}) async-start(), calls=%async_computation.2 | async-start | bytes 10321920 | tf_op jit(solution)/shard_map/reduce_scatter | solution.py:977
  77.2 8.7 %collective-permute-start.16 = (bf16[256,1536]{1,0:T(8,128)(2,1)}, bf16[256,1536]{1,0:T(8,128)(2,1)S(1)}, u32[]{:S(2)}, u32[]{:S(2)}) collective-permute-start(bf16[256,1536]{1,0:T(8,128)(2,1)} %broadcast_select_fusion.2.refs_1_), channel_id=1, source_target_pairs={{0,4},{4,0},{8,12},{12,8},{16,20},{20,16},{24,28},{28,24},{1,5},{5... | collective-permute-start | bytes 2359304 | tf_op jit(solution)/shard_map/ppermute | solution.py:800
  82.1 32.6 %collective-permute-start.18 = (bf16[256,1536]{1,0:T(8,128)(2,1)S(1)}, bf16[256,1536]{1,0:T(8,128)(2,1)}, u32[]{:S(2)}, u32[]{:S(2)}) collective-permute-start(bf16[256,1536]{1,0:T(8,128)(2,1)S(1)} %convert_element_type.194.refs_1_), channel_id=1, source_target_pairs={{0,1},{1,0},{2,3},{3,2},{4,5},{5,4},{6,7},{7,6},{8,9},{9,8},{10,11... | collective-permute-start | bytes 2359304 | tf_op jit(solution)/shard_map/ppermute | solution.py:804
  84.6 29.3 %collective-permute-start.17 = (bf16[192,1536]{1,0:T(8,128)(2,1)}, bf16[192,1536]{1,0:T(8,128)(2,1)}, u32[]{:S(2)}, u32[]{:S(2)}) collective-permute-start(bf16[192,1536]{1,0:T(8,128)(2,1)} %slice.55), channel_id=1, source_target_pairs={{0,2},{2,0},{1,3},{3,1},{4,6},{6,4},{5,7},{7,5},{8,10},{10,8},{9,1... | collective-permute-start | bytes 1769480 | tf_op jit(solution)/shard_map/ppermute | solution.py:808
  114.7 3.8 collective-permute-start.19
  114.7 10.2 %collective-permute-start.21 = (bf16[256,1536]{1,0:T(8,128)(2,1)S(1)}, bf16[256,1536]{1,0:T(8,128)(2,1)S(1)}, u32[]{:S(2)}, u32[]{:S(2)}) collective-permute-start(bf16[256,1536]{1,0:T(8,128)(2,1)S(1)} %convert_element_type.194.refs_1_), channel_id=1, source_target_pairs={{1,2},{2,1},{5,6},{6,5},{9,10},{10,9},{13,14},{14,13},{17,18},{18,... | collective-permute-start | bytes 2359304 | tf_op jit(solution)/shard_map/ppermute | solution.py:812
  120.7 14.1 %collective-permute-start.20 = (bf16[128,1536]{1,0:T(8,128)(2,1)S(1)}, bf16[128,1536]{1,0:T(8,128)(2,1)S(1)}, u32[]{:S(2)}, u32[]{:S(2)}) collective-permute-start(bf16[128,1536]{1,0:T(8,128)(2,1)S(1)} %get-tuple-element.467), channel_id=1, source_target_pairs={{0,1},{1,0},{2,3},{3,2},{4,5},{5,4},{6,7},{7,6},{8,9},{9,8},{10,11... | collective-permute-start | bytes 1179656 | tf_op jit(solution)/shard_map/ppermute | solution.py:804
  124.8 20.9 %collective-permute-start.23 = (bf16[128,1536]{1,0:T(8,128)(2,1)S(1)}, bf16[128,1536]{1,0:T(8,128)(2,1)S(1)}, u32[]{:S(2)}, u32[]{:S(2)}) collective-permute-start(bf16[128,1536]{1,0:T(8,128)(2,1)S(1)} %get-tuple-element.464), channel_id=1, source_target_pairs={{0,1},{1,0},{2,3},{3,2},{4,5},{5,4},{6,7},{7,6},{8,9},{9,8},{10,11... | collective-permute-start | bytes 1179656 | tf_op jit(solution)/shard_map/ppermute | solution.py:804
  134.8 22.6 %collective-permute-start.22 = (bf16[128,1536]{1,0:T(8,128)(2,1)S(1)}, bf16[128,1536]{1,0:T(8,128)(2,1)S(1)}, u32[]{:S(2)}, u32[]{:S(2)}) collective-permute-start(bf16[128,1536]{1,0:T(8,128)(2,1)S(1)} %add_convert_fusion.4), channel_id=1, source_target_pairs={{0,2},{2,0},{1,3},{3,1},{4,6},{6,4},{5,7},{7,5},{8,10},{10,8},{9,1... | collective-permute-start | bytes 1179656 | tf_op jit(solution)/shard_map/ppermute | solution.py:808
  161.3 36.6 %collective-permute-start.25 = (bf16[256,1536]{1,0:T(8,128)(2,1)S(1)}, bf16[256,1536]{1,0:T(8,128)(2,1)}, u32[]{:S(2)}, u32[]{:S(2)}) collective-permute-start(bf16[256,1536]{1,0:T(8,128)(2,1)S(1)} %multiply_convert_fusion.refs_0_), channel_id=1, source_target_pairs={{0,2},{2,0},{1,3},{3,1},{4,6},{6,4},{5,7},{7,5},{8,10},{10,8},{9,1... | collective-permute-start | bytes 2359304 | tf_op jit(solution)/shard_map/ppermute | solution.py:808
  161.4 37.3 %collective-permute-start.26 = (bf16[256,1536]{1,0:T(8,128)(2,1)S(1)}, bf16[256,1536]{1,0:T(8,128)(2,1)}, u32[]{:S(2)}, u32[]{:S(2)}) collective-permute-start(bf16[256,1536]{1,0:T(8,128)(2,1)S(1)} %multiply_convert_fusion.refs_0_), channel_id=1, source_target_pairs={{0,1},{1,0},{2,3},{3,2},{4,5},{5,4},{6,7},{7,6},{8,9},{9,8},{10,11... | collective-permute-start | bytes 2359304 | tf_op jit(solution)/shard_map/ppermute | solution.py:804
  163.3 64.9 %collective-permute-start.29 = (bf16[256,1536]{1,0:T(8,128)(2,1)S(1)}, bf16[256,1536]{1,0:T(8,128)(2,1)}, u32[]{:S(2)}, u32[]{:S(2)}) collective-permute-start(bf16[256,1536]{1,0:T(8,128)(2,1)S(1)} %copy-done.10), channel_id=1, source_target_pairs={{1,0},{2,3},{5,4},{6,7},{9,8},{10,11},{13,12},{14,15},{17,16},{18,... | collective-permute-start | bytes 2359304 | tf_op jit(solution)/shard_map/ppermute | solution.py:820
  198.8 32.9 %collective-permute-start.27 = (bf16[256,1536]{1,0:T(8,128)(2,1)}, bf16[256,1536]{1,0:T(8,128)(2,1)S(1)}, u32[]{:S(2)}, u32[]{:S(2)}) collective-permute-start(bf16[256,1536]{1,0:T(8,128)(2,1)} %collective-permute-done.25.refs_1_), channel_id=1, source_target_pairs={{1,0},{2,3},{5,4},{6,7},{9,8},{10,11},{13,12},{14,15},{17,16},{18,... | collective-permute-start | bytes 2359304 | tf_op jit(solution)/shard_map/ppermute | solution.py:820
  200.1 31.6 %collective-permute-start.28 = (bf16[256,1536]{1,0:T(8,128)(2,1)}, bf16[256,1536]{1,0:T(8,128)(2,1)S(1)}, u32[]{:S(2)}, u32[]{:S(2)}) collective-permute-start(bf16[256,1536]{1,0:T(8,128)(2,1)} %copy-done.11), channel_id=1, source_target_pairs={{1,2},{2,1},{5,6},{6,5},{9,10},{10,9},{13,14},{14,13},{17,18},{18,... | collective-permute-start | bytes 2359304 | tf_op jit(solution)/shard_map/ppermute | solution.py:812
  232.6 35.0 %collective-permute-start.30 = (bf16[256,1536]{1,0:T(8,128)(2,1)}, bf16[256,1536]{1,0:T(8,128)(2,1)S(1)}, u32[]{:S(2)}, u32[]{:S(2)}) collective-permute-start(bf16[256,1536]{1,0:T(8,128)(2,1)} %get-tuple-element.302), channel_id=1, source_target_pairs={{0,1},{1,0},{2,3},{3,2},{4,5},{5,4},{6,7},{7,6},{8,9},{9,8},{10,11... | collective-permute-start | bytes 2359304 | tf_op jit(solution)/shard_map/ppermute | solution.py:804
  234.3 36.2 %collective-permute-start.31 = (bf16[256,1536]{1,0:T(8,128)(2,1)}, bf16[256,1536]{1,0:T(8,128)(2,1)S(1)}, u32[]{:S(2)}, u32[]{:S(2)}) collective-permute-start(bf16[256,1536]{1,0:T(8,128)(2,1)} %get-tuple-element.303), channel_id=1, source_target_pairs={{0,2},{2,0},{1,3},{3,1},{4,6},{6,4},{5,7},{7,5},{8,10},{10,8},{9,1... | collective-permute-start | bytes 2359304 | tf_op jit(solution)/shard_map/ppermute | solution.py:808
  270.5 43.6 %collective-permute-start.32 = (bf16[256,1536]{1,0:T(8,128)(2,1)}, bf16[256,1536]{1,0:T(8,128)(2,1)S(1)}, u32[]{:S(2)}, u32[]{:S(2)}) collective-permute-start(bf16[256,1536]{1,0:T(8,128)(2,1)} %get-tuple-element.321), channel_id=1, source_target_pairs={{0,3},{1,2},{2,1},{3,0},{4,7},{5,6},{6,5},{7,4},{8,11},{9,10},{10,... | collective-permute-start | bytes 2359304 | tf_op jit(solution)/shard_map/ppermute | solution.py:816
  282.7 31.4 %collective-permute-start.33 = (bf16[128,1536]{1,0:T(8,128)(2,1)}, bf16[128,1536]{1,0:T(8,128)(2,1)S(1)}, u32[]{:S(2)}, u32[]{:S(2)}) collective-permute-start(bf16[128,1536]{1,0:T(8,128)(2,1)} %get-tuple-element.473), channel_id=1, source_target_pairs={{0,1},{3,2},{4,5},{7,6},{8,9},{11,10},{12,13},{15,14},{16,17},{19,... | collective-permute-start | bytes 1179656 | tf_op jit(solution)/shard_map/ppermute | solution.py:824
  284.0 30.1 %collective-permute-start.34 = (bf16[128,1536]{1,0:T(8,128)(2,1)S(1)}, bf16[128,1536]{1,0:T(8,128)(2,1)S(1)}, u32[]{:S(2)}, u32[]{:S(2)}) collective-permute-start(bf16[128,1536]{1,0:T(8,128)(2,1)S(1)} %get-tuple-element.472), channel_id=1, source_target_pairs={{0,1},{3,2},{4,5},{7,6},{8,9},{11,10},{12,13},{15,14},{16,17},{19,... | collective-permute-start | bytes 1179656 | tf_op jit(solution)/shard_map/ppermute | solution.py:824
  317.7 13.3 %collective-permute-start.36 = (bf16[4,192,3584]{2,1,0:T(8,128)(2,1)}, bf16[4,192,3584]{2,1,0:T(8,128)(2,1)}, u32[]{:S(2)}, u32[]{:S(2)}) collective-permute-start(bf16[4,192,3584]{2,1,0:T(8,128)(2,1)} %get-tuple-element.337), channel_id=1, source_target_pairs={{0,4},{4,0},{8,12},{12,8},{16,20},{20,16},{24,28},{28,24},{1,5},{5... | collective-permute-start | bytes 16515080 | tf_op jit(solution)/shard_map/ppermute | solution.py:800
  317.7 13.3 %collective-permute-start.37 = (bf16[4,192,1792]{2,1,0:T(8,128)(2,1)}, bf16[4,192,1792]{2,1,0:T(8,128)(2,1)}, u32[]{:S(2)}, u32[]{:S(2)}) collective-permute-start(bf16[4,192,1792]{2,1,0:T(8,128)(2,1)} %get-tuple-element.339), channel_id=1, source_target_pairs={{0,4},{4,0},{8,12},{12,8},{16,20},{20,16},{24,28},{28,24},{1,5},{5... | collective-permute-start | bytes 8257544 | tf_op jit(solution)/shard_map/ppermute | solution.py:800
  318.2 22.1 %collective-permute-start.35 = (bf16[256,1536]{1,0:T(8,128)(2,1)S(1)}, bf16[256,1536]{1,0:T(8,128)(2,1)S(1)}, u32[]{:S(2)}, u32[]{:S(2)}) collective-permute-start(bf16[256,1536]{1,0:T(8,128)(2,1)S(1)} %get-tuple-element.335), channel_id=1, source_target_pairs={{0,1},{4,2},{1,0},{5,3},{6,7},{2,4},{7,6},{3,5},{8,9},{12,10},{9,8... | collective-permute-start | bytes 2359304 | tf_op jit(solution)/shard_map/ppermute | solution.py:838
  341.6 19.0 %collective-permute-start.39 = (bf16[256,1536]{1,0:T(8,128)(2,1)S(1)}, bf16[256,1536]{1,0:T(8,128)(2,1)S(1)}, u32[]{:S(2)}, u32[]{:S(2)}) collective-permute-start(bf16[256,1536]{1,0:T(8,128)(2,1)S(1)} %broadcast_select_fusion.1.refs_0_), channel_id=1, source_target_pairs={{0,4},{4,0},{8,12},{12,8},{16,20},{20,16},{24,28},{28,24},{1,5},{5... | collective-permute-start | bytes 2359304 | tf_op jit(solution)/shard_map/ppermute | solution.py:800
  341.7 20.6 %collective-permute-start.38 = (bf16[256,1536]{1,0:T(8,128)(2,1)S(1)}, bf16[256,1536]{1,0:T(8,128)(2,1)S(1)}, u32[]{:S(2)}, u32[]{:S(2)}) collective-permute-start(bf16[256,1536]{1,0:T(8,128)(2,1)S(1)} %collective-permute-done.35), channel_id=1, source_target_pairs={{4,5},{5,4},{2,3},{3,2},{12,13},{13,12},{10,11},{11,10},{20,21},{2... | collective-permute-start | bytes 2359304 | tf_op jit(solution)/shard_map/ppermute | solution.py:847
  342.6 18.0 %collective-permute-start.40 = (bf16[128,1536]{1,0:T(8,128)(2,1)S(1)}, bf16[128,1536]{1,0:T(8,128)(2,1)S(1)}, u32[]{:S(2)}, u32[]{:S(2)}) collective-permute-start(bf16[128,1536]{1,0:T(8,128)(2,1)S(1)} %slice.58), channel_id=1, source_target_pairs={{0,2},{2,0},{1,3},{3,1},{4,6},{6,4},{5,7},{7,5},{8,10},{10,8},{9,1... | collective-permute-start | bytes 1179656 | tf_op jit(solution)/shard_map/ppermute | solution.py:808
  362.4 10.1 %collective-permute-start.41 = (bf16[256,1536]{1,0:T(8,128)(2,1)S(1)}, bf16[256,1536]{1,0:T(8,128)(2,1)}, u32[]{:S(2)}, u32[]{:S(2)}) collective-permute-start(bf16[256,1536]{1,0:T(8,128)(2,1)S(1)} %broadcast_select_fusion.refs_1_), channel_id=1, source_target_pairs={{0,4},{4,0},{8,12},{12,8},{16,20},{20,16},{24,28},{28,24},{1,5},{5... | collective-permute-start | bytes 2359304 | tf_op jit(solution)/shard_map/ppermute | solution.py:800
  364.7 41.6 %collective-permute-start.44 = (bf16[256,1536]{1,0:T(8,128)(2,1)S(1)}, bf16[256,1536]{1,0:T(8,128)(2,1)S(1)}, u32[]{:S(2)}, u32[]{:S(2)}) collective-permute-start(bf16[256,1536]{1,0:T(8,128)(2,1)S(1)} %copy-done.3), channel_id=1, source_target_pairs={{1,2},{2,1},{5,6},{6,5},{9,10},{10,9},{13,14},{14,13},{17,18},{18,... | collective-permute-start | bytes 2359304 | tf_op jit(solution)/shard_map/ppermute | solution.py:812
  365.6 40.8 %collective-permute-start.43 = (bf16[256,1536]{1,0:T(8,128)(2,1)}, bf16[256,1536]{1,0:T(8,128)(2,1)S(1)}, u32[]{:S(2)}, u32[]{:S(2)}) collective-permute-start(bf16[256,1536]{1,0:T(8,128)(2,1)} %get-tuple-element.365), channel_id=1, source_target_pairs={{0,1},{1,0},{2,3},{3,2},{4,5},{5,4},{6,7},{7,6},{8,9},{9,8},{10,11... | collective-permute-start | bytes 2359304 | tf_op jit(solution)/shard_map/ppermute | solution.py:804
  370.6 35.8 %collective-permute-start.42 = (bf16[128,1536]{1,0:T(8,128)(2,1)S(1)}, bf16[128,1536]{1,0:T(8,128)(2,1)S(1)}, u32[]{:S(2)}, u32[]{:S(2)}) collective-permute-start(bf16[128,1536]{1,0:T(8,128)(2,1)S(1)} %slice.59), channel_id=1, source_target_pairs={{0,2},{2,0},{1,3},{3,1},{4,6},{6,4},{5,7},{7,5},{8,10},{10,8},{9,1... | collective-permute-start | bytes 1179656 | tf_op jit(solution)/shard_map/ppermute | solution.py:808
  381.2 25.2 %collective-permute-start.45 = (bf16[2,192,384]{2,1,0:T(8,128)(2,1)}, bf16[2,192,384]{2,1,0:T(8,128)(2,1)S(1)}, u32[]{:S(2)}, u32[]{:S(2)}) collective-permute-start(bf16[2,192,384]{2,1,0:T(8,128)(2,1)} %get-tuple-element.368), channel_id=1, source_target_pairs={{0,8},{4,12},{8,0},{12,4},{16,24},{20,28},{24,16},{28,20},{1,9},{5... | collective-permute-start | bytes 884744 | tf_op jit(solution)/shard_map/ppermute | solution.py:905
  382.7 23.7 %collective-permute-start.46 = (bf16[2,192,384]{2,1,0:T(8,128)(2,1)}, bf16[2,192,384]{2,1,0:T(8,128)(2,1)S(1)}, u32[]{:S(2)}, u32[]{:S(2)}) collective-permute-start(bf16[2,192,384]{2,1,0:T(8,128)(2,1)} %get-tuple-element.370), channel_id=1, source_target_pairs={{0,16},{4,20},{8,24},{12,28},{16,0},{20,4},{24,8},{28,12},{1,17},{... | collective-permute-start | bytes 884744 | tf_op jit(solution)/shard_map/ppermute | solution.py:905
  407.5 6.5 %collective-permute-start.47 = (bf16[4,128,1536]{2,1,0:T(8,128)(2,1)}, bf16[4,128,1536]{2,1,0:T(8,128)(2,1)S(1)}, u32[]{:S(2)}, u32[]{:S(2)}) collective-permute-start(bf16[4,128,1536]{2,1,0:T(8,128)(2,1)} %get-tuple-element.374), channel_id=1, source_target_pairs={{0,4},{4,0},{8,12},{12,8},{16,20},{20,16},{24,28},{28,24},{1,5},{5... | collective-permute-start | bytes 4718600 | tf_op jit(solution)/shard_map/ppermute | solution.py:800
  416.2 12.3 %collective-permute-start.50 = (bf16[128,1536]{1,0:T(8,128)(2,1)}, bf16[128,1536]{1,0:T(8,128)(2,1)}, u32[]{:S(2)}, u32[]{:S(2)}) collective-permute-start(bf16[128,1536]{1,0:T(8,128)(2,1)} %get-tuple-element.463), channel_id=1, source_target_pairs={{0,1},{1,0},{2,3},{3,2},{4,5},{5,4},{6,7},{7,6},{8,9},{9,8},{10,11... | collective-permute-start | bytes 1179656 | tf_op jit(solution)/shard_map/ppermute | solution.py:804
  418.6 22.1 %collective-permute-start.48 = (bf16[2,192,640]{2,1,0:T(8,128)(2,1)}, bf16[2,192,640]{2,1,0:T(8,128)(2,1)S(1)}, u32[]{:S(2)}, u32[]{:S(2)}) collective-permute-start(bf16[2,192,640]{2,1,0:T(8,128)(2,1)} %get-tuple-element.388), channel_id=1, source_target_pairs={{0,8},{4,12},{8,0},{12,4},{16,24},{20,28},{24,16},{28,20},{1,9},{5... | collective-permute-start | bytes 1474568 | tf_op jit(solution)/shard_map/ppermute | solution.py:905
  419.1 21.6 %collective-permute-start.49 = (bf16[2,192,640]{2,1,0:T(8,128)(2,1)}, bf16[2,192,640]{2,1,0:T(8,128)(2,1)S(1)}, u32[]{:S(2)}, u32[]{:S(2)}) collective-permute-start(bf16[2,192,640]{2,1,0:T(8,128)(2,1)} %get-tuple-element.390), channel_id=1, source_target_pairs={{0,16},{4,20},{8,24},{12,28},{16,0},{20,4},{24,8},{28,12},{1,17},{... | collective-permute-start | bytes 1474568 | tf_op jit(solution)/shard_map/ppermute | solution.py:905
  420.6 28.6 %collective-permute-start.55 = (bf16[128,1536]{1,0:T(8,128)(2,1)}, bf16[128,1536]{1,0:T(8,128)(2,1)S(1)}, u32[]{:S(2)}, u32[]{:S(2)}) collective-permute-start(bf16[128,1536]{1,0:T(8,128)(2,1)} %get-tuple-element.462), channel_id=1, source_target_pairs={{0,1},{1,0},{2,3},{3,2},{4,5},{5,4},{6,7},{7,6},{8,9},{9,8},{10,11... | collective-permute-start | bytes 1179656 | tf_op jit(solution)/shard_map/ppermute | solution.py:804
  420.9 19.8 %collective-permute-start.52 = (f32[3200]{0:T(1024)S(1)}, f32[3200]{0:T(1024)S(1)}, u32[]{:S(2)}, u32[]{:S(2)}) collective-permute-start(f32[3200]{0:T(1024)S(1)} %add.230), channel_id=1, source_target_pairs={{0,8},{4,12},{8,0},{12,4},{16,24},{20,28},{24,16},{28,20},{1,9},{5... | collective-permute-start | bytes 38408 | tf_op jit(solution)/shard_map/ppermute | solution.py:905
  430.5 27.3 %collective-permute-start.56 = (bf16[128,1536]{1,0:T(8,128)(2,1)}, bf16[128,1536]{1,0:T(8,128)(2,1)}, u32[]{:S(2)}, u32[]{:S(2)}) collective-permute-start(bf16[128,1536]{1,0:T(8,128)(2,1)} %fusion), channel_id=1, source_target_pairs={{0,2},{2,0},{1,3},{3,1},{4,6},{6,4},{5,7},{7,5},{8,10},{10,8},{9,1... | collective-permute-start | bytes 1179656 | tf_op jit(solution)/shard_map/ppermute | solution.py:808
  444.8 11.5 %collective-permute-start.53 = (bf16[192,640]{1,0:T(8,128)(2,1)}, bf16[192,640]{1,0:T(8,128)(2,1)}, u32[]{:S(2)}, u32[]{:S(2)}) collective-permute-start(bf16[192,640]{1,0:T(8,128)(2,1)} %get-tuple-element.403), channel_id=1, source_target_pairs={{0,16},{4,20},{8,24},{12,28},{16,0},{20,4},{24,8},{28,12},{1,17},{... | collective-permute-start | bytes 737288 | tf_op jit(solution)/shard_map/ppermute | solution.py:905
  446.3 11.5 %collective-permute-start.54 = (bf16[192,640]{1,0:T(8,128)(2,1)}, bf16[192,640]{1,0:T(8,128)(2,1)}, u32[]{:S(2)}, u32[]{:S(2)}) collective-permute-start(bf16[192,640]{1,0:T(8,128)(2,1)} %get-tuple-element.405), channel_id=1, source_target_pairs={{0,8},{4,12},{8,0},{12,4},{16,24},{20,28},{24,16},{28,20},{1,9},{5... | collective-permute-start | bytes 737288 | tf_op jit(solution)/shard_map/ppermute | solution.py:905
  448.9 11.1 %collective-permute-start.58 = (bf16[192,384]{1,0:T(8,128)(2,1)}, bf16[192,384]{1,0:T(8,128)(2,1)}, u32[]{:S(2)}, u32[]{:S(2)}) collective-permute-start(bf16[192,384]{1,0:T(8,128)(2,1)} %get-tuple-element.426), channel_id=1, source_target_pairs={{0,16},{4,20},{8,24},{12,28},{16,0},{20,4},{24,8},{28,12},{1,17},{... | collective-permute-start | bytes 442376 | tf_op jit(solution)/shard_map/ppermute | solution.py:905
  449.2 10.8 %collective-permute-start.59 = (bf16[192,384]{1,0:T(8,128)(2,1)}, bf16[192,384]{1,0:T(8,128)(2,1)}, u32[]{:S(2)}, u32[]{:S(2)}) collective-permute-start(bf16[192,384]{1,0:T(8,128)(2,1)} %get-tuple-element.428), channel_id=1, source_target_pairs={{0,8},{4,12},{8,0},{12,4},{16,24},{20,28},{24,16},{28,20},{1,9},{5... | collective-permute-start | bytes 442376 | tf_op jit(solution)/shard_map/ppermute | solution.py:905
  456.3 6.3 %collective-permute-start.63 = (f32[3200]{0:T(1024)S(1)}, f32[3200]{0:T(1024)}, u32[]{:S(2)}, u32[]{:S(2)}) collective-permute-start(f32[3200]{0:T(1024)S(1)} %add.231), channel_id=1, source_target_pairs={{0,16},{4,20},{8,24},{12,28},{16,0},{20,4},{24,8},{28,12},{1,17},{... | collective-permute-start | bytes 38408 | tf_op jit(solution)/shard_map/ppermute | solution.py:905
  460.0 9.4 %collective-permute-start.57 = (bf16[192,640]{1,0:T(8,128)(2,1)}, bf16[192,640]{1,0:T(8,128)(2,1)S(1)}, u32[]{:S(2)}, u32[]{:S(2)}) collective-permute-start(bf16[192,640]{1,0:T(8,128)(2,1)} %get-tuple-element.424), channel_id=1, source_target_pairs={{0,4},{4,0},{8,12},{12,8},{16,20},{20,16},{24,28},{28,24},{1,5},{5... | collective-permute-start | bytes 737288 | tf_op jit(solution)/shard_map/ppermute | solution.py:800
  462.1 7.3 %collective-permute-start.60 = (bf16[192,384]{1,0:T(8,128)(2,1)}, bf16[192,384]{1,0:T(8,128)(2,1)S(1)}, u32[]{:S(2)}, u32[]{:S(2)}) collective-permute-start(bf16[192,384]{1,0:T(8,128)(2,1)} %get-tuple-element.433), channel_id=1, source_target_pairs={{0,4},{4,0},{8,12},{12,8},{16,20},{20,16},{24,28},{28,24},{1,5},{5... | collective-permute-start | bytes 442376 | tf_op jit(solution)/shard_map/ppermute | solution.py:800
  463.2 3.7 collective-permute-start.64
  465.9 6.9 %collective-permute-start.62 = (bf16[128,1536]{1,0:T(8,128)(2,1)S(1)}, bf16[128,1536]{1,0:T(8,128)(2,1)S(1)}, u32[]{:S(2)}, u32[]{:S(2)}) collective-permute-start(bf16[128,1536]{1,0:T(8,128)(2,1)S(1)} %fusion.4), channel_id=1, source_target_pairs={{0,4},{4,0},{8,12},{12,8},{16,20},{20,16},{24,28},{28,24},{1,5},{5... | collective-permute-start | bytes 1179656 | tf_op jit(solution)/shard_map/ppermute | solution.py:800
  467.0 10.7 %collective-permute-start.65 = (f32[3200]{0:T(1024)S(1)}, f32[3200]{0:T(1024)S(1)}, u32[]{:S(2)}, u32[]{:S(2)}) collective-permute-start(f32[3200]{0:T(1024)S(1)} %add.249), channel_id=1, source_target_pairs={{0,2},{2,0},{1,3},{3,1},{4,6},{6,4},{5,7},{7,5},{8,10},{10,8},{9,1... | collective-permute-start | bytes 38408 | tf_op jit(solution)/shard_map/ppermute | solution.py:808
  470.3 19.2 %collective-permute-start.61 = (bf16[192,1024]{1,0:T(8,128)(2,1)}, bf16[192,1024]{1,0:T(8,128)(2,1)S(1)}, u32[]{:S(2)}, u32[]{:S(2)}) collective-permute-start(bf16[192,1024]{1,0:T(8,128)(2,1)} %pad_maximum_fusion.5), channel_id=1, source_target_pairs={{0,2},{2,0},{1,3},{3,1},{4,6},{6,4},{5,7},{7,5},{8,10},{10,8},{9,1... | collective-permute-start | bytes 1179656 | tf_op jit(solution)/shard_map/ppermute | solution.py:808
  (66 other events, 492.7 us)
Sparse Core Ops, SparseCore 0:
  76.1 91.9 all-gather.1
  340.5 98.7 reduce-scatter.1

commit v4 on v3

--- a/solution.py
+++ b/solution.py
@@ -557,15 +557,15 @@
 def pack_units_kernel(both_ref, down_ref, out_ref):
     columns = both_ref.shape[2]
     rows = both_ref.shape[1]
-    for i in range(out_ref.shape[1] // (3 * TILE)):
+    steps = out_ref.shape[1] // (3 * TILE)
+    for i in range(steps):
         first, last = i * TILE, min(columns, (i + 1) * TILE)
         parts = (both_ref[0, :, first:last], both_ref[1, :, first:last], down_ref[:, first:last])
-        for k, part in enumerate(parts):
+        for part, at_column in zip(parts, (2 * i * TILE, (2 * i + 1) * TILE, (2 * steps + i) * TILE)):
             if last - first < TILE:
                 part = jnp.concatenate(
                     [part, jnp.zeros((rows, TILE - (last - first)), f32)], axis=1
                 )
-            at_column = (3 * i + k) * TILE
             out_ref[:, at_column : at_column + TILE] = part.astype(bf16)
 
 
@@ -619,7 +619,8 @@
 
 
 def units_forward_kernel(count, pick, pick_ref, *refs):
-    row_refs, grad_refs, units_ref = refs[:count], refs[count : 2 * count], refs[2 * count]
+    row_refs, grad_refs = refs[:count], refs[count : 2 * count]
+    units_ref, down_ref = refs[2 * count : 2 * count + 2]
     rows_out, grads_out, hidden_ref, both_ref = refs[-4:]
 
     @pl.when(pl.program_id(0) == 0)
@@ -639,8 +640,8 @@
 
     rows = rows_out[...]
     gate_out = dot(rows, units_ref[:, :TILE], 1, 0)
-    up_out = dot(rows, units_ref[:, TILE : 2 * TILE], 1, 0)
-    grad_hidden = dot(grads_out[...], units_ref[:, 2 * TILE :], 1, 0)
+    up_out = dot(rows, units_ref[:, TILE:], 1, 0)
+    grad_hidden = dot(grads_out[...], down_ref[...], 1, 0)
     gate_sig = jax.nn.sigmoid(gate_out)
     gate_act = gate_out * gate_sig
     hidden_ref[...] = (gate_act * up_out).astype(bf16)
@@ -662,7 +663,10 @@
         grid=(steps,),
         in_specs=scalars(1)
         + [full] * (2 * count)
-        + [pl.BlockSpec((width, 3 * TILE), lambda i: (0, i))]
+        + [
+            pl.BlockSpec((width, 2 * TILE), lambda i: (0, i)),
+            pl.BlockSpec((width, TILE), lambda i: (0, 2 * steps + i)),
+        ]
         + [pl.BlockSpec(memory_space=pl.ANY)] * len(held),
         out_specs=(
             kept,
@@ -676,10 +680,10 @@
             jax.ShapeDtypeStruct((4 * length, steps * TILE), bf16),
             jax.ShapeDtypeStruct((4 * length, steps * 2 * TILE), bf16),
         ),
-        input_output_aliases={2 * count + 2 + k: k for k in range(len(held))},
+        input_output_aliases={2 * count + 3 + k: k for k in range(len(held))},
         compiler_params=pltpu.CompilerParams(vmem_limit_bytes=VMEM_LIMIT),
         cost_estimate=SMALL,
-    )(jnp.zeros((1,), jnp.int32) if pick is None else pick, *rows, *grads, units, *held)
+    )(jnp.zeros((1,), jnp.int32) if pick is None else pick, *rows, *grads, units, units, *held)
 
 
 def write_blocks(total, out_refs):
@@ -688,42 +692,20 @@
         ref[...] = total[k * rows : (k + 1) * rows].astype(bf16)
 
 
-def units_back_kernel(both_ref, units_ref, *out_refs):
-    total = None
-    for i in range(both_ref.shape[1] // (2 * TILE)):
-        term = dot(
-            both_ref[:, i * 2 * TILE : (i + 1) * 2 * TILE],
-            units_ref[:, i * 3 * TILE : (i * 3 + 2) * TILE],
-            1,
-            1,
-        )
-        total = term if total is None else total + term
-    write_blocks(total, out_refs)
-
-
-def units_down_kernel(hidden_ref, units_ref, *out_refs):
-    total = None
-    for i in range(hidden_ref.shape[1] // TILE):
-        term = dot(
-            hidden_ref[:, i * TILE : (i + 1) * TILE],
-            units_ref[:, (i * 3 + 2) * TILE : (i * 3 + 3) * TILE],
-            1,
-            1,
-        )
-        total = term if total is None else total + term
-    write_blocks(total, out_refs)
-
-
-def units_to_width(kernel, values, units, first, count):
+def units_to_width_kernel(values_ref, units_ref, *out_refs):
+    write_blocks(dot(values_ref[...], units_ref[...], 1, 1), out_refs)
+
+
+def units_to_width(values, units, part, first, count):
     width = units.shape[0]
     block, columns = values.shape[0] // 4, values.shape[1]
     length = block * count
     return pl.pallas_call(
-        kernel,
+        units_to_width_kernel,
         grid=(width // TILE,),
         in_specs=[
             pl.BlockSpec((length, columns), lambda i: (first // count, 0)),
-            pl.BlockSpec((TILE, units.shape[1]), lambda i: (i, 0)),
+            pl.BlockSpec((TILE, columns), lambda i: (i, part)),
         ],
         out_specs=(pl.BlockSpec((block, TILE), lambda i: (0, i)),) * count,
         out_shape=(jax.ShapeDtypeStruct((block, width), bf16),) * count,
@@ -1135,7 +1117,7 @@
     rows_middle = swap_middle(rows_own)
     buffers = units_forward((rows_near, rows_far), (grad_near, grad_far), units, buffers, 0)
     rows_all, grad_all, hidden_b, dboth = buffers
-    back_near, back_far = units_to_width(units_back_kernel, dboth, units, 0, 2)
+    back_near, back_far = units_to_width(dboth, units, 0, 0, 2)
     rows_ends, rows_middle, grad_ends, back_near, back_far, buffers = together(
         rows_ends, rows_middle, grad_ends, back_near, back_far, buffers
     )
@@ -1149,13 +1131,31 @@
         3,
         inner.astype(jnp.int32)[None],
     )
-    back_own, back_last = units_to_width(units_back_kernel, dboth, units, 2, 2)
-    from_near, from_far, back_last, back_own, rows_all, grad_all, hidden_b, dboth = together(
-        from_near, from_far, back_last, back_own, rows_all, grad_all, hidden_b, dboth
+    back_own, back_last = units_to_width(dboth, units, 0, 2, 2)
+    down_kept, down_given = units_gradient_parts(grad_all, hidden_b, core)
+    (
+        from_near,
+        from_far,
+        back_last,
+        back_own,
+        rows_all,
+        hidden_b,
+        dboth,
+        down_kept,
+        down_given,
+    ) = together(
+        from_near,
+        from_far,
+        back_last,
+        back_own,
+        rows_all,
+        hidden_b,
+        dboth,
+        down_kept,
+        down_given,
     )
     from_last = swap_opposite(back_last)
-    down_kept, down_given = units_gradient_parts(grad_all, hidden_b, core)
-    (down_last,) = units_to_width(units_down_kernel, hidden_b, units, 3, 1)
+    (down_last,) = units_to_width(hidden_b, units, 2, 3, 1)
     branch_ends = [from_ends(down_last[:half]), from_ends(down_last[half:])]
     both_kept, both_given = units_gradient_parts(rows_all, dboth, core)
     from_last, branch_ends, down_kept, down_given, both_kept, both_given, down_last = together(
@@ -1184,14 +1184,14 @@
     )
     grad_mid_first = owner_swap(grad_mid_b)
     units_sum = units_add(both_kept, swap_core(both_given), down_kept, swap_core(down_given))
-    down_near, down_far, down_own = units_to_width(units_down_kernel, hidden_b, units, 0, 3)
+    down_near, down_far, down_own = units_to_width(hidden_b, units, 2, 0, 3)
     down_far = add_low(down_far, jnp.concatenate(branch_ends, axis=0))
     grad_mid_first, units_sum, down_near, down_far, down_own = together(
         grad_mid_first, units_sum, down_near, down_far, down_own
     )
     units_sum = units_gradient(units_sum)
     grad_mid_second = guest_swap(grad_mid_first)
-    branch_far = swap_far(down_far[:half])
+    branch_far = swap_far(down_far[: 3 * half // 4])
     grad_mid_mine = jnp.where(own, grad_mid_b, grad_mid_first)
     grad_mid_other = swap_core(grad_mid_mine)
     grad_mid_second, grad_mid_mine, grad_mid_other, branch_far, down_far = together(
@@ -1200,12 +1200,12 @@
     grad_mid_next = jnp.where(own, grad_mid_first, grad_mid_second)
     grad_mid_parts = (grad_mid_mine, grad_mid_next, grad_mid_other, swap_core(grad_mid_next))
 
-    branch_far_rest = swap_far(down_far[half:])
-    branch_near = swap_near(down_near)
+    branch_far_rest = swap_far(down_far[3 * half // 4 :])
     branch_middle = swap_middle(down_last)
     grad_attended, row_dot, *out_pieces = attention_turn(
         place, pair, grad_mid_parts, w_heads, attended
     )
+    branch_near = swap_near(after(down_near, row_dot))
     out_parts = scatter_pairs_begin(tuple(out_pieces))
     grad_projected, part_mine, part_other, head_sums, gain_sums = attention_backward(
         core[None],
@@ -1261,7 +1261,7 @@
             grad_gain_ffn,
         ]
     )
-    gain_total = sum_dp(gain_total, 1, lax.axis_size("dp") // 2)
+    gain_total = sum_dp(gain_total, 1, 2)
     block_out = (
         middle
         + down_own.astype(f32)
@@ -1282,6 +1282,7 @@
         2 * units_sum.shape[1] // 3,
     )
     gain_total = after(gain_total, down_new)
+    gain_total = sum_dp(gain_total, 2, lax.axis_size("dp") // 2)
     gain_last = swap_dp(gain_total, lax.axis_size("dp") // 2)
     qkv_kept, qkv_given = scatter_pairs_end(core, after(qkv_parts, (down_new, far)))
     gain_total = gain_total + after(gain_last, qkv_kept)

time: 506 us -> 499 us (0.986)
  Pallas kernels: 211 us -> 204 us
    pallas_call x4, Pallas kernels: 44.2 us -> 38 us  [units_to_width(): pl.pallas_call(units_to_width_kernel, grid=(width // TILE,), in_specs=[pl...]
    ppermute x9, waiting for transfers between devices: 32.2 us -> 26.1 us  [swap_near(): return lax.ppermute(value, 'tensor', [(0, 1), (1, 0), (2, 3), (3, 2)])]
  transfers between devices with their start and end apart: 68 -> 68, of which waited for: 27 -> 29; matrix products, arithmetic and copies ran while one was open for 8% -> 8% of each run, Pallas kernels for 42% -> 42%
where the time goes in v4:
time: 499 us; the launch traced here: 492 us
  Pallas kernels  204 us (41%)
  waiting for transfers between devices  127 us (25%)
  starting transfers between devices  88.2 us (18%)
  other arithmetic  43.2 us (9%)
  between operations  15.1 us (3%)
  local copies, waits for them, and re-layouts  14.1 us (3%)
    ppermute x11, waiting for transfers between devices, swap_far(): return lax.ppermute(value, 'tensor', [(0, 2), (2, 0), (1, 3), (3, 1)])  59.9 us
    pallas_call x3, Pallas kernels, units_forward(): pl.pallas_call(functools.partial(units_forward_kernel, count, pick is not...  39.5 us
    pallas_call x4, Pallas kernels, units_to_width(): pl.pallas_call(units_to_width_kernel, grid=(width // TILE,), in_specs=[pl...  38 us
    pallas_call x2, Pallas kernels, units_gradient_parts(): pl.pallas_call(units_gradient_kernel, grid_spec=pltpu.PrefetchScalarGridS...  28.7 us
    ppermute x9, waiting for transfers between devices, swap_near(): return lax.ppermute(value, 'tensor', [(0, 1), (1, 0), (2, 3), (3, 2)])  26.1 us
    ppermute x11, starting transfers between devices, swap_far(): return lax.ppermute(value, 'tensor', [(0, 2), (2, 0), (1, 3), (3, 1)])  23.3 us
    pallas_call x1, Pallas kernels, attention_backward(): pl.pallas_call(attention_backward_kernel, grid=(1,), in_specs=scalars(1)...  23.2 us
    ppermute x18, starting transfers between devices, swap_dp(): return lax.ppermute(value, 'dp', [(i, i ^ mask) for i in range(count)])  19.1 us
  transfers between devices with their start and end apart: 68, of which 29 were waited for; matrix products, arithmetic and copies ran while one was open for 8% of the time, Pallas kernels for 42%

profile of v4, /device:TPU:0, one launch (start us, length us, event | category | flops | bytes accessed | tf_op | source)
XLA Modules:
  0.0 492.0 jit_solution(14068137602210610479)
XLA Ops:
  10.1 4.0 collective-permute-start
  15.9 2.1 collective-permute-done.3
  23.8 3.7 shard_map.314
  30.1 3.6 collective-permute-done.6
  41.5 1.9 fusion.12
  43.4 1.9 pad_maximum_fusion.2
  45.9 9.2 %collective-permute-done.7 = bf16[256,1536]{1,0:T(8,128)(2,1)S(1)} collective-permute-done((bf16[256,1536]{1,0:T(8,128)(2,1)}, bf16[256,1536]{1,0:T(8,128)(2,1)S(1)}, u32[]{:S(2)}, u32[]{:S(2)}) %collective-permute-start.7) | collective-permute-done | bytes 786464 | tf_op jit(solution)/shard_map/ppermute | solution.py:820
  55.0 3.2 collective-permute-done.10.refs_6_
  64.3 2.9 collective-permute-start.15
  67.2 6.9 %collective-permute-done.15 = bf16[64,1536]{1,0:T(8,128)(2,1)S(1)} collective-permute-done((bf16[64,1536]{1,0:T(8,128)(2,1)S(1)}, bf16[64,1536]{1,0:T(8,128)(2,1)S(1)}, u32[]{:S(2)}, u32[]{:S(2)}) %collective-permute-start.15) | collective-permute-done | bytes 196640 | tf_op jit(solution)/shard_map/ppermute | solution.py:790
  77.2 4.8 collective-permute-start.16
  86.8 14.7 %shard_map.315 = (bf16[1536,1024]{1,0:T(8,128)(2,1)}, bf16[1024,1536]{1,0:T(8,128)(2,1)}, f32[1024,640]{1,0:T(8,128)}, bf16[6,1024,64]{2,1,0:T(8,128)(2,1)}, bf1...) custom-call(s32[1]{0:T(128)} %bitcast.1.place_ref, ...), custom_call_target="tpu_custom_call" | custom-call | flops 1000 | bytes 1000 | tf_op jit(solution)/shard_map/pallas_call | solution.py:245
  101.5 5.8 %shard_map.316 = (bf16[4,128,1536]{2,1,0:T(8,128)(2,1)}, bf16[4,128,1536]{2,1,0:T(8,128)(2,1)}) custom-call(s32[1]{0:T(128)} %bitcast.core_ref, bf16[1024,384]{1,0:T(8,128)(2,1)} %get-tuple-element.265.attended_ref.refs_5_, bf16[1536,1024]{1,0:T(8,128)(2,1)} %get-tuple-element.266.weight_ref.refs_4_), custom_call_target="tpu_custom_call" | custom-call | flops 1000 | bytes 1000 | tf_op jit(solution)/shard_map/pallas_call | solution.py:260
  107.3 6.7 %collective-permute-done.17 = bf16[192,1536]{1,0:T(8,128)(2,1)} collective-permute-done((bf16[192,1536]{1,0:T(8,128)(2,1)}, bf16[192,1536]{1,0:T(8,128)(2,1)}, u32[]{:S(2)}, u32[]{:S(2)}) %collective-permute-start.17) | collective-permute-done | bytes 589856 | tf_op jit(solution)/shard_map/ppermute | solution.py:790
  116.0 2.0 pad_maximum_fusion.1.refs_3_
  118.5 2.2 fusion.7
  120.6 4.2 collective-permute-start.20
  124.9 9.8 %collective-permute-done.20 = bf16[128,1536]{1,0:T(8,128)(2,1)S(1)} collective-permute-done((bf16[128,1536]{1,0:T(8,128)(2,1)S(1)}, bf16[128,1536]{1,0:T(8,128)(2,1)S(1)}, u32[]{:S(2)}, u32[]{:S(2)}) %collective-permute-start.20) | collective-permute-done | bytes 393248 | tf_op jit(solution)/shard_map/ppermute | solution.py:786
  134.8 5.1 %collective-permute-start.22 = (bf16[128,1536]{1,0:T(8,128)(2,1)S(1)}, bf16[128,1536]{1,0:T(8,128)(2,1)S(1)}, u32[]{:S(2)}, u32[]{:S(2)}) collective-permute-start(bf16[128,1536]{1,0:T(8,128)(2,1)S(1)} %add_convert_fusion.4), channel_id=1, source_target_pairs={{0,2},{2,0},{1,3},{3,1},{4,6},{6,4},{5,7},{7,5},{8,10},{10,8},{9,1... | collective-permute-start | bytes 1179656 | tf_op jit(solution)/shard_map/ppermute | solution.py:790
  139.9 5.9 %collective-permute-done.23 = bf16[128,1536]{1,0:T(8,128)(2,1)S(1)} collective-permute-done((bf16[128,1536]{1,0:T(8,128)(2,1)S(1)}, bf16[128,1536]{1,0:T(8,128)(2,1)S(1)}, u32[]{:S(2)}, u32[]{:S(2)}) %collective-permute-start.23) | collective-permute-done | bytes 393248 | tf_op jit(solution)/shard_map/ppermute | solution.py:786
  145.8 11.7 %collective-permute-done.22 = bf16[128,1536]{1,0:T(8,128)(2,1)S(1)} collective-permute-done((bf16[128,1536]{1,0:T(8,128)(2,1)S(1)}, bf16[128,1536]{1,0:T(8,128)(2,1)S(1)}, u32[]{:S(2)}, u32[]{:S(2)}) %collective-permute-start.22) | collective-permute-done | bytes 393248 | tf_op jit(solution)/shard_map/ppermute | solution.py:790
  157.7 1.8 collective-permute-done.24
  161.4 1.9 collective-permute-start.26
  164.6 3.5 all-gather.2.cloned.1.call-done.refs_2_.refs_3_.refs_4_.refs_5_.units_ref
  168.1 11.7 %shard_map.317 = (bf16[1024,1536]{1,0:T(8,128)(2,1)}, bf16[1024,1536]{1,0:T(8,128)(2,1)}, bf16[1024,1792]{1,0:T(8,128)(2,1)}, bf16[1024,3584]{1,0:T(8,128)(2,1)}) custom-call(s32[1]{0:T(128)} %constant.122.clone.1.pick_ref, bf16[256,1536]{1,0:T(8,128)(2,1)} %copy-done.11, bf16[256,1536]{1,0:T(8,128)(2,1)} %copy-done.1, ...), custom_call_target="tpu_custom_call" | custom-call | flops 1000 | bytes 1000 | tf_op jit(solution)/shard_map/pallas_call | solution.py:661
  179.8 18.0 %collective-permute-done.25.refs_1_ = bf16[256,1536]{1,0:T(8,128)(2,1)} collective-permute-done((bf16[256,1536]{1,0:T(8,128)(2,1)S(1)}, bf16[256,1536]{1,0:T(8,128)(2,1)}, u32[]{:S(2)}, u32[]{:S(2)}) %collective-permute-start.25) | collective-permute-done | bytes 786464 | tf_op jit(solution)/shard_map/ppermute | solution.py:790
  200.8 15.4 %shard_map.318 = (bf16[1024,1536]{1,0:T(8,128)(2,1)}, bf16[1024,1536]{1,0:T(8,128)(2,1)}, bf16[1024,1792]{1,0:T(8,128)(2,1)}, bf16[1024,3584]{1,0:T(8,128)(2,1)}) custom-call(s32[1]{0:T(128)} %constant.122.clone.1.pick_ref, ...), custom_call_target="tpu_custom_call", output_to_operand_aliasing={{0}: (7, {}), {1}: (8, {}), {2}: (9, {}), {3}: (10, {})} | custom-call | flops 1000 | bytes 1000 | tf_op jit(solution)/shard_map/pallas_call | solution.py:661
  216.2 11.2 %shard_map.319 = (bf16[256,1536]{1,0:T(8,128)(2,1)}, bf16[256,1536]{1,0:T(8,128)(2,1)}) custom-call(bf16[1024,3584]{1,0:T(8,128)(2,1)} %get-tuple-element.313.values_ref.refs_9_, bf16[1536,5376]{1,0:T(8,128)(2,1)} %all-gather.2.cloned.1.call-done.refs_2_.refs_3_.refs_4_.refs_5_.units_ref), custom_call_target="tpu_custom_call" | custom-call | flops 1000 | bytes 1000 | tf_op jit(solution)/shard_map/pallas_call | solution.py:703
  227.4 4.3 collective-permute-done.27.refs_0_
  233.4 1.8 collective-permute-start.31
  235.3 12.4 %shard_map.320 = (bf16[1024,1536]{1,0:T(8,128)(2,1)}, bf16[1024,1536]{1,0:T(8,128)(2,1)}, bf16[1024,1792]{1,0:T(8,128)(2,1)}, bf16[1024,3584]{1,0:T(8,128)(2,1)}) custom-call(s32[1]{0:T(128)} %bitcast.17.pick_ref, bf16[256,1536]{1,0:T(8,128)(2,1)} %copy-done.31, ...), custom_call_target="tpu_custom_call", output_to_operand_aliasing={{0}: (7, {}), {1}: (8, {}), {2}: (9, {}), {3}: (10, {})} | custom-call | flops 1000 | bytes 1000 | tf_op jit(solution)/shard_map/pallas_call | solution.py:661
  247.7 11.3 %shard_map.322 = (bf16[4,192,1792]{2,1,0:T(8,128)(2,1)}, bf16[4,192,1792]{2,1,0:T(8,128)(2,1)}) custom-call(s32[1]{0:T(128)} %bitcast.core_ref, bf16[1024,1536]{1,0:T(8,128)(2,1)} %get-tuple-element.319.left_ref, bf16[1024,1792]{1,0:T(8,128)(2,1)} %get-tuple-element.343.right_ref.values_ref), custom_call_target="tpu_custom_call" | custom-call | flops 1000 | bytes 1000 | tf_op jit(solution)/shard_map/pallas_call | solution.py:762
  259.0 11.1 %shard_map.321 = (bf16[256,1536]{1,0:T(8,128)(2,1)}, bf16[256,1536]{1,0:T(8,128)(2,1)}) custom-call(bf16[1024,3584]{1,0:T(8,128)(2,1)} %get-tuple-element.330.values_ref.right_ref, bf16[1536,5376]{1,0:T(8,128)(2,1)} %all-gather.2.cloned.1.call-done.refs_2_.refs_3_.refs_4_.refs_5_.units_ref), custom_call_target="tpu_custom_call" | custom-call | flops 1000 | bytes 1000 | tf_op jit(solution)/shard_map/pallas_call | solution.py:703
  271.9 6.6 %shard_map.323 = bf16[256,1536]{1,0:T(8,128)(2,1)} custom-call(bf16[1024,1792]{1,0:T(8,128)(2,1)} %get-tuple-element.343.right_ref.values_ref, bf16[1536,5376]{1,0:T(8,128)(2,1)} %all-gather.2.cloned.1.call-done.refs_2_.refs_3_.refs_4_.refs_5_.units_ref), custom_call_target="tpu_custom_call" | custom-call | flops 1000 | bytes 1000 | tf_op jit(solution)/shard_map/pallas_call | solution.py:703
  278.5 1.9 fusion.19
  280.4 1.9 collective-permute-start.33
  283.8 17.4 %shard_map.324 = (bf16[4,192,3584]{2,1,0:T(8,128)(2,1)}, bf16[4,192,3584]{2,1,0:T(8,128)(2,1)}) custom-call(s32[1]{0:T(128)} %bitcast.core_ref, bf16[1024,1536]{1,0:T(8,128)(2,1)} %get-tuple-element.329.left_ref, bf16[1024,3584]{1,0:T(8,128)(2,1)} %get-tuple-element.330.values_ref.right_ref), custom_call_target="tpu_custom_call" | custom-call | flops 1000 | bytes 1000 | tf_op jit(solution)/shard_map/pallas_call | solution.py:762
  301.2 3.6 collective-permute-done.34
  306.3 2.0 fusion.18
  308.9 2.5 collective-permute-start.35
  311.4 9.0 %shard_map.326 = (bf16[256,1536]{1,0:T(8,128)(2,1)}, bf16[256,1536]{1,0:T(8,128)(2,1)}, bf16[256,1536]{1,0:T(8,128)(2,1)}) custom-call(bf16[1024,1792]{1,0:T(8,128)(2,1)} %get-tuple-element.343.right_ref.values_ref, bf16[1536,5376]{1,0:T(8,128)(2,1)} %all-gather.2.cloned.1.call-done.refs_2_.refs_3_.refs_4_.refs_5_.units_ref), custom_call_target="tpu_custom_call" | custom-call | flops 1000 | bytes 1000 | tf_op jit(solution)/shard_map/pallas_call | solution.py:703
  321.8 9.3 %shard_map.325 = bf16[4,192,5376]{2,1,0:T(8,128)(2,1)} custom-call(bf16[4,192,3584]{2,1,0:T(8,128)(2,1)} %get-tuple-element.339.refs_0_, bf16[4,192,3584]{2,1,0:T(8,128)(2,1)} %collective-permute-done.36.refs_1_, bf16[4,192,1792]{2,1,0:T(8,128)(2,1)} %get-tuple-element.341.refs_2_, bf16[4,192,1792]{2,1,0:T(8,128)(2,1)} %collective-permute-done.37.refs_3_), custom_call_target="tpu_custom_call" | custom-call | flops 1000 | bytes 1000 | tf_op jit(solution)/shard_map/pallas_call | solution.py:731
  333.3 4.3 collective-permute-start.40
  337.6 9.9 %collective-permute-done.40 = bf16[96,1536]{1,0:T(8,128)(2,1)S(1)} collective-permute-done((bf16[96,1536]{1,0:T(8,128)(2,1)S(1)}, bf16[96,1536]{1,0:T(8,128)(2,1)S(1)}, u32[]{:S(2)}, u32[]{:S(2)}) %collective-permute-start.40) | collective-permute-done | bytes 294944 | tf_op jit(solution)/shard_map/ppermute | solution.py:790
  348.5 4.8 collective-permute-start.41
  355.3 8.7 %shard_map.327 = (bf16[6,1024,64]{2,1,0:T(8,128)(2,1)}, f32[8,1024]{1,0:T(8,128)}, bf16[2,192,384]{2,1,0:T(8,128)(2,1)}, bf16[2,192,384]{2,1,0:T(8,128)(2,1)}, b...) custom-call(s32[1]{0:T(128)} %bitcast.1.place_ref, s32[2]{0:T(128)} %pad_add_fusion.pair_ref, ...), custom_call_target="tpu_custom_call" | custom-call | flops 1000 | bytes 1000 | tf_op jit(solution)/shard_map/pallas_call | solution.py:388
  364.0 4.4 collective-permute-start.43
  372.5 23.2 %shard_map.328 = (bf16[1024,640]{1,0:T(8,128)(2,1)}, bf16[4,128,1536]{2,1,0:T(8,128)(2,1)}, bf16[4,128,1536]{2,1,0:T(8,128)(2,1)}, f32[1,640]{1,0:T(1,128)}, f32[1,1536]{1,0:T(1,128)}) custom-call(s32[1]{0:T(128)} %bitcast.core_ref, bf16[6,1024,64]{2,1,0:T(8,128)(2,1)} %get-tuple-element.350.q_ref, bf16[2,1024,64]{2,1,0:T(8,128)(2,1)} %get-tuple-element.351.k_ref, ...), custom_call_target="tpu_custom_call" | custom-call | flops 1000 | bytes 1000 | tf_op jit(solution)/shard_map/pallas_call | solution.py:511
  395.8 3.9 collective-permute-done.42
  400.8 6.4 %shard_map.329 = (bf16[2,192,640]{2,1,0:T(8,128)(2,1)}, bf16[2,192,640]{2,1,0:T(8,128)(2,1)}, bf16[2,192,640]{2,1,0:T(8,128)(2,1)}, bf16[2,192,640]{2,1,0:T(8,128)(2,1)}) custom-call(s32[2]{0:T(128)} %pad_add_fusion.pair_ref, bf16[1024,1536]{1,0:T(8,128)(2,1)} %get-tuple-element.362.normed_ref.left_ref, bf16[1024,640]{1,0:T(8,128)(2,1)} %get-tuple-element.379.right_ref), custom_call_target="tpu_custom_call" | custom-call | flops 1000 | bytes 1000 | tf_op jit(solution)/shard_map/pallas_call | solution.py:304
  413.8 7.8 %collective-permute-done.50 = bf16[128,1536]{1,0:T(8,128)(2,1)} collective-permute-done((bf16[128,1536]{1,0:T(8,128)(2,1)}, bf16[128,1536]{1,0:T(8,128)(2,1)}, u32[]{:S(2)}, u32[]{:S(2)}) %collective-permute-start.50) | collective-permute-done | bytes 393248 | tf_op jit(solution)/shard_map/ppermute | solution.py:786
  421.6 2.0 fusion
  423.8 3.3 convert_add_fusion
  427.8 3.9 collective-permute-done.48.got_x
  431.7 2.5 shard_map.330
  436.3 2.1 shard_map.331
  438.4 5.3 %shard_map.332 = (f32[1,192,1728]{2,1,0:T(8,128)}, f32[1,192,1728]{2,1,0:T(8,128)}, f32[1,192,1728]{2,1,0:T(8,128)}) custom-call(f32[1,192,1728]{2,1,0:T(8,128)} %bitcast.73, f32[1,192,1728]{2,1,0:T(8,128)} %bitcast.74, f32[1,192,1728]{2,1,0:T(8,128)} %bitcast.75, bf16[192,5376]{1,0:T(8,128)(2,1)} %reduce-scatter.2.cloned.1.call-done.sum_ref), custom_call_target="tpu_custom_call" | custom-call | flops 1000 | bytes 1000 | tf_op jit(solution)/shard_map/pallas_call | solution.py:610
  450.3 2.2 shard_map.333
  453.0 1.9 shard_map.334
  459.9 2.4 collective-permute-start.65
  463.7 2.1 convert_select_fusion.2.kept_ref
  466.5 4.1 shard_map.335
  471.2 8.3 %shard_map.336 = (f32[2,192,1728]{2,1,0:T(8,128)}, f32[2,192,1728]{2,1,0:T(8,128)}, f32[2,192,1728]{2,1,0:T(8,128)}) custom-call(f32[2,192,1728]{2,1,0:T(8,128)} %weight_ref.1, f32[2,192,1728]{2,1,0:T(8,128)} %first_ref.1, f32[2,192,1728]{2,1,0:T(8,128)} %second_ref.1, bf16[192,5376]{1,0:T(8,128)(2,1)} %reduce-scatter.2.cloned.1.call-done.sum_ref), custom_call_target="tpu_custom_call" | custom-call | flops 1000 | bytes 1000 | tf_op jit(solution)/shard_map/pallas_call | solution.py:610
  479.6 2.8 collective-permute-done.60
  (301 shorter events, 89.8 us)
Async XLA Ops:
  7.2 160.9 %all-gather.2.cloned.1.call-start = ((), (), s32[]{:S(2)}) async-start(), calls=%async_computation.1 | async-start | bytes 18579456 | tf_op jit(solution)/shard_map/all_gather | solution.py:1083
  9.5 4.8 collective-permute-start.2
  10.0 19.5 %collective-permute-start.1 = (s32[1024]{0:T(1024)S(1)}, s32[1024]{0:T(1024)S(1)}, u32[]{:S(2)}, u32[]{:S(2)}) collective-permute-start(s32[1024]{0:T(1024)S(1)} %copy-done.54), channel_id=1, source_target_pairs={{0,4},{4,0},{8,12},{12,8},{16,20},{20,16},{24,28},{28,24},{1,5},{5... | collective-permute-start | bytes 12296 | tf_op jit(solution)/shard_map/ppermute | solution.py:782
  10.1 23.7 %collective-permute-start = (bf16[192,1024]{1,0:T(8,128)(2,1)S(1)}, bf16[192,1024]{1,0:T(8,128)(2,1)S(1)}, u32[]{:S(2)}, u32[]{:S(2)}) collective-permute-start(bf16[192,1024]{1,0:T(8,128)(2,1)S(1)} %pad_maximum_fusion.4), channel_id=1, source_target_pairs={{0,2},{2,0},{1,3},{3,1},{4,6},{6,4},{5,7},{7,5},{8,10},{10,8},{9,1... | collective-permute-start | bytes 1179656 | tf_op jit(solution)/shard_map/ppermute | solution.py:790
  21.7 7.3 %collective-permute-start.5 = (f32[8,1,100]{2,0,1:T(8,128)S(1)}, f32[8,1,100]{2,0,1:T(8,128)S(1)}, u32[]{:S(2)}, u32[]{:S(2)}) collective-permute-start(f32[8,1,100]{2,0,1:T(8,128)S(1)} %maximum_bitcast_fusion), channel_id=1, source_target_pairs={{0,1},{1,0},{2,3},{3,2},{4,5},{5,4},{6,7},{7,6},{8,9},{9,8},{10,11... | collective-permute-start | bytes 9608 | tf_op jit(solution)/shard_map/ppermute | solution.py:865
  29.1 4.6 collective-permute-start.6
  35.4 19.6 %collective-permute-start.7 = (bf16[256,1536]{1,0:T(8,128)(2,1)}, bf16[256,1536]{1,0:T(8,128)(2,1)S(1)}, u32[]{:S(2)}, u32[]{:S(2)}) collective-permute-start(bf16[256,1536]{1,0:T(8,128)(2,1)} %multiply_convert_fusion.1), channel_id=1, source_target_pairs={{0,1},{4,2},{1,0},{5,3},{6,7},{2,4},{7,6},{3,5},{8,9},{12,10},{9,8... | collective-permute-start | bytes 2359304 | tf_op jit(solution)/shard_map/ppermute | solution.py:820
  38.4 19.8 %collective-permute-start.10 = (bf16[384,1024]{1,0:T(8,128)(2,1)S(1)}, bf16[384,1024]{1,0:T(8,128)(2,1)S(1)}, u32[]{:S(2)}, u32[]{:S(2)}) collective-permute-start(bf16[384,1024]{1,0:T(8,128)(2,1)S(1)} %pad_maximum_fusion.refs_4_), channel_id=1, source_target_pairs={{0,16},{4,20},{8,24},{12,28},{16,0},{20,4},{24,8},{28,12},{1,17},{... | collective-permute-start | bytes 2359304 | tf_op jit(solution)/shard_map/ppermute | solution.py:887
  40.0 19.4 %collective-permute-start.9 = (bf16[384,1024]{1,0:T(8,128)(2,1)S(1)}, bf16[384,1024]{1,0:T(8,128)(2,1)S(1)}, u32[]{:S(2)}, u32[]{:S(2)}) collective-permute-start(bf16[384,1024]{1,0:T(8,128)(2,1)S(1)} %pad_maximum_fusion.refs_4_), channel_id=1, source_target_pairs={{0,8},{4,12},{8,0},{12,4},{16,24},{20,28},{24,16},{28,20},{1,9},{5... | collective-permute-start | bytes 2359304 | tf_op jit(solution)/shard_map/ppermute | solution.py:887
  60.5 13.7 %collective-permute-start.14 = (bf16[256,1536]{1,0:T(8,128)(2,1)S(1)}, bf16[256,1536]{1,0:T(8,128)(2,1)S(1)}, u32[]{:S(2)}, u32[]{:S(2)}) collective-permute-start(bf16[256,1536]{1,0:T(8,128)(2,1)S(1)} %broadcast_select_fusion.3.refs_0_), channel_id=1, source_target_pairs={{0,4},{4,0},{8,12},{12,8},{16,20},{20,16},{24,28},{28,24},{1,5},{5... | collective-permute-start | bytes 2359304 | tf_op jit(solution)/shard_map/ppermute | solution.py:782
  60.5 15.4 %collective-permute-start.13 = (bf16[256,1536]{1,0:T(8,128)(2,1)S(1)}, bf16[256,1536]{1,0:T(8,128)(2,1)}, u32[]{:S(2)}, u32[]{:S(2)}) collective-permute-start(bf16[256,1536]{1,0:T(8,128)(2,1)S(1)} %collective-permute-done.7), channel_id=1, source_target_pairs={{4,5},{5,4},{2,3},{3,2},{12,13},{13,12},{10,11},{11,10},{20,21},{2... | collective-permute-start | bytes 2359304 | tf_op jit(solution)/shard_map/ppermute | solution.py:829
  62.2 12.0 %collective-permute-start.11 = (bf16[192,1024]{1,0:T(8,128)(2,1)S(1)}, bf16[192,1024]{1,0:T(8,128)(2,1)S(1)}, u32[]{:S(2)}, u32[]{:S(2)}) collective-permute-start(bf16[192,1024]{1,0:T(8,128)(2,1)S(1)} %slice.52), channel_id=1, source_target_pairs={{0,8},{4,12},{8,0},{12,4},{16,24},{20,28},{24,16},{28,20},{1,9},{5... | collective-permute-start | bytes 1179656 | tf_op jit(solution)/shard_map/ppermute | solution.py:887
  63.7 10.5 %collective-permute-start.12 = (bf16[192,1024]{1,0:T(8,128)(2,1)S(1)}, bf16[192,1024]{1,0:T(8,128)(2,1)S(1)}, u32[]{:S(2)}, u32[]{:S(2)}) collective-permute-start(bf16[192,1024]{1,0:T(8,128)(2,1)S(1)} %slice.53), channel_id=1, source_target_pairs={{0,16},{4,20},{8,24},{12,28},{16,0},{20,4},{24,8},{28,12},{1,17},{... | collective-permute-start | bytes 1179656 | tf_op jit(solution)/shard_map/ppermute | solution.py:887
  64.3 9.8 %collective-permute-start.15 = (bf16[64,1536]{1,0:T(8,128)(2,1)S(1)}, bf16[64,1536]{1,0:T(8,128)(2,1)S(1)}, u32[]{:S(2)}, u32[]{:S(2)}) collective-permute-start(bf16[64,1536]{1,0:T(8,128)(2,1)S(1)} %slice.54), channel_id=1, source_target_pairs={{0,2},{2,0},{1,3},{3,1},{4,6},{6,4},{5,7},{7,5},{8,10},{10,8},{9,1... | collective-permute-start | bytes 589832 | tf_op jit(solution)/shard_map/ppermute | solution.py:790
  76.0 362.3 %reduce-scatter.2.cloned.1.call-start = ((), (), s32[]{:S(2)}) async-start(), calls=%async_computation.2 | async-start | bytes 10321920 | tf_op jit(solution)/shard_map/reduce_scatter | solution.py:959
  77.2 8.7 %collective-permute-start.16 = (bf16[256,1536]{1,0:T(8,128)(2,1)}, bf16[256,1536]{1,0:T(8,128)(2,1)S(1)}, u32[]{:S(2)}, u32[]{:S(2)}) collective-permute-start(bf16[256,1536]{1,0:T(8,128)(2,1)} %broadcast_select_fusion.2.refs_1_), channel_id=1, source_target_pairs={{0,4},{4,0},{8,12},{12,8},{16,20},{20,16},{24,28},{28,24},{1,5},{5... | collective-permute-start | bytes 2359304 | tf_op jit(solution)/shard_map/ppermute | solution.py:782
  82.1 32.6 %collective-permute-start.18 = (bf16[256,1536]{1,0:T(8,128)(2,1)S(1)}, bf16[256,1536]{1,0:T(8,128)(2,1)}, u32[]{:S(2)}, u32[]{:S(2)}) collective-permute-start(bf16[256,1536]{1,0:T(8,128)(2,1)S(1)} %convert_element_type.194.refs_1_), channel_id=1, source_target_pairs={{0,1},{1,0},{2,3},{3,2},{4,5},{5,4},{6,7},{7,6},{8,9},{9,8},{10,11... | collective-permute-start | bytes 2359304 | tf_op jit(solution)/shard_map/ppermute | solution.py:786
  84.6 29.3 %collective-permute-start.17 = (bf16[192,1536]{1,0:T(8,128)(2,1)}, bf16[192,1536]{1,0:T(8,128)(2,1)}, u32[]{:S(2)}, u32[]{:S(2)}) collective-permute-start(bf16[192,1536]{1,0:T(8,128)(2,1)} %slice.55), channel_id=1, source_target_pairs={{0,2},{2,0},{1,3},{3,1},{4,6},{6,4},{5,7},{7,5},{8,10},{10,8},{9,1... | collective-permute-start | bytes 1769480 | tf_op jit(solution)/shard_map/ppermute | solution.py:790
  114.7 3.8 collective-permute-start.19
  114.7 10.2 %collective-permute-start.21 = (bf16[256,1536]{1,0:T(8,128)(2,1)S(1)}, bf16[256,1536]{1,0:T(8,128)(2,1)S(1)}, u32[]{:S(2)}, u32[]{:S(2)}) collective-permute-start(bf16[256,1536]{1,0:T(8,128)(2,1)S(1)} %convert_element_type.194.refs_1_), channel_id=1, source_target_pairs={{1,2},{2,1},{5,6},{6,5},{9,10},{10,9},{13,14},{14,13},{17,18},{18,... | collective-permute-start | bytes 2359304 | tf_op jit(solution)/shard_map/ppermute | solution.py:794
  120.6 14.1 %collective-permute-start.20 = (bf16[128,1536]{1,0:T(8,128)(2,1)S(1)}, bf16[128,1536]{1,0:T(8,128)(2,1)S(1)}, u32[]{:S(2)}, u32[]{:S(2)}) collective-permute-start(bf16[128,1536]{1,0:T(8,128)(2,1)S(1)} %get-tuple-element.471), channel_id=1, source_target_pairs={{0,1},{1,0},{2,3},{3,2},{4,5},{5,4},{6,7},{7,6},{8,9},{9,8},{10,11... | collective-permute-start | bytes 1179656 | tf_op jit(solution)/shard_map/ppermute | solution.py:786
  124.8 20.9 %collective-permute-start.23 = (bf16[128,1536]{1,0:T(8,128)(2,1)S(1)}, bf16[128,1536]{1,0:T(8,128)(2,1)S(1)}, u32[]{:S(2)}, u32[]{:S(2)}) collective-permute-start(bf16[128,1536]{1,0:T(8,128)(2,1)S(1)} %get-tuple-element.468), channel_id=1, source_target_pairs={{0,1},{1,0},{2,3},{3,2},{4,5},{5,4},{6,7},{7,6},{8,9},{9,8},{10,11... | collective-permute-start | bytes 1179656 | tf_op jit(solution)/shard_map/ppermute | solution.py:786
  134.8 22.6 %collective-permute-start.22 = (bf16[128,1536]{1,0:T(8,128)(2,1)S(1)}, bf16[128,1536]{1,0:T(8,128)(2,1)S(1)}, u32[]{:S(2)}, u32[]{:S(2)}) collective-permute-start(bf16[128,1536]{1,0:T(8,128)(2,1)S(1)} %add_convert_fusion.4), channel_id=1, source_target_pairs={{0,2},{2,0},{1,3},{3,1},{4,6},{6,4},{5,7},{7,5},{8,10},{10,8},{9,1... | collective-permute-start | bytes 1179656 | tf_op jit(solution)/shard_map/ppermute | solution.py:790
  161.2 36.6 %collective-permute-start.25 = (bf16[256,1536]{1,0:T(8,128)(2,1)S(1)}, bf16[256,1536]{1,0:T(8,128)(2,1)}, u32[]{:S(2)}, u32[]{:S(2)}) collective-permute-start(bf16[256,1536]{1,0:T(8,128)(2,1)S(1)} %multiply_convert_fusion.refs_0_), channel_id=1, source_target_pairs={{0,2},{2,0},{1,3},{3,1},{4,6},{6,4},{5,7},{7,5},{8,10},{10,8},{9,1... | collective-permute-start | bytes 2359304 | tf_op jit(solution)/shard_map/ppermute | solution.py:790
  161.4 37.3 %collective-permute-start.26 = (bf16[256,1536]{1,0:T(8,128)(2,1)S(1)}, bf16[256,1536]{1,0:T(8,128)(2,1)}, u32[]{:S(2)}, u32[]{:S(2)}) collective-permute-start(bf16[256,1536]{1,0:T(8,128)(2,1)S(1)} %multiply_convert_fusion.refs_0_), channel_id=1, source_target_pairs={{0,1},{1,0},{2,3},{3,2},{4,5},{5,4},{6,7},{7,6},{8,9},{9,8},{10,11... | collective-permute-start | bytes 2359304 | tf_op jit(solution)/shard_map/ppermute | solution.py:786
  163.3 64.0 %collective-permute-start.29 = (bf16[256,1536]{1,0:T(8,128)(2,1)S(1)}, bf16[256,1536]{1,0:T(8,128)(2,1)}, u32[]{:S(2)}, u32[]{:S(2)}) collective-permute-start(bf16[256,1536]{1,0:T(8,128)(2,1)S(1)} %copy-done.10), channel_id=1, source_target_pairs={{1,0},{2,3},{5,4},{6,7},{9,8},{10,11},{13,12},{14,15},{17,16},{18,... | collective-permute-start | bytes 2359304 | tf_op jit(solution)/shard_map/ppermute | solution.py:802
  198.8 32.9 %collective-permute-start.27 = (bf16[256,1536]{1,0:T(8,128)(2,1)}, bf16[256,1536]{1,0:T(8,128)(2,1)S(1)}, u32[]{:S(2)}, u32[]{:S(2)}) collective-permute-start(bf16[256,1536]{1,0:T(8,128)(2,1)} %collective-permute-done.25.refs_1_), channel_id=1, source_target_pairs={{1,0},{2,3},{5,4},{6,7},{9,8},{10,11},{13,12},{14,15},{17,16},{18,... | collective-permute-start | bytes 2359304 | tf_op jit(solution)/shard_map/ppermute | solution.py:802
  200.0 31.6 %collective-permute-start.28 = (bf16[256,1536]{1,0:T(8,128)(2,1)}, bf16[256,1536]{1,0:T(8,128)(2,1)S(1)}, u32[]{:S(2)}, u32[]{:S(2)}) collective-permute-start(bf16[256,1536]{1,0:T(8,128)(2,1)} %copy-done.11), channel_id=1, source_target_pairs={{1,2},{2,1},{5,6},{6,5},{9,10},{10,9},{13,14},{14,13},{17,18},{18,... | collective-permute-start | bytes 2359304 | tf_op jit(solution)/shard_map/ppermute | solution.py:794
  232.5 37.6 %collective-permute-start.30 = (bf16[256,1536]{1,0:T(8,128)(2,1)}, bf16[256,1536]{1,0:T(8,128)(2,1)S(1)}, u32[]{:S(2)}, u32[]{:S(2)}) collective-permute-start(bf16[256,1536]{1,0:T(8,128)(2,1)} %get-tuple-element.304), channel_id=1, source_target_pairs={{0,1},{1,0},{2,3},{3,2},{4,5},{5,4},{6,7},{7,6},{8,9},{9,8},{10,11... | collective-permute-start | bytes 2359304 | tf_op jit(solution)/shard_map/ppermute | solution.py:786
  233.4 36.7 %collective-permute-start.31 = (bf16[256,1536]{1,0:T(8,128)(2,1)}, bf16[256,1536]{1,0:T(8,128)(2,1)S(1)}, u32[]{:S(2)}, u32[]{:S(2)}) collective-permute-start(bf16[256,1536]{1,0:T(8,128)(2,1)} %get-tuple-element.305), channel_id=1, source_target_pairs={{0,2},{2,0},{1,3},{3,1},{4,6},{6,4},{5,7},{7,5},{8,10},{10,8},{9,1... | collective-permute-start | bytes 2359304 | tf_op jit(solution)/shard_map/ppermute | solution.py:790
  270.1 34.7 %collective-permute-start.32 = (bf16[256,1536]{1,0:T(8,128)(2,1)}, bf16[256,1536]{1,0:T(8,128)(2,1)S(1)}, u32[]{:S(2)}, u32[]{:S(2)}) collective-permute-start(bf16[256,1536]{1,0:T(8,128)(2,1)} %get-tuple-element.325), channel_id=1, source_target_pairs={{0,3},{1,2},{2,1},{3,0},{4,7},{5,6},{6,5},{7,4},{8,11},{9,10},{10,... | collective-permute-start | bytes 2359304 | tf_op jit(solution)/shard_map/ppermute | solution.py:798
  280.4 20.8 %collective-permute-start.33 = (bf16[128,1536]{1,0:T(8,128)(2,1)}, bf16[128,1536]{1,0:T(8,128)(2,1)S(1)}, u32[]{:S(2)}, u32[]{:S(2)}) collective-permute-start(bf16[128,1536]{1,0:T(8,128)(2,1)} %get-tuple-element.477), channel_id=1, source_target_pairs={{0,1},{3,2},{4,5},{7,6},{8,9},{11,10},{12,13},{15,14},{16,17},{19,... | collective-permute-start | bytes 1179656 | tf_op jit(solution)/shard_map/ppermute | solution.py:806
  282.3 22.5 %collective-permute-start.34 = (bf16[128,1536]{1,0:T(8,128)(2,1)S(1)}, bf16[128,1536]{1,0:T(8,128)(2,1)S(1)}, u32[]{:S(2)}, u32[]{:S(2)}) collective-permute-start(bf16[128,1536]{1,0:T(8,128)(2,1)S(1)} %get-tuple-element.476), channel_id=1, source_target_pairs={{0,1},{3,2},{4,5},{7,6},{8,9},{11,10},{12,13},{15,14},{16,17},{19,... | collective-permute-start | bytes 1179656 | tf_op jit(solution)/shard_map/ppermute | solution.py:806
  308.4 13.4 %collective-permute-start.36 = (bf16[4,192,3584]{2,1,0:T(8,128)(2,1)}, bf16[4,192,3584]{2,1,0:T(8,128)(2,1)}, u32[]{:S(2)}, u32[]{:S(2)}) collective-permute-start(bf16[4,192,3584]{2,1,0:T(8,128)(2,1)} %get-tuple-element.340), channel_id=1, source_target_pairs={{0,4},{4,0},{8,12},{12,8},{16,20},{20,16},{24,28},{28,24},{1,5},{5... | collective-permute-start | bytes 16515080 | tf_op jit(solution)/shard_map/ppermute | solution.py:782
  308.4 13.4 %collective-permute-start.37 = (bf16[4,192,1792]{2,1,0:T(8,128)(2,1)}, bf16[4,192,1792]{2,1,0:T(8,128)(2,1)}, u32[]{:S(2)}, u32[]{:S(2)}) collective-permute-start(bf16[4,192,1792]{2,1,0:T(8,128)(2,1)} %get-tuple-element.342), channel_id=1, source_target_pairs={{0,4},{4,0},{8,12},{12,8},{16,20},{20,16},{24,28},{28,24},{1,5},{5... | collective-permute-start | bytes 8257544 | tf_op jit(solution)/shard_map/ppermute | solution.py:782
  308.9 22.2 %collective-permute-start.35 = (bf16[256,1536]{1,0:T(8,128)(2,1)S(1)}, bf16[256,1536]{1,0:T(8,128)(2,1)S(1)}, u32[]{:S(2)}, u32[]{:S(2)}) collective-permute-start(bf16[256,1536]{1,0:T(8,128)(2,1)S(1)} %get-tuple-element.338), channel_id=1, source_target_pairs={{0,1},{4,2},{1,0},{5,3},{6,7},{2,4},{7,6},{3,5},{8,9},{12,10},{9,8... | collective-permute-start | bytes 2359304 | tf_op jit(solution)/shard_map/ppermute | solution.py:820
  332.4 15.1 %collective-permute-start.39 = (bf16[256,1536]{1,0:T(8,128)(2,1)S(1)}, bf16[256,1536]{1,0:T(8,128)(2,1)S(1)}, u32[]{:S(2)}, u32[]{:S(2)}) collective-permute-start(bf16[256,1536]{1,0:T(8,128)(2,1)S(1)} %broadcast_select_fusion.1.refs_0_), channel_id=1, source_target_pairs={{0,4},{4,0},{8,12},{12,8},{16,20},{20,16},{24,28},{28,24},{1,5},{5... | collective-permute-start | bytes 2359304 | tf_op jit(solution)/shard_map/ppermute | solution.py:782
  332.5 16.0 %collective-permute-start.38 = (bf16[256,1536]{1,0:T(8,128)(2,1)S(1)}, bf16[256,1536]{1,0:T(8,128)(2,1)S(1)}, u32[]{:S(2)}, u32[]{:S(2)}) collective-permute-start(bf16[256,1536]{1,0:T(8,128)(2,1)S(1)} %collective-permute-done.35), channel_id=1, source_target_pairs={{4,5},{5,4},{2,3},{3,2},{12,13},{13,12},{10,11},{11,10},{20,21},{2... | collective-permute-start | bytes 2359304 | tf_op jit(solution)/shard_map/ppermute | solution.py:829
  333.3 14.2 %collective-permute-start.40 = (bf16[96,1536]{1,0:T(8,128)(2,1)S(1)}, bf16[96,1536]{1,0:T(8,128)(2,1)S(1)}, u32[]{:S(2)}, u32[]{:S(2)}) collective-permute-start(bf16[96,1536]{1,0:T(8,128)(2,1)S(1)} %slice.58), channel_id=1, source_target_pairs={{0,2},{2,0},{1,3},{3,1},{4,6},{6,4},{5,7},{7,5},{8,10},{10,8},{9,1... | collective-permute-start | bytes 884744 | tf_op jit(solution)/shard_map/ppermute | solution.py:790
  348.5 6.8 %collective-permute-start.41 = (bf16[256,1536]{1,0:T(8,128)(2,1)S(1)}, bf16[256,1536]{1,0:T(8,128)(2,1)}, u32[]{:S(2)}, u32[]{:S(2)}) collective-permute-start(bf16[256,1536]{1,0:T(8,128)(2,1)S(1)} %broadcast_select_fusion.refs_1_), channel_id=1, source_target_pairs={{0,4},{4,0},{8,12},{12,8},{16,20},{20,16},{24,28},{28,24},{1,5},{5... | collective-permute-start | bytes 2359304 | tf_op jit(solution)/shard_map/ppermute | solution.py:782
  353.9 41.9 %collective-permute-start.44 = (bf16[256,1536]{1,0:T(8,128)(2,1)S(1)}, bf16[256,1536]{1,0:T(8,128)(2,1)S(1)}, u32[]{:S(2)}, u32[]{:S(2)}) collective-permute-start(bf16[256,1536]{1,0:T(8,128)(2,1)S(1)} %copy-done.3), channel_id=1, source_target_pairs={{1,2},{2,1},{5,6},{6,5},{9,10},{10,9},{13,14},{14,13},{17,18},{18,... | collective-permute-start | bytes 2359304 | tf_op jit(solution)/shard_map/ppermute | solution.py:794
  364.0 35.7 %collective-permute-start.43 = (bf16[256,1536]{1,0:T(8,128)(2,1)}, bf16[256,1536]{1,0:T(8,128)(2,1)S(1)}, u32[]{:S(2)}, u32[]{:S(2)}) collective-permute-start(bf16[256,1536]{1,0:T(8,128)(2,1)} %get-tuple-element.369), channel_id=1, source_target_pairs={{0,1},{1,0},{2,3},{3,2},{4,5},{5,4},{6,7},{7,6},{8,9},{9,8},{10,11... | collective-permute-start | bytes 2359304 | tf_op jit(solution)/shard_map/ppermute | solution.py:786
  369.2 30.5 %collective-permute-start.42 = (bf16[160,1536]{1,0:T(8,128)(2,1)}, bf16[160,1536]{1,0:T(8,128)(2,1)S(1)}, u32[]{:S(2)}, u32[]{:S(2)}) collective-permute-start(bf16[160,1536]{1,0:T(8,128)(2,1)} %slice.59), channel_id=1, source_target_pairs={{0,2},{2,0},{1,3},{3,1},{4,6},{6,4},{5,7},{7,5},{8,10},{10,8},{9,1... | collective-permute-start | bytes 1474568 | tf_op jit(solution)/shard_map/ppermute | solution.py:790
  370.5 29.2 %collective-permute-start.45 = (bf16[2,192,384]{2,1,0:T(8,128)(2,1)}, bf16[2,192,384]{2,1,0:T(8,128)(2,1)S(1)}, u32[]{:S(2)}, u32[]{:S(2)}) collective-permute-start(bf16[2,192,384]{2,1,0:T(8,128)(2,1)} %get-tuple-element.372), channel_id=1, source_target_pairs={{0,8},{4,12},{8,0},{12,4},{16,24},{20,28},{24,16},{28,20},{1,9},{5... | collective-permute-start | bytes 884744 | tf_op jit(solution)/shard_map/ppermute | solution.py:887
  372.0 27.7 %collective-permute-start.46 = (bf16[2,192,384]{2,1,0:T(8,128)(2,1)}, bf16[2,192,384]{2,1,0:T(8,128)(2,1)S(1)}, u32[]{:S(2)}, u32[]{:S(2)}) collective-permute-start(bf16[2,192,384]{2,1,0:T(8,128)(2,1)} %get-tuple-element.374), channel_id=1, source_target_pairs={{0,16},{4,20},{8,24},{12,28},{16,0},{20,4},{24,8},{28,12},{1,17},{... | collective-permute-start | bytes 884744 | tf_op jit(solution)/shard_map/ppermute | solution.py:887
  400.8 6.4 %collective-permute-start.47 = (bf16[4,128,1536]{2,1,0:T(8,128)(2,1)}, bf16[4,128,1536]{2,1,0:T(8,128)(2,1)S(1)}, u32[]{:S(2)}, u32[]{:S(2)}) collective-permute-start(bf16[4,128,1536]{2,1,0:T(8,128)(2,1)} %get-tuple-element.378), channel_id=1, source_target_pairs={{0,4},{4,0},{8,12},{12,8},{16,20},{20,16},{24,28},{28,24},{1,5},{5... | collective-permute-start | bytes 4718600 | tf_op jit(solution)/shard_map/ppermute | solution.py:782
  409.4 12.2 %collective-permute-start.50 = (bf16[128,1536]{1,0:T(8,128)(2,1)}, bf16[128,1536]{1,0:T(8,128)(2,1)}, u32[]{:S(2)}, u32[]{:S(2)}) collective-permute-start(bf16[128,1536]{1,0:T(8,128)(2,1)} %get-tuple-element.467), channel_id=1, source_target_pairs={{0,1},{1,0},{2,3},{3,2},{4,5},{5,4},{6,7},{7,6},{8,9},{9,8},{10,11... | collective-permute-start | bytes 1179656 | tf_op jit(solution)/shard_map/ppermute | solution.py:786
  409.9 21.9 %collective-permute-start.48 = (bf16[2,192,640]{2,1,0:T(8,128)(2,1)}, bf16[2,192,640]{2,1,0:T(8,128)(2,1)}, u32[]{:S(2)}, u32[]{:S(2)}) collective-permute-start(bf16[2,192,640]{2,1,0:T(8,128)(2,1)} %get-tuple-element.392), channel_id=1, source_target_pairs={{0,8},{4,12},{8,0},{12,4},{16,24},{20,28},{24,16},{28,20},{1,9},{5... | collective-permute-start | bytes 1474568 | tf_op jit(solution)/shard_map/ppermute | solution.py:887
  411.3 20.4 %collective-permute-start.49 = (bf16[2,192,640]{2,1,0:T(8,128)(2,1)}, bf16[2,192,640]{2,1,0:T(8,128)(2,1)}, u32[]{:S(2)}, u32[]{:S(2)}) collective-permute-start(bf16[2,192,640]{2,1,0:T(8,128)(2,1)} %get-tuple-element.394), channel_id=1, source_target_pairs={{0,16},{4,20},{8,24},{12,28},{16,0},{20,4},{24,8},{28,12},{1,17},{... | collective-permute-start | bytes 1474568 | tf_op jit(solution)/shard_map/ppermute | solution.py:887
  412.1 15.0 %collective-permute-start.51 = (f32[3200]{0:T(1024)S(1)}, f32[3200]{0:T(1024)S(1)}, u32[]{:S(2)}, u32[]{:S(2)}) collective-permute-start(f32[3200]{0:T(1024)S(1)} %concatenate.66), channel_id=1, source_target_pairs={{0,4},{4,0},{8,12},{12,8},{16,20},{20,16},{24,28},{28,24},{1,5},{5... | collective-permute-start | bytes 38408 | tf_op jit(solution)/shard_map/ppermute | solution.py:887
  412.2 26.2 %collective-permute-start.54 = (bf16[128,1536]{1,0:T(8,128)(2,1)}, bf16[128,1536]{1,0:T(8,128)(2,1)S(1)}, u32[]{:S(2)}, u32[]{:S(2)}) collective-permute-start(bf16[128,1536]{1,0:T(8,128)(2,1)} %get-tuple-element.466), channel_id=1, source_target_pairs={{0,1},{1,0},{2,3},{3,2},{4,5},{5,4},{6,7},{7,6},{8,9},{9,8},{10,11... | collective-permute-start | bytes 1179656 | tf_op jit(solution)/shard_map/ppermute | solution.py:786
  423.6 26.7 %collective-permute-start.55 = (bf16[128,1536]{1,0:T(8,128)(2,1)}, bf16[128,1536]{1,0:T(8,128)(2,1)}, u32[]{:S(2)}, u32[]{:S(2)}) collective-permute-start(bf16[128,1536]{1,0:T(8,128)(2,1)} %fusion), channel_id=1, source_target_pairs={{0,2},{2,0},{1,3},{3,1},{4,6},{6,4},{5,7},{7,5},{8,10},{10,8},{9,1... | collective-permute-start | bytes 1179656 | tf_op jit(solution)/shard_map/ppermute | solution.py:790
  434.2 15.5 %collective-permute-start.52 = (bf16[192,640]{1,0:T(8,128)(2,1)}, bf16[192,640]{1,0:T(8,128)(2,1)}, u32[]{:S(2)}, u32[]{:S(2)}) collective-permute-start(bf16[192,640]{1,0:T(8,128)(2,1)} %get-tuple-element.407), channel_id=1, source_target_pairs={{0,16},{4,20},{8,24},{12,28},{16,0},{20,4},{24,8},{28,12},{1,17},{... | collective-permute-start | bytes 737288 | tf_op jit(solution)/shard_map/ppermute | solution.py:887
  435.7 14.6 %collective-permute-start.53 = (bf16[192,640]{1,0:T(8,128)(2,1)}, bf16[192,640]{1,0:T(8,128)(2,1)}, u32[]{:S(2)}, u32[]{:S(2)}) collective-permute-start(bf16[192,640]{1,0:T(8,128)(2,1)} %get-tuple-element.409), channel_id=1, source_target_pairs={{0,8},{4,12},{8,0},{12,4},{16,24},{20,28},{24,16},{28,20},{1,9},{5... | collective-permute-start | bytes 737288 | tf_op jit(solution)/shard_map/ppermute | solution.py:887
  443.7 3.8 collective-permute-start.62
  445.2 7.2 %collective-permute-start.57 = (bf16[192,384]{1,0:T(8,128)(2,1)}, bf16[192,384]{1,0:T(8,128)(2,1)}, u32[]{:S(2)}, u32[]{:S(2)}) collective-permute-start(bf16[192,384]{1,0:T(8,128)(2,1)} %get-tuple-element.430), channel_id=1, source_target_pairs={{0,16},{4,20},{8,24},{12,28},{16,0},{20,4},{24,8},{28,12},{1,17},{... | collective-permute-start | bytes 442376 | tf_op jit(solution)/shard_map/ppermute | solution.py:887
  447.5 5.5 %collective-permute-start.58 = (bf16[192,384]{1,0:T(8,128)(2,1)}, bf16[192,384]{1,0:T(8,128)(2,1)}, u32[]{:S(2)}, u32[]{:S(2)}) collective-permute-start(bf16[192,384]{1,0:T(8,128)(2,1)} %get-tuple-element.432), channel_id=1, source_target_pairs={{0,8},{4,12},{8,0},{12,4},{16,24},{20,28},{24,16},{28,20},{1,9},{5... | collective-permute-start | bytes 442376 | tf_op jit(solution)/shard_map/ppermute | solution.py:887
  449.7 5.7 %collective-permute-start.63 = (f32[3200]{0:T(1024)S(1)}, f32[3200]{0:T(1024)}, u32[]{:S(2)}, u32[]{:S(2)}) collective-permute-start(f32[3200]{0:T(1024)S(1)} %add.247), channel_id=1, source_target_pairs={{0,16},{4,20},{8,24},{12,28},{16,0},{20,4},{24,8},{28,12},{1,17},{... | collective-permute-start | bytes 38408 | tf_op jit(solution)/shard_map/ppermute | solution.py:887
  453.0 9.3 %collective-permute-start.56 = (bf16[192,640]{1,0:T(8,128)(2,1)}, bf16[192,640]{1,0:T(8,128)(2,1)S(1)}, u32[]{:S(2)}, u32[]{:S(2)}) collective-permute-start(bf16[192,640]{1,0:T(8,128)(2,1)} %get-tuple-element.428), channel_id=1, source_target_pairs={{0,4},{4,0},{8,12},{12,8},{16,20},{20,16},{24,28},{28,24},{1,5},{5... | collective-permute-start | bytes 737288 | tf_op jit(solution)/shard_map/ppermute | solution.py:782
  454.9 7.4 %collective-permute-start.59 = (bf16[192,384]{1,0:T(8,128)(2,1)}, bf16[192,384]{1,0:T(8,128)(2,1)S(1)}, u32[]{:S(2)}, u32[]{:S(2)}) collective-permute-start(bf16[192,384]{1,0:T(8,128)(2,1)} %get-tuple-element.437), channel_id=1, source_target_pairs={{0,4},{4,0},{8,12},{12,8},{16,20},{20,16},{24,28},{28,24},{1,5},{5... | collective-permute-start | bytes 442376 | tf_op jit(solution)/shard_map/ppermute | solution.py:782
  456.1 3.7 collective-permute-start.64
  458.8 6.9 %collective-permute-start.61 = (bf16[128,1536]{1,0:T(8,128)(2,1)S(1)}, bf16[128,1536]{1,0:T(8,128)(2,1)S(1)}, u32[]{:S(2)}, u32[]{:S(2)}) collective-permute-start(bf16[128,1536]{1,0:T(8,128)(2,1)S(1)} %fusion.4), channel_id=1, source_target_pairs={{0,4},{4,0},{8,12},{12,8},{16,20},{20,16},{24,28},{28,24},{1,5},{5... | collective-permute-start | bytes 1179656 | tf_op jit(solution)/shard_map/ppermute | solution.py:782
  459.9 10.7 %collective-permute-start.65 = (f32[3200]{0:T(1024)S(1)}, f32[3200]{0:T(1024)S(1)}, u32[]{:S(2)}, u32[]{:S(2)}) collective-permute-start(f32[3200]{0:T(1024)S(1)} %add.249), channel_id=1, source_target_pairs={{0,2},{2,0},{1,3},{3,1},{4,6},{6,4},{5,7},{7,5},{8,10},{10,8},{9,1... | collective-permute-start | bytes 38408 | tf_op jit(solution)/shard_map/ppermute | solution.py:790
  463.2 19.2 %collective-permute-start.60 = (bf16[192,1024]{1,0:T(8,128)(2,1)}, bf16[192,1024]{1,0:T(8,128)(2,1)S(1)}, u32[]{:S(2)}, u32[]{:S(2)}) collective-permute-start(bf16[192,1024]{1,0:T(8,128)(2,1)} %pad_maximum_fusion.5), channel_id=1, source_target_pairs={{0,2},{2,0},{1,3},{3,1},{4,6},{6,4},{5,7},{7,5},{8,10},{10,8},{9,1... | collective-permute-start | bytes 1179656 | tf_op jit(solution)/shard_map/ppermute | solution.py:790
  (66 other events, 546.5 us)
Sparse Core Ops, SparseCore 0:
  76.1 91.9 all-gather.1
  331.3 99.4 reduce-scatter.1

commit v5 on v4

--- a/solution.py
+++ b/solution.py
@@ -696,7 +696,8 @@
     write_blocks(dot(values_ref[...], units_ref[...], 1, 1), out_refs)
 
 
-def units_to_width(values, units, part, first, count):
+def units_to_width(values, units, part, first, count, pieces=None):
+    pieces = pieces or count
     width = units.shape[0]
     block, columns = values.shape[0] // 4, values.shape[1]
     length = block * count
@@ -707,8 +708,8 @@
             pl.BlockSpec((length, columns), lambda i: (first // count, 0)),
             pl.BlockSpec((TILE, columns), lambda i: (i, part)),
         ],
-        out_specs=(pl.BlockSpec((block, TILE), lambda i: (0, i)),) * count,
-        out_shape=(jax.ShapeDtypeStruct((block, width), bf16),) * count,
+        out_specs=(pl.BlockSpec((length // pieces, TILE), lambda i: (0, i)),) * pieces,
+        out_shape=(jax.ShapeDtypeStruct((length // pieces, width), bf16),) * pieces,
         compiler_params=pltpu.CompilerParams(vmem_limit_bytes=VMEM_LIMIT),
         cost_estimate=SMALL,
     )(values, units)
@@ -1155,8 +1156,8 @@
         down_given,
     )
     from_last = swap_opposite(back_last)
-    (down_last,) = units_to_width(hidden_b, units, 2, 3, 1)
-    branch_ends = [from_ends(down_last[:half]), from_ends(down_last[half:])]
+    down_last = units_to_width(hidden_b, units, 2, 3, 1, 2)
+    branch_ends = [from_ends(part) for part in down_last]
     both_kept, both_given = units_gradient_parts(rows_all, dboth, core)
     from_last, branch_ends, down_kept, down_given, both_kept, both_given, down_last = together(
         from_last, branch_ends, down_kept, down_given, both_kept, both_given, down_last
@@ -1201,7 +1202,7 @@
     grad_mid_parts = (grad_mid_mine, grad_mid_next, grad_mid_other, swap_core(grad_mid_next))
 
     branch_far_rest = swap_far(down_far[3 * half // 4 :])
-    branch_middle = swap_middle(down_last)
+    branch_middle = swap_middle(jnp.concatenate(down_last, axis=0))
     grad_attended, row_dot, *out_pieces = attention_turn(
         place, pair, grad_mid_parts, w_heads, attended
     )
@@ -1281,25 +1282,26 @@
         after(units_sum, (near, out_parts[0])),
         2 * units_sum.shape[1] // 3,
     )
-    gain_total = after(gain_total, down_new)
-    gain_total = sum_dp(gain_total, 2, lax.axis_size("dp") // 2)
-    gain_last = swap_dp(gain_total, lax.axis_size("dp") // 2)
+    count = lax.axis_size("dp")
+    gain_last = swap_dp(after(gain_total, down_new), 2)
     qkv_kept, qkv_given = scatter_pairs_end(core, after(qkv_parts, (down_new, far)))
-    gain_total = gain_total + after(gain_last, qkv_kept)
-    gain_last = swap_near(gain_total)
-    out_kept, out_given = scatter_pairs_end(core, after(out_parts, (down_new, far)))
+    gain_total = sum_dp(gain_total + after(gain_last, qkv_kept), 4, count // 2)
+    gain_last = swap_dp(gain_total, count // 2)
+    out_kept, out_given = scatter_pairs_end(core, after(out_parts, qkv_kept))
     qkv_other, out_other = swap_core(qkv_given), swap_core(out_given)
     gain_total = gain_total + after(gain_last, out_kept)
+    gain_last = swap_near(gain_total)
     heads_away = jnp.concatenate(
         [jnp.where(own, qkv_other, qkv_kept), jnp.where(own, out_other, out_kept)], axis=1
     )
     kept, given = heads_scatter_end(home + near.astype(f32), far, own, core)
     units_sum = after(units_sum, heads_away)
+    gain_total = gain_total + after(gain_last, heads_away)
     gain_last = swap_far(gain_total)
     heads_away = swap_far(heads_away)
-    gain_total = gain_total + gain_last
     in_grad = input_gradient(core[None], kept, given, block_in, gain_attn, grad_middle)
     gate_up_new = adam_units(gate_up, gate_up_first, gate_up_second, units_sum, 0)
+    gain_total = gain_total + after(gain_last, gate_up_new)
     heads_away, in_grad, gate_up_new = together(heads_away, in_grad, gate_up_new)
     down_new = tuple(value[0].T for value in down_new)
     qkv_columns = qkv_weight.shape[1]

time: 499 us -> 496 us (level)
  transfers between devices with their start and end apart: 68 -> 68, of which waited for: 29 -> 27; matrix products, arithmetic and copies ran while one was open for 8% -> 7% of each run, Pallas kernels for 42% -> 42%
where the time goes in v5:
time: 496 us; the launch traced here: 489 us
  Pallas kernels  205 us (41%)
  waiting for transfers between devices  127 us (26%)
  starting transfers between devices  89.1 us (18%)
  other arithmetic  42.5 us (9%)
  between operations  15.1 us (3%)
  local copies, waits for them, and re-layouts  10.7 us (2%)
    ppermute x11, waiting for transfers between devices, swap_far(): return lax.ppermute(value, 'tensor', [(0, 2), (2, 0), (1, 3), (3, 1)])  58.4 us
    pallas_call x3, Pallas kernels, units_forward(): pl.pallas_call(functools.partial(units_forward_kernel, count, pick is not...  39.5 us
    pallas_call x4, Pallas kernels, units_to_width(): pl.pallas_call(units_to_width_kernel, grid=(width // TILE,), in_specs=[pl...  38 us
    pallas_call x2, Pallas kernels, units_gradient_parts(): pl.pallas_call(units_gradient_kernel, grid_spec=pltpu.PrefetchScalarGridS...  28.7 us
    ppermute x9, waiting for transfers between devices, swap_near(): return lax.ppermute(value, 'tensor', [(0, 1), (1, 0), (2, 3), (3, 2)])  25.2 us
    ppermute x11, starting transfers between devices, swap_far(): return lax.ppermute(value, 'tensor', [(0, 2), (2, 0), (1, 3), (3, 1)])  24.3 us
    pallas_call x1, Pallas kernels, attention_backward(): pl.pallas_call(attention_backward_kernel, grid=(1,), in_specs=scalars(1)...  23.4 us
    ppermute x18, starting transfers between devices, swap_dp(): return lax.ppermute(value, 'dp', [(i, i ^ mask) for i in range(count)])  19.1 us
  transfers between devices with their start and end apart: 68, of which 27 were waited for; matrix products, arithmetic and copies ran while one was open for 7% of the time, Pallas kernels for 42%

profile of v5, /device:TPU:0, one launch (start us, length us, event | category | flops | bytes accessed | tf_op | source)
XLA Modules:
  0.0 488.9 jit_solution(9909183041031985652)
XLA Ops:
  10.1 4.0 collective-permute-start
  15.9 2.1 collective-permute-done.3
  23.8 3.7 shard_map.314
  30.1 3.6 collective-permute-done.6
  41.5 1.9 fusion.12
  43.4 1.9 pad_maximum_fusion.3
  45.9 9.2 %collective-permute-done.7 = bf16[256,1536]{1,0:T(8,128)(2,1)S(1)} collective-permute-done((bf16[256,1536]{1,0:T(8,128)(2,1)}, bf16[256,1536]{1,0:T(8,128)(2,1)S(1)}, u32[]{:S(2)}, u32[]{:S(2)}) %collective-permute-start.7) | collective-permute-done | bytes 786464 | tf_op jit(solution)/shard_map/ppermute | solution.py:821
  55.0 3.2 collective-permute-done.10.refs_6_
  64.3 2.9 collective-permute-start.15
  67.2 6.9 %collective-permute-done.15 = bf16[64,1536]{1,0:T(8,128)(2,1)S(1)} collective-permute-done((bf16[64,1536]{1,0:T(8,128)(2,1)S(1)}, bf16[64,1536]{1,0:T(8,128)(2,1)S(1)}, u32[]{:S(2)}, u32[]{:S(2)}) %collective-permute-start.15) | collective-permute-done | bytes 196640 | tf_op jit(solution)/shard_map/ppermute | solution.py:791
  77.2 4.8 collective-permute-start.16
  86.8 14.7 %shard_map.315 = (bf16[1536,1024]{1,0:T(8,128)(2,1)}, bf16[1024,1536]{1,0:T(8,128)(2,1)}, f32[1024,640]{1,0:T(8,128)}, bf16[6,1024,64]{2,1,0:T(8,128)(2,1)}, bf1...) custom-call(s32[1]{0:T(128)} %bitcast.1.place_ref, ...), custom_call_target="tpu_custom_call" | custom-call | flops 1000 | bytes 1000 | tf_op jit(solution)/shard_map/pallas_call | solution.py:245
  101.5 5.8 %shard_map.316 = (bf16[4,128,1536]{2,1,0:T(8,128)(2,1)}, bf16[4,128,1536]{2,1,0:T(8,128)(2,1)}) custom-call(s32[1]{0:T(128)} %bitcast.core_ref, bf16[1024,384]{1,0:T(8,128)(2,1)} %get-tuple-element.270.attended_ref.refs_5_, bf16[1536,1024]{1,0:T(8,128)(2,1)} %get-tuple-element.271.weight_ref.refs_4_), custom_call_target="tpu_custom_call" | custom-call | flops 1000 | bytes 1000 | tf_op jit(solution)/shard_map/pallas_call | solution.py:260
  107.3 6.7 %collective-permute-done.17 = bf16[192,1536]{1,0:T(8,128)(2,1)} collective-permute-done((bf16[192,1536]{1,0:T(8,128)(2,1)}, bf16[192,1536]{1,0:T(8,128)(2,1)}, u32[]{:S(2)}, u32[]{:S(2)}) %collective-permute-start.17) | collective-permute-done | bytes 589856 | tf_op jit(solution)/shard_map/ppermute | solution.py:791
  116.0 2.0 pad_maximum_fusion.1.refs_3_
  118.5 2.2 fusion.7
  120.6 4.2 collective-permute-start.20
  124.9 9.8 %collective-permute-done.20 = bf16[128,1536]{1,0:T(8,128)(2,1)S(1)} collective-permute-done((bf16[128,1536]{1,0:T(8,128)(2,1)S(1)}, bf16[128,1536]{1,0:T(8,128)(2,1)S(1)}, u32[]{:S(2)}, u32[]{:S(2)}) %collective-permute-start.20) | collective-permute-done | bytes 393248 | tf_op jit(solution)/shard_map/ppermute | solution.py:787
  134.8 5.1 %collective-permute-start.22 = (bf16[128,1536]{1,0:T(8,128)(2,1)S(1)}, bf16[128,1536]{1,0:T(8,128)(2,1)S(1)}, u32[]{:S(2)}, u32[]{:S(2)}) collective-permute-start(bf16[128,1536]{1,0:T(8,128)(2,1)S(1)} %add_convert_fusion.4), channel_id=1, source_target_pairs={{0,2},{2,0},{1,3},{3,1},{4,6},{6,4},{5,7},{7,5},{8,10},{10,8},{9,1... | collective-permute-start | bytes 1179656 | tf_op jit(solution)/shard_map/ppermute | solution.py:791
  139.9 5.9 %collective-permute-done.23 = bf16[128,1536]{1,0:T(8,128)(2,1)S(1)} collective-permute-done((bf16[128,1536]{1,0:T(8,128)(2,1)S(1)}, bf16[128,1536]{1,0:T(8,128)(2,1)S(1)}, u32[]{:S(2)}, u32[]{:S(2)}) %collective-permute-start.23) | collective-permute-done | bytes 393248 | tf_op jit(solution)/shard_map/ppermute | solution.py:787
  145.8 11.7 %collective-permute-done.22 = bf16[128,1536]{1,0:T(8,128)(2,1)S(1)} collective-permute-done((bf16[128,1536]{1,0:T(8,128)(2,1)S(1)}, bf16[128,1536]{1,0:T(8,128)(2,1)S(1)}, u32[]{:S(2)}, u32[]{:S(2)}) %collective-permute-start.22) | collective-permute-done | bytes 393248 | tf_op jit(solution)/shard_map/ppermute | solution.py:791
  157.7 1.8 collective-permute-done.24
  161.4 1.9 collective-permute-start.26
  164.6 3.5 all-gather.2.cloned.1.call-done.refs_2_.refs_3_.refs_4_.refs_5_.units_ref
  168.1 11.7 %shard_map.317 = (bf16[1024,1536]{1,0:T(8,128)(2,1)}, bf16[1024,1536]{1,0:T(8,128)(2,1)}, bf16[1024,1792]{1,0:T(8,128)(2,1)}, bf16[1024,3584]{1,0:T(8,128)(2,1)}) custom-call(s32[1]{0:T(128)} %constant.122.clone.1.pick_ref, bf16[256,1536]{1,0:T(8,128)(2,1)} %copy-done.10, bf16[256,1536]{1,0:T(8,128)(2,1)} %copy-done.1, ...), custom_call_target="tpu_custom_call" | custom-call | flops 1000 | bytes 1000 | tf_op jit(solution)/shard_map/pallas_call | solution.py:661
  179.8 18.0 %collective-permute-done.25.refs_1_ = bf16[256,1536]{1,0:T(8,128)(2,1)} collective-permute-done((bf16[256,1536]{1,0:T(8,128)(2,1)S(1)}, bf16[256,1536]{1,0:T(8,128)(2,1)}, u32[]{:S(2)}, u32[]{:S(2)}) %collective-permute-start.25) | collective-permute-done | bytes 786464 | tf_op jit(solution)/shard_map/ppermute | solution.py:791
  200.8 15.4 %shard_map.318 = (bf16[1024,1536]{1,0:T(8,128)(2,1)}, bf16[1024,1536]{1,0:T(8,128)(2,1)}, bf16[1024,1792]{1,0:T(8,128)(2,1)}, bf16[1024,3584]{1,0:T(8,128)(2,1)}) custom-call(s32[1]{0:T(128)} %constant.122.clone.1.pick_ref, ...), custom_call_target="tpu_custom_call", output_to_operand_aliasing={{0}: (7, {}), {1}: (8, {}), {2}: (9, {}), {3}: (10, {})} | custom-call | flops 1000 | bytes 1000 | tf_op jit(solution)/shard_map/pallas_call | solution.py:661
  216.2 11.2 %shard_map.319 = (bf16[256,1536]{1,0:T(8,128)(2,1)}, bf16[256,1536]{1,0:T(8,128)(2,1)}) custom-call(bf16[1024,3584]{1,0:T(8,128)(2,1)} %get-tuple-element.318.values_ref.refs_9_, bf16[1536,5376]{1,0:T(8,128)(2,1)} %all-gather.2.cloned.1.call-done.refs_2_.refs_3_.refs_4_.refs_5_.units_ref), custom_call_target="tpu_custom_call" | custom-call | flops 1000 | bytes 1000 | tf_op jit(solution)/shard_map/pallas_call | solution.py:704
  227.4 4.3 collective-permute-done.27.refs_0_
  233.4 1.8 collective-permute-start.31
  235.3 12.4 %shard_map.320 = (bf16[1024,1536]{1,0:T(8,128)(2,1)}, bf16[1024,1536]{1,0:T(8,128)(2,1)}, bf16[1024,1792]{1,0:T(8,128)(2,1)}, bf16[1024,3584]{1,0:T(8,128)(2,1)}) custom-call(s32[1]{0:T(128)} %bitcast.17.pick_ref, bf16[256,1536]{1,0:T(8,128)(2,1)} %copy-done.30, ...), custom_call_target="tpu_custom_call", output_to_operand_aliasing={{0}: (7, {}), {1}: (8, {}), {2}: (9, {}), {3}: (10, {})} | custom-call | flops 1000 | bytes 1000 | tf_op jit(solution)/shard_map/pallas_call | solution.py:661
  247.7 11.3 %shard_map.322 = (bf16[4,192,1792]{2,1,0:T(8,128)(2,1)}, bf16[4,192,1792]{2,1,0:T(8,128)(2,1)}) custom-call(s32[1]{0:T(128)} %bitcast.core_ref, bf16[1024,1536]{1,0:T(8,128)(2,1)} %get-tuple-element.324.left_ref, bf16[1024,1792]{1,0:T(8,128)(2,1)} %get-tuple-element.350.right_ref.values_ref), custom_call_target="tpu_custom_call" | custom-call | flops 1000 | bytes 1000 | tf_op jit(solution)/shard_map/pallas_call | solution.py:763
  259.0 11.1 %shard_map.321 = (bf16[256,1536]{1,0:T(8,128)(2,1)}, bf16[256,1536]{1,0:T(8,128)(2,1)}) custom-call(bf16[1024,3584]{1,0:T(8,128)(2,1)} %get-tuple-element.337.values_ref.right_ref, bf16[1536,5376]{1,0:T(8,128)(2,1)} %all-gather.2.cloned.1.call-done.refs_2_.refs_3_.refs_4_.refs_5_.units_ref), custom_call_target="tpu_custom_call" | custom-call | flops 1000 | bytes 1000 | tf_op jit(solution)/shard_map/pallas_call | solution.py:704
  270.1 1.7 collective-permute-start.32
  271.9 6.6 %shard_map.323 = (bf16[128,1536]{1,0:T(8,128)(2,1)}, bf16[128,1536]{1,0:T(8,128)(2,1)}) custom-call(bf16[1024,1792]{1,0:T(8,128)(2,1)} %get-tuple-element.350.right_ref.values_ref, bf16[1536,5376]{1,0:T(8,128)(2,1)} %all-gather.2.cloned.1.call-done.refs_2_.refs_3_.refs_4_.refs_5_.units_ref), custom_call_target="tpu_custom_call" | custom-call | flops 1000 | bytes 1000 | tf_op jit(solution)/shard_map/pallas_call | solution.py:704
  278.5 1.9 collective-permute-start.33
  281.8 17.4 %shard_map.324 = (bf16[4,192,3584]{2,1,0:T(8,128)(2,1)}, bf16[4,192,3584]{2,1,0:T(8,128)(2,1)}) custom-call(s32[1]{0:T(128)} %bitcast.core_ref, bf16[1024,1536]{1,0:T(8,128)(2,1)} %get-tuple-element.336.left_ref, bf16[1024,3584]{1,0:T(8,128)(2,1)} %get-tuple-element.337.values_ref.right_ref), custom_call_target="tpu_custom_call" | custom-call | flops 1000 | bytes 1000 | tf_op jit(solution)/shard_map/pallas_call | solution.py:763
  299.3 5.6 %collective-permute-done.34 = bf16[128,1536]{1,0:T(8,128)(2,1)S(1)} collective-permute-done((bf16[128,1536]{1,0:T(8,128)(2,1)}, bf16[128,1536]{1,0:T(8,128)(2,1)S(1)}, u32[]{:S(2)}, u32[]{:S(2)}) %collective-permute-start.34) | collective-permute-done | bytes 393248 | tf_op jit(solution)/shard_map/ppermute | solution.py:807
  306.5 2.0 fusion.18
  309.0 2.4 collective-permute-start.35
  311.4 9.0 %shard_map.326 = (bf16[256,1536]{1,0:T(8,128)(2,1)}, bf16[256,1536]{1,0:T(8,128)(2,1)}, bf16[256,1536]{1,0:T(8,128)(2,1)}) custom-call(bf16[1024,1792]{1,0:T(8,128)(2,1)} %get-tuple-element.350.right_ref.values_ref, bf16[1536,5376]{1,0:T(8,128)(2,1)} %all-gather.2.cloned.1.call-done.refs_2_.refs_3_.refs_4_.refs_5_.units_ref), custom_call_target="tpu_custom_call" | custom-call | flops 1000 | bytes 1000 | tf_op jit(solution)/shard_map/pallas_call | solution.py:704
  321.8 9.3 %shard_map.325 = bf16[4,192,5376]{2,1,0:T(8,128)(2,1)} custom-call(bf16[4,192,3584]{2,1,0:T(8,128)(2,1)} %get-tuple-element.346.refs_0_, bf16[4,192,3584]{2,1,0:T(8,128)(2,1)} %collective-permute-done.36.refs_1_, bf16[4,192,1792]{2,1,0:T(8,128)(2,1)} %get-tuple-element.348.refs_2_, bf16[4,192,1792]{2,1,0:T(8,128)(2,1)} %collective-permute-done.37.refs_3_), custom_call_target="tpu_custom_call" | custom-call | flops 1000 | bytes 1000 | tf_op jit(solution)/shard_map/pallas_call | solution.py:732
  333.4 4.3 collective-permute-start.40
  337.6 9.9 %collective-permute-done.40 = bf16[96,1536]{1,0:T(8,128)(2,1)S(1)} collective-permute-done((bf16[96,1536]{1,0:T(8,128)(2,1)S(1)}, bf16[96,1536]{1,0:T(8,128)(2,1)S(1)}, u32[]{:S(2)}, u32[]{:S(2)}) %collective-permute-start.40) | collective-permute-done | bytes 294944 | tf_op jit(solution)/shard_map/ppermute | solution.py:791
  347.6 5.6 %collective-permute-start.41 = (bf16[256,1536]{1,0:T(8,128)(2,1)S(1)}, bf16[256,1536]{1,0:T(8,128)(2,1)}, u32[]{:S(2)}, u32[]{:S(2)}) collective-permute-start(bf16[256,1536]{1,0:T(8,128)(2,1)S(1)} %broadcast_select_fusion.refs_1_), channel_id=1, source_target_pairs={{0,4},{4,0},{8,12},{12,8},{16,20},{20,16},{24,28},{28,24},{1,5},{5... | collective-permute-start | bytes 2359304 | tf_op jit(solution)/shard_map/ppermute | solution.py:783
  355.3 8.6 %shard_map.327 = (bf16[6,1024,64]{2,1,0:T(8,128)(2,1)}, f32[8,1024]{1,0:T(8,128)}, bf16[2,192,384]{2,1,0:T(8,128)(2,1)}, bf16[2,192,384]{2,1,0:T(8,128)(2,1)}, b...) custom-call(s32[1]{0:T(128)} %bitcast.1.place_ref, s32[2]{0:T(128)} %pad_add_fusion.pair_ref, ...), custom_call_target="tpu_custom_call" | custom-call | flops 1000 | bytes 1000 | tf_op jit(solution)/shard_map/pallas_call | solution.py:388
  363.9 3.6 collective-permute-start.43
  370.9 23.4 %shard_map.328 = (bf16[1024,640]{1,0:T(8,128)(2,1)}, bf16[4,128,1536]{2,1,0:T(8,128)(2,1)}, bf16[4,128,1536]{2,1,0:T(8,128)(2,1)}, f32[1,640]{1,0:T(1,128)}, f32[1,1536]{1,0:T(1,128)}) custom-call(s32[1]{0:T(128)} %bitcast.core_ref, bf16[6,1024,64]{2,1,0:T(8,128)(2,1)} %get-tuple-element.357.q_ref, bf16[2,1024,64]{2,1,0:T(8,128)(2,1)} %get-tuple-element.358.k_ref, ...), custom_call_target="tpu_custom_call" | custom-call | flops 1000 | bytes 1000 | tf_op jit(solution)/shard_map/pallas_call | solution.py:511
  394.4 4.5 collective-permute-done.42
  400.0 6.4 %shard_map.329 = (bf16[2,192,640]{2,1,0:T(8,128)(2,1)}, bf16[2,192,640]{2,1,0:T(8,128)(2,1)}, bf16[2,192,640]{2,1,0:T(8,128)(2,1)}, bf16[2,192,640]{2,1,0:T(8,128)(2,1)}) custom-call(s32[2]{0:T(128)} %pad_add_fusion.pair_ref, bf16[1024,1536]{1,0:T(8,128)(2,1)} %get-tuple-element.369.normed_ref.left_ref, bf16[1024,640]{1,0:T(8,128)(2,1)} %get-tuple-element.387.right_ref), custom_call_target="tpu_custom_call" | custom-call | flops 1000 | bytes 1000 | tf_op jit(solution)/shard_map/pallas_call | solution.py:304
  413.1 7.8 %collective-permute-done.50 = bf16[128,1536]{1,0:T(8,128)(2,1)} collective-permute-done((bf16[128,1536]{1,0:T(8,128)(2,1)}, bf16[128,1536]{1,0:T(8,128)(2,1)}, u32[]{:S(2)}, u32[]{:S(2)}) %collective-permute-start.50) | collective-permute-done | bytes 393248 | tf_op jit(solution)/shard_map/ppermute | solution.py:787
  420.9 2.0 fusion
  423.0 3.3 convert_add_fusion
  427.0 4.7 collective-permute-done.48.got_x
  431.7 2.5 shard_map.330
  436.2 2.1 shard_map.331
  440.4 5.3 %shard_map.332 = (f32[1,192,1728]{2,1,0:T(8,128)}, f32[1,192,1728]{2,1,0:T(8,128)}, f32[1,192,1728]{2,1,0:T(8,128)}) custom-call(f32[1,192,1728]{2,1,0:T(8,128)} %bitcast.73, f32[1,192,1728]{2,1,0:T(8,128)} %bitcast.74, f32[1,192,1728]{2,1,0:T(8,128)} %bitcast.75, bf16[192,5376]{1,0:T(8,128)(2,1)} %reduce-scatter.2.cloned.1.call-done.sum_ref), custom_call_target="tpu_custom_call" | custom-call | flops 1000 | bytes 1000 | tf_op jit(solution)/shard_map/pallas_call | solution.py:610
  447.2 2.2 shard_map.333
  449.5 1.9 shard_map.334
  454.5 1.9 collective-permute-done.63
  458.8 2.4 collective-permute-start.60
  462.7 2.1 convert_select_fusion.2.kept_ref
  465.5 4.1 shard_map.335
  469.6 8.3 %shard_map.336 = (f32[2,192,1728]{2,1,0:T(8,128)}, f32[2,192,1728]{2,1,0:T(8,128)}, f32[2,192,1728]{2,1,0:T(8,128)}) custom-call(f32[2,192,1728]{2,1,0:T(8,128)} %weight_ref.1, f32[2,192,1728]{2,1,0:T(8,128)} %first_ref.1, f32[2,192,1728]{2,1,0:T(8,128)} %second_ref.1, bf16[192,5376]{1,0:T(8,128)(2,1)} %reduce-scatter.2.cloned.1.call-done.sum_ref), custom_call_target="tpu_custom_call" | custom-call | flops 1000 | bytes 1000 | tf_op jit(solution)/shard_map/pallas_call | solution.py:610
  (301 shorter events, 84.2 us)
Async XLA Ops:
  7.2 160.9 %all-gather.2.cloned.1.call-start = ((), (), s32[]{:S(2)}) async-start(), calls=%async_computation.1 | async-start | bytes 18579456 | tf_op jit(solution)/shard_map/all_gather | solution.py:1084
  9.5 4.8 collective-permute-start.2
  10.0 19.5 %collective-permute-start.1 = (s32[1024]{0:T(1024)S(1)}, s32[1024]{0:T(1024)S(1)}, u32[]{:S(2)}, u32[]{:S(2)}) collective-permute-start(s32[1024]{0:T(1024)S(1)} %copy-done.54), channel_id=1, source_target_pairs={{0,4},{4,0},{8,12},{12,8},{16,20},{20,16},{24,28},{28,24},{1,5},{5... | collective-permute-start | bytes 12296 | tf_op jit(solution)/shard_map/ppermute | solution.py:783
  10.1 23.7 %collective-permute-start = (bf16[192,1024]{1,0:T(8,128)(2,1)S(1)}, bf16[192,1024]{1,0:T(8,128)(2,1)S(1)}, u32[]{:S(2)}, u32[]{:S(2)}) collective-permute-start(bf16[192,1024]{1,0:T(8,128)(2,1)S(1)} %pad_maximum_fusion.5), channel_id=1, source_target_pairs={{0,2},{2,0},{1,3},{3,1},{4,6},{6,4},{5,7},{7,5},{8,10},{10,8},{9,1... | collective-permute-start | bytes 1179656 | tf_op jit(solution)/shard_map/ppermute | solution.py:791
  21.7 7.3 %collective-permute-start.5 = (f32[8,1,100]{2,0,1:T(8,128)S(1)}, f32[8,1,100]{2,0,1:T(8,128)S(1)}, u32[]{:S(2)}, u32[]{:S(2)}) collective-permute-start(f32[8,1,100]{2,0,1:T(8,128)S(1)} %maximum_bitcast_fusion), channel_id=1, source_target_pairs={{0,1},{1,0},{2,3},{3,2},{4,5},{5,4},{6,7},{7,6},{8,9},{9,8},{10,11... | collective-permute-start | bytes 9608 | tf_op jit(solution)/shard_map/ppermute | solution.py:866
  29.1 4.6 collective-permute-start.6
  35.4 19.6 %collective-permute-start.7 = (bf16[256,1536]{1,0:T(8,128)(2,1)}, bf16[256,1536]{1,0:T(8,128)(2,1)S(1)}, u32[]{:S(2)}, u32[]{:S(2)}) collective-permute-start(bf16[256,1536]{1,0:T(8,128)(2,1)} %multiply_convert_fusion.1), channel_id=1, source_target_pairs={{0,1},{4,2},{1,0},{5,3},{6,7},{2,4},{7,6},{3,5},{8,9},{12,10},{9,8... | collective-permute-start | bytes 2359304 | tf_op jit(solution)/shard_map/ppermute | solution.py:821
  38.4 19.8 %collective-permute-start.10 = (bf16[384,1024]{1,0:T(8,128)(2,1)S(1)}, bf16[384,1024]{1,0:T(8,128)(2,1)S(1)}, u32[]{:S(2)}, u32[]{:S(2)}) collective-permute-start(bf16[384,1024]{1,0:T(8,128)(2,1)S(1)} %pad_maximum_fusion.refs_4_), channel_id=1, source_target_pairs={{0,16},{4,20},{8,24},{12,28},{16,0},{20,4},{24,8},{28,12},{1,17},{... | collective-permute-start | bytes 2359304 | tf_op jit(solution)/shard_map/ppermute | solution.py:888
  40.0 19.4 %collective-permute-start.9 = (bf16[384,1024]{1,0:T(8,128)(2,1)S(1)}, bf16[384,1024]{1,0:T(8,128)(2,1)S(1)}, u32[]{:S(2)}, u32[]{:S(2)}) collective-permute-start(bf16[384,1024]{1,0:T(8,128)(2,1)S(1)} %pad_maximum_fusion.refs_4_), channel_id=1, source_target_pairs={{0,8},{4,12},{8,0},{12,4},{16,24},{20,28},{24,16},{28,20},{1,9},{5... | collective-permute-start | bytes 2359304 | tf_op jit(solution)/shard_map/ppermute | solution.py:888
  60.5 13.7 %collective-permute-start.14 = (bf16[256,1536]{1,0:T(8,128)(2,1)S(1)}, bf16[256,1536]{1,0:T(8,128)(2,1)S(1)}, u32[]{:S(2)}, u32[]{:S(2)}) collective-permute-start(bf16[256,1536]{1,0:T(8,128)(2,1)S(1)} %broadcast_select_fusion.3.refs_0_), channel_id=1, source_target_pairs={{0,4},{4,0},{8,12},{12,8},{16,20},{20,16},{24,28},{28,24},{1,5},{5... | collective-permute-start | bytes 2359304 | tf_op jit(solution)/shard_map/ppermute | solution.py:783
  60.5 15.4 %collective-permute-start.13 = (bf16[256,1536]{1,0:T(8,128)(2,1)S(1)}, bf16[256,1536]{1,0:T(8,128)(2,1)}, u32[]{:S(2)}, u32[]{:S(2)}) collective-permute-start(bf16[256,1536]{1,0:T(8,128)(2,1)S(1)} %collective-permute-done.7), channel_id=1, source_target_pairs={{4,5},{5,4},{2,3},{3,2},{12,13},{13,12},{10,11},{11,10},{20,21},{2... | collective-permute-start | bytes 2359304 | tf_op jit(solution)/shard_map/ppermute | solution.py:830
  62.2 12.0 %collective-permute-start.11 = (bf16[192,1024]{1,0:T(8,128)(2,1)S(1)}, bf16[192,1024]{1,0:T(8,128)(2,1)S(1)}, u32[]{:S(2)}, u32[]{:S(2)}) collective-permute-start(bf16[192,1024]{1,0:T(8,128)(2,1)S(1)} %slice.46), channel_id=1, source_target_pairs={{0,8},{4,12},{8,0},{12,4},{16,24},{20,28},{24,16},{28,20},{1,9},{5... | collective-permute-start | bytes 1179656 | tf_op jit(solution)/shard_map/ppermute | solution.py:888
  63.7 10.5 %collective-permute-start.12 = (bf16[192,1024]{1,0:T(8,128)(2,1)S(1)}, bf16[192,1024]{1,0:T(8,128)(2,1)S(1)}, u32[]{:S(2)}, u32[]{:S(2)}) collective-permute-start(bf16[192,1024]{1,0:T(8,128)(2,1)S(1)} %slice.47), channel_id=1, source_target_pairs={{0,16},{4,20},{8,24},{12,28},{16,0},{20,4},{24,8},{28,12},{1,17},{... | collective-permute-start | bytes 1179656 | tf_op jit(solution)/shard_map/ppermute | solution.py:888
  64.3 9.8 %collective-permute-start.15 = (bf16[64,1536]{1,0:T(8,128)(2,1)S(1)}, bf16[64,1536]{1,0:T(8,128)(2,1)S(1)}, u32[]{:S(2)}, u32[]{:S(2)}) collective-permute-start(bf16[64,1536]{1,0:T(8,128)(2,1)S(1)} %slice.48), channel_id=1, source_target_pairs={{0,2},{2,0},{1,3},{3,1},{4,6},{6,4},{5,7},{7,5},{8,10},{10,8},{9,1... | collective-permute-start | bytes 589832 | tf_op jit(solution)/shard_map/ppermute | solution.py:791
  76.0 364.3 %reduce-scatter.2.cloned.1.call-start = ((), (), s32[]{:S(2)}) async-start(), calls=%async_computation.2 | async-start | bytes 10321920 | tf_op jit(solution)/shard_map/reduce_scatter | solution.py:960
  77.2 8.7 %collective-permute-start.16 = (bf16[256,1536]{1,0:T(8,128)(2,1)}, bf16[256,1536]{1,0:T(8,128)(2,1)S(1)}, u32[]{:S(2)}, u32[]{:S(2)}) collective-permute-start(bf16[256,1536]{1,0:T(8,128)(2,1)} %broadcast_select_fusion.2.refs_1_), channel_id=1, source_target_pairs={{0,4},{4,0},{8,12},{12,8},{16,20},{20,16},{24,28},{28,24},{1,5},{5... | collective-permute-start | bytes 2359304 | tf_op jit(solution)/shard_map/ppermute | solution.py:783
  82.1 32.6 %collective-permute-start.18 = (bf16[256,1536]{1,0:T(8,128)(2,1)S(1)}, bf16[256,1536]{1,0:T(8,128)(2,1)}, u32[]{:S(2)}, u32[]{:S(2)}) collective-permute-start(bf16[256,1536]{1,0:T(8,128)(2,1)S(1)} %convert_element_type.194.refs_1_), channel_id=1, source_target_pairs={{0,1},{1,0},{2,3},{3,2},{4,5},{5,4},{6,7},{7,6},{8,9},{9,8},{10,11... | collective-permute-start | bytes 2359304 | tf_op jit(solution)/shard_map/ppermute | solution.py:787
  84.6 29.3 %collective-permute-start.17 = (bf16[192,1536]{1,0:T(8,128)(2,1)}, bf16[192,1536]{1,0:T(8,128)(2,1)}, u32[]{:S(2)}, u32[]{:S(2)}) collective-permute-start(bf16[192,1536]{1,0:T(8,128)(2,1)} %slice.49), channel_id=1, source_target_pairs={{0,2},{2,0},{1,3},{3,1},{4,6},{6,4},{5,7},{7,5},{8,10},{10,8},{9,1... | collective-permute-start | bytes 1769480 | tf_op jit(solution)/shard_map/ppermute | solution.py:791
  114.7 3.8 collective-permute-start.19
  114.7 10.2 %collective-permute-start.21 = (bf16[256,1536]{1,0:T(8,128)(2,1)S(1)}, bf16[256,1536]{1,0:T(8,128)(2,1)S(1)}, u32[]{:S(2)}, u32[]{:S(2)}) collective-permute-start(bf16[256,1536]{1,0:T(8,128)(2,1)S(1)} %convert_element_type.194.refs_1_), channel_id=1, source_target_pairs={{1,2},{2,1},{5,6},{6,5},{9,10},{10,9},{13,14},{14,13},{17,18},{18,... | collective-permute-start | bytes 2359304 | tf_op jit(solution)/shard_map/ppermute | solution.py:795
  120.6 14.1 %collective-permute-start.20 = (bf16[128,1536]{1,0:T(8,128)(2,1)S(1)}, bf16[128,1536]{1,0:T(8,128)(2,1)S(1)}, u32[]{:S(2)}, u32[]{:S(2)}) collective-permute-start(bf16[128,1536]{1,0:T(8,128)(2,1)S(1)} %get-tuple-element.481), channel_id=1, source_target_pairs={{0,1},{1,0},{2,3},{3,2},{4,5},{5,4},{6,7},{7,6},{8,9},{9,8},{10,11... | collective-permute-start | bytes 1179656 | tf_op jit(solution)/shard_map/ppermute | solution.py:787
  124.8 20.9 %collective-permute-start.23 = (bf16[128,1536]{1,0:T(8,128)(2,1)S(1)}, bf16[128,1536]{1,0:T(8,128)(2,1)S(1)}, u32[]{:S(2)}, u32[]{:S(2)}) collective-permute-start(bf16[128,1536]{1,0:T(8,128)(2,1)S(1)} %get-tuple-element.478), channel_id=1, source_target_pairs={{0,1},{1,0},{2,3},{3,2},{4,5},{5,4},{6,7},{7,6},{8,9},{9,8},{10,11... | collective-permute-start | bytes 1179656 | tf_op jit(solution)/shard_map/ppermute | solution.py:787
  134.8 22.6 %collective-permute-start.22 = (bf16[128,1536]{1,0:T(8,128)(2,1)S(1)}, bf16[128,1536]{1,0:T(8,128)(2,1)S(1)}, u32[]{:S(2)}, u32[]{:S(2)}) collective-permute-start(bf16[128,1536]{1,0:T(8,128)(2,1)S(1)} %add_convert_fusion.4), channel_id=1, source_target_pairs={{0,2},{2,0},{1,3},{3,1},{4,6},{6,4},{5,7},{7,5},{8,10},{10,8},{9,1... | collective-permute-start | bytes 1179656 | tf_op jit(solution)/shard_map/ppermute | solution.py:791
  161.2 36.6 %collective-permute-start.25 = (bf16[256,1536]{1,0:T(8,128)(2,1)S(1)}, bf16[256,1536]{1,0:T(8,128)(2,1)}, u32[]{:S(2)}, u32[]{:S(2)}) collective-permute-start(bf16[256,1536]{1,0:T(8,128)(2,1)S(1)} %multiply_convert_fusion.refs_0_), channel_id=1, source_target_pairs={{0,2},{2,0},{1,3},{3,1},{4,6},{6,4},{5,7},{7,5},{8,10},{10,8},{9,1... | collective-permute-start | bytes 2359304 | tf_op jit(solution)/shard_map/ppermute | solution.py:791
  161.4 37.3 %collective-permute-start.26 = (bf16[256,1536]{1,0:T(8,128)(2,1)S(1)}, bf16[256,1536]{1,0:T(8,128)(2,1)}, u32[]{:S(2)}, u32[]{:S(2)}) collective-permute-start(bf16[256,1536]{1,0:T(8,128)(2,1)S(1)} %multiply_convert_fusion.refs_0_), channel_id=1, source_target_pairs={{0,1},{1,0},{2,3},{3,2},{4,5},{5,4},{6,7},{7,6},{8,9},{9,8},{10,11... | collective-permute-start | bytes 2359304 | tf_op jit(solution)/shard_map/ppermute | solution.py:787
  163.3 64.0 %collective-permute-start.29 = (bf16[256,1536]{1,0:T(8,128)(2,1)S(1)}, bf16[256,1536]{1,0:T(8,128)(2,1)}, u32[]{:S(2)}, u32[]{:S(2)}) collective-permute-start(bf16[256,1536]{1,0:T(8,128)(2,1)S(1)} %copy-done.9), channel_id=1, source_target_pairs={{1,0},{2,3},{5,4},{6,7},{9,8},{10,11},{13,12},{14,15},{17,16},{18,... | collective-permute-start | bytes 2359304 | tf_op jit(solution)/shard_map/ppermute | solution.py:803
  198.8 32.9 %collective-permute-start.27 = (bf16[256,1536]{1,0:T(8,128)(2,1)}, bf16[256,1536]{1,0:T(8,128)(2,1)S(1)}, u32[]{:S(2)}, u32[]{:S(2)}) collective-permute-start(bf16[256,1536]{1,0:T(8,128)(2,1)} %collective-permute-done.25.refs_1_), channel_id=1, source_target_pairs={{1,0},{2,3},{5,4},{6,7},{9,8},{10,11},{13,12},{14,15},{17,16},{18,... | collective-permute-start | bytes 2359304 | tf_op jit(solution)/shard_map/ppermute | solution.py:803
  200.0 31.6 %collective-permute-start.28 = (bf16[256,1536]{1,0:T(8,128)(2,1)}, bf16[256,1536]{1,0:T(8,128)(2,1)S(1)}, u32[]{:S(2)}, u32[]{:S(2)}) collective-permute-start(bf16[256,1536]{1,0:T(8,128)(2,1)} %copy-done.10), channel_id=1, source_target_pairs={{1,2},{2,1},{5,6},{6,5},{9,10},{10,9},{13,14},{14,13},{17,18},{18,... | collective-permute-start | bytes 2359304 | tf_op jit(solution)/shard_map/ppermute | solution.py:795
  232.5 37.6 %collective-permute-start.30 = (bf16[256,1536]{1,0:T(8,128)(2,1)}, bf16[256,1536]{1,0:T(8,128)(2,1)S(1)}, u32[]{:S(2)}, u32[]{:S(2)}) collective-permute-start(bf16[256,1536]{1,0:T(8,128)(2,1)} %get-tuple-element.309), channel_id=1, source_target_pairs={{0,1},{1,0},{2,3},{3,2},{4,5},{5,4},{6,7},{7,6},{8,9},{9,8},{10,11... | collective-permute-start | bytes 2359304 | tf_op jit(solution)/shard_map/ppermute | solution.py:787
  233.4 36.7 %collective-permute-start.31 = (bf16[256,1536]{1,0:T(8,128)(2,1)}, bf16[256,1536]{1,0:T(8,128)(2,1)S(1)}, u32[]{:S(2)}, u32[]{:S(2)}) collective-permute-start(bf16[256,1536]{1,0:T(8,128)(2,1)} %get-tuple-element.310), channel_id=1, source_target_pairs={{0,2},{2,0},{1,3},{3,1},{4,6},{6,4},{5,7},{7,5},{8,10},{10,8},{9,1... | collective-permute-start | bytes 2359304 | tf_op jit(solution)/shard_map/ppermute | solution.py:791
  270.1 34.8 %collective-permute-start.32 = (bf16[256,1536]{1,0:T(8,128)(2,1)}, bf16[256,1536]{1,0:T(8,128)(2,1)S(1)}, u32[]{:S(2)}, u32[]{:S(2)}) collective-permute-start(bf16[256,1536]{1,0:T(8,128)(2,1)} %get-tuple-element.330), channel_id=1, source_target_pairs={{0,3},{1,2},{2,1},{3,0},{4,7},{5,6},{6,5},{7,4},{8,11},{9,10},{10,... | collective-permute-start | bytes 2359304 | tf_op jit(solution)/shard_map/ppermute | solution.py:799
  278.5 20.8 %collective-permute-start.33 = (bf16[128,1536]{1,0:T(8,128)(2,1)}, bf16[128,1536]{1,0:T(8,128)(2,1)S(1)}, u32[]{:S(2)}, u32[]{:S(2)}) collective-permute-start(bf16[128,1536]{1,0:T(8,128)(2,1)} %get-tuple-element.377), channel_id=1, source_target_pairs={{0,1},{3,2},{4,5},{7,6},{8,9},{11,10},{12,13},{15,14},{16,17},{19,... | collective-permute-start | bytes 1179656 | tf_op jit(solution)/shard_map/ppermute | solution.py:807
  280.4 24.5 %collective-permute-start.34 = (bf16[128,1536]{1,0:T(8,128)(2,1)}, bf16[128,1536]{1,0:T(8,128)(2,1)S(1)}, u32[]{:S(2)}, u32[]{:S(2)}) collective-permute-start(bf16[128,1536]{1,0:T(8,128)(2,1)} %get-tuple-element.378), channel_id=1, source_target_pairs={{0,1},{3,2},{4,5},{7,6},{8,9},{11,10},{12,13},{15,14},{16,17},{19,... | collective-permute-start | bytes 1179656 | tf_op jit(solution)/shard_map/ppermute | solution.py:807
  308.5 13.3 %collective-permute-start.36 = (bf16[4,192,3584]{2,1,0:T(8,128)(2,1)}, bf16[4,192,3584]{2,1,0:T(8,128)(2,1)}, u32[]{:S(2)}, u32[]{:S(2)}) collective-permute-start(bf16[4,192,3584]{2,1,0:T(8,128)(2,1)} %get-tuple-element.347), channel_id=1, source_target_pairs={{0,4},{4,0},{8,12},{12,8},{16,20},{20,16},{24,28},{28,24},{1,5},{5... | collective-permute-start | bytes 16515080 | tf_op jit(solution)/shard_map/ppermute | solution.py:783
  308.5 13.3 %collective-permute-start.37 = (bf16[4,192,1792]{2,1,0:T(8,128)(2,1)}, bf16[4,192,1792]{2,1,0:T(8,128)(2,1)}, u32[]{:S(2)}, u32[]{:S(2)}) collective-permute-start(bf16[4,192,1792]{2,1,0:T(8,128)(2,1)} %get-tuple-element.349), channel_id=1, source_target_pairs={{0,4},{4,0},{8,12},{12,8},{16,20},{20,16},{24,28},{28,24},{1,5},{5... | collective-permute-start | bytes 8257544 | tf_op jit(solution)/shard_map/ppermute | solution.py:783
  309.0 22.1 %collective-permute-start.35 = (bf16[256,1536]{1,0:T(8,128)(2,1)S(1)}, bf16[256,1536]{1,0:T(8,128)(2,1)S(1)}, u32[]{:S(2)}, u32[]{:S(2)}) collective-permute-start(bf16[256,1536]{1,0:T(8,128)(2,1)S(1)} %get-tuple-element.345), channel_id=1, source_target_pairs={{0,1},{4,2},{1,0},{5,3},{6,7},{2,4},{7,6},{3,5},{8,9},{12,10},{9,8... | collective-permute-start | bytes 2359304 | tf_op jit(solution)/shard_map/ppermute | solution.py:821
  332.4 15.1 %collective-permute-start.39 = (bf16[256,1536]{1,0:T(8,128)(2,1)S(1)}, bf16[256,1536]{1,0:T(8,128)(2,1)S(1)}, u32[]{:S(2)}, u32[]{:S(2)}) collective-permute-start(bf16[256,1536]{1,0:T(8,128)(2,1)S(1)} %broadcast_select_fusion.1.refs_0_), channel_id=1, source_target_pairs={{0,4},{4,0},{8,12},{12,8},{16,20},{20,16},{24,28},{28,24},{1,5},{5... | collective-permute-start | bytes 2359304 | tf_op jit(solution)/shard_map/ppermute | solution.py:783
  332.5 15.0 %collective-permute-start.38 = (bf16[256,1536]{1,0:T(8,128)(2,1)S(1)}, bf16[256,1536]{1,0:T(8,128)(2,1)S(1)}, u32[]{:S(2)}, u32[]{:S(2)}) collective-permute-start(bf16[256,1536]{1,0:T(8,128)(2,1)S(1)} %collective-permute-done.35), channel_id=1, source_target_pairs={{4,5},{5,4},{2,3},{3,2},{12,13},{13,12},{10,11},{11,10},{20,21},{2... | collective-permute-start | bytes 2359304 | tf_op jit(solution)/shard_map/ppermute | solution.py:830
  333.4 14.2 %collective-permute-start.40 = (bf16[96,1536]{1,0:T(8,128)(2,1)S(1)}, bf16[96,1536]{1,0:T(8,128)(2,1)S(1)}, u32[]{:S(2)}, u32[]{:S(2)}) collective-permute-start(bf16[96,1536]{1,0:T(8,128)(2,1)S(1)} %slice.50), channel_id=1, source_target_pairs={{0,2},{2,0},{1,3},{3,1},{4,6},{6,4},{5,7},{7,5},{8,10},{10,8},{9,1... | collective-permute-start | bytes 884744 | tf_op jit(solution)/shard_map/ppermute | solution.py:791
  347.6 7.6 %collective-permute-start.41 = (bf16[256,1536]{1,0:T(8,128)(2,1)S(1)}, bf16[256,1536]{1,0:T(8,128)(2,1)}, u32[]{:S(2)}, u32[]{:S(2)}) collective-permute-start(bf16[256,1536]{1,0:T(8,128)(2,1)S(1)} %broadcast_select_fusion.refs_1_), channel_id=1, source_target_pairs={{0,4},{4,0},{8,12},{12,8},{16,20},{20,16},{24,28},{28,24},{1,5},{5... | collective-permute-start | bytes 2359304 | tf_op jit(solution)/shard_map/ppermute | solution.py:783
  353.9 40.4 %collective-permute-start.44 = (bf16[256,1536]{1,0:T(8,128)(2,1)S(1)}, bf16[256,1536]{1,0:T(8,128)(2,1)S(1)}, u32[]{:S(2)}, u32[]{:S(2)}) collective-permute-start(bf16[256,1536]{1,0:T(8,128)(2,1)S(1)} %pad_maximum_fusion.2), channel_id=1, source_target_pairs={{1,2},{2,1},{5,6},{6,5},{9,10},{10,9},{13,14},{14,13},{17,18},{18,... | collective-permute-start | bytes 2359304 | tf_op jit(solution)/shard_map/ppermute | solution.py:795
  363.9 35.0 %collective-permute-start.43 = (bf16[256,1536]{1,0:T(8,128)(2,1)}, bf16[256,1536]{1,0:T(8,128)(2,1)S(1)}, u32[]{:S(2)}, u32[]{:S(2)}) collective-permute-start(bf16[256,1536]{1,0:T(8,128)(2,1)} %get-tuple-element.376), channel_id=1, source_target_pairs={{0,1},{1,0},{2,3},{3,2},{4,5},{5,4},{6,7},{7,6},{8,9},{9,8},{10,11... | collective-permute-start | bytes 2359304 | tf_op jit(solution)/shard_map/ppermute | solution.py:787
  367.6 31.3 %collective-permute-start.42 = (bf16[160,1536]{1,0:T(8,128)(2,1)S(1)}, bf16[160,1536]{1,0:T(8,128)(2,1)S(1)}, u32[]{:S(2)}, u32[]{:S(2)}) collective-permute-start(bf16[160,1536]{1,0:T(8,128)(2,1)S(1)} %slice.51), channel_id=1, source_target_pairs={{0,2},{2,0},{1,3},{3,1},{4,6},{6,4},{5,7},{7,5},{8,10},{10,8},{9,1... | collective-permute-start | bytes 1474568 | tf_op jit(solution)/shard_map/ppermute | solution.py:791
  368.9 30.0 %collective-permute-start.45 = (bf16[2,192,384]{2,1,0:T(8,128)(2,1)}, bf16[2,192,384]{2,1,0:T(8,128)(2,1)S(1)}, u32[]{:S(2)}, u32[]{:S(2)}) collective-permute-start(bf16[2,192,384]{2,1,0:T(8,128)(2,1)} %get-tuple-element.380), channel_id=1, source_target_pairs={{0,8},{4,12},{8,0},{12,4},{16,24},{20,28},{24,16},{28,20},{1,9},{5... | collective-permute-start | bytes 884744 | tf_op jit(solution)/shard_map/ppermute | solution.py:888
  370.4 28.5 %collective-permute-start.46 = (bf16[2,192,384]{2,1,0:T(8,128)(2,1)}, bf16[2,192,384]{2,1,0:T(8,128)(2,1)S(1)}, u32[]{:S(2)}, u32[]{:S(2)}) collective-permute-start(bf16[2,192,384]{2,1,0:T(8,128)(2,1)} %get-tuple-element.382), channel_id=1, source_target_pairs={{0,16},{4,20},{8,24},{12,28},{16,0},{20,4},{24,8},{28,12},{1,17},{... | collective-permute-start | bytes 884744 | tf_op jit(solution)/shard_map/ppermute | solution.py:888
  400.0 6.4 %collective-permute-start.47 = (bf16[4,128,1536]{2,1,0:T(8,128)(2,1)}, bf16[4,128,1536]{2,1,0:T(8,128)(2,1)S(1)}, u32[]{:S(2)}, u32[]{:S(2)}) collective-permute-start(bf16[4,128,1536]{2,1,0:T(8,128)(2,1)} %get-tuple-element.386), channel_id=1, source_target_pairs={{0,4},{4,0},{8,12},{12,8},{16,20},{20,16},{24,28},{28,24},{1,5},{5... | collective-permute-start | bytes 4718600 | tf_op jit(solution)/shard_map/ppermute | solution.py:783
  408.7 12.3 %collective-permute-start.50 = (bf16[128,1536]{1,0:T(8,128)(2,1)}, bf16[128,1536]{1,0:T(8,128)(2,1)}, u32[]{:S(2)}, u32[]{:S(2)}) collective-permute-start(bf16[128,1536]{1,0:T(8,128)(2,1)} %get-tuple-element.477), channel_id=1, source_target_pairs={{0,1},{1,0},{2,3},{3,2},{4,5},{5,4},{6,7},{7,6},{8,9},{9,8},{10,11... | collective-permute-start | bytes 1179656 | tf_op jit(solution)/shard_map/ppermute | solution.py:787
  409.1 22.6 %collective-permute-start.48 = (bf16[2,192,640]{2,1,0:T(8,128)(2,1)}, bf16[2,192,640]{2,1,0:T(8,128)(2,1)}, u32[]{:S(2)}, u32[]{:S(2)}) collective-permute-start(bf16[2,192,640]{2,1,0:T(8,128)(2,1)} %get-tuple-element.400), channel_id=1, source_target_pairs={{0,8},{4,12},{8,0},{12,4},{16,24},{20,28},{24,16},{28,20},{1,9},{5... | collective-permute-start | bytes 1474568 | tf_op jit(solution)/shard_map/ppermute | solution.py:888
  410.6 21.1 %collective-permute-start.49 = (bf16[2,192,640]{2,1,0:T(8,128)(2,1)}, bf16[2,192,640]{2,1,0:T(8,128)(2,1)}, u32[]{:S(2)}, u32[]{:S(2)}) collective-permute-start(bf16[2,192,640]{2,1,0:T(8,128)(2,1)} %get-tuple-element.402), channel_id=1, source_target_pairs={{0,16},{4,20},{8,24},{12,28},{16,0},{20,4},{24,8},{28,12},{1,17},{... | collective-permute-start | bytes 1474568 | tf_op jit(solution)/shard_map/ppermute | solution.py:888
  411.4 14.9 %collective-permute-start.51 = (f32[3200]{0:T(1024)S(1)}, f32[3200]{0:T(1024)S(1)}, u32[]{:S(2)}, u32[]{:S(2)}) collective-permute-start(f32[3200]{0:T(1024)S(1)} %concatenate.70), channel_id=1, source_target_pairs={{0,4},{4,0},{8,12},{12,8},{16,20},{20,16},{24,28},{28,24},{1,5},{5... | collective-permute-start | bytes 38408 | tf_op jit(solution)/shard_map/ppermute | solution.py:888
  411.4 28.4 %collective-permute-start.54 = (bf16[128,1536]{1,0:T(8,128)(2,1)}, bf16[128,1536]{1,0:T(8,128)(2,1)S(1)}, u32[]{:S(2)}, u32[]{:S(2)}) collective-permute-start(bf16[128,1536]{1,0:T(8,128)(2,1)} %get-tuple-element.476), channel_id=1, source_target_pairs={{0,1},{1,0},{2,3},{3,2},{4,5},{5,4},{6,7},{7,6},{8,9},{9,8},{10,11... | collective-permute-start | bytes 1179656 | tf_op jit(solution)/shard_map/ppermute | solution.py:787
  422.9 24.3 %collective-permute-start.55 = (bf16[128,1536]{1,0:T(8,128)(2,1)}, bf16[128,1536]{1,0:T(8,128)(2,1)}, u32[]{:S(2)}, u32[]{:S(2)}) collective-permute-start(bf16[128,1536]{1,0:T(8,128)(2,1)} %fusion), channel_id=1, source_target_pairs={{0,2},{2,0},{1,3},{3,1},{4,6},{6,4},{5,7},{7,5},{8,10},{10,8},{9,1... | collective-permute-start | bytes 1179656 | tf_op jit(solution)/shard_map/ppermute | solution.py:791
  434.2 11.5 %collective-permute-start.52 = (bf16[192,640]{1,0:T(8,128)(2,1)}, bf16[192,640]{1,0:T(8,128)(2,1)}, u32[]{:S(2)}, u32[]{:S(2)}) collective-permute-start(bf16[192,640]{1,0:T(8,128)(2,1)} %get-tuple-element.415), channel_id=1, source_target_pairs={{0,16},{4,20},{8,24},{12,28},{16,0},{20,4},{24,8},{28,12},{1,17},{... | collective-permute-start | bytes 737288 | tf_op jit(solution)/shard_map/ppermute | solution.py:888
  435.8 11.4 %collective-permute-start.53 = (bf16[192,640]{1,0:T(8,128)(2,1)}, bf16[192,640]{1,0:T(8,128)(2,1)}, u32[]{:S(2)}, u32[]{:S(2)}) collective-permute-start(bf16[192,640]{1,0:T(8,128)(2,1)} %get-tuple-element.417), channel_id=1, source_target_pairs={{0,8},{4,12},{8,0},{12,4},{16,24},{20,28},{24,16},{28,20},{1,9},{5... | collective-permute-start | bytes 737288 | tf_op jit(solution)/shard_map/ppermute | solution.py:888
  438.3 11.1 %collective-permute-start.57 = (bf16[192,384]{1,0:T(8,128)(2,1)}, bf16[192,384]{1,0:T(8,128)(2,1)}, u32[]{:S(2)}, u32[]{:S(2)}) collective-permute-start(bf16[192,384]{1,0:T(8,128)(2,1)} %get-tuple-element.438), channel_id=1, source_target_pairs={{0,16},{4,20},{8,24},{12,28},{16,0},{20,4},{24,8},{28,12},{1,17},{... | collective-permute-start | bytes 442376 | tf_op jit(solution)/shard_map/ppermute | solution.py:888
  439.8 9.6 %collective-permute-start.58 = (bf16[192,384]{1,0:T(8,128)(2,1)}, bf16[192,384]{1,0:T(8,128)(2,1)}, u32[]{:S(2)}, u32[]{:S(2)}) collective-permute-start(bf16[192,384]{1,0:T(8,128)(2,1)} %get-tuple-element.440), channel_id=1, source_target_pairs={{0,8},{4,12},{8,0},{12,4},{16,24},{20,28},{24,16},{28,20},{1,9},{5... | collective-permute-start | bytes 442376 | tf_op jit(solution)/shard_map/ppermute | solution.py:888
  445.7 6.2 %collective-permute-start.62 = (f32[3200]{0:T(1024)S(1)}, f32[3200]{0:T(1024)}, u32[]{:S(2)}, u32[]{:S(2)}) collective-permute-start(f32[3200]{0:T(1024)S(1)} %add.230), channel_id=1, source_target_pairs={{0,8},{4,12},{8,0},{12,4},{16,24},{20,28},{24,16},{28,20},{1,9},{5... | collective-permute-start | bytes 38408 | tf_op jit(solution)/shard_map/ppermute | solution.py:888
  449.4 8.5 %collective-permute-start.56 = (bf16[192,640]{1,0:T(8,128)(2,1)}, bf16[192,640]{1,0:T(8,128)(2,1)S(1)}, u32[]{:S(2)}, u32[]{:S(2)}) collective-permute-start(bf16[192,640]{1,0:T(8,128)(2,1)} %get-tuple-element.436), channel_id=1, source_target_pairs={{0,4},{4,0},{8,12},{12,8},{16,20},{20,16},{24,28},{28,24},{1,5},{5... | collective-permute-start | bytes 737288 | tf_op jit(solution)/shard_map/ppermute | solution.py:783
  451.5 6.4 %collective-permute-start.59 = (bf16[192,384]{1,0:T(8,128)(2,1)}, bf16[192,384]{1,0:T(8,128)(2,1)S(1)}, u32[]{:S(2)}, u32[]{:S(2)}) collective-permute-start(bf16[192,384]{1,0:T(8,128)(2,1)} %get-tuple-element.445), channel_id=1, source_target_pairs={{0,4},{4,0},{8,12},{12,8},{16,20},{20,16},{24,28},{28,24},{1,5},{5... | collective-permute-start | bytes 442376 | tf_op jit(solution)/shard_map/ppermute | solution.py:783
  452.7 3.7 collective-permute-start.63
  454.4 10.4 %collective-permute-start.61 = (bf16[128,1536]{1,0:T(8,128)(2,1)S(1)}, bf16[128,1536]{1,0:T(8,128)(2,1)S(1)}, u32[]{:S(2)}, u32[]{:S(2)}) collective-permute-start(bf16[128,1536]{1,0:T(8,128)(2,1)S(1)} %fusion.4), channel_id=1, source_target_pairs={{0,4},{4,0},{8,12},{12,8},{16,20},{20,16},{24,28},{28,24},{1,5},{5... | collective-permute-start | bytes 1179656 | tf_op jit(solution)/shard_map/ppermute | solution.py:783
  456.4 4.8 collective-permute-start.64
  458.8 20.5 %collective-permute-start.60 = (bf16[192,1024]{1,0:T(8,128)(2,1)}, bf16[192,1024]{1,0:T(8,128)(2,1)S(1)}, u32[]{:S(2)}, u32[]{:S(2)}) collective-permute-start(bf16[192,1024]{1,0:T(8,128)(2,1)} %pad_maximum_fusion.6), channel_id=1, source_target_pairs={{0,2},{2,0},{1,3},{3,1},{4,6},{6,4},{5,7},{7,5},{8,10},{10,8},{9,1... | collective-permute-start | bytes 1179656 | tf_op jit(solution)/shard_map/ppermute | solution.py:791
  461.2 17.4 %collective-permute-start.65 = (f32[3200]{0:T(1024)S(1)}, f32[3200]{0:T(1024)S(1)}, u32[]{:S(2)}, u32[]{:S(2)}) collective-permute-start(f32[3200]{0:T(1024)S(1)} %add.249), channel_id=1, source_target_pairs={{0,2},{2,0},{1,3},{3,1},{4,6},{6,4},{5,7},{7,5},{8,10},{10,8},{9,1... | collective-permute-start | bytes 38408 | tf_op jit(solution)/shard_map/ppermute | solution.py:791
  (66 other events, 548.2 us)
Sparse Core Ops, SparseCore 0:
  76.1 91.9 all-gather.1
  331.3 100.2 reduce-scatter.1
